TPU v7x, 32 devices: a whole 2x2x4 slice. The times are simulated.
32 devices in a mesh: grp: 2 (over core), blk: 16 (over z, y, x).
Axes of the slice: x: 2, y: 2, z: 4, core: 2. Of those that a mesh axis runs over, the one named last changes fastest.
Arguments:
- cell_input: bfloat16 [2, 2, 1024, 1024], P('grp', None, 'blk'), may hold values from -6 to 6
- lengths: int32 [2, 2], P('grp'), may hold values from 256 to 1024, as said below
- noise_draw: float32 [1, 2, 2, 1024, 512], P(None, 'grp', None, 'blk'), may hold values from -5 to 5
- cotangent: bfloat16 [2, 2, 1024, 1024], P('grp', None, 'blk'), may hold values from -6 to 6
- w_qkv: bfloat16 [1, 1024, 3072], P(None, None, 'blk'), may hold values from -0.1875 to 0.1875
- w_out: bfloat16 [1, 1024, 1024], P(None, None, 'blk'), may hold values from -1 to 1
- w_ffn_in: bfloat16 [1, 1024, 4096], P(None, None, 'blk'), may hold values from -0.1875 to 0.1875
- w_ffn_out: bfloat16 [1, 4096, 1024], P(None, None, 'blk'), may hold values from -0.09375 to 0.09375
- w_latent: bfloat16 [1, 1024, 1024], P(None, None, 'blk'), may hold values from -0.0625 to 0.0625
- w_decode: bfloat16 [1, 512, 1024], P(None, None, 'blk'), may hold values from -0.125 to 0.125
- vectors: bfloat16 [1, 9, 1024], P(None, None, 'blk')
- inner_bias: bfloat16 [1, 5120], P(None, 'blk'), may hold values from -3 to 3
- prior_means: bfloat16 [1, 16, 512], P(None, None, 'blk'), may hold values from -3 to 3
- prior_logvars: bfloat16 [1, 16, 512], P(None, None, 'blk'), may hold values from 2 to 3
Outputs:
- layer_out: float32 [2, 2, 1024, 1024], P('grp', None, 'blk')
- grad_cells: float32 [2, 2, 1024, 1024], P('grp', None, 'blk')
- kl_mean: float32 [], replicated
- grad_qkv: float32 [1, 1024, 3072], P(None, None, 'blk')
- grad_out: float32 [1, 1024, 1024], P(None, None, 'blk')
- grad_ffn_in: float32 [1, 1024, 4096], P(None, None, 'blk')
- grad_ffn_out: float32 [1, 4096, 1024], P(None, None, 'blk')
- grad_latent: float32 [1, 1024, 1024], P(None, None, 'blk')
- grad_decode: float32 [1, 512, 1024], P(None, None, 'blk')
- grad_vectors: float32 [1, 9, 1024], P(None, None, 'blk')
- grad_inner: float32 [1, 5120], P(None, 'blk')
- grad_means: float32 [1, 16, 512], P(None, None, 'blk')
- grad_logvars: float32 [1, 16, 512], P(None, None, 'blk')
Inputs may be any that keep to these rules, and one draw needn't show every extreme that they name: In every group one slide has exactly 1024 cells; a slide's cells are the first lengths of its slot.
All inputs are finite; a program needn't handle non-finite values.
Results may differ from a plain program's by a relative error of at most 0.0085.
Values may be sent and summed in bfloat16 or wider, within the bound.
No kernel may reach another device: no remote copies, remote signals or barrier semaphores. Data moves between devices by JAX's collectives and lax.ppermute only.
A program may use at most 256 MiB of HBM per device.

v0:
```python
import functools
import math

import jax
import jax.numpy as jnp
import numpy as np
from jax import lax
from jax.experimental import pallas as pl
from jax.experimental.pallas import tpu as pltpu
from jax.sharding import Mesh
from jax.sharding import PartitionSpec as P

HEADS = 16
LAYERS = 1
HEAD_DIM = 64


EPS_NORM = 1e-05
MASKED = -1e30


def to_low(values):
    return values.astype(jnp.bfloat16)


def product(left, right):
    return jnp.dot(left, right, preferred_element_type=jnp.float32)


def product_tn(left, right):
    return lax.dot_general(
        left, right, (((0,), (0,)), ((), ())), preferred_element_type=jnp.float32
    )


def product_nt(left, right):
    return lax.dot_general(
        left, right, (((1,), (1,)), ((), ())), preferred_element_type=jnp.float32
    )


def layer_norm(values, norm_gain, norm_shift):
    centre = values - jnp.mean(values, axis=-1, keepdims=True)
    spread = jnp.mean(centre * centre, axis=-1, keepdims=True)
    return centre * lax.rsqrt(spread + EPS_NORM) * norm_gain + norm_shift


def mixture_kl(sample, noise_rows, logvar, mean_rows, logvars):
    own_term = jnp.sum(-0.5 * noise_rows * noise_rows - 0.5 * logvar, axis=-1)
    offset = sample[:, None, :] - mean_rows[None, :, :]
    component = jnp.sum(
        -0.5 * offset * offset * jnp.exp(-logvars)[None] - 0.5 * logvars[None], axis=-1
    ) - math.log(mean_rows.shape[0])
    row_peak = jnp.max(component, axis=-1, keepdims=True)
    mixture = row_peak[:, 0] + jnp.log(jnp.sum(jnp.exp(component - row_peak), axis=-1))
    return own_term - mixture


def bottleneck(latent, noise_rows, live_rows, mean_rows, logvars):
    lat_width = noise_rows.shape[-1]
    mean_part = latent[:, :lat_width]
    logvar = latent[:, lat_width:]
    sample = mean_part + jnp.exp(0.5 * logvar) * noise_rows
    per_cell = mixture_kl(sample, noise_rows, logvar, mean_rows, logvars)
    return (sample, jnp.sum(jnp.where(live_rows, per_cell, 0.0)) / lat_width)


def slot_scores(query_slots, keys_all, slide_len, score_scale):
    slot_count, query_rows, model_width = query_slots.shape
    heads_q = query_slots.reshape(slot_count, query_rows, HEADS, HEAD_DIM)
    heads_k = keys_all.reshape(slot_count, keys_all.shape[1], HEADS, HEAD_DIM)
    raw_scores = (
        jnp.einsum("sqhd,skhd->shqk", heads_q, heads_k, preferred_element_type=jnp.float32)
        * score_scale
    )
    live_keys = jnp.arange(keys_all.shape[1])[None, :] < slide_len[:, None]
    return jnp.where(live_keys[:, None, None, :], raw_scores, MASKED)


def widen(gathered):
    qkv_w, out_w, in_w, back_w, latent_w, decode_w, vec_rows, inner_rows, mean_rows, logvars = (
        gathered
    )
    return (
        qkv_w,
        out_w,
        in_w,
        back_w,
        latent_w,
        decode_w,
        vec_rows.astype(jnp.float32),
        inner_rows.astype(jnp.float32),
        mean_rows.astype(jnp.float32),
        logvars.astype(jnp.float32),
    )


def gather_weights(layer_parts):
    (
        part_qkv,
        part_out,
        part_in,
        part_back,
        part_latent,
        part_decode,
        part_vectors,
        part_inner,
        part_means,
        part_logvars,
    ) = layer_parts
    return widen(
        (
            lax.all_gather(part_qkv, "blk", axis=1, tiled=True),
            lax.all_gather(part_out, "blk", axis=1, tiled=True),
            lax.all_gather(part_in, "blk", axis=1, tiled=True),
            lax.all_gather(part_back, "blk", axis=1, tiled=True),
            lax.all_gather(part_latent, "blk", axis=1, tiled=True),
            lax.all_gather(part_decode, "blk", axis=1, tiled=True),
            lax.all_gather(part_vectors, "blk", axis=1, tiled=True),
            lax.all_gather(part_inner, "blk", axis=0, tiled=True),
            lax.all_gather(part_means, "blk", axis=1, tiled=True),
            lax.all_gather(part_logvars, "blk", axis=1, tiled=True),
        )
    )


def reduce_grads(grads):
    (
        grad_qkv_w,
        grad_out_w,
        grad_in_w,
        grad_back_w,
        grad_latent_w,
        grad_decode_w,
        grad_vec,
        grad_inner,
        grad_mean_rows,
        grad_logvars,
    ) = grads
    (
        shard_qkv,
        shard_out,
        shard_in,
        shard_back,
        shard_latent,
        shard_decode,
        shard_vec,
        shard_inner,
        shard_means,
        shard_logvars,
    ) = (
        lax.psum_scatter(grad_qkv_w, "blk", scatter_dimension=1, tiled=True),
        lax.psum_scatter(grad_out_w, "blk", scatter_dimension=1, tiled=True),
        lax.psum_scatter(grad_in_w, "blk", scatter_dimension=1, tiled=True),
        lax.psum_scatter(grad_back_w, "blk", scatter_dimension=1, tiled=True),
        lax.psum_scatter(grad_latent_w, "blk", scatter_dimension=1, tiled=True),
        lax.psum_scatter(grad_decode_w, "blk", scatter_dimension=1, tiled=True),
        lax.psum_scatter(grad_vec, "blk", scatter_dimension=1, tiled=True),
        lax.psum_scatter(grad_inner, "blk", scatter_dimension=0, tiled=True),
        lax.psum_scatter(grad_mean_rows, "blk", scatter_dimension=1, tiled=True),
        lax.psum_scatter(grad_logvars, "blk", scatter_dimension=1, tiled=True),
    )
    return lax.psum(
        (
            shard_qkv,
            shard_out,
            shard_in,
            shard_back,
            shard_latent,
            shard_decode,
            shard_vec,
            shard_inner,
            shard_means,
            shard_logvars,
        ),
        "grp",
    )


def layer_forward(hidden, full_weights, noise_rows, live_rows, slide_len, score_scale):
    qkv_w, out_w, in_w, back_w, latent_w, decode_w, vec_rows, inner_rows, mean_rows, logvars = (
        full_weights
    )
    model_width = hidden.shape[1]
    slot_count = slide_len.shape[0]
    slot_span = hidden.shape[0] // slot_count
    ff_width = in_w.shape[1]
    normed = to_low(layer_norm(hidden, vec_rows[0], vec_rows[1]))
    qkv_all = product(normed, qkv_w)
    query_low = to_low(qkv_all[:, :model_width] + vec_rows[2])
    keys_own = to_low(qkv_all[:, model_width : 2 * model_width])
    values_own = to_low(qkv_all[:, 2 * model_width :] + vec_rows[3])
    keys_all, values_all = (
        lax.all_gather(
            keys_own.reshape(slot_count, slot_span, model_width), "blk", axis=1, tiled=True
        ),
        lax.all_gather(
            values_own.reshape(slot_count, slot_span, model_width), "blk", axis=1, tiled=True
        ),
    )
    scores = slot_scores(
        query_low.reshape(slot_count, slot_span, model_width), keys_all, slide_len, score_scale
    )
    row_peak = jnp.max(scores, axis=-1, keepdims=True)
    weights = jnp.exp(scores - row_peak)
    totals = jnp.sum(weights, axis=-1, keepdims=True)
    probs_low = to_low(weights / totals)
    log_total = row_peak + jnp.log(totals)
    heads_v = values_all.reshape(slot_count, values_all.shape[1], HEADS, HEAD_DIM)
    mixed_f = jnp.einsum("shqk,skhd->sqhd", probs_low, heads_v, preferred_element_type=jnp.float32)
    mixed_low = to_low(mixed_f.reshape(slot_count * slot_span, model_width))
    attended = hidden + product(mixed_low, out_w) + vec_rows[4]
    normed_two = to_low(layer_norm(attended, vec_rows[5], vec_rows[6]))
    inner_act = product(normed_two, in_w) + inner_rows[:ff_width]
    activated = to_low(jax.nn.gelu(inner_act))
    fed_rows = attended + product(activated, back_w) + vec_rows[7]
    fed_low = to_low(fed_rows)
    latent = product(fed_low, latent_w) + inner_rows[ff_width:]
    sample, kl_part = bottleneck(latent, noise_rows, live_rows, mean_rows, logvars)
    sample_low = to_low(sample)
    output = fed_rows + product(sample_low, decode_w) + vec_rows[8]
    saved_state = (
        hidden,
        normed,
        query_low,
        keys_own,
        values_own,
        log_total,
        mixed_low,
        attended,
        normed_two,
        inner_act,
        activated,
        fed_low,
        latent,
        sample_low,
    )
    return (output, kl_part, saved_state)


def layer_backward(
    grad_out, full_weights, saved_state, noise_rows, live_rows, slide_len, score_scale
):
    qkv_w, out_w, in_w, back_w, latent_w, decode_w, vec_rows, inner_rows, mean_rows, logvars = (
        full_weights
    )
    (
        hidden,
        normed,
        query_low,
        keys_own,
        values_own,
        log_total,
        mixed_low,
        attended,
        normed_two,
        inner_act,
        activated,
        fed_low,
        latent,
        sample_low,
    ) = saved_state
    model_width = hidden.shape[1]
    row_total = hidden.shape[0]
    slot_count = slide_len.shape[0]
    slot_span = row_total // slot_count
    grad_dec_low = to_low(grad_out)
    grad_decode_w = product_tn(sample_low, grad_dec_low)
    grad_sample = product_nt(grad_dec_low, decode_w)

    def bottle(latent_in, means_in, logvars_in):
        return bottleneck(latent_in, noise_rows, live_rows, means_in, logvars_in)

    ignored, bottle_pull = jax.vjp(bottle, latent, mean_rows, logvars)
    grad_latent_f, grad_mean_rows, grad_logvars = bottle_pull(
        (grad_sample, jnp.ones((), jnp.float32))
    )
    grad_latent_low = to_low(grad_latent_f)
    grad_latent_w = product_tn(fed_low, grad_latent_low)
    grad_fed = grad_out + product_nt(grad_latent_low, latent_w)
    grad_fed_low = to_low(grad_fed)
    grad_back_w = product_tn(activated, grad_fed_low)
    grad_act = product_nt(grad_fed_low, back_w)
    ignored_two, gelu_pull = jax.vjp(jax.nn.gelu, inner_act)
    grad_inner_low = to_low(gelu_pull(grad_act)[0])
    grad_in_w = product_tn(normed_two, grad_inner_low)
    grad_normed_two = product_nt(grad_inner_low, in_w)
    ignored_three, second_pull = jax.vjp(layer_norm, attended, vec_rows[5], vec_rows[6])
    grad_att_norm, grad_gain_two, grad_shift_two = second_pull(grad_normed_two)
    grad_attended = grad_fed + grad_att_norm
    grad_proj_low = to_low(grad_attended)
    grad_out_w = product_tn(mixed_low, grad_proj_low)
    grad_mixed_low = to_low(product_nt(grad_proj_low, out_w))
    keys_all, values_all = (
        lax.all_gather(
            keys_own.reshape(slot_count, slot_span, model_width), "blk", axis=1, tiled=True
        ),
        lax.all_gather(
            values_own.reshape(slot_count, slot_span, model_width), "blk", axis=1, tiled=True
        ),
    )
    grad_mixed_heads = grad_mixed_low.reshape(slot_count, slot_span, HEADS, HEAD_DIM)
    heads_k = keys_all.reshape(slot_count, keys_all.shape[1], HEADS, HEAD_DIM)
    heads_v = values_all.reshape(slot_count, values_all.shape[1], HEADS, HEAD_DIM)
    scores = slot_scores(
        query_low.reshape(slot_count, slot_span, model_width), keys_all, slide_len, score_scale
    )
    probs_f = jnp.exp(scores - log_total)
    grad_probs = jnp.einsum(
        "sqhd,skhd->shqk", grad_mixed_heads, heads_v, preferred_element_type=jnp.float32
    )
    centre = jnp.sum(grad_probs * probs_f, axis=-1, keepdims=True)
    grad_scores_low = to_low(probs_f * (grad_probs - centre))
    grad_query = (
        jnp.einsum("shqk,skhd->sqhd", grad_scores_low, heads_k, preferred_element_type=jnp.float32)
        * score_scale
    )
    grad_query_low = to_low(grad_query.reshape(row_total, model_width))
    rows_all, mixed_all = (
        lax.all_gather(
            query_low.reshape(slot_count, slot_span, model_width), "blk", axis=1, tiled=True
        ),
        lax.all_gather(
            grad_mixed_low.reshape(slot_count, slot_span, model_width), "blk", axis=1, tiled=True
        ),
    )
    total_all, centre_all = (
        lax.all_gather(log_total, "blk", axis=2, tiled=True),
        lax.all_gather(centre, "blk", axis=2, tiled=True),
    )
    query_all = rows_all.reshape(slot_count, rows_all.shape[1], HEADS, HEAD_DIM)
    dmixed_all = mixed_all.reshape(slot_count, mixed_all.shape[1], HEADS, HEAD_DIM)
    own_keys = keys_own.reshape(slot_count, slot_span, HEADS, HEAD_DIM)
    own_values = values_own.reshape(slot_count, slot_span, HEADS, HEAD_DIM)
    own_raw = (
        jnp.einsum("sqhd,skhd->shqk", query_all, own_keys, preferred_element_type=jnp.float32)
        * score_scale
    )
    key_places = lax.axis_index("blk") * slot_span + jnp.arange(slot_span)
    live_own = key_places[None, :] < slide_len[:, None]
    own_scores = jnp.where(live_own[:, None, None, :], own_raw, MASKED)
    own_probs = jnp.exp(own_scores - total_all)
    own_dprobs = jnp.einsum(
        "sqhd,skhd->shqk", dmixed_all, own_values, preferred_element_type=jnp.float32
    )
    own_dscores = to_low(own_probs * (own_dprobs - centre_all))
    grad_keys = (
        jnp.einsum("shqk,sqhd->skhd", own_dscores, query_all, preferred_element_type=jnp.float32)
        * score_scale
    )
    grad_values = jnp.einsum(
        "shqk,sqhd->skhd", to_low(own_probs), dmixed_all, preferred_element_type=jnp.float32
    )
    grad_keys_low = to_low(grad_keys.reshape(row_total, model_width))
    grad_values_low = to_low(grad_values.reshape(row_total, model_width))
    grad_qkv_low = jnp.concatenate([grad_query_low, grad_keys_low, grad_values_low], axis=1)
    grad_qkv_w = product_tn(normed, grad_qkv_low)
    grad_normed = product_nt(grad_qkv_low, qkv_w)
    ignored_four, first_pull = jax.vjp(layer_norm, hidden, vec_rows[0], vec_rows[1])
    grad_hid_norm, grad_gain_one, grad_shift_one = first_pull(grad_normed)
    grad_hidden = grad_attended + grad_hid_norm
    grad_vec = jnp.stack(
        [
            grad_gain_one,
            grad_shift_one,
            jnp.sum(grad_query_low.astype(jnp.float32), axis=0),
            jnp.sum(grad_values_low.astype(jnp.float32), axis=0),
            jnp.sum(grad_attended, axis=0),
            grad_gain_two,
            grad_shift_two,
            jnp.sum(grad_fed, axis=0),
            jnp.sum(grad_out, axis=0),
        ]
    )
    grad_inner = jnp.concatenate(
        [
            jnp.sum(grad_inner_low.astype(jnp.float32), axis=0),
            jnp.sum(grad_latent_low.astype(jnp.float32), axis=0),
        ]
    )
    return (
        grad_hidden,
        (
            grad_qkv_w,
            grad_out_w,
            grad_in_w,
            grad_back_w,
            grad_latent_w,
            grad_decode_w,
            grad_vec,
            grad_inner,
            grad_mean_rows,
            grad_logvars,
        ),
    )


def per_device(
    cell_input,
    lengths,
    noise_draw,
    cotangent,
    w_qkv,
    w_out,
    w_ffn_in,
    w_ffn_out,
    w_latent,
    w_decode,
    vectors,
    inner_bias,
    prior_means,
    prior_logvars,
):
    slot_count = cell_input.shape[1]
    slot_span = cell_input.shape[2]
    model_width = cell_input.shape[3]
    row_total = slot_count * slot_span
    lat_width = noise_draw.shape[-1]
    cycle_size = lax.axis_size("blk")
    score_scale = 1.0 / math.sqrt(HEAD_DIM)
    slide_len = lengths[0]
    positions = lax.axis_index("blk") * slot_span + jnp.arange(slot_span)
    live_rows = (positions[None, :] < slide_len[:, None]).reshape(row_total)
    hidden = cell_input[0].reshape(row_total, model_width).astype(jnp.float32)
    stacks = (
        w_qkv,
        w_out,
        w_ffn_in,
        w_ffn_out,
        w_latent,
        w_decode,
        vectors,
        inner_bias,
        prior_means,
        prior_logvars,
    )
    layer_idx = 0
    full_weights = gather_weights([stacked[layer_idx] for stacked in stacks])
    kept_weights = [full_weights]
    hidden, kl_part, saved_state = layer_forward(
        hidden,
        full_weights,
        noise_draw[layer_idx, 0].reshape(row_total, lat_width),
        live_rows,
        slide_len,
        score_scale,
    )
    saved_layers = [saved_state]
    layer_out = hidden.reshape(1, slot_count, slot_span, model_width)
    kl_total = lax.psum(kl_part, ("grp", "blk"))
    kl_mean = kl_total / (lax.axis_size("grp") * cycle_size * row_total)
    grad_rows = cotangent[0].reshape(row_total, model_width).astype(jnp.float32)
    reduced = [None] * LAYERS
    for layer_idx in reversed(range(LAYERS)):
        full_weights = kept_weights[layer_idx]
        grad_rows, grads = layer_backward(
            grad_rows,
            full_weights,
            saved_layers[layer_idx],
            noise_draw[layer_idx, 0].reshape(row_total, lat_width),
            live_rows,
            slide_len,
            score_scale,
        )
        reduced[layer_idx] = reduce_grads(grads)
    grad_cells = grad_rows.reshape(1, slot_count, slot_span, model_width)
    stacked_grads = [jnp.stack([reduced[0][member]]) for member in range(10)]
    return (
        layer_out,
        grad_cells,
        kl_mean,
        stacked_grads[0],
        stacked_grads[1],
        stacked_grads[2],
        stacked_grads[3],
        stacked_grads[4],
        stacked_grads[5],
        stacked_grads[6],
        stacked_grads[7],
        stacked_grads[8],
        stacked_grads[9],
    )


EVERY = ("grp", "z", "y", "x")
CHIPS = ("z", "y", "x")
PLANE = ("grp", "y", "x")
PAIR = 2 * HEAD_DIM
SMALL = 16
VMEM_LIMIT = 20 * 1024 * 1024


def hop(values, axis, step=1):
    size = lax.axis_size(axis)
    return lax.ppermute(values, axis, [(i, i ^ step) for i in range(size)])


def other_core(values):
    return hop(values, "grp")


def after(values, done):
    return lax.optimization_barrier((values, done))[0]


def ordered(own, other, axis_name, axis):
    first = lax.axis_index(axis_name) == 0
    return jnp.concatenate(
        [jnp.where(first, own, other), jnp.where(first, other, own)], axis=axis
    )


def half_of(values, axis, axis_name, mine):
    part = values.shape[axis] // 2
    place = lax.axis_index(axis_name)
    place = place if mine else 1 - place
    return lax.dynamic_slice_in_dim(values, place * part, part, axis)


def flip(place, step):
    high = (place // 2 + step // 2) % 2
    low_bit = (place % 2 + step % 2) % 2
    return high * 2 + low_bit


def slide_routes(k):
    return [
        (g * 4 + z, (z // 2) * 4 + 2 * g + ((z % 2) ^ k)) for g in range(2) for z in range(4)
    ]


def pick_slot(slots, k):
    odd = (lax.axis_index("z") + k) % 2 == 1
    return jnp.where(odd, slots[1], slots[0])


def to_slides(slots):
    return jnp.stack(
        [lax.ppermute(pick_slot(slots, k), ("grp", "z"), slide_routes(k)) for k in range(2)]
    )


def from_slides(blocks):
    came = [
        lax.ppermute(
            blocks[k], ("grp", "z"), [(there, here) for here, there in slide_routes(k)]
        )
        for k in range(2)
    ]
    return jnp.stack([pick_slot(came, 0), pick_slot(came, 1)])


def head_routes(single, k):
    routes = []
    for core in range(2):
        for chip in range(16):
            odd = chip % 2
            block = 3 * chip + (2 - 2 * odd if single else odd)
            pair = (block % 16) // 2
            plane = 2 * core + (odd ^ k)
            target = (pair // 4) * 16 + plane * 4 + pair % 4
            routes.append((core * 16 + chip, target))
    return routes


ARRIVALS = [(single, k) for k in range(2) for single in (False, True)]


def low_shape(*shape):
    return jax.ShapeDtypeStruct(shape, jnp.bfloat16)


def wide(values):
    return values.astype(jnp.float32)


def z_hops(values):
    return [hop(values[step - 1], "z", step) for step in (1, 2, 3)]


def plane_hops(values):
    return [
        hop(values[0], "x"),
        hop(values[1], "y"),
        lax.ppermute(values[2], ("y", "x"), [(i, i ^ 3) for i in range(4)]),
    ]


NEAR = ((0, 0), (0, 1), (1, 0), (1, 1))


def z_at(step, part):
    return pl.ds(pl.multiple_of(flip(lax.axis_index("z"), step) * part, part), part)


def chip_place(step):
    return flip(lax.axis_index("y"), step[0]) * 2 + flip(lax.axis_index("x"), step[1])


def wide_shape(*shape):
    return jax.ShapeDtypeStruct(shape, jnp.float32)


def whole_call(body, operands, out_shapes, scratch=(), left_out=()):
    vmem = pl.BlockSpec(memory_space=pltpu.VMEM)
    specs = [
        pl.BlockSpec(memory_space=pltpu.HBM) if i in left_out else vmem
        for i in range(len(operands))
    ]
    return pl.pallas_call(
        body,
        out_shape=out_shapes,
        in_specs=specs,
        out_specs=[vmem] * len(out_shapes),
        scratch_shapes=list(scratch),
        compiler_params=pltpu.CompilerParams(vmem_limit_bytes=VMEM_LIMIT),
    )(*operands)


def enter_body(cells_ref, lens_ref, vectors_ref, inner_ref, means_ref, logvars_ref, *outs):
    span = cells_ref.shape[0] // 2
    lens = lens_ref[...]
    lens = jnp.concatenate([lens >> 5, lens & 31], axis=1).astype(jnp.float32)
    for k, ref in enumerate(outs):
        slot = (lax.axis_index("z") + k) % 2
        ref[:span] = cells_ref[pl.ds(pl.multiple_of(slot * span, span), span)]
        ref[span:] = jnp.zeros((SMALL, ref.shape[1]), jnp.bfloat16)
        ref[span : span + 9, 0:64] = vectors_ref[...]
        ref[span:, 128:160] = means_ref[...]
        ref[span:, 256:288] = logvars_ref[...]
        ref[span : span + 1, 384:704] = inner_ref[...]
        ref[span : span + 1, 768:772] = to_low(lens)


def chunk_place(block, step=(0, 0), core_step=0):
    core = flip(lax.axis_index("grp"), core_step)
    return pl.multiple_of(((block * 4 + chip_place(step)) * 2 + core) * 128, 128)


LAT_ROW, FF_ROW, LEN_ROW = 9, 10, 11


def unpack(small_ref, vec_ref, means_ref, logvars_ref, inner_ref):
    count = small_ref.shape[0]

    def lanes(row, rows, first, width):
        return jnp.concatenate(
            [wide(small_ref[i, row : row + rows, first : first + width]) for i in range(count)],
            axis=1,
        )

    vec_ref[...] = lanes(0, SMALL, 0, vec_ref.shape[1] // count)
    means_ref[...] = lanes(0, SMALL, 128, means_ref.shape[1] // count)
    logvars_ref[...] = lanes(0, SMALL, 256, means_ref.shape[1] // count)
    inner_ref[...] = lanes(0, 1, 384, inner_ref.shape[1] // count)
    width = vec_ref.shape[1]
    vec_ref[LAT_ROW : LAT_ROW + 1] = inner_ref[:, inner_ref.shape[1] - width :]
    for block in range(4):
        vec_ref[FF_ROW : FF_ROW + 1, block * 128 : block * 128 + 128] = inner_ref[
            :, pl.ds(chunk_place(block), 128)
        ]
    lens = wide(small_ref[0, 0:1, 768:896])
    even = lax.axis_index("z") % 2 == 0
    high = jnp.where(even, lens[:, 0:1], lens[:, 1:2])
    rest = jnp.where(even, lens[:, 2:3], lens[:, 3:4])
    vec_ref[LEN_ROW : LEN_ROW + 1] = jnp.broadcast_to(high * 32 + rest, (1, width))


def row_stats(values):
    centre = values - jnp.mean(values, axis=-1, keepdims=True)
    scale = lax.rsqrt(jnp.mean(centre * centre, axis=-1, keepdims=True) + EPS_NORM)
    return centre * scale, scale


def norm_back(grad, unit, scale, gain):
    inner = grad * gain
    along = jnp.mean(inner * unit, axis=-1, keepdims=True)
    return scale * (inner - jnp.mean(inner, axis=-1, keepdims=True) - unit * along)


def column_sum(values):
    return jnp.sum(values, axis=0, keepdims=True)


def slide_place(core, block, k, row, span):
    zi = lax.axis_index("z")
    chip = (core * 2 + ((zi + k) & 1)) * 4 + block
    return chip * span + row


def head_lanes(rows):
    return lax.broadcasted_iota(jnp.int32, (rows, PAIR), 1) < HEAD_DIM


def own_pair():
    place = (lax.axis_index("grp") * 2 + lax.axis_index("y")) * 2 + lax.axis_index("x")
    return pl.multiple_of(place * PAIR, PAIR)


def head_row(single, k):
    place = (lax.axis_index("grp") * 2 + lax.axis_index("y")) * 2 + lax.axis_index("x")
    parity = (lax.axis_index("z") + k) % 2
    row = 0
    for role in range(3):
        block = 16 * role + 2 * place
        split = (block % 3) // 2
        odd = (block // 3) % 2
        if single:
            here = split * PAIR * role + split * HEAD_DIM * ((odd + parity) % 2)
        else:
            here = (1 - split) * (1 - (odd + parity) % 2) * PAIR * role
        row = row + here
    return pl.multiple_of(row, HEAD_DIM)


def device_place(step, core_step):
    return flip(lax.axis_index("grp"), core_step) * 4 + chip_place(step)


def attend_body(own_ref, other_ref, *refs):
    came, rest = refs[:4], refs[4:]
    vec_ref, means_ref, logvars_ref, normed_ref, qkv_ref, head_w_ref = rest[:6]
    mixed_ref, lse_ref, bias_ref, small_ref, inner_ref = rest[6:]
    span = own_ref.shape[2] - SMALL
    for core_step, ref in enumerate((own_ref, other_ref)):
        for i, step in enumerate(NEAR):
            place = device_place(step, core_step)
            for k in range(2):
                chip = ((place // 4) * 2 + (lax.axis_index("z") + k) % 2) * 4 + place % 4
                small_ref[chip] = ref[i, k, span:]
    unpack(small_ref, vec_ref, means_ref, logvars_ref, inner_ref)
    for ref, (single, k) in zip(came, ARRIVALS):
        head_w_ref[pl.ds(head_row(single, k), ref.shape[0])] = ref[...]
    total_rows = normed_ref.shape[0]
    gain, shift = vec_ref[0:1], vec_ref[1:2]
    bias_q = vec_ref[2:3, pl.ds(own_pair(), PAIR)]
    bias_v = vec_ref[3:4, pl.ds(own_pair(), PAIR)]
    for core_step, ref in enumerate((own_ref, other_ref)):
        for i, step in enumerate(NEAR):
            cells = jnp.concatenate([ref[i, 0, :span], ref[i, 1, :span]])
            unit, _ = row_stats(wide(cells))
            at = device_place(step, core_step) * (2 * span)
            normed_ref[pl.ds(pl.multiple_of(at, 2 * span), 2 * span)] = to_low(unit * gain + shift)
    step = 256
    for start in range(0, total_rows, step):
        qkv = product_nt(normed_ref[start : start + step], head_w_ref[...])
        qkv_ref[start : start + step, :PAIR] = to_low(
            wide(to_low(qkv[:, :PAIR] + bias_q)) * HEAD_DIM**-0.5
        )
        qkv_ref[start : start + step, PAIR : 2 * PAIR] = to_low(qkv[:, PAIR : 2 * PAIR])
        qkv_ref[start : start + step, 2 * PAIR :] = to_low(qkv[:, 2 * PAIR :] + bias_v)
    lane = lax.broadcasted_iota(jnp.int32, (1, total_rows), 1)
    place = slide_place(
        lane // (8 * span), (lane // (2 * span)) & 3, (lane // span) & 1, lane & (span - 1), span
    )
    bias = jnp.where(place.astype(jnp.float32) < vec_ref[LEN_ROW : LEN_ROW + 1], 0.0, MASKED)
    bias_ref[...] = bias
    keys = qkv_ref[:, PAIR : 2 * PAIR]
    values = qkv_ref[:, 2 * PAIR :]
    first_head = head_lanes(step)
    for start in range(0, total_rows, step):
        query = qkv_ref[start : start + step, :PAIR]
        outs, totals = [], []
        for head in range(2):
            mine = first_head if head == 0 else jnp.logical_not(first_head)
            part = jnp.where(mine, query, jnp.zeros_like(query))
            scores = product_nt(part, keys) + bias
            peak = jnp.max(scores, axis=-1, keepdims=True)
            weights = jnp.exp(scores - peak)
            total = jnp.sum(weights, axis=-1, keepdims=True)
            outs.append(product(to_low(weights / total), values))
            totals.append(jnp.broadcast_to(peak + jnp.log(total), (step, PAIR)))
        mixed_ref[start : start + step] = to_low(jnp.where(first_head, outs[0], outs[1]))
        lse_ref[start : start + step] = jnp.where(first_head, totals[0], totals[1])


def attend(own, other, came, lat, inner):
    rows, width = 16 * (own.shape[2] - SMALL), own.shape[3]
    return whole_call(
        attend_body,
        (own, other, *came),
        [
            wide_shape(SMALL, width),
            wide_shape(SMALL, lat),
            wide_shape(SMALL, lat),
            low_shape(rows, width),
            low_shape(rows, 3 * PAIR),
            low_shape(3 * PAIR, width),
            low_shape(rows, PAIR),
            wide_shape(rows, PAIR),
            wide_shape(1, rows),
        ],
        [
            pltpu.VMEM((16, SMALL, width), jnp.bfloat16),
            pltpu.VMEM((1, inner), jnp.float32),
        ],
    )


def side_rows(ref, core_step, start, rows):
    first = flip(lax.axis_index("grp"), core_step) * (ref.shape[0] // 2) + start
    return ref[pl.ds(pl.multiple_of(first, rows), rows)]


def mix_far_body(mixed_ref, out_t_ref, far_ref):
    for start in range(0, far_ref.shape[0], 256):
        far_ref[start : start + 256] = to_low(
            product_nt(side_rows(mixed_ref, 1, start, 256), out_t_ref[...])
        )


def mix_near_body(mixed_ref, out_t_ref, came_ref, keep_ref, *sends):
    rows = keep_ref.shape[0]
    for i, step in enumerate(NEAR):
        first = chip_place(step) * rows
        came = came_ref[pl.ds(pl.multiple_of(first, rows), rows)]
        part = product_nt(side_rows(mixed_ref, 0, first, rows), out_t_ref[...]) + wide(came)
        if i == 0:
            keep_ref[...] = part
        else:
            sends[i - 1][...] = to_low(part)


def part_shapes(rows, width):
    return [wide_shape(rows, width)] + [low_shape(rows, width)] * 3


def mix_out(mixed, out_t, ready):
    rows, width = mixed.shape[0], out_t.shape[0]
    (far,) = whole_call(mix_far_body, (mixed, out_t), [low_shape(rows // 2, width)])
    keep, *sends = whole_call(
        mix_near_body, (mixed, out_t, after(other_core(far), ready)), part_shapes(rows // 8, width)
    )
    return keep, *plane_hops(sends)


def attend_back_body(
    qkv_ref,
    bias_ref,
    lse_ref,
    out_t_ref,
    head_w_ref,
    *refs,
):
    pieces, (dqkv_ref, far_ref, datt_ref) = refs[:8], refs[8:11]
    dmixed_ref, dk_ref, dv_ref, sems = refs[11:]
    rows = qkv_ref.shape[0]
    stack_rows(pieces, datt_ref, sems, lambda i: device_place(NEAR[i % 4], i // 4))
    for start in range(0, rows, 256):
        at = slice(start, start + 256)
        dmixed_ref[at] = to_low(product(datt_ref[at], out_t_ref[...]))
    keys = qkv_ref[:, PAIR : 2 * PAIR]
    values = qkv_ref[:, 2 * PAIR :]
    bias = bias_ref[...]
    step = 256
    first_head = head_lanes(step)
    for start in range(0, rows, step):
        query = qkv_ref[start : start + step, :PAIR]
        dmixed = dmixed_ref[start : start + step]
        dqueries = []
        for head in range(2):
            mine = first_head if head == 0 else jnp.logical_not(first_head)
            part = jnp.where(mine, query, jnp.zeros_like(query))
            dpart = jnp.where(mine, dmixed, jnp.zeros_like(dmixed))
            lse = lse_ref[start : start + step, head * HEAD_DIM : head * HEAD_DIM + 1]
            probs = jnp.exp(product_nt(part, keys) + bias - lse)
            dprobs = product_nt(dpart, values)
            centre = jnp.sum(dprobs * probs, axis=-1, keepdims=True)
            dscores = to_low(probs * (dprobs - centre))
            dqueries.append(product(dscores, keys))
            dkeys = product_tn(dscores, part)
            dvalues = product_tn(to_low(probs), dpart)
            if start == 0 and head == 0:
                dk_ref[...] = dkeys
                dv_ref[...] = dvalues
            else:
                dk_ref[...] += dkeys
                dv_ref[...] += dvalues
        dquery = jnp.where(first_head, dqueries[0], dqueries[1]) * (HEAD_DIM**-0.5)
        dqkv_ref[start : start + step, :PAIR] = to_low(dquery)
    dqkv_ref[:, PAIR : 2 * PAIR] = to_low(dk_ref[...])
    dqkv_ref[:, 2 * PAIR :] = to_low(dv_ref[...])
    for start in range(0, rows // 2, step):
        far_ref[start : start + step] = to_low(
            product(side_rows(dqkv_ref, 1, start, step), head_w_ref[...])
        )


def attend_back(qkv, bias, lse, out_t, head_w, pieces):
    rows, width = qkv.shape[0], head_w.shape[1]
    return whole_call(
        attend_back_body,
        (qkv, bias, lse, out_t, head_w, *pieces),
        [low_shape(rows, 3 * PAIR), low_shape(rows // 2, width), low_shape(rows, width)],
        [
            pltpu.VMEM((rows, PAIR), jnp.bfloat16),
            pltpu.VMEM((rows, PAIR), jnp.float32),
            pltpu.VMEM((rows, PAIR), jnp.float32),
            pltpu.SemaphoreType.DMA((8,)),
        ],
        range(5, 13),
    )


def dnormed_body(dqkv_ref, head_w_ref, came_ref, keep_ref, *sends):
    rows = keep_ref.shape[0]
    for i, step in enumerate(NEAR):
        first = chip_place(step) * rows
        came = came_ref[pl.ds(pl.multiple_of(first, rows), rows)]
        part = product(side_rows(dqkv_ref, 0, first, rows), head_w_ref[...]) + wide(came)
        if i == 0:
            keep_ref[...] = part
        else:
            sends[i - 1][...] = to_low(part)


def dnormed(dqkv, head_w, came):
    rows, width = dqkv.shape[0] // 8, head_w.shape[1]
    return whole_call(dnormed_body, (dqkv, head_w, came), part_shapes(rows, width))


def head_grad_body(dqkv_ref, normed_ref, *refs):
    homes, sums_ref, grad_w_ref = refs[:4], refs[4], refs[5]
    dqkv = dqkv_ref[...]
    sums_ref[...] = column_sum(wide(dqkv))
    grad_w_ref[...] = to_low(product_tn(dqkv, normed_ref[...]))
    for ref, (single, k) in zip(homes, ARRIVALS):
        ref[...] = grad_w_ref[pl.ds(head_row(single, k), ref.shape[0])]


def head_grads(dqkv, normed):
    width = normed.shape[1]
    outs = whole_call(
        head_grad_body,
        (dqkv, normed),
        [low_shape(HEAD_DIM if single else PAIR, width) for single, _ in ARRIVALS]
        + [wide_shape(1, 3 * PAIR)],
        [pltpu.VMEM((3 * PAIR, width), jnp.bfloat16)],
    )
    return outs[:4], outs[4]


def home_body(*refs):
    pair = wide(refs[0][...]) + wide(refs[2][...])
    single = wide(refs[1][...]) + wide(refs[3][...])
    odd = lax.axis_index("x") % 2
    refs[4][pl.ds(pl.multiple_of(odd * HEAD_DIM, HEAD_DIM), PAIR)] = pair
    refs[4][pl.ds(pl.multiple_of((1 - odd) * PAIR, HEAD_DIM), HEAD_DIM)] = single


LAT_LANES, DEC_LANES = slice(0, 512), slice(512, 768)


def project_body(
    keep_ref, came_x_ref, came_y_ref, came_far_ref, blocks_ref, vec_ref, attended_ref, normed_ref, hidden_ref
):
    span = blocks_ref.shape[1] - SMALL
    hidden = jnp.concatenate([blocks_ref[0, :span], blocks_ref[1, :span]])
    hidden_ref[...] = hidden
    parts = z_sum((keep_ref, came_x_ref, came_y_ref, came_far_ref))
    total = wide(hidden) + parts + vec_ref[4:5]
    attended_ref[...] = total
    unit, _ = row_stats(total)
    normed_ref[...] = to_low(unit * vec_ref[5:6] + vec_ref[6:7])


def project(parts, blocks, vec):
    shape = parts[0].shape
    return whole_call(
        project_body,
        (*parts, blocks, vec),
        [wide_shape(*shape), low_shape(*shape), low_shape(*shape)],
    )


GELU_SCALE = math.sqrt(2.0 / math.pi)
GELU_CUBE = 0.044715


def stack_rows(refs, target_ref, sems, order=None):
    rows = refs[0].shape[0]
    copies = []
    for i, ref in enumerate(refs):
        place = i if order is None else order(i)
        target = target_ref.at[pl.ds(pl.multiple_of(place * rows, rows), rows)]
        copies.append(pltpu.make_async_copy(ref, target, sems.at[i]))
    for copy in copies:
        copy.start()
    for copy in copies:
        copy.wait()


FF_STEP = 256


def load_all(rows_in, weights_ref, all_ref, in_ref, back_ref, sems):
    copies = []
    for i, ref in enumerate(rows_in):
        rows = ref.shape[0]
        copies.append((ref, all_ref.at[i * rows : (i + 1) * rows]))
    for z in range(4):
        part = weights_ref.at[z * 256 : z * 256 + 256]
        copies.append((part.at[:128], in_ref.at[z * 128 : (z + 1) * 128]))
        for half in range(2):
            at = z * 256 + half * 128
            copies.append(
                (part.at[128:, half * 512 : half * 512 + 512], back_ref.at[at : at + 128])
            )
    copies = [pltpu.make_async_copy(*copy, sems.at[i]) for i, copy in enumerate(copies)]
    for copy in copies:
        copy.start()
    for copy in copies:
        copy.wait()


def feed_scratch(rows, width, hidden):
    return [
        pltpu.VMEM((rows, width), jnp.bfloat16),
        pltpu.VMEM((hidden, width), jnp.bfloat16),
        pltpu.VMEM((width, hidden), jnp.bfloat16),
        pltpu.SemaphoreType.DMA((16,)),
    ]


def feed_body(*refs, last):
    rows_in, weights_ref, vec_ref, rest = refs[:4], refs[4], refs[5], list(refs[6:])
    came_ref = rest.pop(0) if last else None
    (act_ref, slope_ref), outs = rest[:2], rest[2:-4]
    all_ref, in_ref, back_ref, sems = rest[-4:]
    load_all(rows_in, weights_ref, all_ref, in_ref, back_ref, sems)
    bias = vec_ref[FF_ROW : FF_ROW + 1, : in_ref.shape[0]]
    step = rows_in[0].shape[0] * 2
    for start in range(0, all_ref.shape[0], step):
        at = slice(start, start + step)
        total = None
        for unit in range(0, in_ref.shape[0], FF_STEP):
            lanes = slice(unit, unit + FF_STEP)
            inner = product_nt(all_ref[at], in_ref[lanes]) + bias[:, lanes]
            square = inner * inner
            bend = jnp.tanh(GELU_SCALE * (inner + GELU_CUBE * (inner * square)))
            half = 0.5 * (1.0 + bend)
            act = to_low(inner * half)
            act_ref[at, lanes] = act
            slope_ref[at, lanes] = half + (0.5 * GELU_SCALE) * inner * (1.0 - bend * bend) * (
                1.0 + (3.0 * GELU_CUBE) * square
            )
            part = product_nt(act, back_ref[:, lanes])
            total = part if total is None else total + part
        put_parts(outs, came_ref, start, total)


def put_parts(outs, came_ref, start, total):
    if came_ref is None:
        outs[0][start : start + total.shape[0]] = to_low(total)
        return
    total = total + wide(came_ref[start : start + total.shape[0]])
    rows = outs[0].shape[0]
    for i in range(start // rows, (start + total.shape[0]) // rows):
        piece = total[i * rows - start : (i + 1) * rows - start]
        outs[i][...] = piece if i == 0 else to_low(piece)


def feed_call(body, pieces, weights, more, came, side_shapes):
    rows, width = pieces[0].shape
    last = came is not None
    operands = (*pieces, weights, *more) + ((came,) if last else ())
    outs = part_shapes(rows, width) if last else [low_shape(4 * rows, width)]
    return whole_call(
        functools.partial(body, last=last),
        operands,
        side_shapes + outs,
        feed_scratch(4 * rows, width, 512),
        range(5),
    )


def feed(pieces, weights, vec, came=None):
    count = 4 * pieces[0].shape[0]
    return feed_call(
        feed_body, pieces, weights, (vec,), came, [low_shape(count, 512), wide_shape(count, 512)]
    )


def feed_back_body(*refs, last):
    rows_in, weights_ref, slope_ref, rest = refs[:4], refs[4], refs[5], list(refs[6:])
    came_ref = rest.pop(0) if last else None
    (du_ref, sums_ref), outs = rest[:2], rest[2:-4]
    all_ref, in_ref, back_ref, sems = rest[-4:]
    load_all(rows_in, weights_ref, all_ref, in_ref, back_ref, sems)
    sums = [None] * (in_ref.shape[0] // FF_STEP)
    step = rows_in[0].shape[0] * 2
    for start in range(0, all_ref.shape[0], step):
        at = slice(start, start + step)
        total = None
        for i in range(len(sums)):
            lanes = slice(i * FF_STEP, (i + 1) * FF_STEP)
            du = to_low(product(all_ref[at], back_ref[:, lanes]) * slope_ref[at, lanes])
            du_ref[at, lanes] = du
            summed = column_sum(wide(du))
            sums[i] = summed if sums[i] is None else sums[i] + summed
            part = product(du, in_ref[lanes])
            total = part if total is None else total + part
        put_parts(outs, came_ref, start, total)
    for i, summed in enumerate(sums):
        sums_ref[:, i * FF_STEP : (i + 1) * FF_STEP] = summed


def feed_back(pieces, weights, slope, came=None):
    count = 4 * pieces[0].shape[0]
    return feed_call(
        feed_back_body, pieces, weights, (slope,), came, [low_shape(count, 512), wide_shape(1, 512)]
    )


def plane_rows(values):
    near = [values, *plane_hops([values] * 3)]
    return (*near, *(other_core(part) for part in near))


GRAD_ROWS = 512


def pair_grad_body(*refs):
    fed_in, two_in, whole_ref, halves = refs[:8], refs[8:16], refs[16], refs[17:21]
    out_ref, fed_ref, two_ref, act_ref, du_ref, sems = refs[21:]
    copies = []
    for pieces, target in ((fed_in, fed_ref), (two_in, two_ref), (halves[:2], act_ref), (halves[2:], du_ref)):
        rows = pieces[0].shape[0]
        for i, ref in enumerate(pieces):
            copies.append((ref, target.at[i * rows : (i + 1) * rows]))
    copies = [pltpu.make_async_copy(*copy, sems.at[i]) for i, copy in enumerate(copies)]
    for copy in copies:
        copy.start()
    for copy in copies:
        copy.wait()
    width = whole_ref.shape[1]
    for z in range(out_ref.shape[0] // GRAD_ROWS):
        at = z * GRAD_ROWS
        for lane in range(0, out_ref.shape[1], 512):
            lanes = slice(lane, lane + 512)
            out_ref[at : at + 128, lanes] = to_low(
                product_tn(du_ref[:, z * 128 : (z + 1) * 128], two_ref[:, lanes])
            )
        grad = to_low(product_tn(fed_ref[:, z * 256 : (z + 1) * 256], act_ref[...]))
        out_ref[at + 128 : at + 256] = jnp.concatenate([grad[:128], grad[128:]], axis=1)
        out_ref[at + 256 : at + GRAD_ROWS, :width] = whole_ref[z * 256 : (z + 1) * 256]
        out_ref[at + 256 : at + GRAD_ROWS, width:] = jnp.zeros(
            (256, out_ref.shape[1] - width), jnp.bfloat16
        )


def pair_grads(rows_fed, rows_two, whole, acts, dus):
    rows, width = rows_fed[0].shape
    hidden = acts[0].shape[1]
    return whole_call(
        pair_grad_body,
        (*rows_fed, *rows_two, whole, *acts, *dus),
        [low_shape(4 * GRAD_ROWS, width)],
        [pltpu.VMEM((8 * rows, width), jnp.bfloat16)] * 2
        + [pltpu.VMEM((8 * rows, hidden), jnp.bfloat16)] * 2
        + [pltpu.SemaphoreType.DMA((20,))],
        [*range(16), *range(17, 21)],
    )[0]


def split_grad_body(sum_ref, in_ref, *outs):
    in_ref[...] = wide(sum_ref[:128])
    rows, half = outs[0].shape[0], sum_ref.shape[1] // 2
    for i, step in enumerate(NEAR):
        place = chip_place(step)
        at = pl.ds(pl.multiple_of(128 + (place % 2) * rows, rows), rows)
        lanes = pl.ds(pl.multiple_of((place // 2) * half, half), half)
        outs[i][:, :half] = sum_ref[at, lanes]
        whole = pl.ds(pl.multiple_of(256 + place * rows, rows), rows)
        outs[i][:, half:] = sum_ref[whole, : outs[i].shape[1] - half]


def z_sum(refs):
    total = wide(refs[0][...])
    for ref in refs[1:]:
        total = total + wide(ref[...])
    return total


def pick_body(out_ref, back_ref, pairs_ref, *outs):
    for chip in range(16):
        pair = pl.multiple_of((lax.axis_index("grp") * 4 + chip % 4) * PAIR, PAIR)
        pairs_ref[chip] = out_ref[:, pl.ds(pair, PAIR)]
    for i, step in enumerate(NEAR):
        for block in range(4):
            outs[i][:, block * 128 : (block + 1) * 128] = back_ref[
                :, pl.ds(chunk_place(block, step), 128)
            ]


def lay_body(*refs):
    out_ref = refs[5]
    out_ref[:128] = refs[0][...]
    half = refs[1].shape[1]
    for i, step in enumerate(NEAR):
        place = chip_place(step)
        rows = pl.ds(pl.multiple_of(128 + (place % 2) * 64, 64), 64)
        out_ref[rows, pl.ds(pl.multiple_of((place // 2) * half, half), half)] = refs[1 + i][...]


def core_order(own, other):
    first = lax.axis_index("grp") == 0
    return jnp.concatenate(
        [jnp.where(first, own, other), jnp.where(first, other, own)], axis=1
    )


def core_halves(values):
    part = values.shape[1] // 2
    first = lax.axis_index("grp") == 0
    low_half, high_half = values[:, :part], values[:, part:]
    return (
        jnp.where(first, low_half, high_half),
        jnp.where(first, high_half, low_half),
    )


def halves_nt(values, own_ref, other_ref, lanes):
    own, other = core_halves(values)
    return product_nt(own, own_ref[:, lanes]) + product_nt(other, other_ref[:, lanes])


def bottle_body(
    attended_ref,
    keep_ref,
    came_x_ref,
    came_y_ref,
    came_far_ref,
    vec_ref,
    own_ref,
    other_ref,
    noise_ref,
    cot_ref,
    means_ref,
    logvars_ref,
    out_ref,
    fed_ref,
    sample_ref,
    dlat_ref,
    dfed_ref,
    dfed_low_ref,
    dmeans_ref,
    dlogvars_ref,
    sums_ref,
):
    rows, width = attended_ref.shape
    lat = noise_ref.shape[1]
    comps = means_ref.shape[0]
    parts = z_sum((keep_ref, came_x_ref, came_y_ref, came_far_ref))
    fed = attended_ref[...] + parts + vec_ref[7:8]
    fed_low = to_low(fed)
    fed_ref[...] = fed_low
    latent = halves_nt(fed_low, own_ref, other_ref, LAT_LANES) + vec_ref[LAT_ROW : LAT_ROW + 1]
    logvar = latent[:, lat:]
    noise = noise_ref[...]
    spread = jnp.exp(0.5 * logvar) * noise
    sample = latent[:, :lat] + spread
    sample_low = to_low(sample)
    sample_ref[...] = sample_low
    out_ref[...] = fed + halves_nt(sample_low, own_ref, other_ref, DEC_LANES) + vec_ref[8:9]
    cot = cot_ref[...]
    dsample = core_order(
        product(cot, own_ref[:, DEC_LANES]), product(cot, other_ref[:, DEC_LANES])
    )

    span = rows // 2
    row = lax.broadcasted_iota(jnp.int32, (rows, 1), 0)
    block = lax.axis_index("y") * 2 + lax.axis_index("x")
    place = slide_place(lax.axis_index("grp"), block, row // span, row & (span - 1), span)
    live = place.astype(jnp.float32) < vec_ref[LEN_ROW : LEN_ROW + 1, 0:1]
    share = jnp.where(live, 1.0 / lat, 0.0)
    own_term = jnp.sum(-0.5 * noise * noise - 0.5 * logvar, axis=-1, keepdims=True)
    logvars = logvars_ref[...]
    inverse = jnp.exp(-logvars)
    terms = []
    for c in range(comps):
        offset = sample - means_ref[c : c + 1]
        terms.append(
            jnp.sum(
                -0.5 * offset * offset * inverse[c : c + 1] - 0.5 * logvars[c : c + 1],
                axis=-1,
                keepdims=True,
            )
            - math.log(comps)
        )
    peak = terms[0]
    for term in terms[1:]:
        peak = jnp.maximum(peak, term)
    weights = [jnp.exp(term - peak) for term in terms]
    total = weights[0]
    for weight in weights[1:]:
        total = total + weight
    kl_cell = own_term - (peak + jnp.log(total))
    kl = jnp.sum(jnp.where(live, kl_cell, 0.0), axis=0, keepdims=True) / lat
    scale = share / total
    for c in range(comps):
        offset = sample - means_ref[c : c + 1]
        slope = offset * inverse[c : c + 1]
        part = weights[c] * scale
        pull = part * slope
        dsample = dsample + pull
        dmeans_ref[c : c + 1] = -column_sum(pull)
        dlogvars_ref[c : c + 1] = column_sum(0.5 * part - 0.5 * (pull * offset))
    dlat = jnp.concatenate([dsample, 0.5 * dsample * spread - 0.5 * share], axis=1)
    dlat_low = to_low(dlat)
    dlat_ref[...] = dlat_low
    grad_out = wide(cot)
    dfed = grad_out + core_order(
        product(dlat_low, own_ref[:, LAT_LANES]), product(dlat_low, other_ref[:, LAT_LANES])
    )
    dfed_ref[...] = dfed
    dfed_low_ref[...] = to_low(dfed)
    sums_ref[...] = jnp.concatenate(
        [
            column_sum(wide(dlat_low)),
            column_sum(dfed),
            column_sum(grad_out),
            jnp.broadcast_to(kl, (1, width)),
            jnp.zeros((4, width), jnp.float32),
        ]
    )


def bottle_call(attended, parts, vec, weights, noise, cot, means, logvars):
    rows, width = attended.shape
    lat = noise.shape[1]
    return whole_call(
        bottle_body,
        (attended, *parts, vec, *weights, noise, cot, means, logvars),
        [
            wide_shape(rows, width),
            low_shape(rows, width),
            low_shape(rows, lat),
            low_shape(rows, width),
            wide_shape(rows, width),
            low_shape(rows, width),
            wide_shape(*means.shape),
            wide_shape(*means.shape),
            wide_shape(8, width),
        ],
    )


def project_back_body(
    keep_ref,
    came_x_ref,
    came_y_ref,
    came_far_ref,
    attended_ref,
    dfed_ref,
    vec_ref,
    datt_ref,
    datt_low_ref,
    sums_ref,
):
    grad = z_sum((keep_ref, came_x_ref, came_y_ref, came_far_ref))
    unit, scale = row_stats(attended_ref[...])
    datt = dfed_ref[...] + norm_back(grad, unit, scale, vec_ref[5:6])
    datt_ref[...] = datt
    datt_low_ref[...] = to_low(datt)
    sums_ref[...] = jnp.concatenate(
        [
            column_sum(grad * unit),
            column_sum(grad),
            column_sum(datt),
            jnp.zeros((5, datt.shape[1]), jnp.float32),
        ]
    )


def project_back(parts, attended, dfed, vec):
    rows, width = attended.shape
    return whole_call(
        project_back_body,
        (*parts, attended, dfed, vec),
        [wide_shape(rows, width), low_shape(rows, width), wide_shape(8, width)],
    )


def whole_grads_body(*refs):
    out_ref = refs[-1]
    for lanes, (left, left_other, right, right_other) in (
        (LAT_LANES, refs[:4]),
        (DEC_LANES, refs[4:8]),
    ):
        grads = jnp.concatenate([left[...], left_other[...]])
        values = jnp.concatenate([core_halves(right[...])[0], core_halves(right_other[...])[0]])
        out_ref[:, lanes] = to_low(product_tn(grads, values))


def whole_grads(pairs):
    operands = []
    for values in pairs:
        operands += [values, other_core(values)]
    width = pairs[0].shape[1]
    return whole_call(whole_grads_body, operands, [low_shape(width, DEC_LANES.stop)])[0]


def sum_body(*refs):
    refs[-1][...] = z_sum(refs[:-1])


def last_grad_body(*refs):
    out_ref, wholes = refs[8], refs[9:]
    half = out_ref.shape[1] // 8
    for i, ref in enumerate(refs[:8]):
        for block in range(4):
            place = chunk_place(block, NEAR[i % 4], i // 4)
            out_ref[:, pl.ds(place, 128)] = wide(ref[:, block * 128 : (block + 1) * 128])
    for core in range(2):
        wholes[core][...] = z_sum([ref.at[:, half:] for ref in refs[core * 4 : core * 4 + 4]])


def cells_back_body(
    keep_ref,
    came_x_ref,
    came_y_ref,
    came_far_ref,
    hidden_ref,
    datt_ref,
    vec_ref,
    bottle_sums_ref,
    project_sums_ref,
    head_sums_ref,
    ff_sums_ref,
    ff_more_ref,
    dmeans_ref,
    dlogvars_ref,
    out_grad_ref,
    grad_ref,
    packed_ref,
    inner_ref,
    rows_ref,
):
    grad = z_sum((keep_ref, came_x_ref, came_y_ref, came_far_ref))
    unit, scale = row_stats(wide(hidden_ref[...]))
    grad_ref[...] = datt_ref[...] + norm_back(grad, unit, scale, vec_ref[0:1])
    width = grad.shape[1]
    count = packed_ref.shape[0]
    inner_ref[...] = jnp.zeros_like(inner_ref)
    for block in range(4):
        lanes = slice(block * 128, block * 128 + 128)
        inner_ref[:, pl.ds(chunk_place(block), 128)] = (
            ff_sums_ref[:, lanes] + ff_more_ref[:, lanes]
        )
    inner_ref[:, inner_ref.shape[1] - width :] = bottle_sums_ref[0:1]
    rows_ref[...] = jnp.zeros_like(rows_ref)
    rows_ref[0:1] = column_sum(grad * unit)
    rows_ref[1:2] = column_sum(grad)
    rows_ref[2:3, pl.ds(own_pair(), PAIR)] = head_sums_ref[:, :PAIR]
    rows_ref[3:4, pl.ds(own_pair(), PAIR)] = head_sums_ref[:, 2 * PAIR :]
    rows_ref[4:5] = project_sums_ref[2:3]
    rows_ref[5:7] = project_sums_ref[0:2]
    rows_ref[7:9] = bottle_sums_ref[1:3]
    part = width // count
    pieces = inner_ref.shape[1] // width
    for i in range(pieces):
        rows_ref[9 + i : 10 + i] = jnp.concatenate(
            [
                inner_ref[:, (b * pieces + i) * part : (b * pieces + i + 1) * part]
                for b in range(count)
            ],
            axis=1,
        )
    rows_ref[14:15] = bottle_sums_ref[3:4]
    lat_part = dmeans_ref.shape[1] // count
    for b in range(count):
        sums = jnp.concatenate(
            [
                rows_ref[:, b * part : (b + 1) * part],
                dmeans_ref[:, b * lat_part : (b + 1) * lat_part],
                dlogvars_ref[:, b * lat_part : (b + 1) * lat_part],
            ],
            axis=1,
        )
        high = to_low(sums)
        packed_ref[b, :part] = out_grad_ref[b]
        packed_ref[b, part : part + SMALL] = high
        packed_ref[b, part + SMALL :] = to_low(sums - wide(high))


def last_sum_body(came_ref, out_ref):
    count, rows = came_ref.shape[0], came_ref.shape[1] - 2 * SMALL
    for chip in range(4):
        total = z_sum([came_ref.at[z * 4 + chip, :rows] for z in range(4)])
        out_ref[:rows, chip * PAIR : (chip + 1) * PAIR] = total
    small = z_sum([came_ref.at[i, rows : rows + SMALL] for i in range(count)])
    rest = z_sum([came_ref.at[i, rows + SMALL :] for i in range(count)])
    out_ref[rows:] = jnp.zeros((SMALL, out_ref.shape[1]), jnp.float32)
    out_ref[rows:, :PAIR] = small + rest


def last_body(own_ref, other_ref, grad_ref, small_ref):
    rows, half = grad_ref.shape[0], own_ref.shape[1]
    for ref, place in ((own_ref, 0), (other_ref, 1)):
        core = flip(lax.axis_index("grp"), place)
        grad_ref[:, pl.ds(pl.multiple_of(core * half, half), half)] = ref[:rows]
    small_ref[...] = own_ref[rows:, :PAIR] + other_ref[rows:, :PAIR]


def cells_back(operands, inner):
    rows, width = operands[0].shape
    return whole_call(
        cells_back_body,
        operands,
        [wide_shape(rows, width), low_shape(16, width // 16 + 2 * SMALL, PAIR)],
        [pltpu.VMEM((1, inner), jnp.float32), pltpu.VMEM((SMALL, width), jnp.float32)],
    )


def exchange(blocks, axes):
    return lax.all_to_all(blocks, axes, split_axis=0, concat_axis=0, tiled=True)


def to_all(values, count):
    return jnp.broadcast_to(values[None], (count, *values.shape))


def fast_device(
    cell_input,
    lengths,
    noise_draw,
    cotangent,
    w_qkv,
    w_out,
    w_ffn_in,
    w_ffn_out,
    w_latent,
    w_decode,
    vectors,
    inner_bias,
    prior_means,
    prior_logvars,
):
    slots, span, width = cell_input.shape[1:]
    rows = slots * span
    lat = noise_draw.shape[-1]
    comps = prior_means.shape[1]
    ff = w_ffn_out.shape[1]
    inner = 16 * inner_bias.shape[1]

    blocks = whole_call(
        enter_body,
        (
            cell_input.reshape(rows, width),
            lengths,
            vectors[0],
            inner_bias,
            prior_means[0],
            prior_logvars[0],
        ),
        [low_shape(span + SMALL, width)] * 2,
    )
    first = jnp.stack(
        [lax.ppermute(blocks[k], ("grp", "z"), slide_routes(k)) for k in range(2)]
    )

    qkv_t = w_qkv[0].T
    at_x = lax.axis_index("x") % 2
    head_parts = (
        lax.dynamic_slice_in_dim(qkv_t, at_x * HEAD_DIM, PAIR),
        lax.dynamic_slice_in_dim(qkv_t, (1 - at_x) * PAIR, HEAD_DIM),
    )
    came = [
        lax.ppermute(head_parts[int(single)], EVERY, head_routes(single, k))
        for single, k in ARRIVALS
    ]
    plane_near = jnp.stack([first, hop(first, "x")])
    plane_own = jnp.concatenate([plane_near, hop(after(plane_near, came), "y")])
    plane_other = other_core(plane_own)

    part = width // 16
    out_pairs, *back_cols = whole_call(
        pick_body,
        (w_out[0].T, w_ffn_out[0].T),
        [low_shape(16, part, PAIR)] + [low_shape(part, ff // 8)] * 4,
    )
    out_t = exchange(after(out_pairs, first), CHIPS).reshape(width, PAIR)
    in_own = half_of(w_ffn_in[0], 1, "grp", True).T
    back_cols = (back_cols[0], *plane_hops(after(back_cols[1:], plane_near)))
    (pair_own,) = whole_call(lay_body, (in_own, *back_cols), [low_shape(256, width)])

    shard = jnp.concatenate(
        [half_of(w[0], 0, "grp", True).T for w in (w_latent, w_decode)], axis=1
    )
    shard_width = shard.shape[1]
    whole = lax.all_gather(shard, CHIPS, axis=0, tiled=True)
    pair_w = lax.all_gather(after(pair_own, came), "z", axis=0, tiled=True)

    vec, means, logvars, normed, qkv, head_w, mixed, lse, bias = attend(
        plane_own, plane_other, after(came, pair_own), lat, inner
    )
    mix_parts = mix_out(mixed, out_t, out_t)

    noise_high = to_low(noise_draw[0, 0])
    noise_rest = to_low(noise_draw[0, 0] - wide(noise_high))
    extra = jnp.concatenate(
        [cotangent[0], jnp.concatenate([noise_high, noise_rest], axis=2)], axis=1
    )
    extra = to_slides(after(extra, mixed))
    cot = extra[:, :span].reshape(rows, width)
    noise = extra[:, span:].reshape(rows, width)
    noise = wide(noise[:, :lat]) + wide(noise[:, lat:])

    attended, normed_two, hidden = project(mix_parts, first, vec)
    rows_two = plane_rows(normed_two)
    whole = after(whole, rows_two)
    wholes = (whole, other_core(whole))
    act_far, slope_far, fed_far = feed(rows_two[4:], pair_w, vec)
    act, slope, keep, *sends = feed(rows_two[:4], pair_w, vec, other_core(fed_far))
    fed_parts = (keep, *plane_hops(sends))
    output, fed_low, sample_low, dlat_low, dfed, dfed_low, dmeans, dlogvars, bottle_sums = (
        bottle_call(
            attended, fed_parts, vec, wholes, noise, cot, means, logvars
        )
    )

    rows_fed = plane_rows(dfed_low)
    layer_out = from_slides(after(output, rows_fed).reshape(slots, span, width))
    whole_grad = whole_grads((dlat_low, fed_low, cot, sample_low))
    du_far, ff_far, norm_far = feed_back(rows_fed[4:], pair_w, slope_far)
    du, ff_sums, keep, *sends = feed_back(
        rows_fed[:4], pair_w, slope, after(other_core(norm_far), whole_grad)
    )
    norm_parts = (keep, *plane_hops(sends))
    grads = pair_grads(rows_fed, rows_two, whole_grad, (act, act_far), (du, du_far))
    grads_sum = lax.psum_scatter(grads, "z", scatter_dimension=0, tiled=True)
    datt, datt_low, project_sums = project_back(after(norm_parts, grads), attended, dfed, vec)
    rows_datt = plane_rows(datt_low)
    dqkv, dn_far, all_datt = attend_back(qkv, bias, lse, out_t, head_w, rows_datt)
    dn_keep, *dn_sends = dnormed(dqkv, head_w, other_core(dn_far))
    homes, head_sums = head_grads(dqkv, after(normed, dn_sends))
    dn_parts = (dn_keep, *plane_hops(dn_sends))
    grad_rows, packed = cells_back(
        (
            *dn_parts,
            hidden,
            datt,
            vec,
            bottle_sums,
            project_sums,
            head_sums,
            ff_sums,
            ff_far,
            dmeans,
            dlogvars,
            to_low(product_tn(all_datt, mixed)).reshape(16, part, PAIR),
        ),
        inner,
    )
    grad_cells = from_slides(grad_rows.reshape(slots, span, width))
    sum_in, *sums = whole_call(
        split_grad_body,
        (after(grads_sum, dn_parts),),
        [wide_shape(128, width)] + [low_shape(part, ff // 8 + shard_width)] * 4,
    )
    sums = [sums[0], *plane_hops(sums[1:])]
    sums += [other_core(total) for total in sums]

    homes = [
        lax.ppermute(grad, EVERY, [(there, here) for here, there in head_routes(single, k)])
        for grad, (single, k) in zip(homes, ARRIVALS)
    ]
    (home,) = whole_call(home_body, homes, [wide_shape(3 * HEAD_DIM, width)])
    grad_qkv = (home + other_core(home)).T

    (last,) = whole_call(
        last_sum_body, (exchange(packed, CHIPS),), [wide_shape(part + SMALL, 4 * PAIR)]
    )
    grad_out_w, small_sums = whole_call(
        last_body, (last, other_core(last)), [wide_shape(part, width), wide_shape(SMALL, PAIR)]
    )
    grad_out_w = grad_out_w.T
    vec_out = small_sums[:9, :part]
    inner_out = small_sums[9 : 9 + inner // width, :part].reshape(1, -1)
    means_out = small_sums[:, part : part + lat // 16]
    logvars_out = small_sums[:, part + lat // 16 :]
    kl_mean = small_sums[14, 0] / (32 * rows)

    grad_in_w = ordered(sum_in.T, other_core(sum_in).T, "grp", 1)
    grad_back_w, whole_own, whole_other = whole_call(
        last_grad_body,
        sums,
        [wide_shape(part, ff)] + [wide_shape(part, shard_width)] * 2,
    )
    grad_back_w = grad_back_w.T
    grad_lat_w, grad_dec_w = (
        ordered(whole_own[:, lanes].T, whole_other[:, lanes].T, "grp", 0)
        for lanes in (LAT_LANES, DEC_LANES)
    )
    return (
        layer_out.reshape(1, slots, span, width),
        grad_cells.reshape(1, slots, span, width),
        kl_mean,
        grad_qkv[None],
        grad_out_w[None],
        grad_in_w[None],
        grad_back_w[None],
        grad_lat_w[None],
        grad_dec_w[None],
        vec_out[None],
        inner_out,
        means_out[None],
        logvars_out[None],
    )


def solution(mesh):
    chips = mesh.shape["blk"]
    if (mesh.shape["grp"], chips) == (2, HEADS):
        mesh = Mesh(mesh.devices.reshape(2, chips // 4, 2, 2), EVERY)
        blk, run = CHIPS, fast_device
    else:
        blk, run = "blk", per_device
    cells = P("grp", None, blk, None)
    columns = P(None, None, blk)
    return jax.shard_map(
        run,
        mesh=mesh,
        in_specs=(cells, P("grp", None), P(None, "grp", None, blk, None), cells)
        + (columns,) * 7
        + (P(None, blk), columns, columns),
        out_specs=(cells, cells, P()) + (columns,) * 7 + (P(None, blk), columns, columns),
        check_vma=False,
    )
```

profile of v0, /device:TPU:0, one launch (start us, length us, event | category | flops | bytes accessed | tf_op | source)
XLA Modules:
  0.0 377.5 jit_solution(14816911513057833089)
XLA Ops:
  14.8 3.1 collective-permute-start.1
  17.9 3.3 collective-permute-done.1
  21.2 2.0 collective-permute-start.2
  23.9 9.0 %collective-permute-start.5 = (bf16[128,1024]{1,0:T(8,128)(2,1)S(1)}, bf16[128,1024]{1,0:T(8,128)(2,1)S(1)}, u32[]{:S(2)}, u32[]{:S(2)}) collective-permute-start(bf16[128,1024]{1,0:T(8,128)(2,1)S(1)} %dynamic-slice_bitcast_fusion), channel_id=1, source_target_pairs={{0,4},{1,2},{2,7},{3,17},{4,22},{5,0},{6,5},{7,3},{8,20},{9,18},{1... | collective-permute-start | bytes 786440 | tf_op jit(solution)/shard_map/ppermute | solution.py:1570
  33.0 6.7 %collective-permute-start.6 = (bf16[64,1024]{1,0:T(8,128)(2,1)S(1)}, bf16[64,1024]{1,0:T(8,128)(2,1)S(1)}, u32[]{:S(2)}, u32[]{:S(2)}) collective-permute-start(bf16[64,1024]{1,0:T(8,128)(2,1)S(1)} %dynamic-slice_bitcast_fusion.1), channel_id=1, source_target_pairs={{0,5},{1,1},{2,20},{3,16},{4,23},{5,19},{6,6},{7,2},{8,21},{9,17},... | collective-permute-start | bytes 393224 | tf_op jit(solution)/shard_map/ppermute | solution.py:1570
  39.8 16.7 %collective-permute-done.4.refs_1_ = bf16[64,1024]{1,0:T(8,128)(2,1)S(1)} collective-permute-done((bf16[64,1024]{1,0:T(8,128)(2,1)S(1)}, bf16[64,1024]{1,0:T(8,128)(2,1)S(1)}, u32[]{:S(2)}, u32[]{:S(2)}) %collective-permute-start.4) | collective-permute-done | bytes 131104 | tf_op jit(solution)/shard_map/ppermute | solution.py:1570
  56.5 3.1 collective-permute-done.6.refs_3_
  60.3 18.8 %collective-permute-done.7 = bf16[2,2,80,1024]{3,2,1,0:T(8,128)(2,1)S(1)} collective-permute-done((bf16[2,2,80,1024]{3,2,1,0:T(8,128)(2,1)S(1)}, bf16[2,2,80,1024]{3,2,1,0:T(8,128)(2,1)S(1)}, u32[]{:S(2)}, u32[]{:S(2)}) %collective-permute-start.7) | collective-permute-done | bytes 655392 | tf_op jit(solution)/shard_map/ppermute | solution.py:495
  83.9 1.4 collective-permute-start.11
  87.8 2.1 collective-permute-done.11.refs_4_
  91.3 5.2 %all-to-all-start = ((bf16[16,64,128]{2,1,0:T(8,128)(2,1)}), bf16[16,64,128]{2,1,0:T(8,128)(2,1)S(1)}, u32[]{:S(2)}, u32[]{:S(2)}) async-start(bf16[16,64,128]{2,1,0:T(8,128)(2,1)} %get-tuple-element.127), calls=%async_computation | async-start | bytes 524288 | tf_op jit(solution)/shard_map/all_to_all | solution.py:1517
  98.6 9.9 %shard_map.240 = (f32[16,1024]{1,0:T(8,128)S(1)}, f32[16,512]{1,0:T(8,128)S(1)}, f32[16,512]{1,0:T(8,128)S(1)}, bf16[1024,1024]{1,0:T(8,128)(2,1)S(1)}, bf16[102...) custom-call(bf16[4,2,80,1024]{3,2,1,0:T(8,128)(2,1)S(1)} %pad_maximu, ...), custom_call_target="tpu_custom_call" | custom-call | tf_op jit(solution)/shard_map/pallas_call | solution.py:610
  109.4 1.4 copy-done.7
  112.4 2.4 collective-permute-done.12.came_ref
  115.3 2.0 collective-permute-start.13
  117.3 1.5 collective-permute-start.14
  118.8 5.6 %collective-permute-done.13.came_x_ref = bf16[128,1024]{1,0:T(8,128)(2,1)S(1)} collective-permute-done((bf16[128,1024]{1,0:T(8,128)(2,1)S(1)}, bf16[128,1024]{1,0:T(8,128)(2,1)S(1)}, u32[]{:S(2)}, u32[]{:S(2)}) %collective-permute-start.13) | collective-permute-done | bytes 262176 | tf_op jit(solution)/shard_map/ppermute | solution.py:495
  124.5 6.5 %collective-permute-done.14.came_y_ref = bf16[128,1024]{1,0:T(8,128)(2,1)S(1)} collective-permute-done((bf16[128,1024]{1,0:T(8,128)(2,1)S(1)}, bf16[128,1024]{1,0:T(8,128)(2,1)S(1)}, u32[]{:S(2)}, u32[]{:S(2)}) %collective-permute-start.14) | collective-permute-done | bytes 262176 | tf_op jit(solution)/shard_map/ppermute | solution.py:495
  134.9 1.5 collective-permute-start.18
  136.3 5.8 %collective-permute-done.16.refs_1_.refs_9_ = bf16[128,1024]{1,0:T(8,128)(2,1)S(1)} collective-permute-done((bf16[128,1024]{1,0:T(8,128)(2,1)S(1)}, bf16[128,1024]{1,0:T(8,128)(2,1)S(1)}, u32[]{:S(2)}, u32[]{:S(2)}) %collective-permute-start.16) | collective-permute-done | bytes 262176 | tf_op jit(solution)/shard_map/ppermute | solution.py:495
  142.8 4.2 %collective-permute-done.17.refs_2_.refs_10_ = bf16[128,1024]{1,0:T(8,128)(2,1)S(1)} collective-permute-done((bf16[128,1024]{1,0:T(8,128)(2,1)S(1)}, bf16[128,1024]{1,0:T(8,128)(2,1)S(1)}, u32[]{:S(2)}, u32[]{:S(2)}) %collective-permute-start.17) | collective-permute-done | bytes 262176 | tf_op jit(solution)/shard_map/ppermute | solution.py:495
  149.7 1.6 copy-done.2
  151.3 3.3 shard_map.244
  161.5 1.5 collective-permute-start.29
  165.9 4.0 %shard_map.245 = (bf16[512,512]{1,0:T(8,128)(2,1)S(1)}, f32[512,512]{1,0:T(8,128)S(1)}, f32[128,1024]{1,0:T(8,128)S(1)}, bf16[128,1024]{1,0:T(8,128)(2,1)S(1)}, ...) custom-call(bf16[128,1024]{1,0:T(8,128)(2,1)S(1)} %get-tuple-element.135.refs_0_.refs_8_, ...), custom_call_target="tpu_custom_call" | custom-call | tf_op jit(solution)/shard_map/pallas_call | solution.py:610
  171.0 2.5 collective-permute-start.26
  173.6 2.8 collective-permute-done.24.came_x_ref
  176.4 2.2 collective-permute-done.25.came_y_ref
  178.5 3.4 collective-permute-done.26.came_far_ref
  181.9 5.6 %shard_map.246 = (f32[128,1024]{1,0:T(8,128)S(1)}, bf16[128,1024]{1,0:T(8,128)(2,1)S(1)}, bf16[128,512]{1,0:T(8,128)(2,1)S(1)}, bf16[128,1024]{1,0:T(8,128)(2,1)...) custom-call(f32[128,1024]{1,0:T(8,128)S(1)} %copy-done.10, ...), custom_call_target="tpu_custom_call" | custom-call | tf_op jit(solution)/shard_map/pallas_call | solution.py:610
  189.1 1.6 collective-permute-start.31
  191.9 2.5 collective-permute-start.33
  195.2 5.0 %collective-permute-start.34 = (bf16[128,1024]{1,0:T(8,128)(2,1)S(1)}, bf16[128,1024]{1,0:T(8,128)(2,1)S(1)}, u32[]{:S(2)}, u32[]{:S(2)}) collective-permute-start(bf16[128,1024]{1,0:T(8,128)(2,1)S(1)} %collective-permute-done.30.refs_1_), channel_id=1, source_target_pairs={{0,16},{16,0},{1,17},{17,1},{2,18},{18,2},{3,19},{19,3},{4,20},{20... | collective-permute-start | bytes 786440 | tf_op jit(solution)/shard_map/ppermute | solution.py:495
  200.2 3.0 collective-permute-start.35
  205.1 1.9 shard_map.247
  208.5 1.6 collective-permute-done.42.refs_5_
  211.8 1.9 shard_map.249
  216.7 3.4 shard_map.250
  220.1 2.0 copy-done.4
  223.0 1.5 collective-permute-start.44
  224.5 1.4 collective-permute-start.45
  226.5 5.6 %collective-permute-done.44.came_x_ref = bf16[128,1024]{1,0:T(8,128)(2,1)S(1)} collective-permute-done((bf16[128,1024]{1,0:T(8,128)(2,1)S(1)}, bf16[128,1024]{1,0:T(8,128)(2,1)S(1)}, u32[]{:S(2)}, u32[]{:S(2)}) %collective-permute-start.44) | collective-permute-done | bytes 262176 | tf_op jit(solution)/shard_map/ppermute | solution.py:495
  232.1 5.3 %collective-permute-done.45.came_y_ref = bf16[128,1024]{1,0:T(8,128)(2,1)S(1)} collective-permute-done((bf16[128,1024]{1,0:T(8,128)(2,1)S(1)}, bf16[128,1024]{1,0:T(8,128)(2,1)S(1)}, u32[]{:S(2)}, u32[]{:S(2)}) %collective-permute-start.45) | collective-permute-done | bytes 262176 | tf_op jit(solution)/shard_map/ppermute | solution.py:495
  242.6 5.7 %collective-permute-done.47.refs_1_ = bf16[128,1024]{1,0:T(8,128)(2,1)S(1)} collective-permute-done((bf16[128,1024]{1,0:T(8,128)(2,1)S(1)}, bf16[128,1024]{1,0:T(8,128)(2,1)S(1)}, u32[]{:S(2)}, u32[]{:S(2)}) %collective-permute-start.47) | collective-permute-done | bytes 262176 | tf_op jit(solution)/shard_map/ppermute | solution.py:495
  248.3 5.1 %collective-permute-done.48.refs_2_ = bf16[128,1024]{1,0:T(8,128)(2,1)S(1)} collective-permute-done((bf16[128,1024]{1,0:T(8,128)(2,1)S(1)}, bf16[128,1024]{1,0:T(8,128)(2,1)S(1)}, u32[]{:S(2)}, u32[]{:S(2)}) %collective-permute-start.48) | collective-permute-done | bytes 262176 | tf_op jit(solution)/shard_map/ppermute | solution.py:495
  255.4 9.2 %shard_map.252 = (bf16[1024,384]{1,0:T(8,128)(2,1)S(1)}, bf16[512,1024]{1,0:T(8,128)(2,1)S(1)}, bf16[1024,1024]{1,0:T(8,128)(2,1)S(1)}) custom-call(bf16[1024,384]{1,0:T(8,128)(2,1)S(1)} %copy-done.34, f32[1,1024]{1,0:T(1,128)S(1)} %get-tuple-element.150.bias_ref, f32[1024,128]{1,0:T(8,128)S(1)} %copy-done.36, bf16[1024,128]{1,0:T(8,128)(2,1)S(1)} %bitcast.102, ...), custom_call_target="tpu_custom_call" | custom-call | tf_op jit(solution)/shard_map/pallas_call | solution.py:610
  265.5 1.8 collective-permute-done.54.came_ref
  270.1 1.5 collective-permute-start.57
  273.4 2.7 collective-permute-start.63
  278.6 4.1 %collective-permute-done.56.came_y_ref = bf16[128,1024]{1,0:T(8,128)(2,1)S(1)} collective-permute-done((bf16[128,1024]{1,0:T(8,128)(2,1)S(1)}, bf16[128,1024]{1,0:T(8,128)(2,1)S(1)}, u32[]{:S(2)}, u32[]{:S(2)}) %collective-permute-start.56) | collective-permute-done | bytes 262176 | tf_op jit(solution)/shard_map/ppermute | solution.py:495
  283.2 4.1 %collective-permute-start.64 = (bf16[64,1024]{1,0:T(8,128)(2,1)S(1)}, bf16[64,1024]{1,0:T(8,128)(2,1)S(1)}, u32[]{:S(2)}, u32[]{:S(2)}) collective-permute-start(bf16[64,1024]{1,0:T(8,128)(2,1)S(1)} %get-tuple-element.198), channel_id=1, source_target_pairs={{5,0},{1,1},{20,2},{16,3},{23,4},{19,5},{6,6},{2,7},{21,8},{17,9},... | collective-permute-start | bytes 393224 | tf_op jit(solution)/shard_map/ppermute | solution.py:1666
  287.3 1.4 shard_map.255
  288.8 16.6 %collective-permute-done.62.refs_1_ = bf16[64,1024]{1,0:T(8,128)(2,1)S(1)} collective-permute-done((bf16[64,1024]{1,0:T(8,128)(2,1)S(1)}, bf16[64,1024]{1,0:T(8,128)(2,1)S(1)}, u32[]{:S(2)}, u32[]{:S(2)}) %collective-permute-start.62) | collective-permute-done | bytes 131104 | tf_op jit(solution)/shard_map/ppermute | solution.py:1666
  305.4 1.4 collective-permute-start.38
  306.8 9.7 %collective-permute-done.64.refs_3_ = bf16[64,1024]{1,0:T(8,128)(2,1)S(1)} collective-permute-done((bf16[64,1024]{1,0:T(8,128)(2,1)S(1)}, bf16[64,1024]{1,0:T(8,128)(2,1)S(1)}, u32[]{:S(2)}, u32[]{:S(2)}) %collective-permute-start.64) | collective-permute-done | bytes 131104 | tf_op jit(solution)/shard_map/ppermute | solution.py:1666
  316.4 1.5 collective-permute-start.58
  317.9 1.5 collective-permute-start.59
  319.5 6.8 %collective-permute-start.65 = (f32[192,1024]{1,0:T(8,128)S(1)}, f32[192,1024]{1,0:T(8,128)S(1)}, u32[]{:S(2)}, u32[]{:S(2)}) collective-permute-start(f32[192,1024]{1,0:T(8,128)S(1)} %shard_map.258), channel_id=1, source_target_pairs={{0,16},{16,0},{1,17},{17,1},{2,18},{18,2},{3,19},{19,3},{4,20},{20... | collective-permute-start | bytes 2359304 | tf_op jit(solution)/shard_map/ppermute | solution.py:495
  326.3 3.9 %all-to-all-start.1 = ((bf16[16,96,128]{2,1,0:T(8,128)(2,1)}), bf16[16,96,128]{2,1,0:T(8,128)(2,1)S(1)}, u32[]{:S(2)}, u32[]{:S(2)}) async-start(bf16[16,96,128]{2,1,0:T(8,128)(2,1)} %get-tuple-element.193), calls=%async_computation.1 | async-start | bytes 786432 | tf_op jit(solution)/shard_map/all_to_all | solution.py:1517
  333.3 14.7 %all-to-all-done.1.came_ref = bf16[16,96,128]{2,1,0:T(8,128)(2,1)S(1)} async-done(((bf16[16,96,128]{2,1,0:T(8,128)(2,1)}), bf16[16,96,128]{2,1,0:T(8,128)(2,1)S(1)}, u32[]{:S(2)}, u32[]{:S(2)}) %all-to-all-start.1) | async-done | bytes 393248 | tf_op jit(solution)/shard_map/all_to_all | solution.py:1517
  352.5 1.6 collective-permute-start.67
  354.5 1.6 collective-permute-start.69
  358.1 1.6 collective-permute-done.67.refs_1_
  359.6 4.2 %collective-permute-done.68.refs_2_ = bf16[64,1280]{1,0:T(8,128)(2,1)S(1)} collective-permute-done((bf16[64,1280]{1,0:T(8,128)(2,1)S(1)}, bf16[64,1280]{1,0:T(8,128)(2,1)S(1)}, u32[]{:S(2)}, u32[]{:S(2)}) %collective-permute-start.68) | collective-permute-done | bytes 163872 | tf_op jit(solution)/shard_map/ppermute | solution.py:495
  (314 shorter events, 84.5 us)
Async XLA Ops:
  7.2 141.7 %all-gather.5.cloned.1.call-start = ((), (), s32[]{:S(2)}) async-start(), calls=%async_computation.4 | async-start | bytes 1671168 | tf_op jit(solution)/shard_map/all_gather | solution.py:1592
  9.6 140.1 %all-gather.3.cloned.1.call-start = ((), (), s32[]{:S(2)}) async-start(), calls=%async_computation.3 | async-start | bytes 2621440 | tf_op jit(solution)/shard_map/all_gather | solution.py:1593
  14.1 3.8 collective-permute-start
  14.8 6.4 %collective-permute-start.1 = (bf16[80,1024]{1,0:T(8,128)(2,1)S(1)}, bf16[80,1024]{1,0:T(8,128)(2,1)S(1)}, u32[]{:S(2)}, u32[]{:S(2)}) collective-permute-start(bf16[80,1024]{1,0:T(8,128)(2,1)S(1)} %get-tuple-element.112), channel_id=1, source_target_pairs={{0,4},{4,0},{8,20},{12,16},{16,12},{20,8},{24,28},{28,24},{1,5},{5... | collective-permute-start | bytes 491528 | tf_op jit(solution)/shard_map/ppermute | solution.py:1560
  21.2 18.4 %collective-permute-start.2 = (bf16[2,80,1024]{2,1,0:T(8,128)(2,1)S(1)}, bf16[2,80,1024]{2,1,0:T(8,128)(2,1)S(1)}, u32[]{:S(2)}, u32[]{:S(2)}) collective-permute-start(bf16[2,80,1024]{2,1,0:T(8,128)(2,1)S(1)} %get-tuple-element.243.blocks_ref), channel_id=1, source_target_pairs={{0,1},{1,0},{2,3},{3,2},{4,5},{5,4},{6,7},{7,6},{8,9},{9,8},{10,11... | collective-permute-start | bytes 983048 | tf_op jit(solution)/shard_map/ppermute | solution.py:495
  23.3 37.0 %collective-permute-start.3 = (bf16[128,1024]{1,0:T(8,128)(2,1)S(1)}, bf16[128,1024]{1,0:T(8,128)(2,1)S(1)}, u32[]{:S(2)}, u32[]{:S(2)}) collective-permute-start(bf16[128,1024]{1,0:T(8,128)(2,1)S(1)} %dynamic-slice_bitcast_fusion), channel_id=1, source_target_pairs={{0,0},{1,6},{2,3},{3,21},{4,18},{5,4},{6,1},{7,7},{8,16},{9,22},{1... | collective-permute-start | bytes 786440 | tf_op jit(solution)/shard_map/ppermute | solution.py:1570
  23.9 36.3 %collective-permute-start.5 = (bf16[128,1024]{1,0:T(8,128)(2,1)S(1)}, bf16[128,1024]{1,0:T(8,128)(2,1)S(1)}, u32[]{:S(2)}, u32[]{:S(2)}) collective-permute-start(bf16[128,1024]{1,0:T(8,128)(2,1)S(1)} %dynamic-slice_bitcast_fusion), channel_id=1, source_target_pairs={{0,4},{1,2},{2,7},{3,17},{4,22},{5,0},{6,5},{7,3},{8,20},{9,18},{1... | collective-permute-start | bytes 786440 | tf_op jit(solution)/shard_map/ppermute | solution.py:1570
  32.9 23.6 %collective-permute-start.4 = (bf16[64,1024]{1,0:T(8,128)(2,1)S(1)}, bf16[64,1024]{1,0:T(8,128)(2,1)S(1)}, u32[]{:S(2)}, u32[]{:S(2)}) collective-permute-start(bf16[64,1024]{1,0:T(8,128)(2,1)S(1)} %dynamic-slice_bitcast_fusion.1), channel_id=1, source_target_pairs={{0,1},{1,5},{2,16},{3,20},{4,19},{5,23},{6,2},{7,6},{8,17},{9,21},... | collective-permute-start | bytes 393224 | tf_op jit(solution)/shard_map/ppermute | solution.py:1570
  33.0 26.6 %collective-permute-start.6 = (bf16[64,1024]{1,0:T(8,128)(2,1)S(1)}, bf16[64,1024]{1,0:T(8,128)(2,1)S(1)}, u32[]{:S(2)}, u32[]{:S(2)}) collective-permute-start(bf16[64,1024]{1,0:T(8,128)(2,1)S(1)} %dynamic-slice_bitcast_fusion.1), channel_id=1, source_target_pairs={{0,5},{1,1},{2,20},{3,16},{4,23},{5,19},{6,6},{7,2},{8,21},{9,17},... | collective-permute-start | bytes 393224 | tf_op jit(solution)/shard_map/ppermute | solution.py:1570
  60.2 18.8 %collective-permute-start.7 = (bf16[2,2,80,1024]{3,2,1,0:T(8,128)(2,1)S(1)}, bf16[2,2,80,1024]{3,2,1,0:T(8,128)(2,1)S(1)}, u32[]{:S(2)}, u32[]{:S(2)}) collective-permute-start(bf16[2,2,80,1024]{3,2,1,0:T(8,128)(2,1)S(1)} %pad_maximum_fusion.1), channel_id=1, source_target_pairs={{0,2},{2,0},{1,3},{3,1},{4,6},{6,4},{5,7},{7,5},{8,10},{10,8},{9,1... | collective-permute-start | bytes 1966088 | tf_op jit(solution)/shard_map/ppermute | solution.py:495
  80.3 16.4 %collective-permute-start.8 = (bf16[4,2,80,1024]{3,2,1,0:T(8,128)(2,1)S(1)}, bf16[4,2,80,1024]{3,2,1,0:T(8,128)(2,1)}, u32[]{:S(2)}, u32[]{:S(2)}) collective-permute-start(bf16[4,2,80,1024]{3,2,1,0:T(8,128)(2,1)S(1)} %pad_maximum_fusion.own_ref), channel_id=1, source_target_pairs={{0,16},{16,0},{1,17},{17,1},{2,18},{18,2},{3,19},{19,3},{4,20},{20... | collective-permute-start | bytes 3932168 | tf_op jit(solution)/shard_map/ppermute | solution.py:495
  83.1 4.7 %collective-permute-start.10 = (bf16[64,512]{1,0:T(8,128)(2,1)}, bf16[64,512]{1,0:T(8,128)(2,1)S(1)}, u32[]{:S(2)}, u32[]{:S(2)}) collective-permute-start(bf16[64,512]{1,0:T(8,128)(2,1)} %copy-done.75), channel_id=1, source_target_pairs={{0,2},{2,0},{1,3},{3,1},{4,6},{6,4},{5,7},{7,5},{8,10},{10,8},{9,1... | collective-permute-start | bytes 196616 | tf_op jit(solution)/shard_map/ppermute | solution.py:495
  83.9 6.0 %collective-permute-start.11 = (bf16[64,512]{1,0:T(8,128)(2,1)}, bf16[64,512]{1,0:T(8,128)(2,1)S(1)}, u32[]{:S(2)}, u32[]{:S(2)}) collective-permute-start(bf16[64,512]{1,0:T(8,128)(2,1)} %copy-done.74), channel_id=1, source_target_pairs={{0,3},{1,2},{2,1},{3,0},{4,7},{5,6},{6,5},{7,4},{8,11},{9,10},{10,... | collective-permute-start | bytes 196616 | tf_op jit(solution)/shard_map/ppermute | solution.py:585
  85.3 5.1 %collective-permute-start.9 = (bf16[64,512]{1,0:T(8,128)(2,1)}, bf16[64,512]{1,0:T(8,128)(2,1)S(1)}, u32[]{:S(2)}, u32[]{:S(2)}) collective-permute-start(bf16[64,512]{1,0:T(8,128)(2,1)} %copy-done.73), channel_id=1, source_target_pairs={{0,1},{1,0},{2,3},{3,2},{4,5},{5,4},{6,7},{7,6},{8,9},{9,8},{10,11... | collective-permute-start | bytes 196616 | tf_op jit(solution)/shard_map/ppermute | solution.py:495
  91.3 20.4 %all-to-all-start = ((bf16[16,64,128]{2,1,0:T(8,128)(2,1)}), bf16[16,64,128]{2,1,0:T(8,128)(2,1)S(1)}, u32[]{:S(2)}, u32[]{:S(2)}) async-start(bf16[16,64,128]{2,1,0:T(8,128)(2,1)} %get-tuple-element.127), calls=%async_computation | async-start | bytes 524288 | tf_op jit(solution)/shard_map/all_to_all | solution.py:1517
  96.5 254.7 %reduce-scatter.2.cloned.1.call-start = ((), (), s32[]{:S(2)}) async-start(), calls=%async_computation.5 | async-start | bytes 5242880 | tf_op jit(solution)/shard_map/reduce_scatter | solution.py:1632
  115.3 9.2 %collective-permute-start.13 = (bf16[128,1024]{1,0:T(8,128)(2,1)S(1)}, bf16[128,1024]{1,0:T(8,128)(2,1)S(1)}, u32[]{:S(2)}, u32[]{:S(2)}) collective-permute-start(bf16[128,1024]{1,0:T(8,128)(2,1)S(1)} %get-tuple-element.130), channel_id=1, source_target_pairs={{0,1},{1,0},{2,3},{3,2},{4,5},{5,4},{6,7},{7,6},{8,9},{9,8},{10,11... | collective-permute-start | bytes 786440 | tf_op jit(solution)/shard_map/ppermute | solution.py:495
  117.3 13.7 %collective-permute-start.14 = (bf16[128,1024]{1,0:T(8,128)(2,1)S(1)}, bf16[128,1024]{1,0:T(8,128)(2,1)S(1)}, u32[]{:S(2)}, u32[]{:S(2)}) collective-permute-start(bf16[128,1024]{1,0:T(8,128)(2,1)S(1)} %get-tuple-element.131), channel_id=1, source_target_pairs={{0,2},{2,0},{1,3},{3,1},{4,6},{6,4},{5,7},{7,5},{8,10},{10,8},{9,1... | collective-permute-start | bytes 786440 | tf_op jit(solution)/shard_map/ppermute | solution.py:495
  118.7 12.2 %collective-permute-start.15 = (bf16[128,1024]{1,0:T(8,128)(2,1)S(1)}, bf16[128,1024]{1,0:T(8,128)(2,1)S(1)}, u32[]{:S(2)}, u32[]{:S(2)}) collective-permute-start(bf16[128,1024]{1,0:T(8,128)(2,1)S(1)} %get-tuple-element.132), channel_id=1, source_target_pairs={{0,3},{1,2},{2,1},{3,0},{4,7},{5,6},{6,5},{7,4},{8,11},{9,10},{10,... | collective-permute-start | bytes 786440 | tf_op jit(solution)/shard_map/ppermute | solution.py:585
  132.8 9.2 %collective-permute-start.16 = (bf16[128,1024]{1,0:T(8,128)(2,1)S(1)}, bf16[128,1024]{1,0:T(8,128)(2,1)S(1)}, u32[]{:S(2)}, u32[]{:S(2)}) collective-permute-start(bf16[128,1024]{1,0:T(8,128)(2,1)S(1)} %get-tuple-element.135.refs_0_.refs_8_), channel_id=1, source_target_pairs={{0,1},{1,0},{2,3},{3,2},{4,5},{5,4},{6,7},{7,6},{8,9},{9,8},{10,11... | collective-permute-start | bytes 786440 | tf_op jit(solution)/shard_map/ppermute | solution.py:495
  134.0 13.0 %collective-permute-start.17 = (bf16[128,1024]{1,0:T(8,128)(2,1)S(1)}, bf16[128,1024]{1,0:T(8,128)(2,1)S(1)}, u32[]{:S(2)}, u32[]{:S(2)}) collective-permute-start(bf16[128,1024]{1,0:T(8,128)(2,1)S(1)} %get-tuple-element.135.refs_0_.refs_8_), channel_id=1, source_target_pairs={{0,2},{2,0},{1,3},{3,1},{4,6},{6,4},{5,7},{7,5},{8,10},{10,8},{9,1... | collective-permute-start | bytes 786440 | tf_op jit(solution)/shard_map/ppermute | solution.py:495
  134.9 12.8 %collective-permute-start.18 = (bf16[128,1024]{1,0:T(8,128)(2,1)S(1)}, bf16[128,1024]{1,0:T(8,128)(2,1)S(1)}, u32[]{:S(2)}, u32[]{:S(2)}) collective-permute-start(bf16[128,1024]{1,0:T(8,128)(2,1)S(1)} %get-tuple-element.135.refs_0_.refs_8_), channel_id=1, source_target_pairs={{0,3},{1,2},{2,1},{3,0},{4,7},{5,6},{6,5},{7,4},{8,11},{9,10},{10,... | collective-permute-start | bytes 786440 | tf_op jit(solution)/shard_map/ppermute | solution.py:585
  136.3 12.6 %collective-permute-start.19 = (bf16[128,1024]{1,0:T(8,128)(2,1)S(1)}, bf16[128,1024]{1,0:T(8,128)(2,1)S(1)}, u32[]{:S(2)}, u32[]{:S(2)}) collective-permute-start(bf16[128,1024]{1,0:T(8,128)(2,1)S(1)} %get-tuple-element.135.refs_0_.refs_8_), channel_id=1, source_target_pairs={{0,16},{16,0},{1,17},{17,1},{2,18},{18,2},{3,19},{19,3},{4,20},{20... | collective-permute-start | bytes 786440 | tf_op jit(solution)/shard_map/ppermute | solution.py:495
  142.1 6.8 %collective-permute-start.20 = (bf16[128,1024]{1,0:T(8,128)(2,1)S(1)}, bf16[128,1024]{1,0:T(8,128)(2,1)S(1)}, u32[]{:S(2)}, u32[]{:S(2)}) collective-permute-start(bf16[128,1024]{1,0:T(8,128)(2,1)S(1)} %collective-permute-done.16.refs_1_.refs_9_), channel_id=1, source_target_pairs={{0,16},{16,0},{1,17},{17,1},{2,18},{18,2},{3,19},{19,3},{4,20},{20... | collective-permute-start | bytes 786440 | tf_op jit(solution)/shard_map/ppermute | solution.py:495
  149.4 32.6 %collective-permute-start.27 = (bf16[1024,768]{1,0:T(8,128)(2,1)}, bf16[1024,768]{1,0:T(8,128)(2,1)}, u32[]{:S(2)}, u32[]{:S(2)}) collective-permute-start(bf16[1024,768]{1,0:T(8,128)(2,1)} %all-gather.5.cloned.1.call-done.own_ref), channel_id=1, source_target_pairs={{0,16},{16,0},{1,17},{17,1},{2,18},{18,2},{3,19},{19,3},{4,20},{20... | collective-permute-start | bytes 4718600 | tf_op jit(solution)/shard_map/ppermute | solution.py:495
  158.4 4.6 %collective-permute-start.23 = (bf16[512,1024]{1,0:T(8,128)(2,1)}, bf16[512,1024]{1,0:T(8,128)(2,1)}, u32[]{:S(2)}, u32[]{:S(2)}) collective-permute-start(bf16[512,1024]{1,0:T(8,128)(2,1)} %get-tuple-element.137), channel_id=1, source_target_pairs={{0,16},{16,0},{1,17},{17,1},{2,18},{18,2},{3,19},{19,3},{4,20},{20... | collective-permute-start | bytes 3145736 | tf_op jit(solution)/shard_map/ppermute | solution.py:495
  160.8 10.2 %collective-permute-start.28 = (bf16[128,1024]{1,0:T(8,128)(2,1)S(1)}, bf16[128,1024]{1,0:T(8,128)(2,1)S(1)}, u32[]{:S(2)}, u32[]{:S(2)}) collective-permute-start(bf16[128,1024]{1,0:T(8,128)(2,1)S(1)} %get-tuple-element.237), channel_id=1, source_target_pairs={{0,0},{4,4},{8,16},{12,20},{16,8},{20,12},{24,24},{28,28},{1,1},{5... | collective-permute-start | bytes 786440 | tf_op jit(solution)/shard_map/ppermute | solution.py:539
  161.5 12.0 %collective-permute-start.29 = (bf16[128,1024]{1,0:T(8,128)(2,1)S(1)}, bf16[128,1024]{1,0:T(8,128)(2,1)S(1)}, u32[]{:S(2)}, u32[]{:S(2)}) collective-permute-start(bf16[128,1024]{1,0:T(8,128)(2,1)S(1)} %get-tuple-element.236), channel_id=1, source_target_pairs={{0,4},{4,0},{8,20},{12,16},{16,12},{20,8},{24,28},{28,24},{1,5},{5... | collective-permute-start | bytes 786440 | tf_op jit(solution)/shard_map/ppermute | solution.py:539
  169.9 6.4 %collective-permute-start.24 = (bf16[128,1024]{1,0:T(8,128)(2,1)S(1)}, bf16[128,1024]{1,0:T(8,128)(2,1)S(1)}, u32[]{:S(2)}, u32[]{:S(2)}) collective-permute-start(bf16[128,1024]{1,0:T(8,128)(2,1)S(1)} %get-tuple-element.139), channel_id=1, source_target_pairs={{0,1},{1,0},{2,3},{3,2},{4,5},{5,4},{6,7},{7,6},{8,9},{9,8},{10,11... | collective-permute-start | bytes 786440 | tf_op jit(solution)/shard_map/ppermute | solution.py:495
  170.6 7.9 %collective-permute-start.25 = (bf16[128,1024]{1,0:T(8,128)(2,1)S(1)}, bf16[128,1024]{1,0:T(8,128)(2,1)S(1)}, u32[]{:S(2)}, u32[]{:S(2)}) collective-permute-start(bf16[128,1024]{1,0:T(8,128)(2,1)S(1)} %get-tuple-element.140), channel_id=1, source_target_pairs={{0,2},{2,0},{1,3},{3,1},{4,6},{6,4},{5,7},{7,5},{8,10},{10,8},{9,1... | collective-permute-start | bytes 786440 | tf_op jit(solution)/shard_map/ppermute | solution.py:495
  171.0 10.9 %collective-permute-start.26 = (bf16[128,1024]{1,0:T(8,128)(2,1)S(1)}, bf16[128,1024]{1,0:T(8,128)(2,1)S(1)}, u32[]{:S(2)}, u32[]{:S(2)}) collective-permute-start(bf16[128,1024]{1,0:T(8,128)(2,1)S(1)} %get-tuple-element.141), channel_id=1, source_target_pairs={{0,3},{1,2},{2,1},{3,0},{4,7},{5,6},{6,5},{7,4},{8,11},{9,10},{10,... | collective-permute-start | bytes 786440 | tf_op jit(solution)/shard_map/ppermute | solution.py:585
  188.4 6.8 %collective-permute-start.30 = (bf16[128,1024]{1,0:T(8,128)(2,1)S(1)}, bf16[128,1024]{1,0:T(8,128)(2,1)S(1)}, u32[]{:S(2)}, u32[]{:S(2)}) collective-permute-start(bf16[128,1024]{1,0:T(8,128)(2,1)S(1)} %get-tuple-element.147.refs_0_), channel_id=1, source_target_pairs={{0,1},{1,0},{2,3},{3,2},{4,5},{5,4},{6,7},{7,6},{8,9},{9,8},{10,11... | collective-permute-start | bytes 786440 | tf_op jit(solution)/shard_map/ppermute | solution.py:495
  189.1 11.1 %collective-permute-start.31 = (bf16[128,1024]{1,0:T(8,128)(2,1)S(1)}, bf16[128,1024]{1,0:T(8,128)(2,1)S(1)}, u32[]{:S(2)}, u32[]{:S(2)}) collective-permute-start(bf16[128,1024]{1,0:T(8,128)(2,1)S(1)} %get-tuple-element.147.refs_0_), channel_id=1, source_target_pairs={{0,2},{2,0},{1,3},{3,1},{4,6},{6,4},{5,7},{7,5},{8,10},{10,8},{9,1... | collective-permute-start | bytes 786440 | tf_op jit(solution)/shard_map/ppermute | solution.py:495
  190.8 12.4 %collective-permute-start.32 = (bf16[128,1024]{1,0:T(8,128)(2,1)S(1)}, bf16[128,1024]{1,0:T(8,128)(2,1)S(1)}, u32[]{:S(2)}, u32[]{:S(2)}) collective-permute-start(bf16[128,1024]{1,0:T(8,128)(2,1)S(1)} %get-tuple-element.147.refs_0_), channel_id=1, source_target_pairs={{0,3},{1,2},{2,1},{3,0},{4,7},{5,6},{6,5},{7,4},{8,11},{9,10},{10,... | collective-permute-start | bytes 786440 | tf_op jit(solution)/shard_map/ppermute | solution.py:585
  191.9 12.0 %collective-permute-start.33 = (bf16[128,1024]{1,0:T(8,128)(2,1)S(1)}, bf16[128,1024]{1,0:T(8,128)(2,1)S(1)}, u32[]{:S(2)}, u32[]{:S(2)}) collective-permute-start(bf16[128,1024]{1,0:T(8,128)(2,1)S(1)} %get-tuple-element.147.refs_0_), channel_id=1, source_target_pairs={{0,16},{16,0},{1,17},{17,1},{2,18},{18,2},{3,19},{19,3},{4,20},{20... | collective-permute-start | bytes 786440 | tf_op jit(solution)/shard_map/ppermute | solution.py:495
  195.2 8.8 %collective-permute-start.34 = (bf16[128,1024]{1,0:T(8,128)(2,1)S(1)}, bf16[128,1024]{1,0:T(8,128)(2,1)S(1)}, u32[]{:S(2)}, u32[]{:S(2)}) collective-permute-start(bf16[128,1024]{1,0:T(8,128)(2,1)S(1)} %collective-permute-done.30.refs_1_), channel_id=1, source_target_pairs={{0,16},{16,0},{1,17},{17,1},{2,18},{18,2},{3,19},{19,3},{4,20},{20... | collective-permute-start | bytes 786440 | tf_op jit(solution)/shard_map/ppermute | solution.py:495
  200.2 4.2 %collective-permute-start.35 = (bf16[128,1024]{1,0:T(8,128)(2,1)S(1)}, bf16[128,1024]{1,0:T(8,128)(2,1)S(1)}, u32[]{:S(2)}, u32[]{:S(2)}) collective-permute-start(bf16[128,1024]{1,0:T(8,128)(2,1)S(1)} %collective-permute-done.31.refs_2_), channel_id=1, source_target_pairs={{0,16},{16,0},{1,17},{17,1},{2,18},{18,2},{3,19},{19,3},{4,20},{20... | collective-permute-start | bytes 786440 | tf_op jit(solution)/shard_map/ppermute | solution.py:495
  207.0 4.7 %collective-permute-start.39 = (bf16[512,1024]{1,0:T(8,128)(2,1)S(1)}, bf16[512,1024]{1,0:T(8,128)(2,1)S(1)}, u32[]{:S(2)}, u32[]{:S(2)}) collective-permute-start(bf16[512,1024]{1,0:T(8,128)(2,1)S(1)} %get-tuple-element.155), channel_id=1, source_target_pairs={{0,16},{16,0},{1,17},{17,1},{2,18},{18,2},{3,19},{19,3},{4,20},{20... | collective-permute-start | bytes 3145736 | tf_op jit(solution)/shard_map/ppermute | solution.py:495
  223.0 9.1 %collective-permute-start.44 = (bf16[128,1024]{1,0:T(8,128)(2,1)S(1)}, bf16[128,1024]{1,0:T(8,128)(2,1)S(1)}, u32[]{:S(2)}, u32[]{:S(2)}) collective-permute-start(bf16[128,1024]{1,0:T(8,128)(2,1)S(1)} %copy-done.72), channel_id=1, source_target_pairs={{0,1},{1,0},{2,3},{3,2},{4,5},{5,4},{6,7},{7,6},{8,9},{9,8},{10,11... | collective-permute-start | bytes 786440 | tf_op jit(solution)/shard_map/ppermute | solution.py:495
  224.5 12.9 %collective-permute-start.45 = (bf16[128,1024]{1,0:T(8,128)(2,1)S(1)}, bf16[128,1024]{1,0:T(8,128)(2,1)S(1)}, u32[]{:S(2)}, u32[]{:S(2)}) collective-permute-start(bf16[128,1024]{1,0:T(8,128)(2,1)S(1)} %copy-done.70), channel_id=1, source_target_pairs={{0,2},{2,0},{1,3},{3,1},{4,6},{6,4},{5,7},{7,5},{8,10},{10,8},{9,1... | collective-permute-start | bytes 786440 | tf_op jit(solution)/shard_map/ppermute | solution.py:495
  226.0 12.5 %collective-permute-start.46 = (bf16[128,1024]{1,0:T(8,128)(2,1)S(1)}, bf16[128,1024]{1,0:T(8,128)(2,1)S(1)}, u32[]{:S(2)}, u32[]{:S(2)}) collective-permute-start(bf16[128,1024]{1,0:T(8,128)(2,1)S(1)} %copy-done.68), channel_id=1, source_target_pairs={{0,3},{1,2},{2,1},{3,0},{4,7},{5,6},{6,5},{7,4},{8,11},{9,10},{10,... | collective-permute-start | bytes 786440 | tf_op jit(solution)/shard_map/ppermute | solution.py:585
  239.0 9.3 %collective-permute-start.47 = (bf16[128,1024]{1,0:T(8,128)(2,1)S(1)}, bf16[128,1024]{1,0:T(8,128)(2,1)S(1)}, u32[]{:S(2)}, u32[]{:S(2)}) collective-permute-start(bf16[128,1024]{1,0:T(8,128)(2,1)S(1)} %get-tuple-element.173.refs_0_), channel_id=1, source_target_pairs={{0,1},{1,0},{2,3},{3,2},{4,5},{5,4},{6,7},{7,6},{8,9},{9,8},{10,11... | collective-permute-start | bytes 786440 | tf_op jit(solution)/shard_map/ppermute | solution.py:495
  240.2 13.2 %collective-permute-start.48 = (bf16[128,1024]{1,0:T(8,128)(2,1)S(1)}, bf16[128,1024]{1,0:T(8,128)(2,1)S(1)}, u32[]{:S(2)}, u32[]{:S(2)}) collective-permute-start(bf16[128,1024]{1,0:T(8,128)(2,1)S(1)} %get-tuple-element.173.refs_0_), channel_id=1, source_target_pairs={{0,2},{2,0},{1,3},{3,1},{4,6},{6,4},{5,7},{7,5},{8,10},{10,8},{9,1... | collective-permute-start | bytes 786440 | tf_op jit(solution)/shard_map/ppermute | solution.py:495
  241.4 12.1 %collective-permute-start.49 = (bf16[128,1024]{1,0:T(8,128)(2,1)S(1)}, bf16[128,1024]{1,0:T(8,128)(2,1)S(1)}, u32[]{:S(2)}, u32[]{:S(2)}) collective-permute-start(bf16[128,1024]{1,0:T(8,128)(2,1)S(1)} %get-tuple-element.173.refs_0_), channel_id=1, source_target_pairs={{0,3},{1,2},{2,1},{3,0},{4,7},{5,6},{6,5},{7,4},{8,11},{9,10},{10,... | collective-permute-start | bytes 786440 | tf_op jit(solution)/shard_map/ppermute | solution.py:585
  242.6 11.4 %collective-permute-start.50 = (bf16[128,1024]{1,0:T(8,128)(2,1)S(1)}, bf16[128,1024]{1,0:T(8,128)(2,1)S(1)}, u32[]{:S(2)}, u32[]{:S(2)}) collective-permute-start(bf16[128,1024]{1,0:T(8,128)(2,1)S(1)} %get-tuple-element.173.refs_0_), channel_id=1, source_target_pairs={{0,16},{16,0},{1,17},{17,1},{2,18},{18,2},{3,19},{19,3},{4,20},{20... | collective-permute-start | bytes 786440 | tf_op jit(solution)/shard_map/ppermute | solution.py:495
  248.3 5.7 %collective-permute-start.51 = (bf16[128,1024]{1,0:T(8,128)(2,1)S(1)}, bf16[128,1024]{1,0:T(8,128)(2,1)S(1)}, u32[]{:S(2)}, u32[]{:S(2)}) collective-permute-start(bf16[128,1024]{1,0:T(8,128)(2,1)S(1)} %collective-permute-done.47.refs_1_), channel_id=1, source_target_pairs={{0,16},{16,0},{1,17},{17,1},{2,18},{18,2},{3,19},{19,3},{4,20},{20... | collective-permute-start | bytes 786440 | tf_op jit(solution)/shard_map/ppermute | solution.py:495
  268.1 9.2 %collective-permute-start.55 = (bf16[128,1024]{1,0:T(8,128)(2,1)S(1)}, bf16[128,1024]{1,0:T(8,128)(2,1)S(1)}, u32[]{:S(2)}, u32[]{:S(2)}) collective-permute-start(bf16[128,1024]{1,0:T(8,128)(2,1)S(1)} %get-tuple-element.177), channel_id=1, source_target_pairs={{0,1},{1,0},{2,3},{3,2},{4,5},{5,4},{6,7},{7,6},{8,9},{9,8},{10,11... | collective-permute-start | bytes 786440 | tf_op jit(solution)/shard_map/ppermute | solution.py:495
  269.0 13.7 %collective-permute-start.56 = (bf16[128,1024]{1,0:T(8,128)(2,1)S(1)}, bf16[128,1024]{1,0:T(8,128)(2,1)S(1)}, u32[]{:S(2)}, u32[]{:S(2)}) collective-permute-start(bf16[128,1024]{1,0:T(8,128)(2,1)S(1)} %get-tuple-element.178), channel_id=1, source_target_pairs={{0,2},{2,0},{1,3},{3,1},{4,6},{6,4},{5,7},{7,5},{8,10},{10,8},{9,1... | collective-permute-start | bytes 786440 | tf_op jit(solution)/shard_map/ppermute | solution.py:495
  270.1 13.1 %collective-permute-start.57 = (bf16[128,1024]{1,0:T(8,128)(2,1)S(1)}, bf16[128,1024]{1,0:T(8,128)(2,1)S(1)}, u32[]{:S(2)}, u32[]{:S(2)}) collective-permute-start(bf16[128,1024]{1,0:T(8,128)(2,1)S(1)} %get-tuple-element.179), channel_id=1, source_target_pairs={{0,3},{1,2},{2,1},{3,0},{4,7},{5,6},{6,5},{7,4},{8,11},{9,10},{10,... | collective-permute-start | bytes 786440 | tf_op jit(solution)/shard_map/ppermute | solution.py:585
  272.7 45.2 %collective-permute-start.61 = (bf16[128,1024]{1,0:T(8,128)(2,1)S(1)}, bf16[128,1024]{1,0:T(8,128)(2,1)S(1)}, u32[]{:S(2)}, u32[]{:S(2)}) collective-permute-start(bf16[128,1024]{1,0:T(8,128)(2,1)S(1)} %get-tuple-element.195), channel_id=1, source_target_pairs={{0,0},{6,1},{3,2},{21,3},{18,4},{4,5},{1,6},{7,7},{16,8},{22,9},{1... | collective-permute-start | bytes 786440 | tf_op jit(solution)/shard_map/ppermute | solution.py:1666
  273.4 46.0 %collective-permute-start.63 = (bf16[128,1024]{1,0:T(8,128)(2,1)S(1)}, bf16[128,1024]{1,0:T(8,128)(2,1)S(1)}, u32[]{:S(2)}, u32[]{:S(2)}) collective-permute-start(bf16[128,1024]{1,0:T(8,128)(2,1)S(1)} %get-tuple-element.197), channel_id=1, source_target_pairs={{4,0},{2,1},{7,2},{17,3},{22,4},{0,5},{5,6},{3,7},{20,8},{18,9},{2... | collective-permute-start | bytes 786440 | tf_op jit(solution)/shard_map/ppermute | solution.py:1666
  277.3 53.0 %collective-permute-start.37 = (f32[64,1024]{1,0:T(8,128)}, f32[64,1024]{1,0:T(8,128)}, u32[]{:S(2)}, u32[]{:S(2)}) collective-permute-start(f32[64,1024]{1,0:T(8,128)} %get-tuple-element.233), channel_id=1, source_target_pairs={{4,0},{0,4},{20,8},{16,12},{12,16},{8,20},{28,24},{24,28},{5,1},{1... | collective-permute-start | bytes 786440 | tf_op jit(solution)/shard_map/ppermute | solution.py:545
  282.7 22.7 %collective-permute-start.62 = (bf16[64,1024]{1,0:T(8,128)(2,1)S(1)}, bf16[64,1024]{1,0:T(8,128)(2,1)S(1)}, u32[]{:S(2)}, u32[]{:S(2)}) collective-permute-start(bf16[64,1024]{1,0:T(8,128)(2,1)S(1)} %get-tuple-element.196), channel_id=1, source_target_pairs={{1,0},{5,1},{16,2},{20,3},{19,4},{23,5},{2,6},{6,7},{17,8},{21,9},... | collective-permute-start | bytes 393224 | tf_op jit(solution)/shard_map/ppermute | solution.py:1666
  283.2 33.2 %collective-permute-start.64 = (bf16[64,1024]{1,0:T(8,128)(2,1)S(1)}, bf16[64,1024]{1,0:T(8,128)(2,1)S(1)}, u32[]{:S(2)}, u32[]{:S(2)}) collective-permute-start(bf16[64,1024]{1,0:T(8,128)(2,1)S(1)} %get-tuple-element.198), channel_id=1, source_target_pairs={{5,0},{1,1},{20,2},{16,3},{23,4},{19,5},{6,6},{2,7},{21,8},{17,9},... | collective-permute-start | bytes 393224 | tf_op jit(solution)/shard_map/ppermute | solution.py:1666
  305.4 24.9 %collective-permute-start.38 = (f32[64,1024]{1,0:T(8,128)S(1)}, f32[64,1024]{1,0:T(8,128)}, u32[]{:S(2)}, u32[]{:S(2)}) collective-permute-start(f32[64,1024]{1,0:T(8,128)S(1)} %get-tuple-element.232), channel_id=1, source_target_pairs={{0,0},{4,4},{16,8},{20,12},{8,16},{12,20},{24,24},{28,28},{1,1},{5... | collective-permute-start | bytes 786440 | tf_op jit(solution)/shard_map/ppermute | solution.py:545
  316.4 13.8 %collective-permute-start.58 = (f32[64,1024]{1,0:T(8,128)S(1)}, f32[64,1024]{1,0:T(8,128)}, u32[]{:S(2)}, u32[]{:S(2)}) collective-permute-start(f32[64,1024]{1,0:T(8,128)S(1)} %get-tuple-element.229), channel_id=1, source_target_pairs={{4,0},{0,4},{20,8},{16,12},{12,16},{8,20},{28,24},{24,28},{5,1},{1... | collective-permute-start | bytes 786440 | tf_op jit(solution)/shard_map/ppermute | solution.py:545
  317.9 12.4 %collective-permute-start.59 = (f32[64,1024]{1,0:T(8,128)S(1)}, f32[64,1024]{1,0:T(8,128)}, u32[]{:S(2)}, u32[]{:S(2)}) collective-permute-start(f32[64,1024]{1,0:T(8,128)S(1)} %get-tuple-element.228), channel_id=1, source_target_pairs={{0,0},{4,4},{16,8},{20,12},{8,16},{12,20},{24,24},{28,28},{1,1},{5... | collective-permute-start | bytes 786440 | tf_op jit(solution)/shard_map/ppermute | solution.py:545
  319.5 29.4 %collective-permute-start.65 = (f32[192,1024]{1,0:T(8,128)S(1)}, f32[192,1024]{1,0:T(8,128)S(1)}, u32[]{:S(2)}, u32[]{:S(2)}) collective-permute-start(f32[192,1024]{1,0:T(8,128)S(1)} %shard_map.258), channel_id=1, source_target_pairs={{0,16},{16,0},{1,17},{17,1},{2,18},{18,2},{3,19},{19,3},{4,20},{20... | collective-permute-start | bytes 2359304 | tf_op jit(solution)/shard_map/ppermute | solution.py:495
  326.3 21.7 %all-to-all-start.1 = ((bf16[16,96,128]{2,1,0:T(8,128)(2,1)}), bf16[16,96,128]{2,1,0:T(8,128)(2,1)S(1)}, u32[]{:S(2)}, u32[]{:S(2)}) async-start(bf16[16,96,128]{2,1,0:T(8,128)(2,1)} %get-tuple-element.193), calls=%async_computation.1 | async-start | bytes 786432 | tf_op jit(solution)/shard_map/all_to_all | solution.py:1517
  352.5 7.1 %collective-permute-start.67 = (bf16[64,1280]{1,0:T(8,128)(2,1)S(1)}, bf16[64,1280]{1,0:T(8,128)(2,1)S(1)}, u32[]{:S(2)}, u32[]{:S(2)}) collective-permute-start(bf16[64,1280]{1,0:T(8,128)(2,1)S(1)} %get-tuple-element.203), channel_id=1, source_target_pairs={{0,1},{1,0},{2,3},{3,2},{4,5},{5,4},{6,7},{7,6},{8,9},{9,8},{10,11... | collective-permute-start | bytes 491528 | tf_op jit(solution)/shard_map/ppermute | solution.py:495
  354.2 9.7 %collective-permute-start.68 = (bf16[64,1280]{1,0:T(8,128)(2,1)S(1)}, bf16[64,1280]{1,0:T(8,128)(2,1)S(1)}, u32[]{:S(2)}, u32[]{:S(2)}) collective-permute-start(bf16[64,1280]{1,0:T(8,128)(2,1)S(1)} %get-tuple-element.204), channel_id=1, source_target_pairs={{0,2},{2,0},{1,3},{3,1},{4,6},{6,4},{5,7},{7,5},{8,10},{10,8},{9,1... | collective-permute-start | bytes 491528 | tf_op jit(solution)/shard_map/ppermute | solution.py:495
  354.5 9.4 %collective-permute-start.69 = (bf16[64,1280]{1,0:T(8,128)(2,1)S(1)}, bf16[64,1280]{1,0:T(8,128)(2,1)S(1)}, u32[]{:S(2)}, u32[]{:S(2)}) collective-permute-start(bf16[64,1280]{1,0:T(8,128)(2,1)S(1)} %get-tuple-element.205), channel_id=1, source_target_pairs={{0,3},{1,2},{2,1},{3,0},{4,7},{5,6},{6,5},{7,4},{8,11},{9,10},{10,... | collective-permute-start | bytes 491528 | tf_op jit(solution)/shard_map/ppermute | solution.py:585
  358.0 7.1 %collective-permute-start.70 = (bf16[64,1280]{1,0:T(8,128)(2,1)S(1)}, bf16[64,1280]{1,0:T(8,128)(2,1)S(1)}, u32[]{:S(2)}, u32[]{:S(2)}) collective-permute-start(bf16[64,1280]{1,0:T(8,128)(2,1)S(1)} %get-tuple-element.202.refs_0_), channel_id=1, source_target_pairs={{0,16},{16,0},{1,17},{17,1},{2,18},{18,2},{3,19},{19,3},{4,20},{20... | collective-permute-start | bytes 491528 | tf_op jit(solution)/shard_map/ppermute | solution.py:495
  359.6 5.4 %collective-permute-start.71 = (bf16[64,1280]{1,0:T(8,128)(2,1)S(1)}, bf16[64,1280]{1,0:T(8,128)(2,1)S(1)}, u32[]{:S(2)}, u32[]{:S(2)}) collective-permute-start(bf16[64,1280]{1,0:T(8,128)(2,1)S(1)} %collective-permute-done.67.refs_1_), channel_id=1, source_target_pairs={{0,16},{16,0},{1,17},{17,1},{2,18},{18,2},{3,19},{19,3},{4,20},{20... | collective-permute-start | bytes 491528 | tf_op jit(solution)/shard_map/ppermute | solution.py:495
  (94 other events, 733.2 us)
Sparse Core Ops, SparseCore 0:
  11.4 69.4 all-gather.4
  91.4 47.4 all-gather.2
  222.2 95.5 reduce-scatter.1
where the time goes:
time: 381 us; the launch traced here: 378 us
  waiting for transfers between devices  161 us (42%)
  starting transfers between devices  102 us (27%)
  Pallas kernels  48.7 us (13%)
  local copies, waits for them, and re-layouts  38.4 us (10%)
  between operations  16.7 us (4%)
  other arithmetic  9.86 us (3%)
    ppermute x49, waiting for transfers between devices, hop(): return lax.ppermute(values, axis, [(i, i ^ step) for i in range(size)])  90.4 us
    pallas_call x24, Pallas kernels, whole_call(): pl.pallas_call(body, out_shape=out_shapes, in_specs=specs, out_specs=[vme...  48.7 us
    ppermute x49, starting transfers between devices, hop(): return lax.ppermute(values, axis, [(i, i ^ step) for i in range(size)])  45.2 us
    unnamed x160, local copies, waits for them, and re-layouts  33.9 us
    ppermute x4, waiting for transfers between devices, fast_device(): lax.ppermute(grad, EVERY, [(there, here) for here, there in head_routes(s...  26.3 us
    ppermute x4, waiting for transfers between devices, fast_device(): lax.ppermute(head_parts[int(single)], EVERY, head_routes(single, k))  19.8 us
    ppermute x4, starting transfers between devices, fast_device(): lax.ppermute(head_parts[int(single)], EVERY, head_routes(single, k))  16.3 us
    all_to_all x2, waiting for transfers between devices, exchange(): return lax.all_to_all(blocks, axes, split_axis=0, concat_axis=0, tiled=True)  14.7 us
  transfers between devices with their start and end apart: 79, of which 39 were waited for; matrix products, arithmetic and copies ran while one was open for 3% of the time, Pallas kernels for 10%

commit v1 on v0

--- a/solution.py
+++ b/solution.py
@@ -601,19 +601,84 @@
     return jax.ShapeDtypeStruct(shape, jnp.float32)
 
 
-def whole_call(body, operands, out_shapes, scratch=(), left_out=()):
-    vmem = pl.BlockSpec(memory_space=pltpu.VMEM)
-    specs = [
-        pl.BlockSpec(memory_space=pltpu.HBM) if i in left_out else vmem
-        for i in range(len(operands))
+FLOPS_PER_US = 1.1e9
+TIMES = {
+    "attend_body": 10.0,
+    "feed_body": 3.5,
+    "bottle_body": 5.7,
+    "feed_back_body": 2.0,
+    "pair_grad_body": 3.4,
+    "attend_back_body": 9.2,
+    "whole_grads_body": 1.3,
+    "cells_back_body": 1.4,
+}
+
+
+def took(body):
+    inner = body.func if isinstance(body, functools.partial) else body
+    return TIMES.get(inner.__name__, 0.8)
+
+
+def whole_call(
+    body, operands, out_shapes, scratch=(), left_out=(), loaded=(), kept=(), early=False
+):
+    vmem, hbm = pl.BlockSpec(memory_space=pltpu.VMEM), pl.BlockSpec(memory_space=pltpu.HBM)
+    n_in, n_out, n_own = len(operands), len(out_shapes), len(scratch)
+    left_out, loaded, kept = list(left_out), list(loaded), list(kept)
+
+    def run(*refs):
+        ins, outs = list(refs[:n_in]), list(refs[n_in : n_in + n_out])
+        own = refs[n_in + n_out : n_in + n_out + n_own]
+        rest = refs[n_in + n_out + n_own :]
+        in_copies = []
+        for at, i in enumerate(loaded):
+            in_copies.append(pltpu.make_async_copy(ins[i], rest[at], rest[-1].at[at]))
+            ins[i] = rest[at]
+        for copy in in_copies:
+            copy.start()
+        out_copies = {}
+        for at, i in enumerate(kept, len(loaded)):
+            out_copies[i] = pltpu.make_async_copy(rest[at], outs[i], rest[-1].at[at])
+            outs[i] = rest[at]
+        for copy in in_copies:
+            copy.wait()
+        started = []
+
+        def store(i):
+            out_copies[i].start()
+            started.append(i)
+
+        body(*ins, *outs, *own, **({"store": store} if early else {}))
+        for i in out_copies:
+            if i not in started:
+                out_copies[i].start()
+        for copy in out_copies.values():
+            copy.wait()
+
+    operands = [
+        pltpu.with_memory_space_constraint(part, pltpu.HBM)
+        if i in loaded
+        else part
+        for i, part in enumerate(operands)
+    ]
+    buffers = [pltpu.VMEM(operands[i].shape, operands[i].dtype) for i in loaded]
+    buffers += [pltpu.VMEM(out_shapes[i].shape, out_shapes[i].dtype) for i in kept]
+    if buffers:
+        buffers.append(pltpu.SemaphoreType.DMA((len(buffers),)))
+    out_shapes = [
+        pltpu.HBM(part.shape, part.dtype) if i in kept else part
+        for i, part in enumerate(out_shapes)
     ]
     return pl.pallas_call(
-        body,
+        run,
         out_shape=out_shapes,
-        in_specs=specs,
-        out_specs=[vmem] * len(out_shapes),
-        scratch_shapes=list(scratch),
+        in_specs=[hbm if i in left_out or i in loaded else vmem for i in range(n_in)],
+        out_specs=[hbm if i in kept else vmem for i in range(n_out)],
+        scratch_shapes=[*scratch, *buffers],
         compiler_params=pltpu.CompilerParams(vmem_limit_bytes=VMEM_LIMIT),
+        cost_estimate=pl.CostEstimate(
+            flops=int(took(body) * FLOPS_PER_US), bytes_accessed=0, transcendentals=0
+        ),
     )(*operands)
 
 
@@ -794,6 +859,7 @@
             pltpu.VMEM((16, SMALL, width), jnp.bfloat16),
             pltpu.VMEM((1, inner), jnp.float32),
         ],
+        loaded=range(2, 6),
     )
 
 
@@ -834,18 +900,41 @@
     return keep, *plane_hops(sends)
 
 
+def out_grad_body(*refs):
+    pieces, mixed_ref, out_ref, datt_ref, sems = refs[:8], *refs[8:]
+    stack_rows(pieces, datt_ref, sems, lambda i: device_place(NEAR[i % 4], i // 4))
+    rows = out_ref.shape[1]
+    for chip in range(0, out_ref.shape[0], 4):
+        lanes = slice(chip * rows, (chip + 4) * rows)
+        grad = to_low(product_tn(datt_ref[:, lanes], mixed_ref[...]))
+        out_ref[chip : chip + 4] = grad.reshape(4, rows, PAIR)
+
+
+def out_grads(pieces, mixed):
+    rows, width = pieces[0].shape
+    return whole_call(
+        out_grad_body,
+        (*pieces, mixed),
+        [low_shape(16, width // 16, PAIR), low_shape(8 * rows, width)],
+        [pltpu.SemaphoreType.DMA((8,))],
+        range(8),
+    )
+
+
 def attend_back_body(
     qkv_ref,
     bias_ref,
     lse_ref,
     out_t_ref,
     head_w_ref,
-    *refs,
+    datt_ref,
+    dqkv_ref,
+    far_ref,
+    dmixed_ref,
+    dk_ref,
+    dv_ref,
 ):
-    pieces, (dqkv_ref, far_ref, datt_ref) = refs[:8], refs[8:11]
-    dmixed_ref, dk_ref, dv_ref, sems = refs[11:]
     rows = qkv_ref.shape[0]
-    stack_rows(pieces, datt_ref, sems, lambda i: device_place(NEAR[i % 4], i // 4))
     for start in range(0, rows, 256):
         at = slice(start, start + 256)
         dmixed_ref[at] = to_low(product(datt_ref[at], out_t_ref[...]))
@@ -886,19 +975,17 @@
         )
 
 
-def attend_back(qkv, bias, lse, out_t, head_w, pieces):
+def attend_back(qkv, bias, lse, out_t, head_w, datt):
     rows, width = qkv.shape[0], head_w.shape[1]
     return whole_call(
         attend_back_body,
-        (qkv, bias, lse, out_t, head_w, *pieces),
-        [low_shape(rows, 3 * PAIR), low_shape(rows // 2, width), low_shape(rows, width)],
+        (qkv, bias, lse, out_t, head_w, datt),
+        [low_shape(rows, 3 * PAIR), low_shape(rows // 2, width)],
         [
             pltpu.VMEM((rows, PAIR), jnp.bfloat16),
             pltpu.VMEM((rows, PAIR), jnp.float32),
             pltpu.VMEM((rows, PAIR), jnp.float32),
-            pltpu.SemaphoreType.DMA((8,)),
         ],
-        range(5, 13),
     )
 
 
@@ -1108,7 +1195,12 @@
 def feed_back(pieces, weights, slope, came=None):
     count = 4 * pieces[0].shape[0]
     return feed_call(
-        feed_back_body, pieces, weights, (slope,), came, [low_shape(count, 512), wide_shape(1, 512)]
+        feed_back_body,
+        pieces,
+        weights,
+        (slope,),
+        came,
+        [low_shape(count, 512), wide_shape(1, 512)],
     )
 
 
@@ -1117,7 +1209,7 @@
     return (*near, *(other_core(part) for part in near))
 
 
-GRAD_ROWS = 512
+GRAD_ROWS = 448
 
 
 def pair_grad_body(*refs):
@@ -1143,10 +1235,11 @@
             )
         grad = to_low(product_tn(fed_ref[:, z * 256 : (z + 1) * 256], act_ref[...]))
         out_ref[at + 128 : at + 256] = jnp.concatenate([grad[:128], grad[128:]], axis=1)
-        out_ref[at + 256 : at + GRAD_ROWS, :width] = whole_ref[z * 256 : (z + 1) * 256]
-        out_ref[at + 256 : at + GRAD_ROWS, width:] = jnp.zeros(
-            (256, out_ref.shape[1] - width), jnp.bfloat16
-        )
+        out_ref[at + 256 : at + GRAD_ROWS, :width] = whole_ref[z * 256 : z * 256 + 192]
+        for piece in range(3):
+            out_ref[at + 256 + piece * 64 : at + 320 + piece * 64, width:] = whole_ref[
+                z * 256 + 192 : (z + 1) * 256, piece * 256 : (piece + 1) * 256
+            ]
 
 
 def pair_grads(rows_fed, rows_two, whole, acts, dus):
@@ -1171,8 +1264,13 @@
         at = pl.ds(pl.multiple_of(128 + (place % 2) * rows, rows), rows)
         lanes = pl.ds(pl.multiple_of((place // 2) * half, half), half)
         outs[i][:, :half] = sum_ref[at, lanes]
-        whole = pl.ds(pl.multiple_of(256 + place * rows, rows), rows)
-        outs[i][:, half:] = sum_ref[whole, : outs[i].shape[1] - half]
+        first = pl.multiple_of(256 + jnp.minimum(place, 2) * rows, rows)
+        whole = sum_ref[pl.ds(first, rows), : outs[i].shape[1] - half]
+        fourth = jnp.concatenate(
+            [sum_ref[256 + q * rows : 256 + (q + 1) * rows, whole.shape[1] :] for q in range(3)],
+            axis=1,
+        )
+        outs[i][:, half:] = jnp.where(place == 3, fourth, whole)
 
 
 def z_sum(refs):
@@ -1186,21 +1284,25 @@
     for chip in range(16):
         pair = pl.multiple_of((lax.axis_index("grp") * 4 + chip % 4) * PAIR, PAIR)
         pairs_ref[chip] = out_ref[:, pl.ds(pair, PAIR)]
-    for i, step in enumerate(NEAR):
+    half = outs[0].shape[1]
+    for i, (step, lane) in enumerate(zip((0, 1, 2, 1), (0, 0, 0, half))):
         for block in range(4):
-            outs[i][:, block * 128 : (block + 1) * 128] = back_ref[
-                :, pl.ds(chunk_place(block, step), 128)
+            outs[step][:, lane + block * 128 : lane + (block + 1) * 128] = back_ref[
+                :, pl.ds(chunk_place(block, NEAR[i]), 128)
             ]
 
 
-def lay_body(*refs):
-    out_ref = refs[5]
-    out_ref[:128] = refs[0][...]
-    half = refs[1].shape[1]
-    for i, step in enumerate(NEAR):
-        place = chip_place(step)
+def lay_body(in_ref, own_ref, came_x_ref, came_y_ref, out_ref):
+    out_ref[:128] = in_ref[...]
+    half = own_ref.shape[1]
+    for i, (ref, lane) in enumerate(
+        ((own_ref, 0), (came_x_ref, 0), (came_y_ref, 0), (came_y_ref, half))
+    ):
+        place = chip_place(NEAR[i])
         rows = pl.ds(pl.multiple_of(128 + (place % 2) * 64, 64), 64)
-        out_ref[rows, pl.ds(pl.multiple_of((place // 2) * half, half), half)] = refs[1 + i][...]
+        out_ref[rows, pl.ds(pl.multiple_of((place // 2) * half, half), half)] = ref[
+            :, lane : lane + half
+        ]
 
 
 def core_order(own, other):
@@ -1544,10 +1646,25 @@
     ff = w_ffn_out.shape[1]
     inner = 16 * inner_bias.shape[1]
 
+    part = width // 16
+    shard = jnp.concatenate(
+        [half_of(w[0], 0, "grp", True).T for w in (w_latent, w_decode)], axis=1
+    )
+    shard_width = shard.shape[1]
+    whole = lax.all_gather(shard, CHIPS, axis=0, tiled=True)
+
+    out_pairs, back_own, back_x, back_y = whole_call(
+        pick_body,
+        after((w_out[0].T, w_ffn_out[0].T), shard),
+        [low_shape(16, part, PAIR)]
+        + [low_shape(part, ff // 8 * count) for count in (1, 2, 1)],
+    )
+    out_t = exchange(out_pairs, CHIPS).reshape(width, PAIR)
+
     blocks = whole_call(
         enter_body,
         (
-            cell_input.reshape(rows, width),
+            after(cell_input.reshape(rows, width), out_pairs),
             lengths,
             vectors[0],
             inner_bias,
@@ -1570,38 +1687,40 @@
         lax.ppermute(head_parts[int(single)], EVERY, head_routes(single, k))
         for single, k in ARRIVALS
     ]
-    plane_near = jnp.stack([first, hop(first, "x")])
-    plane_own = jnp.concatenate([plane_near, hop(after(plane_near, came), "y")])
-    plane_other = other_core(plane_own)
-
-    part = width // 16
-    out_pairs, *back_cols = whole_call(
-        pick_body,
-        (w_out[0].T, w_ffn_out[0].T),
-        [low_shape(16, part, PAIR)] + [low_shape(part, ff // 8)] * 4,
-    )
-    out_t = exchange(after(out_pairs, first), CHIPS).reshape(width, PAIR)
+
     in_own = half_of(w_ffn_in[0], 1, "grp", True).T
-    back_cols = (back_cols[0], *plane_hops(after(back_cols[1:], plane_near)))
-    (pair_own,) = whole_call(lay_body, (in_own, *back_cols), [low_shape(256, width)])
-
-    shard = jnp.concatenate(
-        [half_of(w[0], 0, "grp", True).T for w in (w_latent, w_decode)], axis=1
-    )
-    shard_width = shard.shape[1]
-    whole = lax.all_gather(shard, CHIPS, axis=0, tiled=True)
-    pair_w = lax.all_gather(after(pair_own, came), "z", axis=0, tiled=True)
-
-    vec, means, logvars, normed, qkv, head_w, mixed, lse, bias = attend(
-        plane_own, plane_other, after(came, pair_own), lat, inner
-    )
-    mix_parts = mix_out(mixed, out_t, out_t)
-
     noise_high = to_low(noise_draw[0, 0])
     noise_rest = to_low(noise_draw[0, 0] - wide(noise_high))
     extra = jnp.concatenate(
         [cotangent[0], jnp.concatenate([noise_high, noise_rest], axis=2)], axis=1
     )
+    size = span + SMALL
+    one, two = first[0], first[1]
+    one_x = hop(jnp.concatenate([one, back_x]), "x")
+    two_y = hop(two, "y")
+    sent = jnp.concatenate(
+        [one, one_x[:size], jnp.concatenate([back_y, one_x[size:, ff // 8 :]], axis=1)]
+    )
+    sent_y, sent_x = after((sent, jnp.concatenate([two, two_y])), (came, extra, out_t))
+    near_y = hop(sent_y, "y")
+    near_x = hop(sent_x, "x")
+    plane_own = jnp.concatenate(
+        [one, two, one_x[:size], near_x[:size], near_y[:size], two_y]
+        + [near_y[size : 2 * size], near_x[size:]]
+    ).reshape(4, 2, size, width)
+    plane_other = other_core(plane_own)
+    (pair_own,) = whole_call(
+        lay_body,
+        (in_own, back_own, one_x[size:], near_y[2 * size :]),
+        [low_shape(256, width)],
+    )
+    pair_w = lax.all_gather(pair_own, "z", axis=0, tiled=True)
+
+    vec, means, logvars, normed, qkv, head_w, mixed, lse, bias = attend(
+        plane_own, plane_other, after(came, pair_own), lat, inner
+    )
+    mix_parts = mix_out(mixed, out_t, whole)
+
     extra = to_slides(after(extra, mixed))
     cot = extra[:, :span].reshape(rows, width)
     noise = extra[:, span:].reshape(rows, width)
@@ -1609,11 +1728,10 @@
 
     attended, normed_two, hidden = project(mix_parts, first, vec)
     rows_two = plane_rows(normed_two)
-    whole = after(whole, rows_two)
-    wholes = (whole, other_core(whole))
     act_far, slope_far, fed_far = feed(rows_two[4:], pair_w, vec)
     act, slope, keep, *sends = feed(rows_two[:4], pair_w, vec, other_core(fed_far))
     fed_parts = (keep, *plane_hops(sends))
+    wholes = (whole, other_core(whole))
     output, fed_low, sample_low, dlat_low, dfed, dfed_low, dmeans, dlogvars, bottle_sums = (
         bottle_call(
             attended, fed_parts, vec, wholes, noise, cot, means, logvars
@@ -1621,7 +1739,9 @@
     )
 
     rows_fed = plane_rows(dfed_low)
-    layer_out = from_slides(after(output, rows_fed).reshape(slots, span, width))
+    layer_out = wide(
+        from_slides(after(to_low(output), rows_fed).reshape(slots, span, width))
+    )
     whole_grad = whole_grads((dlat_low, fed_low, cot, sample_low))
     du_far, ff_far, norm_far = feed_back(rows_fed[4:], pair_w, slope_far)
     du, ff_sums, keep, *sends = feed_back(
@@ -1630,9 +1750,12 @@
     norm_parts = (keep, *plane_hops(sends))
     grads = pair_grads(rows_fed, rows_two, whole_grad, (act, act_far), (du, du_far))
     grads_sum = lax.psum_scatter(grads, "z", scatter_dimension=0, tiled=True)
-    datt, datt_low, project_sums = project_back(after(norm_parts, grads), attended, dfed, vec)
+    datt, datt_low, project_sums = project_back(
+        after(norm_parts, (grads, layer_out)), attended, dfed, vec
+    )
     rows_datt = plane_rows(datt_low)
-    dqkv, dn_far, all_datt = attend_back(qkv, bias, lse, out_t, head_w, rows_datt)
+    out_grad, all_datt = out_grads(rows_datt, mixed)
+    dqkv, dn_far = attend_back(qkv, bias, lse, out_t, head_w, all_datt)
     dn_keep, *dn_sends = dnormed(dqkv, head_w, other_core(dn_far))
     homes, head_sums = head_grads(dqkv, after(normed, dn_sends))
     dn_parts = (dn_keep, *plane_hops(dn_sends))
@@ -1649,33 +1772,33 @@
             ff_far,
             dmeans,
             dlogvars,
-            to_low(product_tn(all_datt, mixed)).reshape(16, part, PAIR),
+            out_grad,
         ),
         inner,
     )
-    grad_cells = from_slides(grad_rows.reshape(slots, span, width))
+    grad_cells = wide(from_slides(to_low(grad_rows).reshape(slots, span, width)))
     sum_in, *sums = whole_call(
         split_grad_body,
-        (after(grads_sum, dn_parts),),
+        (after(grads_sum, packed),),
         [wide_shape(128, width)] + [low_shape(part, ff // 8 + shard_width)] * 4,
     )
     sums = [sums[0], *plane_hops(sums[1:])]
     sums += [other_core(total) for total in sums]
 
+    (last,) = whole_call(
+        last_sum_body, (exchange(packed, CHIPS),), [wide_shape(part + SMALL, 4 * PAIR)]
+    )
+    grad_out_w, small_sums = whole_call(
+        last_body, (last, other_core(last)), [wide_shape(part, width), wide_shape(SMALL, PAIR)]
+    )
+    grad_out_w = grad_out_w.T
+    homes = after(homes, (last, sums[0]))
     homes = [
         lax.ppermute(grad, EVERY, [(there, here) for here, there in head_routes(single, k)])
         for grad, (single, k) in zip(homes, ARRIVALS)
     ]
     (home,) = whole_call(home_body, homes, [wide_shape(3 * HEAD_DIM, width)])
     grad_qkv = (home + other_core(home)).T
-
-    (last,) = whole_call(
-        last_sum_body, (exchange(packed, CHIPS),), [wide_shape(part + SMALL, 4 * PAIR)]
-    )
-    grad_out_w, small_sums = whole_call(
-        last_body, (last, other_core(last)), [wide_shape(part, width), wide_shape(SMALL, PAIR)]
-    )
-    grad_out_w = grad_out_w.T
     vec_out = small_sums[:9, :part]
     inner_out = small_sums[9 : 9 + inner // width, :part].reshape(1, -1)
     means_out = small_sums[:, part : part + lat // 16]

time: 381 us -> 352 us (0.924)
  waiting for transfers between devices: 161 us -> 141 us
  starting transfers between devices: 102 us -> 90.3 us
    ppermute x4, waiting for transfers between devices: 26.3 us -> 0.01 us  [fast_device(): lax.ppermute(grad, EVERY, [(there, here) for here, there in head_routes(s...]
    all_to_all x2, waiting for transfers between devices: 14.7 us -> 3.21 us  [exchange(): return lax.all_to_all(blocks, axes, split_axis=0, concat_axis=0, tiled=True)]
    ppermute x9 -> x8, waiting for transfers between devices: 6.53 us -> 16.4 us  [plane_hops(): lax.ppermute(values[2], ('y', 'x'), [(i, i ^ 3) for i in range(4)])]
    ppermute x4, waiting for transfers between devices: 0.01 us -> 8.52 us  [from_slides(): lax.ppermute(blocks[k], ('grp', 'z'), [(there, here) for here, there in s...]
    ppermute x4, waiting for transfers between devices: 19.8 us -> 13.2 us  [fast_device(): lax.ppermute(head_parts[int(single)], EVERY, head_routes(single, k))]
    ppermute x49, waiting for transfers between devices: 90.4 us -> 96.4 us  [hop(): return lax.ppermute(values, axis, [(i, i ^ step) for i in range(size)])]
    ppermute x49, starting transfers between devices: 45.2 us -> 40.5 us  [hop(): return lax.ppermute(values, axis, [(i, i ^ step) for i in range(size)])]
    ppermute x4, starting transfers between devices: 16.3 us -> 12 us  [fast_device(): lax.ppermute(head_parts[int(single)], EVERY, head_routes(single, k))]
  transfers between devices with their start and end apart: 79 -> 78, of which waited for: 39 -> 35; matrix products, arithmetic and copies ran while one was open for 3% -> 5% of each run, Pallas kernels for 10% -> 10%
where the time goes in v1:
time: 352 us; the launch traced here: 348 us
  waiting for transfers between devices  141 us (40%)
  starting transfers between devices  90.3 us (26%)
  Pallas kernels  49.2 us (14%)
  local copies, waits for them, and re-layouts  41.9 us (12%)
  between operations  16.8 us (5%)
  other arithmetic  8.95 us (3%)
    ppermute x49, waiting for transfers between devices, hop(): return lax.ppermute(values, axis, [(i, i ^ step) for i in range(size)])  96.4 us
    pallas_call x25, Pallas kernels, whole_call(): pl.pallas_call(run, out_shape=out_shapes, in_specs=[hbm if i in left_out...  49.2 us
    ppermute x49, starting transfers between devices, hop(): return lax.ppermute(values, axis, [(i, i ^ step) for i in range(size)])  40.5 us
    unnamed x166, local copies, waits for them, and re-layouts  31.5 us
    ppermute x8, waiting for transfers between devices, plane_hops(): lax.ppermute(values[2], ('y', 'x'), [(i, i ^ 3) for i in range(4)])  16.4 us
    ppermute x4, waiting for transfers between devices, fast_device(): lax.ppermute(head_parts[int(single)], EVERY, head_routes(single, k))  13.2 us
    ppermute x4, starting transfers between devices, fast_device(): lax.ppermute(head_parts[int(single)], EVERY, head_routes(single, k))  12 us
    ppermute x8, starting transfers between devices, plane_hops(): lax.ppermute(values[2], ('y', 'x'), [(i, i ^ 3) for i in range(4)])  11.2 us
  transfers between devices with their start and end apart: 78, of which 35 were waited for; matrix products, arithmetic and copies ran while one was open for 5% of the time, Pallas kernels for 10%

profile of v1, /device:TPU:0, one launch (start us, length us, event | category | flops | bytes accessed | tf_op | source)
XLA Modules:
  0.0 348.3 jit_solution(15242087598294070013)
XLA Ops:
  7.3 1.7 dynamic-slice_bitcast_fusion
  9.0 3.6 %collective-permute-start.4 = (bf16[128,1024]{1,0:T(8,128)(2,1)}, bf16[128,1024]{1,0:T(8,128)(2,1)}, u32[]{:S(2)}, u32[]{:S(2)}) collective-permute-start(bf16[128,1024]{1,0:T(8,128)(2,1)} %dynamic-slice_bitcast_fusion), channel_id=1, source_target_pairs={{0,0},{1,6},{2,3},{3,21},{4,18},{5,4},{6,1},{7,7},{8,16},{9,22},{1... | collective-permute-start | bytes 786440 | tf_op jit(solution)/shard_map/ppermute | solution.py:1687
  12.6 2.2 collective-permute-start.6
  19.9 7.4 %all-to-all-start = ((bf16[16,64,128]{2,1,0:T(8,128)(2,1)}), bf16[16,64,128]{2,1,0:T(8,128)(2,1)S(1)}, u32[]{:S(2)}, u32[]{:S(2)}) async-start(bf16[16,64,128]{2,1,0:T(8,128)(2,1)} %get-tuple-element.115), calls=%async_computation | async-start | bytes 524288 | tf_op jit(solution)/shard_map/all_to_all | solution.py:1619
  28.3 2.0 collective-permute-start.1
  31.2 1.5 collective-permute-start.5
  34.3 3.3 collective-permute-done.1
  37.6 2.0 collective-permute-start.3
  39.6 3.3 collective-permute-done.3
  42.9 4.6 %collective-permute-start.7 = (bf16[64,1024]{1,0:T(8,128)(2,1)S(1)}, bf16[64,1024]{1,0:T(8,128)(2,1)S(1)}, u32[]{:S(2)}, u32[]{:S(2)}) collective-permute-start(bf16[64,1024]{1,0:T(8,128)(2,1)S(1)} %dynamic-slice_bitcast_fusion.1), channel_id=1, source_target_pairs={{0,5},{1,1},{2,20},{3,16},{4,23},{5,19},{6,6},{7,2},{8,21},{9,17},... | collective-permute-start | bytes 393224 | tf_op jit(solution)/shard_map/ppermute | solution.py:1687
  49.1 13.2 %collective-permute-done.7.refs_5_ = bf16[64,1024]{1,0:T(8,128)(2,1)S(1)} collective-permute-done((bf16[64,1024]{1,0:T(8,128)(2,1)S(1)}, bf16[64,1024]{1,0:T(8,128)(2,1)S(1)}, u32[]{:S(2)}, u32[]{:S(2)}) %collective-permute-start.7) | collective-permute-done | bytes 131104 | tf_op jit(solution)/shard_map/ppermute | solution.py:1687
  64.2 10.7 %collective-permute-done.8 = bf16[160,1024]{1,0:T(8,128)(2,1)S(1)} collective-permute-done((bf16[160,1024]{1,0:T(8,128)(2,1)}, bf16[160,1024]{1,0:T(8,128)(2,1)S(1)}, u32[]{:S(2)}, u32[]{:S(2)}) %collective-permute-start.8) | collective-permute-done | bytes 327712 | tf_op jit(solution)/shard_map/ppermute | solution.py:495
  74.8 5.6 %collective-permute-done.9 = bf16[224,1024]{1,0:T(8,128)(2,1)S(1)} collective-permute-done((bf16[224,1024]{1,0:T(8,128)(2,1)S(1)}, bf16[224,1024]{1,0:T(8,128)(2,1)S(1)}, u32[]{:S(2)}, u32[]{:S(2)}) %collective-permute-start.9) | collective-permute-done | bytes 458784 | tf_op jit(solution)/shard_map/ppermute | solution.py:495
  86.0 9.7 %shard_map.240 = (f32[16,1024]{1,0:T(8,128)S(1)}, f32[16,512]{1,0:T(8,128)S(1)}, f32[16,512]{1,0:T(8,128)S(1)}, bf16[1024,1024]{1,0:T(8,128)(2,1)S(1)}, bf16[102...) custom-call(bf16[4,2,80,1024]{3,2,1,0:T(8,128)(2,1)S(1)} %bitcast.99, ...), custom_call_target="tpu_custom_call" | custom-call | flops 11000000512 | tf_op jit(solution)/shard_map/pallas_call | solution.py:672
  99.6 2.3 collective-permute-done.11.refs_2_
  103.9 1.7 collective-permute-start.13
  106.9 5.6 %collective-permute-done.12.refs_1_ = bf16[128,1024]{1,0:T(8,128)(2,1)S(1)} collective-permute-done((bf16[128,1024]{1,0:T(8,128)(2,1)S(1)}, bf16[128,1024]{1,0:T(8,128)(2,1)S(1)}, u32[]{:S(2)}, u32[]{:S(2)}) %collective-permute-start.12) | collective-permute-done | bytes 262176 | tf_op jit(solution)/shard_map/ppermute | solution.py:495
  112.5 4.6 %collective-permute-done.13.refs_2_ = bf16[128,1024]{1,0:T(8,128)(2,1)S(1)} collective-permute-done((bf16[128,1024]{1,0:T(8,128)(2,1)S(1)}, bf16[128,1024]{1,0:T(8,128)(2,1)S(1)}, u32[]{:S(2)}, u32[]{:S(2)}) %collective-permute-start.13) | collective-permute-done | bytes 262176 | tf_op jit(solution)/shard_map/ppermute | solution.py:495
  117.1 1.6 collective-permute-done.14.refs_3_
  121.2 1.7 collective-permute-start.16
  124.0 5.7 %collective-permute-done.15.refs_1_.refs_9_ = bf16[128,1024]{1,0:T(8,128)(2,1)S(1)} collective-permute-done((bf16[128,1024]{1,0:T(8,128)(2,1)S(1)}, bf16[128,1024]{1,0:T(8,128)(2,1)S(1)}, u32[]{:S(2)}, u32[]{:S(2)}) %collective-permute-start.15) | collective-permute-done | bytes 262176 | tf_op jit(solution)/shard_map/ppermute | solution.py:495
  129.7 4.6 %collective-permute-done.16.refs_2_.refs_10_ = bf16[128,1024]{1,0:T(8,128)(2,1)S(1)} collective-permute-done((bf16[128,1024]{1,0:T(8,128)(2,1)S(1)}, bf16[128,1024]{1,0:T(8,128)(2,1)S(1)}, u32[]{:S(2)}, u32[]{:S(2)}) %collective-permute-start.16) | collective-permute-done | bytes 262176 | tf_op jit(solution)/shard_map/ppermute | solution.py:495
  139.1 1.6 copy-done.3
  144.5 3.3 shard_map.244
  153.8 4.0 %shard_map.245 = (bf16[512,512]{1,0:T(8,128)(2,1)S(1)}, f32[512,512]{1,0:T(8,128)S(1)}, f32[128,1024]{1,0:T(8,128)S(1)}, bf16[128,1024]{1,0:T(8,128)(2,1)S(1)}, ...) custom-call(bf16[128,1024]{1,0:T(8,128)(2,1)S(1)} %get-tuple-element.136.refs_0_.refs_8_, ...), custom_call_target="tpu_custom_call" | custom-call | flops 3849999872 | tf_op jit(solution)/shard_map/pallas_call | solution.py:672
  161.4 3.2 collective-permute-done.23.refs_2_
  164.6 4.0 %collective-permute-done.24.refs_3_ = bf16[128,1024]{1,0:T(8,128)(2,1)S(1)} collective-permute-done((bf16[128,1024]{1,0:T(8,128)(2,1)S(1)}, bf16[128,1024]{1,0:T(8,128)(2,1)S(1)}, u32[]{:S(2)}, u32[]{:S(2)}) %collective-permute-start.24) | collective-permute-done | bytes 262176 | tf_op jit(solution)/shard_map/ppermute | solution.py:495
  168.6 2.8 collective-permute-done.25.refs_4_
  171.5 5.6 %shard_map.246 = (f32[128,1024]{1,0:T(8,128)S(1)}, bf16[128,1024]{1,0:T(8,128)(2,1)S(1)}, bf16[128,512]{1,0:T(8,128)(2,1)S(1)}, bf16[128,1024]{1,0:T(8,128)(2,1)...) custom-call(f32[128,1024]{1,0:T(8,128)S(1)} %copy-done.44, ...), custom_call_target="tpu_custom_call" | custom-call | flops 6270000128 | tf_op jit(solution)/shard_map/pallas_call | solution.py:672
  178.3 2.3 collective-permute-start.30
  181.4 1.5 collective-permute-start.32
  182.9 2.8 collective-permute-done.29.refs_1_
  185.7 2.9 collective-permute-start.33
  188.6 4.0 %collective-permute-done.30.refs_2_ = bf16[128,1024]{1,0:T(8,128)(2,1)S(1)} collective-permute-done((bf16[128,1024]{1,0:T(8,128)(2,1)S(1)}, bf16[128,1024]{1,0:T(8,128)(2,1)S(1)}, u32[]{:S(2)}, u32[]{:S(2)}) %collective-permute-start.30) | collective-permute-done | bytes 262176 | tf_op jit(solution)/shard_map/ppermute | solution.py:495
  194.8 1.9 shard_map.247
  198.1 1.6 collective-permute-done.41.refs_5_
  201.4 1.9 shard_map.249
  206.3 3.3 shard_map.250
  209.6 1.8 copy-done.2
  214.8 1.5 collective-permute-start.45
  216.2 5.3 %collective-permute-done.43.refs_1_ = bf16[128,1024]{1,0:T(8,128)(2,1)S(1)} collective-permute-done((bf16[128,1024]{1,0:T(8,128)(2,1)S(1)}, bf16[128,1024]{1,0:T(8,128)(2,1)S(1)}, u32[]{:S(2)}, u32[]{:S(2)}) %collective-permute-start.43) | collective-permute-done | bytes 262176 | tf_op jit(solution)/shard_map/ppermute | solution.py:495
  221.5 4.8 %collective-permute-done.44.refs_2_ = bf16[128,1024]{1,0:T(8,128)(2,1)S(1)} collective-permute-done((bf16[128,1024]{1,0:T(8,128)(2,1)S(1)}, bf16[128,1024]{1,0:T(8,128)(2,1)S(1)}, u32[]{:S(2)}, u32[]{:S(2)}) %collective-permute-start.44) | collective-permute-done | bytes 262176 | tf_op jit(solution)/shard_map/ppermute | solution.py:495
  226.3 1.8 collective-permute-done.45.refs_3_
  229.4 1.7 collective-permute-start.47
  232.3 5.8 %collective-permute-done.46.refs_1_ = bf16[128,1024]{1,0:T(8,128)(2,1)S(1)} collective-permute-done((bf16[128,1024]{1,0:T(8,128)(2,1)S(1)}, bf16[128,1024]{1,0:T(8,128)(2,1)S(1)}, u32[]{:S(2)}, u32[]{:S(2)}) %collective-permute-start.46) | collective-permute-done | bytes 262176 | tf_op jit(solution)/shard_map/ppermute | solution.py:495
  238.0 4.4 %collective-permute-done.47.refs_2_ = bf16[128,1024]{1,0:T(8,128)(2,1)S(1)} collective-permute-done((bf16[128,1024]{1,0:T(8,128)(2,1)S(1)}, bf16[128,1024]{1,0:T(8,128)(2,1)S(1)}, u32[]{:S(2)}, u32[]{:S(2)}) %collective-permute-start.47) | collective-permute-done | bytes 262176 | tf_op jit(solution)/shard_map/ppermute | solution.py:495
  245.4 8.9 %shard_map.253 = (bf16[1024,384]{1,0:T(8,128)(2,1)S(1)}, bf16[512,1024]{1,0:T(8,128)(2,1)S(1)}) custom-call(bf16[1024,384]{1,0:T(8,128)(2,1)S(1)} %copy-done.62, f32[1,1024]{1,0:T(1,128)S(1)} %get-tuple-element.149.refs_1_, f32[1024,128]{1,0:T(8,128)S(1)} %copy-done.64, bf16[1024,128]{1,0:T(8,128)(2,1)S(1)} %bitcast.93, bf16[384,1024]{1,0:T(8,128)(2,1)S(1)} %copy-done.42, ...), custom_call_target="tpu_custom_call" | custom-call | flops 10119999488 | tf_op jit(solution)/shard_map/pallas_call | solution.py:672
  254.5 2.5 collective-permute-done.53.refs_2_
  257.7 1.4 collective-permute-start.54
  259.2 2.1 collective-permute-start.56
  264.4 2.5 collective-permute-done.54.refs_1_
  266.9 5.9 %collective-permute-done.55.refs_2_ = bf16[128,1024]{1,0:T(8,128)(2,1)S(1)} collective-permute-done((bf16[128,1024]{1,0:T(8,128)(2,1)S(1)}, bf16[128,1024]{1,0:T(8,128)(2,1)S(1)}, u32[]{:S(2)}, u32[]{:S(2)}) %collective-permute-start.55) | collective-permute-done | bytes 262176 | tf_op jit(solution)/shard_map/ppermute | solution.py:495
  274.3 3.6 %all-to-all-start.1 = ((bf16[16,96,128]{2,1,0:T(8,128)(2,1)}), bf16[16,96,128]{2,1,0:T(8,128)(2,1)S(1)}, u32[]{:S(2)}, u32[]{:S(2)}) async-start(bf16[16,96,128]{2,1,0:T(8,128)(2,1)} %get-tuple-element.193), calls=%async_computation.1 | async-start | bytes 786432 | tf_op jit(solution)/shard_map/all_to_all | solution.py:1619
  278.0 2.0 collective-permute-start.57
  280.9 8.5 %collective-permute-done.57 = bf16[64,1024]{1,0:T(8,128)(2,1)S(1)} collective-permute-done((bf16[64,1024]{1,0:T(8,128)(2,1)S(1)}, bf16[64,1024]{1,0:T(8,128)(2,1)S(1)}, u32[]{:S(2)}, u32[]{:S(2)}) %collective-permute-start.57) | collective-permute-done | bytes 131104 | tf_op jit(solution)/shard_map/ppermute | solution.py:545
  290.2 3.2 all-to-all-done.1.refs_0_
  293.5 5.1 %collective-permute-start.59 = (f32[80,512]{1,0:T(8,128)S(1)}, f32[80,512]{1,0:T(8,128)S(1)}, u32[]{:S(2)}, u32[]{:S(2)}) collective-permute-start(f32[80,512]{1,0:T(8,128)S(1)} %shard_map.257.refs_0_), channel_id=1, source_target_pairs={{0,16},{16,0},{1,17},{17,1},{2,18},{18,2},{3,19},{19,3},{4,20},{20... | collective-permute-start | bytes 491528 | tf_op jit(solution)/shard_map/ppermute | solution.py:495
  300.7 5.3 %collective-permute-start.63 = (bf16[64,1024]{1,0:T(8,128)(2,1)S(1)}, bf16[64,1024]{1,0:T(8,128)(2,1)S(1)}, u32[]{:S(2)}, u32[]{:S(2)}) collective-permute-start(bf16[64,1024]{1,0:T(8,128)(2,1)S(1)} %get-tuple-element.204), channel_id=1, source_target_pairs={{5,0},{1,1},{20,2},{16,3},{23,4},{19,5},{6,6},{2,7},{21,8},{17,9},... | collective-permute-start | bytes 393224 | tf_op jit(solution)/shard_map/ppermute | solution.py:1797
  308.3 3.7 %collective-permute-start.67 = (bf16[64,1280]{1,0:T(8,128)(2,1)S(1)}, bf16[64,1280]{1,0:T(8,128)(2,1)S(1)}, u32[]{:S(2)}, u32[]{:S(2)}) collective-permute-start(bf16[64,1280]{1,0:T(8,128)(2,1)S(1)} %get-tuple-element.208), channel_id=1, source_target_pairs={{0,2},{2,0},{1,3},{3,1},{4,6},{6,4},{5,7},{7,5},{8,10},{10,8},{9,1... | collective-permute-start | bytes 491528 | tf_op jit(solution)/shard_map/ppermute | solution.py:495
  312.0 1.9 collective-permute-start.68
  315.3 2.0 collective-permute-start.69
  317.3 2.7 collective-permute-done.67.refs_2_
  320.3 10.2 %collective-permute-done.68.refs_3_ = bf16[64,1280]{1,0:T(8,128)(2,1)S(1)} collective-permute-done((bf16[64,1280]{1,0:T(8,128)(2,1)S(1)}, bf16[64,1280]{1,0:T(8,128)(2,1)S(1)}, u32[]{:S(2)}, u32[]{:S(2)}) %collective-permute-start.68) | collective-permute-done | bytes 163872 | tf_op jit(solution)/shard_map/ppermute | solution.py:585
  338.3 2.1 add_bitcast_fusion
  (326 shorter events, 85.3 us)
Async XLA Ops:
  7.2 92.4 %all-gather.3.cloned.1.call-start = ((), (), s32[]{:S(2)}) async-start(), calls=%async_computation.3 | async-start | bytes 1671168 | tf_op jit(solution)/shard_map/all_gather | solution.py:1654
  9.0 53.3 %collective-permute-start.4 = (bf16[128,1024]{1,0:T(8,128)(2,1)}, bf16[128,1024]{1,0:T(8,128)(2,1)}, u32[]{:S(2)}, u32[]{:S(2)}) collective-permute-start(bf16[128,1024]{1,0:T(8,128)(2,1)} %dynamic-slice_bitcast_fusion), channel_id=1, source_target_pairs={{0,0},{1,6},{2,3},{3,21},{4,18},{5,4},{6,1},{7,7},{8,16},{9,22},{1... | collective-permute-start | bytes 786440 | tf_op jit(solution)/shard_map/ppermute | solution.py:1687
  12.6 50.4 %collective-permute-start.6 = (bf16[128,1024]{1,0:T(8,128)(2,1)}, bf16[128,1024]{1,0:T(8,128)(2,1)}, u32[]{:S(2)}, u32[]{:S(2)}) collective-permute-start(bf16[128,1024]{1,0:T(8,128)(2,1)} %dynamic-slice_bitcast_fusion), channel_id=1, source_target_pairs={{0,4},{1,2},{2,7},{3,17},{4,22},{5,0},{6,5},{7,3},{8,20},{9,18},{1... | collective-permute-start | bytes 786440 | tf_op jit(solution)/shard_map/ppermute | solution.py:1687
  19.9 43.0 %all-to-all-start = ((bf16[16,64,128]{2,1,0:T(8,128)(2,1)}), bf16[16,64,128]{2,1,0:T(8,128)(2,1)S(1)}, u32[]{:S(2)}, u32[]{:S(2)}) async-start(bf16[16,64,128]{2,1,0:T(8,128)(2,1)} %get-tuple-element.115), calls=%async_computation | async-start | bytes 524288 | tf_op jit(solution)/shard_map/all_to_all | solution.py:1619
  27.3 109.7 %all-gather.5.cloned.1.call-start = ((), (), s32[]{:S(2)}) async-start(), calls=%async_computation.4 | async-start | bytes 2621440 | tf_op jit(solution)/shard_map/all_gather | solution.py:1717
  27.5 6.1 %collective-permute-start = (bf16[80,1024]{1,0:T(8,128)(2,1)S(1)}, bf16[80,1024]{1,0:T(8,128)(2,1)S(1)}, u32[]{:S(2)}, u32[]{:S(2)}) collective-permute-start(bf16[80,1024]{1,0:T(8,128)(2,1)S(1)} %get-tuple-element.117), channel_id=1, source_target_pairs={{0,0},{4,4},{8,16},{12,20},{16,8},{20,12},{24,24},{28,28},{1,1},{5... | collective-permute-start | bytes 491528 | tf_op jit(solution)/shard_map/ppermute | solution.py:1677
  28.3 9.3 %collective-permute-start.1 = (bf16[80,1024]{1,0:T(8,128)(2,1)S(1)}, bf16[80,1024]{1,0:T(8,128)(2,1)S(1)}, u32[]{:S(2)}, u32[]{:S(2)}) collective-permute-start(bf16[80,1024]{1,0:T(8,128)(2,1)S(1)} %get-tuple-element.118), channel_id=1, source_target_pairs={{0,4},{4,0},{8,20},{12,16},{16,12},{20,8},{24,28},{28,24},{1,5},{5... | collective-permute-start | bytes 491528 | tf_op jit(solution)/shard_map/ppermute | solution.py:1677
  31.2 17.9 %collective-permute-start.5 = (bf16[64,1024]{1,0:T(8,128)(2,1)S(1)}, bf16[64,1024]{1,0:T(8,128)(2,1)S(1)}, u32[]{:S(2)}, u32[]{:S(2)}) collective-permute-start(bf16[64,1024]{1,0:T(8,128)(2,1)S(1)} %dynamic-slice_bitcast_fusion.1), channel_id=1, source_target_pairs={{0,1},{1,5},{2,16},{3,20},{4,19},{5,23},{6,2},{7,6},{8,17},{9,21},... | collective-permute-start | bytes 393224 | tf_op jit(solution)/shard_map/ppermute | solution.py:1687
  33.6 14.6 %collective-permute-start.2 = (bf16[144,1024]{1,0:T(8,128)(2,1)S(1)}, bf16[144,1024]{1,0:T(8,128)(2,1)S(1)}, u32[]{:S(2)}, u32[]{:S(2)}) collective-permute-start(bf16[144,1024]{1,0:T(8,128)(2,1)S(1)} %pad_maximum_fusion.2), channel_id=1, source_target_pairs={{0,1},{1,0},{2,3},{3,2},{4,5},{5,4},{6,7},{7,6},{8,9},{9,8},{10,11... | collective-permute-start | bytes 884744 | tf_op jit(solution)/shard_map/ppermute | solution.py:495
  37.6 5.3 %collective-permute-start.3 = (bf16[80,1024]{1,0:T(8,128)(2,1)S(1)}, bf16[80,1024]{1,0:T(8,128)(2,1)S(1)}, u32[]{:S(2)}, u32[]{:S(2)}) collective-permute-start(bf16[80,1024]{1,0:T(8,128)(2,1)S(1)} %collective-permute-done.1), channel_id=1, source_target_pairs={{0,2},{2,0},{1,3},{3,1},{4,6},{6,4},{5,7},{7,5},{8,10},{10,8},{9,1... | collective-permute-start | bytes 491528 | tf_op jit(solution)/shard_map/ppermute | solution.py:495
  42.9 19.4 %collective-permute-start.7 = (bf16[64,1024]{1,0:T(8,128)(2,1)S(1)}, bf16[64,1024]{1,0:T(8,128)(2,1)S(1)}, u32[]{:S(2)}, u32[]{:S(2)}) collective-permute-start(bf16[64,1024]{1,0:T(8,128)(2,1)S(1)} %dynamic-slice_bitcast_fusion.1), channel_id=1, source_target_pairs={{0,5},{1,1},{2,20},{3,16},{4,23},{5,19},{6,6},{7,2},{8,21},{9,17},... | collective-permute-start | bytes 393224 | tf_op jit(solution)/shard_map/ppermute | solution.py:1687
  62.9 11.9 %collective-permute-start.8 = (bf16[160,1024]{1,0:T(8,128)(2,1)}, bf16[160,1024]{1,0:T(8,128)(2,1)S(1)}, u32[]{:S(2)}, u32[]{:S(2)}) collective-permute-start(bf16[160,1024]{1,0:T(8,128)(2,1)} %pad_maximum_fusion), channel_id=1, source_target_pairs={{0,1},{1,0},{2,3},{3,2},{4,5},{5,4},{6,7},{7,6},{8,9},{9,8},{10,11... | collective-permute-start | bytes 983048 | tf_op jit(solution)/shard_map/ppermute | solution.py:495
  63.0 17.5 %collective-permute-start.9 = (bf16[224,1024]{1,0:T(8,128)(2,1)S(1)}, bf16[224,1024]{1,0:T(8,128)(2,1)S(1)}, u32[]{:S(2)}, u32[]{:S(2)}) collective-permute-start(bf16[224,1024]{1,0:T(8,128)(2,1)S(1)} %maximum_maximum_fusion.1), channel_id=1, source_target_pairs={{0,2},{2,0},{1,3},{3,1},{4,6},{6,4},{5,7},{7,5},{8,10},{10,8},{9,1... | collective-permute-start | bytes 1376264 | tf_op jit(solution)/shard_map/ppermute | solution.py:495
  81.2 4.8 %collective-permute-start.10 = (bf16[4,2,80,1024]{3,2,1,0:T(8,128)(2,1)S(1)}, bf16[4,2,80,1024]{3,2,1,0:T(8,128)(2,1)S(1)}, u32[]{:S(2)}, u32[]{:S(2)}) collective-permute-start(bf16[4,2,80,1024]{3,2,1,0:T(8,128)(2,1)S(1)} %bitcast.98), channel_id=1, source_target_pairs={{0,16},{16,0},{1,17},{17,1},{2,18},{18,2},{3,19},{19,3},{4,20},{20... | collective-permute-start | bytes 3932168 | tf_op jit(solution)/shard_map/ppermute | solution.py:495
  85.8 212.9 %reduce-scatter.2.cloned.1.call-start = ((), (), s32[]{:S(2)}) async-start(), calls=%async_computation.5 | async-start | bytes 4587520 | tf_op jit(solution)/shard_map/reduce_scatter | solution.py:1752
  103.3 9.2 %collective-permute-start.12 = (bf16[128,1024]{1,0:T(8,128)(2,1)S(1)}, bf16[128,1024]{1,0:T(8,128)(2,1)S(1)}, u32[]{:S(2)}, u32[]{:S(2)}) collective-permute-start(bf16[128,1024]{1,0:T(8,128)(2,1)S(1)} %get-tuple-element.131), channel_id=1, source_target_pairs={{0,1},{1,0},{2,3},{3,2},{4,5},{5,4},{6,7},{7,6},{8,9},{9,8},{10,11... | collective-permute-start | bytes 786440 | tf_op jit(solution)/shard_map/ppermute | solution.py:495
  103.9 13.2 %collective-permute-start.13 = (bf16[128,1024]{1,0:T(8,128)(2,1)S(1)}, bf16[128,1024]{1,0:T(8,128)(2,1)S(1)}, u32[]{:S(2)}, u32[]{:S(2)}) collective-permute-start(bf16[128,1024]{1,0:T(8,128)(2,1)S(1)} %get-tuple-element.132), channel_id=1, source_target_pairs={{0,2},{2,0},{1,3},{3,1},{4,6},{6,4},{5,7},{7,5},{8,10},{10,8},{9,1... | collective-permute-start | bytes 786440 | tf_op jit(solution)/shard_map/ppermute | solution.py:495
  105.6 13.0 %collective-permute-start.14 = (bf16[128,1024]{1,0:T(8,128)(2,1)S(1)}, bf16[128,1024]{1,0:T(8,128)(2,1)S(1)}, u32[]{:S(2)}, u32[]{:S(2)}) collective-permute-start(bf16[128,1024]{1,0:T(8,128)(2,1)S(1)} %get-tuple-element.133), channel_id=1, source_target_pairs={{0,3},{1,2},{2,1},{3,0},{4,7},{5,6},{6,5},{7,4},{8,11},{9,10},{10,... | collective-permute-start | bytes 786440 | tf_op jit(solution)/shard_map/ppermute | solution.py:585
  120.5 9.2 %collective-permute-start.15 = (bf16[128,1024]{1,0:T(8,128)(2,1)S(1)}, bf16[128,1024]{1,0:T(8,128)(2,1)S(1)}, u32[]{:S(2)}, u32[]{:S(2)}) collective-permute-start(bf16[128,1024]{1,0:T(8,128)(2,1)S(1)} %get-tuple-element.136.refs_0_.refs_8_), channel_id=1, source_target_pairs={{0,1},{1,0},{2,3},{3,2},{4,5},{5,4},{6,7},{7,6},{8,9},{9,8},{10,11... | collective-permute-start | bytes 786440 | tf_op jit(solution)/shard_map/ppermute | solution.py:495
  121.2 13.2 %collective-permute-start.16 = (bf16[128,1024]{1,0:T(8,128)(2,1)S(1)}, bf16[128,1024]{1,0:T(8,128)(2,1)S(1)}, u32[]{:S(2)}, u32[]{:S(2)}) collective-permute-start(bf16[128,1024]{1,0:T(8,128)(2,1)S(1)} %get-tuple-element.136.refs_0_.refs_8_), channel_id=1, source_target_pairs={{0,2},{2,0},{1,3},{3,1},{4,6},{6,4},{5,7},{7,5},{8,10},{10,8},{9,1... | collective-permute-start | bytes 786440 | tf_op jit(solution)/shard_map/ppermute | solution.py:495
  122.8 12.2 %collective-permute-start.17 = (bf16[128,1024]{1,0:T(8,128)(2,1)S(1)}, bf16[128,1024]{1,0:T(8,128)(2,1)S(1)}, u32[]{:S(2)}, u32[]{:S(2)}) collective-permute-start(bf16[128,1024]{1,0:T(8,128)(2,1)S(1)} %get-tuple-element.136.refs_0_.refs_8_), channel_id=1, source_target_pairs={{0,3},{1,2},{2,1},{3,0},{4,7},{5,6},{6,5},{7,4},{8,11},{9,10},{10,... | collective-permute-start | bytes 786440 | tf_op jit(solution)/shard_map/ppermute | solution.py:585
  124.0 12.2 %collective-permute-start.18 = (bf16[128,1024]{1,0:T(8,128)(2,1)S(1)}, bf16[128,1024]{1,0:T(8,128)(2,1)S(1)}, u32[]{:S(2)}, u32[]{:S(2)}) collective-permute-start(bf16[128,1024]{1,0:T(8,128)(2,1)S(1)} %get-tuple-element.136.refs_0_.refs_8_), channel_id=1, source_target_pairs={{0,16},{16,0},{1,17},{17,1},{2,18},{18,2},{3,19},{19,3},{4,20},{20... | collective-permute-start | bytes 786440 | tf_op jit(solution)/shard_map/ppermute | solution.py:495
  129.7 7.2 %collective-permute-start.19 = (bf16[128,1024]{1,0:T(8,128)(2,1)S(1)}, bf16[128,1024]{1,0:T(8,128)(2,1)S(1)}, u32[]{:S(2)}, u32[]{:S(2)}) collective-permute-start(bf16[128,1024]{1,0:T(8,128)(2,1)S(1)} %collective-permute-done.15.refs_1_.refs_9_), channel_id=1, source_target_pairs={{0,16},{16,0},{1,17},{17,1},{2,18},{18,2},{3,19},{19,3},{4,20},{20... | collective-permute-start | bytes 786440 | tf_op jit(solution)/shard_map/ppermute | solution.py:495
  148.7 12.7 %collective-permute-start.26 = (bf16[1024,768]{1,0:T(8,128)(2,1)}, bf16[1024,768]{1,0:T(8,128)(2,1)}, u32[]{:S(2)}, u32[]{:S(2)}) collective-permute-start(bf16[1024,768]{1,0:T(8,128)(2,1)} %all-gather.3.cloned.1.call-done.refs_6_), channel_id=1, source_target_pairs={{0,16},{16,0},{1,17},{17,1},{2,18},{18,2},{3,19},{19,3},{4,20},{20... | collective-permute-start | bytes 4718600 | tf_op jit(solution)/shard_map/ppermute | solution.py:495
  150.3 9.6 %collective-permute-start.27 = (bf16[128,1024]{1,0:T(8,128)(2,1)S(1)}, bf16[128,1024]{1,0:T(8,128)(2,1)S(1)}, u32[]{:S(2)}, u32[]{:S(2)}) collective-permute-start(bf16[128,1024]{1,0:T(8,128)(2,1)S(1)} %get-tuple-element.233), channel_id=1, source_target_pairs={{0,0},{4,4},{8,16},{12,20},{16,8},{20,12},{24,24},{28,28},{1,1},{5... | collective-permute-start | bytes 786440 | tf_op jit(solution)/shard_map/ppermute | solution.py:539
  151.0 10.3 %collective-permute-start.28 = (bf16[128,1024]{1,0:T(8,128)(2,1)S(1)}, bf16[128,1024]{1,0:T(8,128)(2,1)S(1)}, u32[]{:S(2)}, u32[]{:S(2)}) collective-permute-start(bf16[128,1024]{1,0:T(8,128)(2,1)S(1)} %get-tuple-element.232), channel_id=1, source_target_pairs={{0,4},{4,0},{8,20},{12,16},{16,12},{20,8},{24,28},{28,24},{1,5},{5... | collective-permute-start | bytes 786440 | tf_op jit(solution)/shard_map/ppermute | solution.py:539
  157.8 6.8 %collective-permute-start.23 = (bf16[128,1024]{1,0:T(8,128)(2,1)S(1)}, bf16[128,1024]{1,0:T(8,128)(2,1)S(1)}, u32[]{:S(2)}, u32[]{:S(2)}) collective-permute-start(bf16[128,1024]{1,0:T(8,128)(2,1)S(1)} %get-tuple-element.139), channel_id=1, source_target_pairs={{0,1},{1,0},{2,3},{3,2},{4,5},{5,4},{6,7},{7,6},{8,9},{9,8},{10,11... | collective-permute-start | bytes 786440 | tf_op jit(solution)/shard_map/ppermute | solution.py:495
  159.2 9.5 %collective-permute-start.24 = (bf16[128,1024]{1,0:T(8,128)(2,1)S(1)}, bf16[128,1024]{1,0:T(8,128)(2,1)S(1)}, u32[]{:S(2)}, u32[]{:S(2)}) collective-permute-start(bf16[128,1024]{1,0:T(8,128)(2,1)S(1)} %get-tuple-element.140), channel_id=1, source_target_pairs={{0,2},{2,0},{1,3},{3,1},{4,6},{6,4},{5,7},{7,5},{8,10},{10,8},{9,1... | collective-permute-start | bytes 786440 | tf_op jit(solution)/shard_map/ppermute | solution.py:495
  159.9 11.6 %collective-permute-start.25 = (bf16[128,1024]{1,0:T(8,128)(2,1)S(1)}, bf16[128,1024]{1,0:T(8,128)(2,1)S(1)}, u32[]{:S(2)}, u32[]{:S(2)}) collective-permute-start(bf16[128,1024]{1,0:T(8,128)(2,1)S(1)} %get-tuple-element.141), channel_id=1, source_target_pairs={{0,3},{1,2},{2,1},{3,0},{4,7},{5,6},{6,5},{7,4},{8,11},{9,10},{10,... | collective-permute-start | bytes 786440 | tf_op jit(solution)/shard_map/ppermute | solution.py:585
  177.9 7.8 %collective-permute-start.29 = (bf16[128,1024]{1,0:T(8,128)(2,1)S(1)}, bf16[128,1024]{1,0:T(8,128)(2,1)S(1)}, u32[]{:S(2)}, u32[]{:S(2)}) collective-permute-start(bf16[128,1024]{1,0:T(8,128)(2,1)S(1)} %get-tuple-element.146.refs_0_), channel_id=1, source_target_pairs={{0,1},{1,0},{2,3},{3,2},{4,5},{5,4},{6,7},{7,6},{8,9},{9,8},{10,11... | collective-permute-start | bytes 786440 | tf_op jit(solution)/shard_map/ppermute | solution.py:495
  178.3 14.4 %collective-permute-start.30 = (bf16[128,1024]{1,0:T(8,128)(2,1)S(1)}, bf16[128,1024]{1,0:T(8,128)(2,1)S(1)}, u32[]{:S(2)}, u32[]{:S(2)}) collective-permute-start(bf16[128,1024]{1,0:T(8,128)(2,1)S(1)} %get-tuple-element.146.refs_0_), channel_id=1, source_target_pairs={{0,2},{2,0},{1,3},{3,1},{4,6},{6,4},{5,7},{7,5},{8,10},{10,8},{9,1... | collective-permute-start | bytes 786440 | tf_op jit(solution)/shard_map/ppermute | solution.py:495
  180.6 12.6 %collective-permute-start.31 = (bf16[128,1024]{1,0:T(8,128)(2,1)S(1)}, bf16[128,1024]{1,0:T(8,128)(2,1)S(1)}, u32[]{:S(2)}, u32[]{:S(2)}) collective-permute-start(bf16[128,1024]{1,0:T(8,128)(2,1)S(1)} %get-tuple-element.146.refs_0_), channel_id=1, source_target_pairs={{0,3},{1,2},{2,1},{3,0},{4,7},{5,6},{6,5},{7,4},{8,11},{9,10},{10,... | collective-permute-start | bytes 786440 | tf_op jit(solution)/shard_map/ppermute | solution.py:585
  181.4 11.8 %collective-permute-start.32 = (bf16[128,1024]{1,0:T(8,128)(2,1)S(1)}, bf16[128,1024]{1,0:T(8,128)(2,1)S(1)}, u32[]{:S(2)}, u32[]{:S(2)}) collective-permute-start(bf16[128,1024]{1,0:T(8,128)(2,1)S(1)} %get-tuple-element.146.refs_0_), channel_id=1, source_target_pairs={{0,16},{16,0},{1,17},{17,1},{2,18},{18,2},{3,19},{19,3},{4,20},{20... | collective-permute-start | bytes 786440 | tf_op jit(solution)/shard_map/ppermute | solution.py:495
  185.7 7.5 %collective-permute-start.33 = (bf16[128,1024]{1,0:T(8,128)(2,1)S(1)}, bf16[128,1024]{1,0:T(8,128)(2,1)S(1)}, u32[]{:S(2)}, u32[]{:S(2)}) collective-permute-start(bf16[128,1024]{1,0:T(8,128)(2,1)S(1)} %collective-permute-done.29.refs_1_), channel_id=1, source_target_pairs={{0,16},{16,0},{1,17},{17,1},{2,18},{18,2},{3,19},{19,3},{4,20},{20... | collective-permute-start | bytes 786440 | tf_op jit(solution)/shard_map/ppermute | solution.py:495
  196.7 4.7 %collective-permute-start.38 = (bf16[512,1024]{1,0:T(8,128)(2,1)S(1)}, bf16[512,1024]{1,0:T(8,128)(2,1)S(1)}, u32[]{:S(2)}, u32[]{:S(2)}) collective-permute-start(bf16[512,1024]{1,0:T(8,128)(2,1)S(1)} %get-tuple-element.154), channel_id=1, source_target_pairs={{0,16},{16,0},{1,17},{17,1},{2,18},{18,2},{3,19},{19,3},{4,20},{20... | collective-permute-start | bytes 3145736 | tf_op jit(solution)/shard_map/ppermute | solution.py:495
  212.4 9.1 %collective-permute-start.43 = (bf16[128,1024]{1,0:T(8,128)(2,1)S(1)}, bf16[128,1024]{1,0:T(8,128)(2,1)S(1)}, u32[]{:S(2)}, u32[]{:S(2)}) collective-permute-start(bf16[128,1024]{1,0:T(8,128)(2,1)S(1)} %copy-done.32), channel_id=1, source_target_pairs={{0,1},{1,0},{2,3},{3,2},{4,5},{5,4},{6,7},{7,6},{8,9},{9,8},{10,11... | collective-permute-start | bytes 786440 | tf_op jit(solution)/shard_map/ppermute | solution.py:495
  213.5 12.8 %collective-permute-start.44 = (bf16[128,1024]{1,0:T(8,128)(2,1)S(1)}, bf16[128,1024]{1,0:T(8,128)(2,1)S(1)}, u32[]{:S(2)}, u32[]{:S(2)}) collective-permute-start(bf16[128,1024]{1,0:T(8,128)(2,1)S(1)} %copy-done.30), channel_id=1, source_target_pairs={{0,2},{2,0},{1,3},{3,1},{4,6},{6,4},{5,7},{7,5},{8,10},{10,8},{9,1... | collective-permute-start | bytes 786440 | tf_op jit(solution)/shard_map/ppermute | solution.py:495
  214.8 13.3 %collective-permute-start.45 = (bf16[128,1024]{1,0:T(8,128)(2,1)S(1)}, bf16[128,1024]{1,0:T(8,128)(2,1)S(1)}, u32[]{:S(2)}, u32[]{:S(2)}) collective-permute-start(bf16[128,1024]{1,0:T(8,128)(2,1)S(1)} %copy-done.28), channel_id=1, source_target_pairs={{0,3},{1,2},{2,1},{3,0},{4,7},{5,6},{6,5},{7,4},{8,11},{9,10},{10,... | collective-permute-start | bytes 786440 | tf_op jit(solution)/shard_map/ppermute | solution.py:585
  228.7 9.3 %collective-permute-start.46 = (bf16[128,1024]{1,0:T(8,128)(2,1)S(1)}, bf16[128,1024]{1,0:T(8,128)(2,1)S(1)}, u32[]{:S(2)}, u32[]{:S(2)}) collective-permute-start(bf16[128,1024]{1,0:T(8,128)(2,1)S(1)} %get-tuple-element.172.refs_0_), channel_id=1, source_target_pairs={{0,1},{1,0},{2,3},{3,2},{4,5},{5,4},{6,7},{7,6},{8,9},{9,8},{10,11... | collective-permute-start | bytes 786440 | tf_op jit(solution)/shard_map/ppermute | solution.py:495
  229.4 13.0 %collective-permute-start.47 = (bf16[128,1024]{1,0:T(8,128)(2,1)S(1)}, bf16[128,1024]{1,0:T(8,128)(2,1)S(1)}, u32[]{:S(2)}, u32[]{:S(2)}) collective-permute-start(bf16[128,1024]{1,0:T(8,128)(2,1)S(1)} %get-tuple-element.172.refs_0_), channel_id=1, source_target_pairs={{0,2},{2,0},{1,3},{3,1},{4,6},{6,4},{5,7},{7,5},{8,10},{10,8},{9,1... | collective-permute-start | bytes 786440 | tf_op jit(solution)/shard_map/ppermute | solution.py:495
  231.1 11.3 %collective-permute-start.48 = (bf16[128,1024]{1,0:T(8,128)(2,1)S(1)}, bf16[128,1024]{1,0:T(8,128)(2,1)S(1)}, u32[]{:S(2)}, u32[]{:S(2)}) collective-permute-start(bf16[128,1024]{1,0:T(8,128)(2,1)S(1)} %get-tuple-element.172.refs_0_), channel_id=1, source_target_pairs={{0,3},{1,2},{2,1},{3,0},{4,7},{5,6},{6,5},{7,4},{8,11},{9,10},{10,... | collective-permute-start | bytes 786440 | tf_op jit(solution)/shard_map/ppermute | solution.py:585
  232.3 10.6 %collective-permute-start.49 = (bf16[128,1024]{1,0:T(8,128)(2,1)S(1)}, bf16[128,1024]{1,0:T(8,128)(2,1)S(1)}, u32[]{:S(2)}, u32[]{:S(2)}) collective-permute-start(bf16[128,1024]{1,0:T(8,128)(2,1)S(1)} %get-tuple-element.172.refs_0_), channel_id=1, source_target_pairs={{0,16},{16,0},{1,17},{17,1},{2,18},{18,2},{3,19},{19,3},{4,20},{20... | collective-permute-start | bytes 786440 | tf_op jit(solution)/shard_map/ppermute | solution.py:495
  238.0 4.9 %collective-permute-start.50 = (bf16[128,1024]{1,0:T(8,128)(2,1)S(1)}, bf16[128,1024]{1,0:T(8,128)(2,1)S(1)}, u32[]{:S(2)}, u32[]{:S(2)}) collective-permute-start(bf16[128,1024]{1,0:T(8,128)(2,1)S(1)} %collective-permute-done.46.refs_1_), channel_id=1, source_target_pairs={{0,16},{16,0},{1,17},{17,1},{2,18},{18,2},{3,19},{19,3},{4,20},{20... | collective-permute-start | bytes 786440 | tf_op jit(solution)/shard_map/ppermute | solution.py:495
  257.7 9.2 %collective-permute-start.54 = (bf16[128,1024]{1,0:T(8,128)(2,1)S(1)}, bf16[128,1024]{1,0:T(8,128)(2,1)S(1)}, u32[]{:S(2)}, u32[]{:S(2)}) collective-permute-start(bf16[128,1024]{1,0:T(8,128)(2,1)S(1)} %get-tuple-element.177), channel_id=1, source_target_pairs={{0,1},{1,0},{2,3},{3,2},{4,5},{5,4},{6,7},{7,6},{8,9},{9,8},{10,11... | collective-permute-start | bytes 786440 | tf_op jit(solution)/shard_map/ppermute | solution.py:495
  259.1 13.7 %collective-permute-start.55 = (bf16[128,1024]{1,0:T(8,128)(2,1)S(1)}, bf16[128,1024]{1,0:T(8,128)(2,1)S(1)}, u32[]{:S(2)}, u32[]{:S(2)}) collective-permute-start(bf16[128,1024]{1,0:T(8,128)(2,1)S(1)} %get-tuple-element.178), channel_id=1, source_target_pairs={{0,2},{2,0},{1,3},{3,1},{4,6},{6,4},{5,7},{7,5},{8,10},{10,8},{9,1... | collective-permute-start | bytes 786440 | tf_op jit(solution)/shard_map/ppermute | solution.py:495
  259.2 13.6 %collective-permute-start.56 = (bf16[128,1024]{1,0:T(8,128)(2,1)S(1)}, bf16[128,1024]{1,0:T(8,128)(2,1)S(1)}, u32[]{:S(2)}, u32[]{:S(2)}) collective-permute-start(bf16[128,1024]{1,0:T(8,128)(2,1)S(1)} %get-tuple-element.179), channel_id=1, source_target_pairs={{0,3},{1,2},{2,1},{3,0},{4,7},{5,6},{6,5},{7,4},{8,11},{9,10},{10,... | collective-permute-start | bytes 786440 | tf_op jit(solution)/shard_map/ppermute | solution.py:585
  261.9 18.9 %collective-permute-start.36 = (bf16[64,1024]{1,0:T(8,128)(2,1)}, bf16[64,1024]{1,0:T(8,128)(2,1)S(1)}, u32[]{:S(2)}, u32[]{:S(2)}) collective-permute-start(bf16[64,1024]{1,0:T(8,128)(2,1)} %get-tuple-element.247), channel_id=1, source_target_pairs={{4,0},{0,4},{20,8},{16,12},{12,16},{8,20},{28,24},{24,28},{5,1},{1... | collective-permute-start | bytes 393224 | tf_op jit(solution)/shard_map/ppermute | solution.py:545
  262.6 18.2 %collective-permute-start.37 = (bf16[64,1024]{1,0:T(8,128)(2,1)S(1)}, bf16[64,1024]{1,0:T(8,128)(2,1)S(1)}, u32[]{:S(2)}, u32[]{:S(2)}) collective-permute-start(bf16[64,1024]{1,0:T(8,128)(2,1)S(1)} %get-tuple-element.246), channel_id=1, source_target_pairs={{0,0},{4,4},{16,8},{20,12},{8,16},{12,20},{24,24},{28,28},{1,1},{5... | collective-permute-start | bytes 393224 | tf_op jit(solution)/shard_map/ppermute | solution.py:545
  274.3 19.2 %all-to-all-start.1 = ((bf16[16,96,128]{2,1,0:T(8,128)(2,1)}), bf16[16,96,128]{2,1,0:T(8,128)(2,1)S(1)}, u32[]{:S(2)}, u32[]{:S(2)}) async-start(bf16[16,96,128]{2,1,0:T(8,128)(2,1)} %get-tuple-element.193), calls=%async_computation.1 | async-start | bytes 786432 | tf_op jit(solution)/shard_map/all_to_all | solution.py:1619
  278.0 11.4 %collective-permute-start.57 = (bf16[64,1024]{1,0:T(8,128)(2,1)S(1)}, bf16[64,1024]{1,0:T(8,128)(2,1)S(1)}, u32[]{:S(2)}, u32[]{:S(2)}) collective-permute-start(bf16[64,1024]{1,0:T(8,128)(2,1)S(1)} %get-tuple-element.243), channel_id=1, source_target_pairs={{4,0},{0,4},{20,8},{16,12},{12,16},{8,20},{28,24},{24,28},{5,1},{1... | collective-permute-start | bytes 393224 | tf_op jit(solution)/shard_map/ppermute | solution.py:545
  280.0 9.4 %collective-permute-start.58 = (bf16[64,1024]{1,0:T(8,128)(2,1)S(1)}, bf16[64,1024]{1,0:T(8,128)(2,1)S(1)}, u32[]{:S(2)}, u32[]{:S(2)}) collective-permute-start(bf16[64,1024]{1,0:T(8,128)(2,1)S(1)} %get-tuple-element.242), channel_id=1, source_target_pairs={{0,0},{4,4},{16,8},{20,12},{8,16},{12,20},{24,24},{28,28},{1,1},{5... | collective-permute-start | bytes 393224 | tf_op jit(solution)/shard_map/ppermute | solution.py:545
  293.5 14.0 %collective-permute-start.59 = (f32[80,512]{1,0:T(8,128)S(1)}, f32[80,512]{1,0:T(8,128)S(1)}, u32[]{:S(2)}, u32[]{:S(2)}) collective-permute-start(f32[80,512]{1,0:T(8,128)S(1)} %shard_map.257.refs_0_), channel_id=1, source_target_pairs={{0,16},{16,0},{1,17},{17,1},{2,18},{18,2},{3,19},{19,3},{4,20},{20... | collective-permute-start | bytes 491528 | tf_op jit(solution)/shard_map/ppermute | solution.py:495
  300.0 12.0 %collective-permute-start.61 = (bf16[64,1024]{1,0:T(8,128)(2,1)S(1)}, bf16[64,1024]{1,0:T(8,128)(2,1)S(1)}, u32[]{:S(2)}, u32[]{:S(2)}) collective-permute-start(bf16[64,1024]{1,0:T(8,128)(2,1)S(1)} %get-tuple-element.202), channel_id=1, source_target_pairs={{1,0},{5,1},{16,2},{20,3},{19,4},{23,5},{2,6},{6,7},{17,8},{21,9},... | collective-permute-start | bytes 393224 | tf_op jit(solution)/shard_map/ppermute | solution.py:1797
  300.7 13.3 %collective-permute-start.63 = (bf16[64,1024]{1,0:T(8,128)(2,1)S(1)}, bf16[64,1024]{1,0:T(8,128)(2,1)S(1)}, u32[]{:S(2)}, u32[]{:S(2)}) collective-permute-start(bf16[64,1024]{1,0:T(8,128)(2,1)S(1)} %get-tuple-element.204), channel_id=1, source_target_pairs={{5,0},{1,1},{20,2},{16,3},{23,4},{19,5},{6,6},{2,7},{21,8},{17,9},... | collective-permute-start | bytes 393224 | tf_op jit(solution)/shard_map/ppermute | solution.py:1797
  306.8 23.6 %collective-permute-start.60 = (bf16[128,1024]{1,0:T(8,128)(2,1)S(1)}, bf16[128,1024]{1,0:T(8,128)(2,1)S(1)}, u32[]{:S(2)}, u32[]{:S(2)}) collective-permute-start(bf16[128,1024]{1,0:T(8,128)(2,1)S(1)} %get-tuple-element.201), channel_id=1, source_target_pairs={{0,0},{6,1},{3,2},{21,3},{18,4},{4,5},{1,6},{7,7},{16,8},{22,9},{1... | collective-permute-start | bytes 786440 | tf_op jit(solution)/shard_map/ppermute | solution.py:1797
  308.2 7.1 %collective-permute-start.66 = (bf16[64,1280]{1,0:T(8,128)(2,1)S(1)}, bf16[64,1280]{1,0:T(8,128)(2,1)S(1)}, u32[]{:S(2)}, u32[]{:S(2)}) collective-permute-start(bf16[64,1280]{1,0:T(8,128)(2,1)S(1)} %get-tuple-element.207), channel_id=1, source_target_pairs={{0,1},{1,0},{2,3},{3,2},{4,5},{5,4},{6,7},{7,6},{8,9},{9,8},{10,11... | collective-permute-start | bytes 491528 | tf_op jit(solution)/shard_map/ppermute | solution.py:495
  308.3 11.7 %collective-permute-start.67 = (bf16[64,1280]{1,0:T(8,128)(2,1)S(1)}, bf16[64,1280]{1,0:T(8,128)(2,1)S(1)}, u32[]{:S(2)}, u32[]{:S(2)}) collective-permute-start(bf16[64,1280]{1,0:T(8,128)(2,1)S(1)} %get-tuple-element.208), channel_id=1, source_target_pairs={{0,2},{2,0},{1,3},{3,1},{4,6},{6,4},{5,7},{7,5},{8,10},{10,8},{9,1... | collective-permute-start | bytes 491528 | tf_op jit(solution)/shard_map/ppermute | solution.py:495
  312.0 18.4 %collective-permute-start.68 = (bf16[64,1280]{1,0:T(8,128)(2,1)S(1)}, bf16[64,1280]{1,0:T(8,128)(2,1)S(1)}, u32[]{:S(2)}, u32[]{:S(2)}) collective-permute-start(bf16[64,1280]{1,0:T(8,128)(2,1)S(1)} %get-tuple-element.209), channel_id=1, source_target_pairs={{0,3},{1,2},{2,1},{3,0},{4,7},{5,6},{6,5},{7,4},{8,11},{9,10},{10,... | collective-permute-start | bytes 491528 | tf_op jit(solution)/shard_map/ppermute | solution.py:585
  314.0 19.4 %collective-permute-start.62 = (bf16[128,1024]{1,0:T(8,128)(2,1)S(1)}, bf16[128,1024]{1,0:T(8,128)(2,1)S(1)}, u32[]{:S(2)}, u32[]{:S(2)}) collective-permute-start(bf16[128,1024]{1,0:T(8,128)(2,1)S(1)} %get-tuple-element.203), channel_id=1, source_target_pairs={{4,0},{2,1},{7,2},{17,3},{22,4},{0,5},{5,6},{3,7},{20,8},{18,9},{2... | collective-permute-start | bytes 786440 | tf_op jit(solution)/shard_map/ppermute | solution.py:1797
  315.3 18.2 %collective-permute-start.69 = (bf16[64,1280]{1,0:T(8,128)(2,1)S(1)}, bf16[64,1280]{1,0:T(8,128)(2,1)S(1)}, u32[]{:S(2)}, u32[]{:S(2)}) collective-permute-start(bf16[64,1280]{1,0:T(8,128)(2,1)S(1)} %get-tuple-element.200.refs_0_), channel_id=1, source_target_pairs={{0,16},{16,0},{1,17},{17,1},{2,18},{18,2},{3,19},{19,3},{4,20},{20... | collective-permute-start | bytes 491528 | tf_op jit(solution)/shard_map/ppermute | solution.py:495
  320.0 14.1 %collective-permute-start.70 = (bf16[64,1280]{1,0:T(8,128)(2,1)S(1)}, bf16[64,1280]{1,0:T(8,128)(2,1)S(1)}, u32[]{:S(2)}, u32[]{:S(2)}) collective-permute-start(bf16[64,1280]{1,0:T(8,128)(2,1)S(1)} %collective-permute-done.66.refs_1_), channel_id=1, source_target_pairs={{0,16},{16,0},{1,17},{17,1},{2,18},{18,2},{3,19},{19,3},{4,20},{20... | collective-permute-start | bytes 491528 | tf_op jit(solution)/shard_map/ppermute | solution.py:495
  330.5 3.7 %collective-permute-start.71 = (bf16[64,1280]{1,0:T(8,128)(2,1)S(1)}, bf16[64,1280]{1,0:T(8,128)(2,1)S(1)}, u32[]{:S(2)}, u32[]{:S(2)}) collective-permute-start(bf16[64,1280]{1,0:T(8,128)(2,1)S(1)} %collective-permute-done.67.refs_2_), channel_id=1, source_target_pairs={{0,16},{16,0},{1,17},{17,1},{2,18},{18,2},{3,19},{19,3},{4,20},{20... | collective-permute-start | bytes 491528 | tf_op jit(solution)/shard_map/ppermute | solution.py:495
  330.5 3.7 %collective-permute-start.72 = (bf16[64,1280]{1,0:T(8,128)(2,1)S(1)}, bf16[64,1280]{1,0:T(8,128)(2,1)S(1)}, u32[]{:S(2)}, u32[]{:S(2)}) collective-permute-start(bf16[64,1280]{1,0:T(8,128)(2,1)S(1)} %collective-permute-done.68.refs_3_), channel_id=1, source_target_pairs={{0,16},{16,0},{1,17},{17,1},{2,18},{18,2},{3,19},{19,3},{4,20},{20... | collective-permute-start | bytes 491528 | tf_op jit(solution)/shard_map/ppermute | solution.py:495
  333.6 4.7 %collective-permute-start.64 = (f32[192,1024]{1,0:T(8,128)S(1)}, f32[192,1024]{1,0:T(8,128)}, u32[]{:S(2)}, u32[]{:S(2)}) collective-permute-start(f32[192,1024]{1,0:T(8,128)S(1)} %shard_map.260), channel_id=1, source_target_pairs={{0,16},{16,0},{1,17},{17,1},{2,18},{18,2},{3,19},{19,3},{4,20},{20... | collective-permute-start | bytes 2359304 | tf_op jit(solution)/shard_map/ppermute | solution.py:495
  (93 other events, 571.1 us)
Sparse Core Ops, SparseCore 0:
  17.2 67.5 all-gather.2
  87.0 44.8 all-gather.4
  211.6 71.1 reduce-scatter.1

commit v2 on v1

--- a/solution.py
+++ b/solution.py
@@ -597,6 +597,10 @@
     return flip(lax.axis_index("y"), step[0]) * 2 + flip(lax.axis_index("x"), step[1])
 
 
+def pinned(values):
+    return [pltpu.with_memory_space_constraint(part, pltpu.HBM) for part in values]
+
+
 def wide_shape(*shape):
     return jax.ShapeDtypeStruct(shape, jnp.float32)
 
@@ -620,7 +624,7 @@
 
 
 def whole_call(
-    body, operands, out_shapes, scratch=(), left_out=(), loaded=(), kept=(), early=False
+    body, operands, out_shapes, scratch=(), left_out=(), loaded=(), kept=(), early=False, placed=()
 ):
     vmem, hbm = pl.BlockSpec(memory_space=pltpu.VMEM), pl.BlockSpec(memory_space=pltpu.HBM)
     n_in, n_out, n_own = len(operands), len(out_shapes), len(scratch)
@@ -666,14 +670,14 @@
     if buffers:
         buffers.append(pltpu.SemaphoreType.DMA((len(buffers),)))
     out_shapes = [
-        pltpu.HBM(part.shape, part.dtype) if i in kept else part
+        pltpu.HBM(part.shape, part.dtype) if i in kept or i in placed else part
         for i, part in enumerate(out_shapes)
     ]
     return pl.pallas_call(
         run,
         out_shape=out_shapes,
         in_specs=[hbm if i in left_out or i in loaded else vmem for i in range(n_in)],
-        out_specs=[hbm if i in kept else vmem for i in range(n_out)],
+        out_specs=[hbm if i in kept or i in placed else vmem for i in range(n_out)],
         scratch_shapes=[*scratch, *buffers],
         compiler_params=pltpu.CompilerParams(vmem_limit_bytes=VMEM_LIMIT),
         cost_estimate=pl.CostEstimate(
@@ -1214,7 +1218,7 @@
 
 def pair_grad_body(*refs):
     fed_in, two_in, whole_ref, halves = refs[:8], refs[8:16], refs[16], refs[17:21]
-    out_ref, fed_ref, two_ref, act_ref, du_ref, sems = refs[21:]
+    target_ref, out_ref, fed_ref, two_ref, act_ref, du_ref, sems, out_sems = refs[21:]
     copies = []
     for pieces, target in ((fed_in, fed_ref), (two_in, two_ref), (halves[:2], act_ref), (halves[2:], du_ref)):
         rows = pieces[0].shape[0]
@@ -1226,6 +1230,7 @@
     for copy in copies:
         copy.wait()
     width = whole_ref.shape[1]
+    stores = []
     for z in range(out_ref.shape[0] // GRAD_ROWS):
         at = z * GRAD_ROWS
         for lane in range(0, out_ref.shape[1], 512):
@@ -1240,6 +1245,13 @@
             out_ref[at + 256 + piece * 64 : at + 320 + piece * 64, width:] = whole_ref[
                 z * 256 + 192 : (z + 1) * 256, piece * 256 : (piece + 1) * 256
             ]
+        rows = slice(at, at + GRAD_ROWS)
+        stores.append(
+            pltpu.make_async_copy(out_ref.at[rows], target_ref.at[rows], out_sems.at[z])
+        )
+        stores[-1].start()
+    for copy in stores:
+        copy.wait()
 
 
 def pair_grads(rows_fed, rows_two, whole, acts, dus):
@@ -1249,10 +1261,12 @@
         pair_grad_body,
         (*rows_fed, *rows_two, whole, *acts, *dus),
         [low_shape(4 * GRAD_ROWS, width)],
-        [pltpu.VMEM((8 * rows, width), jnp.bfloat16)] * 2
+        [pltpu.VMEM((4 * GRAD_ROWS, width), jnp.bfloat16)]
+        + [pltpu.VMEM((8 * rows, width), jnp.bfloat16)] * 2
         + [pltpu.VMEM((8 * rows, hidden), jnp.bfloat16)] * 2
-        + [pltpu.SemaphoreType.DMA((20,))],
+        + [pltpu.SemaphoreType.DMA((20,)), pltpu.SemaphoreType.DMA((4,))],
         [*range(16), *range(17, 21)],
+        placed=(0,),
     )[0]
 
 
@@ -1456,6 +1470,7 @@
     attended_ref,
     dfed_ref,
     vec_ref,
+    sent_ref,
     datt_ref,
     datt_low_ref,
     sums_ref,
@@ -1475,12 +1490,13 @@
     )
 
 
-def project_back(parts, attended, dfed, vec):
+def project_back(parts, attended, dfed, vec, sent):
     rows, width = attended.shape
     return whole_call(
         project_back_body,
-        (*parts, attended, dfed, vec),
+        (*parts, attended, dfed, vec, sent),
         [wide_shape(rows, width), low_shape(rows, width), wide_shape(8, width)],
+        left_out=(7,),
     )
 
 
@@ -1701,13 +1717,14 @@
     sent = jnp.concatenate(
         [one, one_x[:size], jnp.concatenate([back_y, one_x[size:, ff // 8 :]], axis=1)]
     )
-    sent_y, sent_x = after((sent, jnp.concatenate([two, two_y])), (came, extra, out_t))
+    sent_y, sent_x = after((sent, jnp.concatenate([two, two_y])), (came[:2], extra, out_t))
     near_y = hop(sent_y, "y")
     near_x = hop(sent_x, "x")
     plane_own = jnp.concatenate(
         [one, two, one_x[:size], near_x[:size], near_y[:size], two_y]
         + [near_y[size : 2 * size], near_x[size:]]
     ).reshape(4, 2, size, width)
+    plane_own, came = lax.optimization_barrier((plane_own, came))
     plane_other = other_core(plane_own)
     (pair_own,) = whole_call(
         lay_body,
@@ -1728,8 +1745,10 @@
 
     attended, normed_two, hidden = project(mix_parts, first, vec)
     rows_two = plane_rows(normed_two)
-    act_far, slope_far, fed_far = feed(rows_two[4:], pair_w, vec)
-    act, slope, keep, *sends = feed(rows_two[:4], pair_w, vec, other_core(fed_far))
+    act_far, slope_far, fed_far = feed(pinned(rows_two[4:]), pinned([pair_w])[0], vec)
+    act, slope, keep, *sends = feed(
+        pinned(rows_two[:4]), pinned([pair_w])[0], vec, other_core(fed_far)
+    )
     fed_parts = (keep, *plane_hops(sends))
     wholes = (whole, other_core(whole))
     output, fed_low, sample_low, dlat_low, dfed, dfed_low, dmeans, dlogvars, bottle_sums = (
@@ -1739,19 +1758,17 @@
     )
 
     rows_fed = plane_rows(dfed_low)
-    layer_out = wide(
-        from_slides(after(to_low(output), rows_fed).reshape(slots, span, width))
-    )
+    layer_out = from_slides(after(to_low(output), rows_fed).reshape(slots, span, width))
     whole_grad = whole_grads((dlat_low, fed_low, cot, sample_low))
     du_far, ff_far, norm_far = feed_back(rows_fed[4:], pair_w, slope_far)
     du, ff_sums, keep, *sends = feed_back(
         rows_fed[:4], pair_w, slope, after(other_core(norm_far), whole_grad)
     )
     norm_parts = (keep, *plane_hops(sends))
-    grads = pair_grads(rows_fed, rows_two, whole_grad, (act, act_far), (du, du_far))
+    grads = pair_grads(rows_fed, pinned(rows_two), whole_grad, (act, act_far), (du, du_far))
     grads_sum = lax.psum_scatter(grads, "z", scatter_dimension=0, tiled=True)
     datt, datt_low, project_sums = project_back(
-        after(norm_parts, (grads, layer_out)), attended, dfed, vec
+        after(norm_parts, grads), attended, dfed, vec, layer_out
     )
     rows_datt = plane_rows(datt_low)
     out_grad, all_datt = out_grads(rows_datt, mixed)
@@ -1792,12 +1809,13 @@
         last_body, (last, other_core(last)), [wide_shape(part, width), wide_shape(SMALL, PAIR)]
     )
     grad_out_w = grad_out_w.T
-    homes = after(homes, (last, sums[0]))
     homes = [
         lax.ppermute(grad, EVERY, [(there, here) for here, there in head_routes(single, k)])
         for grad, (single, k) in zip(homes, ARRIVALS)
     ]
-    (home,) = whole_call(home_body, homes, [wide_shape(3 * HEAD_DIM, width)])
+    (home,) = whole_call(
+        home_body, after(homes, (packed, sums[1:4])), [wide_shape(3 * HEAD_DIM, width)]
+    )
     grad_qkv = (home + other_core(home)).T
     vec_out = small_sums[:9, :part]
     inner_out = small_sums[9 : 9 + inner // width, :part].reshape(1, -1)
@@ -1817,7 +1835,7 @@
         for lanes in (LAT_LANES, DEC_LANES)
     )
     return (
-        layer_out.reshape(1, slots, span, width),
+        wide(layer_out).reshape(1, slots, span, width),
         grad_cells.reshape(1, slots, span, width),
         kl_mean,
         grad_qkv[None],

time: 352 us -> 327 us (0.929)
  local copies, waits for them, and re-layouts: 41.9 us -> 18.7 us
  waiting for transfers between devices: 141 us -> 122 us
  starting transfers between devices: 90.3 us -> 102 us
  Pallas kernels: 49.2 us -> 53.8 us
    unnamed x166 -> x114, local copies, waits for them, and re-layouts: 31.5 us -> 13.3 us
    ppermute x49, waiting for transfers between devices: 96.4 us -> 108 us  [hop(): return lax.ppermute(values, axis, [(i, i ^ step) for i in range(size)])]
    ppermute x4, starting transfers between devices: 6.69 us -> 17.4 us  [fast_device(): lax.ppermute(grad, EVERY, [(there, here) for here, there in head_routes(s...]
    ppermute x8, waiting for transfers between devices: 16.4 us -> 6.12 us  [plane_hops(): lax.ppermute(values[2], ('y', 'x'), [(i, i ^ 3) for i in range(4)])]
    ppermute x4, waiting for transfers between devices: 8.52 us -> 0.48 us  [from_slides(): lax.ppermute(blocks[k], ('grp', 'z'), [(there, here) for here, there in s...]
    ppermute x4, waiting for transfers between devices: 13.2 us -> 6 us  [fast_device(): lax.ppermute(head_parts[int(single)], EVERY, head_routes(single, k))]
    ppermute x49, starting transfers between devices: 40.5 us -> 46.7 us  [hop(): return lax.ppermute(values, axis, [(i, i ^ step) for i in range(size)])]
    pallas_call x25, Pallas kernels: 49.2 us -> 53.8 us  [whole_call(): pl.pallas_call(run, out_shape=out_shapes, in_specs=[hbm if i in left_out...]
  transfers between devices with their start and end apart: 78 -> 78, of which waited for: 35 -> 35; matrix products, arithmetic and copies ran while one was open for 5% -> 4% of each run, Pallas kernels for 10% -> 11%
where the time goes in v2:
time: 327 us; the launch traced here: 324 us
  waiting for transfers between devices  122 us (37%)
  starting transfers between devices  102 us (31%)
  Pallas kernels  53.8 us (16%)
  local copies, waits for them, and re-layouts  18.7 us (6%)
  between operations  16.7 us (5%)
  other arithmetic  10.5 us (3%)
    ppermute x49, waiting for transfers between devices, hop(): return lax.ppermute(values, axis, [(i, i ^ step) for i in range(size)])  108 us
    pallas_call x25, Pallas kernels, whole_call(): pl.pallas_call(run, out_shape=out_shapes, in_specs=[hbm if i in left_out...  53.8 us
    ppermute x49, starting transfers between devices, hop(): return lax.ppermute(values, axis, [(i, i ^ step) for i in range(size)])  46.7 us
    ppermute x4, starting transfers between devices, fast_device(): lax.ppermute(grad, EVERY, [(there, here) for here, there in head_routes(s...  17.4 us
    unnamed x114, local copies, waits for them, and re-layouts  13.3 us
    all_to_all x2, starting transfers between devices, exchange(): return lax.all_to_all(blocks, axes, split_axis=0, concat_axis=0, tiled=True)  12 us
    ppermute x4, starting transfers between devices, fast_device(): lax.ppermute(head_parts[int(single)], EVERY, head_routes(single, k))  9.73 us
    ppermute x8, starting transfers between devices, plane_hops(): lax.ppermute(values[2], ('y', 'x'), [(i, i ^ 3) for i in range(4)])  8.05 us
  transfers between devices with their start and end apart: 78, of which 35 were waited for; matrix products, arithmetic and copies ran while one was open for 4% of the time, Pallas kernels for 11%

profile of v2, /device:TPU:0, one launch (start us, length us, event | category | flops | bytes accessed | tf_op | source)
XLA Modules:
  0.0 323.5 jit_solution(8867449732078131089)
XLA Ops:
  12.4 8.3 %all-to-all-start = ((bf16[16,64,128]{2,1,0:T(8,128)(2,1)}), bf16[16,64,128]{2,1,0:T(8,128)(2,1)S(1)}, u32[]{:S(2)}, u32[]{:S(2)}) async-start(bf16[16,64,128]{2,1,0:T(8,128)(2,1)} %get-tuple-element.120), calls=%async_computation | async-start | bytes 524288 | tf_op jit(solution)/shard_map/all_to_all | solution.py:1635
  21.7 2.0 collective-permute-start.1
  24.5 3.6 %collective-permute-start.4 = (bf16[128,1024]{1,0:T(8,128)(2,1)}, bf16[128,1024]{1,0:T(8,128)(2,1)}, u32[]{:S(2)}, u32[]{:S(2)}) collective-permute-start(bf16[128,1024]{1,0:T(8,128)(2,1)} %dynamic-slice_bitcast_fusion), channel_id=1, source_target_pairs={{0,0},{1,6},{2,3},{3,21},{4,18},{5,4},{6,1},{7,7},{8,16},{9,22},{1... | collective-permute-start | bytes 786440 | tf_op jit(solution)/shard_map/ppermute | solution.py:1703
  28.1 1.3 collective-permute-start.5
  31.1 3.0 collective-permute-start.3
  34.2 6.4 %collective-permute-done.3 = bf16[80,1024]{1,0:T(8,128)(2,1)S(1)} collective-permute-done((bf16[80,1024]{1,0:T(8,128)(2,1)S(1)}, bf16[80,1024]{1,0:T(8,128)(2,1)S(1)}, u32[]{:S(2)}, u32[]{:S(2)}) %collective-permute-start.3) | collective-permute-done | bytes 163872 | tf_op jit(solution)/shard_map/ppermute | solution.py:495
  42.2 6.0 %collective-permute-done.5.refs_3_ = bf16[64,1024]{1,0:T(8,128)(2,1)S(1)} collective-permute-done((bf16[64,1024]{1,0:T(8,128)(2,1)S(1)}, bf16[64,1024]{1,0:T(8,128)(2,1)S(1)}, u32[]{:S(2)}, u32[]{:S(2)}) %collective-permute-start.5) | collective-permute-done | bytes 131104 | tf_op jit(solution)/shard_map/ppermute | solution.py:1703
  48.9 2.4 collective-permute-start.7
  52.3 3.8 %collective-permute-start.9 = (bf16[64,1024]{1,0:T(8,128)(2,1)}, bf16[64,1024]{1,0:T(8,128)(2,1)S(1)}, u32[]{:S(2)}, u32[]{:S(2)}) collective-permute-start(bf16[64,1024]{1,0:T(8,128)(2,1)} %copy-done.44), channel_id=1, source_target_pairs={{0,5},{1,1},{2,20},{3,16},{4,23},{5,19},{6,6},{7,2},{8,21},{9,17},... | collective-permute-start | bytes 393224 | tf_op jit(solution)/shard_map/ppermute | solution.py:1703
  56.1 13.2 %collective-permute-done.6 = bf16[160,1024]{1,0:T(8,128)(2,1)S(1)} collective-permute-done((bf16[160,1024]{1,0:T(8,128)(2,1)}, bf16[160,1024]{1,0:T(8,128)(2,1)S(1)}, u32[]{:S(2)}, u32[]{:S(2)}) %collective-permute-start.6) | collective-permute-done | bytes 327712 | tf_op jit(solution)/shard_map/ppermute | solution.py:495
  73.9 11.0 %shard_map.240 = (f32[16,1024]{1,0:T(8,128)S(1)}, f32[16,512]{1,0:T(8,128)S(1)}, f32[16,512]{1,0:T(8,128)S(1)}, bf16[1024,1024]{1,0:T(8,128)(2,1)S(1)}, bf16[102...) custom-call(bf16[4,2,80,1024]{3,2,1,0:T(8,128)(2,1)S(1)} %bitcast.10, ...), custom_call_target="tpu_custom_call" | custom-call | flops 11000000512 | tf_op jit(solution)/shard_map/pallas_call | solution.py:676
  88.4 2.5 collective-permute-done.11.refs_2_
  91.3 6.0 %collective-permute-start.12 = (bf16[128,1024]{1,0:T(8,128)(2,1)S(1)}, bf16[128,1024]{1,0:T(8,128)(2,1)S(1)}, u32[]{:S(2)}, u32[]{:S(2)}) collective-permute-start(bf16[128,1024]{1,0:T(8,128)(2,1)S(1)} %get-tuple-element.141), channel_id=1, source_target_pairs={{0,1},{1,0},{2,3},{3,2},{4,5},{5,4},{6,7},{7,6},{8,9},{9,8},{10,11... | collective-permute-start | bytes 786440 | tf_op jit(solution)/shard_map/ppermute | solution.py:495
  97.3 1.9 collective-permute-start.13
  99.2 1.4 collective-permute-start.14
  100.6 3.8 %collective-permute-done.12.refs_1_ = bf16[128,1024]{1,0:T(8,128)(2,1)S(1)} collective-permute-done((bf16[128,1024]{1,0:T(8,128)(2,1)S(1)}, bf16[128,1024]{1,0:T(8,128)(2,1)S(1)}, u32[]{:S(2)}, u32[]{:S(2)}) %collective-permute-start.12) | collective-permute-done | bytes 262176 | tf_op jit(solution)/shard_map/ppermute | solution.py:495
  104.4 6.3 %collective-permute-done.13.refs_2_ = bf16[128,1024]{1,0:T(8,128)(2,1)S(1)} collective-permute-done((bf16[128,1024]{1,0:T(8,128)(2,1)S(1)}, bf16[128,1024]{1,0:T(8,128)(2,1)S(1)}, u32[]{:S(2)}, u32[]{:S(2)}) %collective-permute-start.13) | collective-permute-done | bytes 262176 | tf_op jit(solution)/shard_map/ppermute | solution.py:495
  110.7 1.8 collective-permute-done.14.refs_3_
  114.9 1.7 collective-permute-start.16
  117.9 5.8 %collective-permute-done.15.refs_1_.refs_9_ = bf16[128,1024]{1,0:T(8,128)(2,1)S(1)} collective-permute-done((bf16[128,1024]{1,0:T(8,128)(2,1)S(1)}, bf16[128,1024]{1,0:T(8,128)(2,1)S(1)}, u32[]{:S(2)}, u32[]{:S(2)}) %collective-permute-start.15) | collective-permute-done | bytes 262176 | tf_op jit(solution)/shard_map/ppermute | solution.py:495
  123.6 4.4 %collective-permute-done.16.refs_2_.refs_10_ = bf16[128,1024]{1,0:T(8,128)(2,1)S(1)} collective-permute-done((bf16[128,1024]{1,0:T(8,128)(2,1)S(1)}, bf16[128,1024]{1,0:T(8,128)(2,1)S(1)}, u32[]{:S(2)}, u32[]{:S(2)}) %collective-permute-start.16) | collective-permute-done | bytes 262176 | tf_op jit(solution)/shard_map/ppermute | solution.py:495
  130.0 4.8 %shard_map.244 = (bf16[512,512]{1,0:T(8,128)(2,1)S(1)}, f32[512,512]{1,0:T(8,128)S(1)}, bf16[512,1024]{1,0:T(8,128)(2,1)}) custom-call(bf16[128,1024]{1,0:T(8,128)(2,1)} %copy-done.48, bf16[128,1024]{1,0:T(8,128)(2,1)} %copy-done.49, bf16[128,1024]{1,0:T(8,128)(2,1)} %collective-permute-done.20.refs_2_.refs_14_, ...), custom_call_target="tpu_custom_call" | custom-call | flops 3849999872 | tf_op jit(solution)/shard_map/pallas_call | solution.py:676
  139.8 3.8 %shard_map.245 = (bf16[512,512]{1,0:T(8,128)(2,1)S(1)}, f32[512,512]{1,0:T(8,128)S(1)}, f32[128,1024]{1,0:T(8,128)S(1)}, bf16[128,1024]{1,0:T(8,128)(2,1)S(1)}, ...) custom-call(bf16[128,1024]{1,0:T(8,128)(2,1)} %copy-done.7, bf16[128,1024]{1,0:T(8,128)(2,1)} %copy-done.45, ...), custom_call_target="tpu_custom_call" | custom-call | flops 3849999872 | tf_op jit(solution)/shard_map/pallas_call | solution.py:676
  143.6 1.5 collective-permute-start.23
  145.1 2.0 collective-permute-start.24
  147.3 3.0 collective-permute-done.23.refs_2_
  150.3 8.1 %collective-permute-done.24.refs_3_ = bf16[128,1024]{1,0:T(8,128)(2,1)S(1)} collective-permute-done((bf16[128,1024]{1,0:T(8,128)(2,1)S(1)}, bf16[128,1024]{1,0:T(8,128)(2,1)S(1)}, u32[]{:S(2)}, u32[]{:S(2)}) %collective-permute-start.24) | collective-permute-done | bytes 262176 | tf_op jit(solution)/shard_map/ppermute | solution.py:495
  158.5 5.7 %shard_map.246 = (f32[128,1024]{1,0:T(8,128)S(1)}, bf16[128,1024]{1,0:T(8,128)(2,1)S(1)}, bf16[128,512]{1,0:T(8,128)(2,1)S(1)}, bf16[128,1024]{1,0:T(8,128)(2,1)...) custom-call(f32[128,1024]{1,0:T(8,128)S(1)} %copy-done.19, ...), custom_call_target="tpu_custom_call" | custom-call | flops 6270000128 | tf_op jit(solution)/shard_map/pallas_call | solution.py:676
  165.4 1.6 collective-permute-start.30
  167.0 1.4 collective-permute-start.31
  168.4 4.7 %collective-permute-done.29.refs_1_ = bf16[128,1024]{1,0:T(8,128)(2,1)S(1)} collective-permute-done((bf16[128,1024]{1,0:T(8,128)(2,1)S(1)}, bf16[128,1024]{1,0:T(8,128)(2,1)S(1)}, u32[]{:S(2)}, u32[]{:S(2)}) %collective-permute-start.29) | collective-permute-done | bytes 262176 | tf_op jit(solution)/shard_map/ppermute | solution.py:495
  173.9 5.1 %collective-permute-done.30.refs_2_ = bf16[128,1024]{1,0:T(8,128)(2,1)S(1)} collective-permute-done((bf16[128,1024]{1,0:T(8,128)(2,1)S(1)}, bf16[128,1024]{1,0:T(8,128)(2,1)S(1)}, u32[]{:S(2)}, u32[]{:S(2)}) %collective-permute-start.30) | collective-permute-done | bytes 262176 | tf_op jit(solution)/shard_map/ppermute | solution.py:495
  179.0 1.8 collective-permute-done.31.refs_3_
  180.8 1.5 collective-permute-done.35.refs_3_.refs_7_
  182.3 1.9 shard_map.247
  185.5 1.9 collective-permute-done.41.refs_5_
  188.9 1.9 shard_map.249
  190.8 5.2 %shard_map.250 = bf16[1792,1024]{1,0:T(8,128)(2,1)} custom-call(bf16[128,1024]{1,0:T(8,128)(2,1)S(1)} %get-tuple-element.156.refs_0_, bf16[128,1024]{1,0:T(8,128)(2,1)S(1)} %collective-permute-done.29.refs_1_, bf16[128,1024]{1,0:T(8,128)(2,1)S(1)} %collective-permute-done.30.refs_2_, bf16[128,1024]{1,0:T(8,128)(2,1)S(1)} %collective-permute-done.31.refs_3_, ...), custom_call_target="tpu_custom_call" | custom-call | flops 3740000000 | tf_op jit(solution)/shard_map/pallas_call | solution.py:676
  197.9 1.7 collective-permute-start.44
  201.9 2.8 collective-permute-done.43.refs_1_
  204.7 6.7 %collective-permute-done.44.refs_2_ = bf16[128,1024]{1,0:T(8,128)(2,1)S(1)} collective-permute-done((bf16[128,1024]{1,0:T(8,128)(2,1)S(1)}, bf16[128,1024]{1,0:T(8,128)(2,1)S(1)}, u32[]{:S(2)}, u32[]{:S(2)}) %collective-permute-start.44) | collective-permute-done | bytes 262176 | tf_op jit(solution)/shard_map/ppermute | solution.py:495
  212.0 1.9 collective-permute-start.46
  214.8 1.4 collective-permute-start.48
  216.6 4.0 %collective-permute-done.46.refs_1_ = bf16[128,1024]{1,0:T(8,128)(2,1)S(1)} collective-permute-done((bf16[128,1024]{1,0:T(8,128)(2,1)S(1)}, bf16[128,1024]{1,0:T(8,128)(2,1)S(1)}, u32[]{:S(2)}, u32[]{:S(2)}) %collective-permute-start.46) | collective-permute-done | bytes 262176 | tf_op jit(solution)/shard_map/ppermute | solution.py:495
  220.6 1.8 collective-permute-start.50
  222.4 4.2 %collective-permute-done.47.refs_2_ = bf16[128,1024]{1,0:T(8,128)(2,1)S(1)} collective-permute-done((bf16[128,1024]{1,0:T(8,128)(2,1)S(1)}, bf16[128,1024]{1,0:T(8,128)(2,1)S(1)}, u32[]{:S(2)}, u32[]{:S(2)}) %collective-permute-start.47) | collective-permute-done | bytes 262176 | tf_op jit(solution)/shard_map/ppermute | solution.py:495
  227.2 1.4 collective-permute-done.48.refs_3_
  228.6 1.5 collective-permute-done.52.refs_7_
  231.3 8.9 %shard_map.253 = (bf16[1024,384]{1,0:T(8,128)(2,1)S(1)}, bf16[512,1024]{1,0:T(8,128)(2,1)S(1)}) custom-call(bf16[1024,384]{1,0:T(8,128)(2,1)S(1)} %copy-done.31, f32[1,1024]{1,0:T(1,128)S(1)} %get-tuple-element.159.refs_1_, f32[1024,128]{1,0:T(8,128)S(1)} %copy-done.33, bf16[1024,128]{1,0:T(8,128)(2,1)S(1)} %bitcast.97, bf16[384,1024]{1,0:T(8,128)(2,1)S(1)} %copy-done.17, ...), custom_call_target="tpu_custom_call" | custom-call | flops 10119999488 | tf_op jit(solution)/shard_map/pallas_call | solution.py:676
  240.4 2.5 collective-permute-done.53.refs_2_
  243.7 1.3 collective-permute-start.54
  245.0 1.4 collective-permute-start.55
  248.3 4.6 %collective-permute-done.54.refs_1_ = bf16[128,1024]{1,0:T(8,128)(2,1)S(1)} collective-permute-done((bf16[128,1024]{1,0:T(8,128)(2,1)S(1)}, bf16[128,1024]{1,0:T(8,128)(2,1)S(1)}, u32[]{:S(2)}, u32[]{:S(2)}) %collective-permute-start.54) | collective-permute-done | bytes 262176 | tf_op jit(solution)/shard_map/ppermute | solution.py:495
  252.9 5.9 %collective-permute-done.55.refs_2_ = bf16[128,1024]{1,0:T(8,128)(2,1)S(1)} collective-permute-done((bf16[128,1024]{1,0:T(8,128)(2,1)S(1)}, bf16[128,1024]{1,0:T(8,128)(2,1)S(1)}, u32[]{:S(2)}, u32[]{:S(2)}) %collective-permute-start.55) | collective-permute-done | bytes 262176 | tf_op jit(solution)/shard_map/ppermute | solution.py:495
  258.8 1.4 shard_map.256
  260.2 3.7 %all-to-all-start.1 = ((bf16[16,96,128]{2,1,0:T(8,128)(2,1)}), bf16[16,96,128]{2,1,0:T(8,128)(2,1)S(1)}, u32[]{:S(2)}, u32[]{:S(2)}) async-start(bf16[16,96,128]{2,1,0:T(8,128)(2,1)} %get-tuple-element.203), calls=%async_computation.1 | async-start | bytes 786432 | tf_op jit(solution)/shard_map/all_to_all | solution.py:1635
  264.0 1.9 collective-permute-start.57
  268.1 9.6 %collective-permute-start.62 = (bf16[128,1024]{1,0:T(8,128)(2,1)S(1)}, bf16[128,1024]{1,0:T(8,128)(2,1)S(1)}, u32[]{:S(2)}, u32[]{:S(2)}) collective-permute-start(bf16[128,1024]{1,0:T(8,128)(2,1)S(1)} %get-tuple-element.207), channel_id=1, source_target_pairs={{4,0},{2,1},{7,2},{17,3},{22,4},{0,5},{5,6},{3,7},{20,8},{18,9},{2... | collective-permute-start | bytes 786440 | tf_op jit(solution)/shard_map/ppermute | solution.py:1813
  277.7 2.0 collective-permute-start.61
  279.8 5.0 %collective-permute-start.63 = (bf16[64,1024]{1,0:T(8,128)(2,1)S(1)}, bf16[64,1024]{1,0:T(8,128)(2,1)S(1)}, u32[]{:S(2)}, u32[]{:S(2)}) collective-permute-start(bf16[64,1024]{1,0:T(8,128)(2,1)S(1)} %get-tuple-element.208), channel_id=1, source_target_pairs={{5,0},{1,1},{20,2},{16,3},{23,4},{19,5},{6,6},{2,7},{21,8},{17,9},... | collective-permute-start | bytes 393224 | tf_op jit(solution)/shard_map/ppermute | solution.py:1813
  288.4 3.8 %collective-permute-start.64 = (bf16[64,1280]{1,0:T(8,128)(2,1)S(1)}, bf16[64,1280]{1,0:T(8,128)(2,1)S(1)}, u32[]{:S(2)}, u32[]{:S(2)}) collective-permute-start(bf16[64,1280]{1,0:T(8,128)(2,1)S(1)} %get-tuple-element.210), channel_id=1, source_target_pairs={{0,1},{1,0},{2,3},{3,2},{4,5},{5,4},{6,7},{7,6},{8,9},{9,8},{10,11... | collective-permute-start | bytes 491528 | tf_op jit(solution)/shard_map/ppermute | solution.py:495
  292.2 5.4 %collective-permute-start.65 = (bf16[64,1280]{1,0:T(8,128)(2,1)S(1)}, bf16[64,1280]{1,0:T(8,128)(2,1)S(1)}, u32[]{:S(2)}, u32[]{:S(2)}) collective-permute-start(bf16[64,1280]{1,0:T(8,128)(2,1)S(1)} %get-tuple-element.211), channel_id=1, source_target_pairs={{0,2},{2,0},{1,3},{3,1},{4,6},{6,4},{5,7},{7,5},{8,10},{10,8},{9,1... | collective-permute-start | bytes 491528 | tf_op jit(solution)/shard_map/ppermute | solution.py:495
  299.5 5.6 %collective-permute-done.65.refs_2_ = bf16[64,1280]{1,0:T(8,128)(2,1)S(1)} collective-permute-done((bf16[64,1280]{1,0:T(8,128)(2,1)S(1)}, bf16[64,1280]{1,0:T(8,128)(2,1)S(1)}, u32[]{:S(2)}, u32[]{:S(2)}) %collective-permute-start.65) | collective-permute-done | bytes 163872 | tf_op jit(solution)/shard_map/ppermute | solution.py:495
  313.5 2.1 add_bitcast_fusion
  (276 shorter events, 61.9 us)
Async XLA Ops:
  7.2 81.2 %all-gather.3.cloned.1.call-start = ((), (), s32[]{:S(2)}) async-start(), calls=%async_computation.3 | async-start | bytes 1671168 | tf_op jit(solution)/shard_map/all_gather | solution.py:1670
  12.4 36.5 %all-to-all-start = ((bf16[16,64,128]{2,1,0:T(8,128)(2,1)}), bf16[16,64,128]{2,1,0:T(8,128)(2,1)S(1)}, u32[]{:S(2)}, u32[]{:S(2)}) async-start(bf16[16,64,128]{2,1,0:T(8,128)(2,1)} %get-tuple-element.120), calls=%async_computation | async-start | bytes 524288 | tf_op jit(solution)/shard_map/all_to_all | solution.py:1635
  20.7 108.0 %all-gather.5.cloned.1.call-start = ((), (), s32[]{:S(2)}) async-start(), calls=%async_computation.4 | async-start | bytes 2621440 | tf_op jit(solution)/shard_map/all_gather | solution.py:1734
  20.9 9.4 %collective-permute-start = (bf16[80,1024]{1,0:T(8,128)(2,1)S(1)}, bf16[80,1024]{1,0:T(8,128)(2,1)S(1)}, u32[]{:S(2)}, u32[]{:S(2)}) collective-permute-start(bf16[80,1024]{1,0:T(8,128)(2,1)S(1)} %get-tuple-element.122), channel_id=1, source_target_pairs={{0,0},{4,4},{8,16},{12,20},{16,8},{20,12},{24,24},{28,28},{1,1},{5... | collective-permute-start | bytes 491528 | tf_op jit(solution)/shard_map/ppermute | solution.py:1693
  21.7 9.4 %collective-permute-start.1 = (bf16[80,1024]{1,0:T(8,128)(2,1)S(1)}, bf16[80,1024]{1,0:T(8,128)(2,1)S(1)}, u32[]{:S(2)}, u32[]{:S(2)}) collective-permute-start(bf16[80,1024]{1,0:T(8,128)(2,1)S(1)} %get-tuple-element.123), channel_id=1, source_target_pairs={{0,4},{4,0},{8,20},{12,16},{16,12},{20,8},{24,28},{28,24},{1,5},{5... | collective-permute-start | bytes 491528 | tf_op jit(solution)/shard_map/ppermute | solution.py:1693
  24.5 24.4 %collective-permute-start.4 = (bf16[128,1024]{1,0:T(8,128)(2,1)}, bf16[128,1024]{1,0:T(8,128)(2,1)}, u32[]{:S(2)}, u32[]{:S(2)}) collective-permute-start(bf16[128,1024]{1,0:T(8,128)(2,1)} %dynamic-slice_bitcast_fusion), channel_id=1, source_target_pairs={{0,0},{1,6},{2,3},{3,21},{4,18},{5,4},{6,1},{7,7},{8,16},{9,22},{1... | collective-permute-start | bytes 786440 | tf_op jit(solution)/shard_map/ppermute | solution.py:1703
  28.1 20.1 %collective-permute-start.5 = (bf16[64,1024]{1,0:T(8,128)(2,1)S(1)}, bf16[64,1024]{1,0:T(8,128)(2,1)S(1)}, u32[]{:S(2)}, u32[]{:S(2)}) collective-permute-start(bf16[64,1024]{1,0:T(8,128)(2,1)S(1)} %dynamic-slice_bitcast_fusion.1), channel_id=1, source_target_pairs={{0,1},{1,5},{2,16},{3,20},{4,19},{5,23},{6,2},{7,6},{8,17},{9,21},... | collective-permute-start | bytes 393224 | tf_op jit(solution)/shard_map/ppermute | solution.py:1703
  30.3 11.0 %collective-permute-start.2 = (bf16[144,1024]{1,0:T(8,128)(2,1)S(1)}, bf16[144,1024]{1,0:T(8,128)(2,1)S(1)}, u32[]{:S(2)}, u32[]{:S(2)}) collective-permute-start(bf16[144,1024]{1,0:T(8,128)(2,1)S(1)} %pad_maximum_fusion.2), channel_id=1, source_target_pairs={{0,1},{1,0},{2,3},{3,2},{4,5},{5,4},{6,7},{7,6},{8,9},{9,8},{10,11... | collective-permute-start | bytes 884744 | tf_op jit(solution)/shard_map/ppermute | solution.py:495
  31.1 9.5 %collective-permute-start.3 = (bf16[80,1024]{1,0:T(8,128)(2,1)S(1)}, bf16[80,1024]{1,0:T(8,128)(2,1)S(1)}, u32[]{:S(2)}, u32[]{:S(2)}) collective-permute-start(bf16[80,1024]{1,0:T(8,128)(2,1)S(1)} %collective-permute-done.1), channel_id=1, source_target_pairs={{0,2},{2,0},{1,3},{3,1},{4,6},{6,4},{5,7},{7,5},{8,10},{10,8},{9,1... | collective-permute-start | bytes 491528 | tf_op jit(solution)/shard_map/ppermute | solution.py:495
  48.9 20.4 %collective-permute-start.6 = (bf16[160,1024]{1,0:T(8,128)(2,1)}, bf16[160,1024]{1,0:T(8,128)(2,1)S(1)}, u32[]{:S(2)}, u32[]{:S(2)}) collective-permute-start(bf16[160,1024]{1,0:T(8,128)(2,1)} %pad_maximum_fusion), channel_id=1, source_target_pairs={{0,1},{1,0},{2,3},{3,2},{4,5},{5,4},{6,7},{7,6},{8,9},{9,8},{10,11... | collective-permute-start | bytes 983048 | tf_op jit(solution)/shard_map/ppermute | solution.py:495
  48.9 20.4 %collective-permute-start.7 = (bf16[224,1024]{1,0:T(8,128)(2,1)}, bf16[224,1024]{1,0:T(8,128)(2,1)S(1)}, u32[]{:S(2)}, u32[]{:S(2)}) collective-permute-start(bf16[224,1024]{1,0:T(8,128)(2,1)} %maximum_maximum_fusion.1), channel_id=1, source_target_pairs={{0,2},{2,0},{1,3},{3,1},{4,6},{6,4},{5,7},{7,5},{8,10},{10,8},{9,1... | collective-permute-start | bytes 1376264 | tf_op jit(solution)/shard_map/ppermute | solution.py:495
  51.2 18.2 %collective-permute-start.8 = (bf16[128,1024]{1,0:T(8,128)(2,1)}, bf16[128,1024]{1,0:T(8,128)(2,1)S(1)}, u32[]{:S(2)}, u32[]{:S(2)}) collective-permute-start(bf16[128,1024]{1,0:T(8,128)(2,1)} %dynamic-slice_bitcast_fusion), channel_id=1, source_target_pairs={{0,4},{1,2},{2,7},{3,17},{4,22},{5,0},{6,5},{7,3},{8,20},{9,18},{1... | collective-permute-start | bytes 786440 | tf_op jit(solution)/shard_map/ppermute | solution.py:1703
  52.3 17.1 %collective-permute-start.9 = (bf16[64,1024]{1,0:T(8,128)(2,1)}, bf16[64,1024]{1,0:T(8,128)(2,1)S(1)}, u32[]{:S(2)}, u32[]{:S(2)}) collective-permute-start(bf16[64,1024]{1,0:T(8,128)(2,1)} %copy-done.44), channel_id=1, source_target_pairs={{0,5},{1,1},{2,20},{3,16},{4,23},{5,19},{6,6},{7,2},{8,21},{9,17},... | collective-permute-start | bytes 393224 | tf_op jit(solution)/shard_map/ppermute | solution.py:1703
  72.8 214.3 %reduce-scatter.2.cloned.1.call-start = ((), (), s32[]{:S(2)}) async-start(), calls=%async_computation.5 | async-start | bytes 4587520 | tf_op jit(solution)/shard_map/reduce_scatter | solution.py:1769
  91.3 13.1 %collective-permute-start.12 = (bf16[128,1024]{1,0:T(8,128)(2,1)S(1)}, bf16[128,1024]{1,0:T(8,128)(2,1)S(1)}, u32[]{:S(2)}, u32[]{:S(2)}) collective-permute-start(bf16[128,1024]{1,0:T(8,128)(2,1)S(1)} %get-tuple-element.141), channel_id=1, source_target_pairs={{0,1},{1,0},{2,3},{3,2},{4,5},{5,4},{6,7},{7,6},{8,9},{9,8},{10,11... | collective-permute-start | bytes 786440 | tf_op jit(solution)/shard_map/ppermute | solution.py:495
  97.3 13.4 %collective-permute-start.13 = (bf16[128,1024]{1,0:T(8,128)(2,1)S(1)}, bf16[128,1024]{1,0:T(8,128)(2,1)S(1)}, u32[]{:S(2)}, u32[]{:S(2)}) collective-permute-start(bf16[128,1024]{1,0:T(8,128)(2,1)S(1)} %get-tuple-element.142), channel_id=1, source_target_pairs={{0,2},{2,0},{1,3},{3,1},{4,6},{6,4},{5,7},{7,5},{8,10},{10,8},{9,1... | collective-permute-start | bytes 786440 | tf_op jit(solution)/shard_map/ppermute | solution.py:495
  99.2 13.3 %collective-permute-start.14 = (bf16[128,1024]{1,0:T(8,128)(2,1)S(1)}, bf16[128,1024]{1,0:T(8,128)(2,1)S(1)}, u32[]{:S(2)}, u32[]{:S(2)}) collective-permute-start(bf16[128,1024]{1,0:T(8,128)(2,1)S(1)} %get-tuple-element.143), channel_id=1, source_target_pairs={{0,3},{1,2},{2,1},{3,0},{4,7},{5,6},{6,5},{7,4},{8,11},{9,10},{10,... | collective-permute-start | bytes 786440 | tf_op jit(solution)/shard_map/ppermute | solution.py:585
  114.4 9.2 %collective-permute-start.15 = (bf16[128,1024]{1,0:T(8,128)(2,1)S(1)}, bf16[128,1024]{1,0:T(8,128)(2,1)S(1)}, u32[]{:S(2)}, u32[]{:S(2)}) collective-permute-start(bf16[128,1024]{1,0:T(8,128)(2,1)S(1)} %get-tuple-element.146.refs_0_.refs_8_), channel_id=1, source_target_pairs={{0,1},{1,0},{2,3},{3,2},{4,5},{5,4},{6,7},{7,6},{8,9},{9,8},{10,11... | collective-permute-start | bytes 786440 | tf_op jit(solution)/shard_map/ppermute | solution.py:495
  114.9 13.0 %collective-permute-start.16 = (bf16[128,1024]{1,0:T(8,128)(2,1)S(1)}, bf16[128,1024]{1,0:T(8,128)(2,1)S(1)}, u32[]{:S(2)}, u32[]{:S(2)}) collective-permute-start(bf16[128,1024]{1,0:T(8,128)(2,1)S(1)} %get-tuple-element.146.refs_0_.refs_8_), channel_id=1, source_target_pairs={{0,2},{2,0},{1,3},{3,1},{4,6},{6,4},{5,7},{7,5},{8,10},{10,8},{9,1... | collective-permute-start | bytes 786440 | tf_op jit(solution)/shard_map/ppermute | solution.py:495
  116.7 11.3 %collective-permute-start.17 = (bf16[128,1024]{1,0:T(8,128)(2,1)S(1)}, bf16[128,1024]{1,0:T(8,128)(2,1)S(1)}, u32[]{:S(2)}, u32[]{:S(2)}) collective-permute-start(bf16[128,1024]{1,0:T(8,128)(2,1)S(1)} %get-tuple-element.146.refs_0_.refs_8_), channel_id=1, source_target_pairs={{0,3},{1,2},{2,1},{3,0},{4,7},{5,6},{6,5},{7,4},{8,11},{9,10},{10,... | collective-permute-start | bytes 786440 | tf_op jit(solution)/shard_map/ppermute | solution.py:585
  117.9 10.6 %collective-permute-start.18 = (bf16[128,1024]{1,0:T(8,128)(2,1)S(1)}, bf16[128,1024]{1,0:T(8,128)(2,1)S(1)}, u32[]{:S(2)}, u32[]{:S(2)}) collective-permute-start(bf16[128,1024]{1,0:T(8,128)(2,1)S(1)} %get-tuple-element.146.refs_0_.refs_8_), channel_id=1, source_target_pairs={{0,16},{16,0},{1,17},{17,1},{2,18},{18,2},{3,19},{19,3},{4,20},{20... | collective-permute-start | bytes 786440 | tf_op jit(solution)/shard_map/ppermute | solution.py:495
  123.6 5.1 %collective-permute-start.19 = (bf16[128,1024]{1,0:T(8,128)(2,1)S(1)}, bf16[128,1024]{1,0:T(8,128)(2,1)S(1)}, u32[]{:S(2)}, u32[]{:S(2)}) collective-permute-start(bf16[128,1024]{1,0:T(8,128)(2,1)S(1)} %collective-permute-done.15.refs_1_.refs_9_), channel_id=1, source_target_pairs={{0,16},{16,0},{1,17},{17,1},{2,18},{18,2},{3,19},{19,3},{4,20},{20... | collective-permute-start | bytes 786440 | tf_op jit(solution)/shard_map/ppermute | solution.py:495
  136.7 10.6 %collective-permute-start.26 = (bf16[1024,768]{1,0:T(8,128)(2,1)S(1)}, bf16[1024,768]{1,0:T(8,128)(2,1)}, u32[]{:S(2)}, u32[]{:S(2)}) collective-permute-start(bf16[1024,768]{1,0:T(8,128)(2,1)S(1)} %copy-done.3), channel_id=1, source_target_pairs={{0,16},{16,0},{1,17},{17,1},{2,18},{18,2},{3,19},{19,3},{4,20},{20... | collective-permute-start | bytes 4718600 | tf_op jit(solution)/shard_map/ppermute | solution.py:495
  138.2 8.9 %collective-permute-start.27 = (bf16[128,1024]{1,0:T(8,128)(2,1)S(1)}, bf16[128,1024]{1,0:T(8,128)(2,1)S(1)}, u32[]{:S(2)}, u32[]{:S(2)}) collective-permute-start(bf16[128,1024]{1,0:T(8,128)(2,1)S(1)} %get-tuple-element.243), channel_id=1, source_target_pairs={{0,0},{4,4},{8,16},{12,20},{16,8},{20,12},{24,24},{28,28},{1,1},{5... | collective-permute-start | bytes 786440 | tf_op jit(solution)/shard_map/ppermute | solution.py:539
  139.3 8.0 %collective-permute-start.28 = (bf16[128,1024]{1,0:T(8,128)(2,1)S(1)}, bf16[128,1024]{1,0:T(8,128)(2,1)S(1)}, u32[]{:S(2)}, u32[]{:S(2)}) collective-permute-start(bf16[128,1024]{1,0:T(8,128)(2,1)S(1)} %get-tuple-element.242), channel_id=1, source_target_pairs={{0,4},{4,0},{8,20},{12,16},{16,12},{20,8},{24,28},{28,24},{1,5},{5... | collective-permute-start | bytes 786440 | tf_op jit(solution)/shard_map/ppermute | solution.py:539
  143.6 6.7 %collective-permute-start.23 = (bf16[128,1024]{1,0:T(8,128)(2,1)S(1)}, bf16[128,1024]{1,0:T(8,128)(2,1)S(1)}, u32[]{:S(2)}, u32[]{:S(2)}) collective-permute-start(bf16[128,1024]{1,0:T(8,128)(2,1)S(1)} %get-tuple-element.149), channel_id=1, source_target_pairs={{0,1},{1,0},{2,3},{3,2},{4,5},{5,4},{6,7},{7,6},{8,9},{9,8},{10,11... | collective-permute-start | bytes 786440 | tf_op jit(solution)/shard_map/ppermute | solution.py:495
  145.1 13.3 %collective-permute-start.24 = (bf16[128,1024]{1,0:T(8,128)(2,1)S(1)}, bf16[128,1024]{1,0:T(8,128)(2,1)S(1)}, u32[]{:S(2)}, u32[]{:S(2)}) collective-permute-start(bf16[128,1024]{1,0:T(8,128)(2,1)S(1)} %get-tuple-element.150), channel_id=1, source_target_pairs={{0,2},{2,0},{1,3},{3,1},{4,6},{6,4},{5,7},{7,5},{8,10},{10,8},{9,1... | collective-permute-start | bytes 786440 | tf_op jit(solution)/shard_map/ppermute | solution.py:495
  147.1 11.4 %collective-permute-start.25 = (bf16[128,1024]{1,0:T(8,128)(2,1)S(1)}, bf16[128,1024]{1,0:T(8,128)(2,1)S(1)}, u32[]{:S(2)}, u32[]{:S(2)}) collective-permute-start(bf16[128,1024]{1,0:T(8,128)(2,1)S(1)} %get-tuple-element.151), channel_id=1, source_target_pairs={{0,3},{1,2},{2,1},{3,0},{4,7},{5,6},{6,5},{7,4},{8,11},{9,10},{10,... | collective-permute-start | bytes 786440 | tf_op jit(solution)/shard_map/ppermute | solution.py:585
  164.2 8.9 %collective-permute-start.29 = (bf16[128,1024]{1,0:T(8,128)(2,1)S(1)}, bf16[128,1024]{1,0:T(8,128)(2,1)S(1)}, u32[]{:S(2)}, u32[]{:S(2)}) collective-permute-start(bf16[128,1024]{1,0:T(8,128)(2,1)S(1)} %get-tuple-element.156.refs_0_), channel_id=1, source_target_pairs={{0,1},{1,0},{2,3},{3,2},{4,5},{5,4},{6,7},{7,6},{8,9},{9,8},{10,11... | collective-permute-start | bytes 786440 | tf_op jit(solution)/shard_map/ppermute | solution.py:495
  165.4 13.6 %collective-permute-start.30 = (bf16[128,1024]{1,0:T(8,128)(2,1)S(1)}, bf16[128,1024]{1,0:T(8,128)(2,1)S(1)}, u32[]{:S(2)}, u32[]{:S(2)}) collective-permute-start(bf16[128,1024]{1,0:T(8,128)(2,1)S(1)} %get-tuple-element.156.refs_0_), channel_id=1, source_target_pairs={{0,2},{2,0},{1,3},{3,1},{4,6},{6,4},{5,7},{7,5},{8,10},{10,8},{9,1... | collective-permute-start | bytes 786440 | tf_op jit(solution)/shard_map/ppermute | solution.py:495
  167.0 13.8 %collective-permute-start.31 = (bf16[128,1024]{1,0:T(8,128)(2,1)S(1)}, bf16[128,1024]{1,0:T(8,128)(2,1)S(1)}, u32[]{:S(2)}, u32[]{:S(2)}) collective-permute-start(bf16[128,1024]{1,0:T(8,128)(2,1)S(1)} %get-tuple-element.156.refs_0_), channel_id=1, source_target_pairs={{0,3},{1,2},{2,1},{3,0},{4,7},{5,6},{6,5},{7,4},{8,11},{9,10},{10,... | collective-permute-start | bytes 786440 | tf_op jit(solution)/shard_map/ppermute | solution.py:585
  168.4 12.4 %collective-permute-start.32 = (bf16[128,1024]{1,0:T(8,128)(2,1)S(1)}, bf16[128,1024]{1,0:T(8,128)(2,1)S(1)}, u32[]{:S(2)}, u32[]{:S(2)}) collective-permute-start(bf16[128,1024]{1,0:T(8,128)(2,1)S(1)} %get-tuple-element.156.refs_0_), channel_id=1, source_target_pairs={{0,16},{16,0},{1,17},{17,1},{2,18},{18,2},{3,19},{19,3},{4,20},{20... | collective-permute-start | bytes 786440 | tf_op jit(solution)/shard_map/ppermute | solution.py:495
  173.1 7.7 %collective-permute-start.33 = (bf16[128,1024]{1,0:T(8,128)(2,1)S(1)}, bf16[128,1024]{1,0:T(8,128)(2,1)S(1)}, u32[]{:S(2)}, u32[]{:S(2)}) collective-permute-start(bf16[128,1024]{1,0:T(8,128)(2,1)S(1)} %collective-permute-done.29.refs_1_), channel_id=1, source_target_pairs={{0,16},{16,0},{1,17},{17,1},{2,18},{18,2},{3,19},{19,3},{4,20},{20... | collective-permute-start | bytes 786440 | tf_op jit(solution)/shard_map/ppermute | solution.py:495
  184.2 4.7 %collective-permute-start.38 = (bf16[512,1024]{1,0:T(8,128)(2,1)S(1)}, bf16[512,1024]{1,0:T(8,128)(2,1)S(1)}, u32[]{:S(2)}, u32[]{:S(2)}) collective-permute-start(bf16[512,1024]{1,0:T(8,128)(2,1)S(1)} %get-tuple-element.164), channel_id=1, source_target_pairs={{0,16},{16,0},{1,17},{17,1},{2,18},{18,2},{3,19},{19,3},{4,20},{20... | collective-permute-start | bytes 3145736 | tf_op jit(solution)/shard_map/ppermute | solution.py:495
  184.8 3.5 %collective-permute-start.39 = (bf16[128,1024]{1,0:T(8,128)(2,1)S(1)}, bf16[128,1024]{1,0:T(8,128)(2,1)S(1)}, u32[]{:S(2)}, u32[]{:S(2)}) collective-permute-start(bf16[128,1024]{1,0:T(8,128)(2,1)S(1)} %get-tuple-element.165.refs_0_), channel_id=1, source_target_pairs={{0,16},{16,0},{1,17},{17,1},{2,18},{18,2},{3,19},{19,3},{4,20},{20... | collective-permute-start | bytes 786440 | tf_op jit(solution)/shard_map/ppermute | solution.py:495
  185.0 3.3 %collective-permute-start.40 = (bf16[128,1024]{1,0:T(8,128)(2,1)S(1)}, bf16[128,1024]{1,0:T(8,128)(2,1)S(1)}, u32[]{:S(2)}, u32[]{:S(2)}) collective-permute-start(bf16[128,1024]{1,0:T(8,128)(2,1)S(1)} %get-tuple-element.166.refs_2_), channel_id=1, source_target_pairs={{0,16},{16,0},{1,17},{17,1},{2,18},{18,2},{3,19},{19,3},{4,20},{20... | collective-permute-start | bytes 786440 | tf_op jit(solution)/shard_map/ppermute | solution.py:495
  196.1 5.0 %collective-permute-start.36 = (bf16[64,1024]{1,0:T(8,128)(2,1)S(1)}, bf16[64,1024]{1,0:T(8,128)(2,1)S(1)}, u32[]{:S(2)}, u32[]{:S(2)}) collective-permute-start(bf16[64,1024]{1,0:T(8,128)(2,1)S(1)} %get-tuple-element.259), channel_id=1, source_target_pairs={{4,0},{0,4},{20,8},{16,12},{12,16},{8,20},{28,24},{24,28},{5,1},{1... | collective-permute-start | bytes 393224 | tf_op jit(solution)/shard_map/ppermute | solution.py:545
  196.5 4.7 %collective-permute-start.37 = (bf16[64,1024]{1,0:T(8,128)(2,1)S(1)}, bf16[64,1024]{1,0:T(8,128)(2,1)S(1)}, u32[]{:S(2)}, u32[]{:S(2)}) collective-permute-start(bf16[64,1024]{1,0:T(8,128)(2,1)S(1)} %get-tuple-element.258), channel_id=1, source_target_pairs={{0,0},{4,4},{16,8},{20,12},{8,16},{12,20},{24,24},{28,28},{1,1},{5... | collective-permute-start | bytes 393224 | tf_op jit(solution)/shard_map/ppermute | solution.py:545
  197.1 7.6 %collective-permute-start.43 = (bf16[128,1024]{1,0:T(8,128)(2,1)S(1)}, bf16[128,1024]{1,0:T(8,128)(2,1)S(1)}, u32[]{:S(2)}, u32[]{:S(2)}) collective-permute-start(bf16[128,1024]{1,0:T(8,128)(2,1)S(1)} %get-tuple-element.170), channel_id=1, source_target_pairs={{0,1},{1,0},{2,3},{3,2},{4,5},{5,4},{6,7},{7,6},{8,9},{9,8},{10,11... | collective-permute-start | bytes 786440 | tf_op jit(solution)/shard_map/ppermute | solution.py:495
  197.9 13.5 %collective-permute-start.44 = (bf16[128,1024]{1,0:T(8,128)(2,1)S(1)}, bf16[128,1024]{1,0:T(8,128)(2,1)S(1)}, u32[]{:S(2)}, u32[]{:S(2)}) collective-permute-start(bf16[128,1024]{1,0:T(8,128)(2,1)S(1)} %get-tuple-element.171), channel_id=1, source_target_pairs={{0,2},{2,0},{1,3},{3,1},{4,6},{6,4},{5,7},{7,5},{8,10},{10,8},{9,1... | collective-permute-start | bytes 786440 | tf_op jit(solution)/shard_map/ppermute | solution.py:495
  199.6 11.8 %collective-permute-start.45 = (bf16[128,1024]{1,0:T(8,128)(2,1)S(1)}, bf16[128,1024]{1,0:T(8,128)(2,1)S(1)}, u32[]{:S(2)}, u32[]{:S(2)}) collective-permute-start(bf16[128,1024]{1,0:T(8,128)(2,1)S(1)} %get-tuple-element.172), channel_id=1, source_target_pairs={{0,3},{1,2},{2,1},{3,0},{4,7},{5,6},{6,5},{7,4},{8,11},{9,10},{10,... | collective-permute-start | bytes 786440 | tf_op jit(solution)/shard_map/ppermute | solution.py:585
  212.0 8.6 %collective-permute-start.46 = (bf16[128,1024]{1,0:T(8,128)(2,1)S(1)}, bf16[128,1024]{1,0:T(8,128)(2,1)S(1)}, u32[]{:S(2)}, u32[]{:S(2)}) collective-permute-start(bf16[128,1024]{1,0:T(8,128)(2,1)S(1)} %get-tuple-element.182.refs_0_), channel_id=1, source_target_pairs={{0,1},{1,0},{2,3},{3,2},{4,5},{5,4},{6,7},{7,6},{8,9},{9,8},{10,11... | collective-permute-start | bytes 786440 | tf_op jit(solution)/shard_map/ppermute | solution.py:495
  213.9 12.6 %collective-permute-start.47 = (bf16[128,1024]{1,0:T(8,128)(2,1)S(1)}, bf16[128,1024]{1,0:T(8,128)(2,1)S(1)}, u32[]{:S(2)}, u32[]{:S(2)}) collective-permute-start(bf16[128,1024]{1,0:T(8,128)(2,1)S(1)} %get-tuple-element.182.refs_0_), channel_id=1, source_target_pairs={{0,2},{2,0},{1,3},{3,1},{4,6},{6,4},{5,7},{7,5},{8,10},{10,8},{9,1... | collective-permute-start | bytes 786440 | tf_op jit(solution)/shard_map/ppermute | solution.py:495
  214.8 13.8 %collective-permute-start.48 = (bf16[128,1024]{1,0:T(8,128)(2,1)S(1)}, bf16[128,1024]{1,0:T(8,128)(2,1)S(1)}, u32[]{:S(2)}, u32[]{:S(2)}) collective-permute-start(bf16[128,1024]{1,0:T(8,128)(2,1)S(1)} %get-tuple-element.182.refs_0_), channel_id=1, source_target_pairs={{0,3},{1,2},{2,1},{3,0},{4,7},{5,6},{6,5},{7,4},{8,11},{9,10},{10,... | collective-permute-start | bytes 786440 | tf_op jit(solution)/shard_map/ppermute | solution.py:585
  216.2 12.4 %collective-permute-start.49 = (bf16[128,1024]{1,0:T(8,128)(2,1)S(1)}, bf16[128,1024]{1,0:T(8,128)(2,1)S(1)}, u32[]{:S(2)}, u32[]{:S(2)}) collective-permute-start(bf16[128,1024]{1,0:T(8,128)(2,1)S(1)} %get-tuple-element.182.refs_0_), channel_id=1, source_target_pairs={{0,16},{16,0},{1,17},{17,1},{2,18},{18,2},{3,19},{19,3},{4,20},{20... | collective-permute-start | bytes 786440 | tf_op jit(solution)/shard_map/ppermute | solution.py:495
  220.6 8.0 %collective-permute-start.50 = (bf16[128,1024]{1,0:T(8,128)(2,1)S(1)}, bf16[128,1024]{1,0:T(8,128)(2,1)S(1)}, u32[]{:S(2)}, u32[]{:S(2)}) collective-permute-start(bf16[128,1024]{1,0:T(8,128)(2,1)S(1)} %collective-permute-done.46.refs_1_), channel_id=1, source_target_pairs={{0,16},{16,0},{1,17},{17,1},{2,18},{18,2},{3,19},{19,3},{4,20},{20... | collective-permute-start | bytes 786440 | tf_op jit(solution)/shard_map/ppermute | solution.py:495
  243.7 9.2 %collective-permute-start.54 = (bf16[128,1024]{1,0:T(8,128)(2,1)S(1)}, bf16[128,1024]{1,0:T(8,128)(2,1)S(1)}, u32[]{:S(2)}, u32[]{:S(2)}) collective-permute-start(bf16[128,1024]{1,0:T(8,128)(2,1)S(1)} %get-tuple-element.187), channel_id=1, source_target_pairs={{0,1},{1,0},{2,3},{3,2},{4,5},{5,4},{6,7},{7,6},{8,9},{9,8},{10,11... | collective-permute-start | bytes 786440 | tf_op jit(solution)/shard_map/ppermute | solution.py:495
  245.0 13.8 %collective-permute-start.55 = (bf16[128,1024]{1,0:T(8,128)(2,1)S(1)}, bf16[128,1024]{1,0:T(8,128)(2,1)S(1)}, u32[]{:S(2)}, u32[]{:S(2)}) collective-permute-start(bf16[128,1024]{1,0:T(8,128)(2,1)S(1)} %get-tuple-element.188), channel_id=1, source_target_pairs={{0,2},{2,0},{1,3},{3,1},{4,6},{6,4},{5,7},{7,5},{8,10},{10,8},{9,1... | collective-permute-start | bytes 786440 | tf_op jit(solution)/shard_map/ppermute | solution.py:495
  246.4 12.4 %collective-permute-start.56 = (bf16[128,1024]{1,0:T(8,128)(2,1)S(1)}, bf16[128,1024]{1,0:T(8,128)(2,1)S(1)}, u32[]{:S(2)}, u32[]{:S(2)}) collective-permute-start(bf16[128,1024]{1,0:T(8,128)(2,1)S(1)} %get-tuple-element.189), channel_id=1, source_target_pairs={{0,3},{1,2},{2,1},{3,0},{4,7},{5,6},{6,5},{7,4},{8,11},{9,10},{10,... | collective-permute-start | bytes 786440 | tf_op jit(solution)/shard_map/ppermute | solution.py:585
  260.2 19.5 %all-to-all-start.1 = ((bf16[16,96,128]{2,1,0:T(8,128)(2,1)}), bf16[16,96,128]{2,1,0:T(8,128)(2,1)S(1)}, u32[]{:S(2)}, u32[]{:S(2)}) async-start(bf16[16,96,128]{2,1,0:T(8,128)(2,1)} %get-tuple-element.203), calls=%async_computation.1 | async-start | bytes 786432 | tf_op jit(solution)/shard_map/all_to_all | solution.py:1635
  264.0 15.8 %collective-permute-start.57 = (bf16[64,1024]{1,0:T(8,128)(2,1)S(1)}, bf16[64,1024]{1,0:T(8,128)(2,1)S(1)}, u32[]{:S(2)}, u32[]{:S(2)}) collective-permute-start(bf16[64,1024]{1,0:T(8,128)(2,1)S(1)} %get-tuple-element.253), channel_id=1, source_target_pairs={{4,0},{0,4},{20,8},{16,12},{12,16},{8,20},{28,24},{24,28},{5,1},{1... | collective-permute-start | bytes 393224 | tf_op jit(solution)/shard_map/ppermute | solution.py:545
  265.9 19.0 %collective-permute-start.58 = (bf16[64,1024]{1,0:T(8,128)(2,1)S(1)}, bf16[64,1024]{1,0:T(8,128)(2,1)S(1)}, u32[]{:S(2)}, u32[]{:S(2)}) collective-permute-start(bf16[64,1024]{1,0:T(8,128)(2,1)S(1)} %get-tuple-element.252), channel_id=1, source_target_pairs={{0,0},{4,4},{16,8},{20,12},{8,16},{12,20},{24,24},{28,28},{1,1},{5... | collective-permute-start | bytes 393224 | tf_op jit(solution)/shard_map/ppermute | solution.py:545
  267.4 31.6 %collective-permute-start.60 = (bf16[128,1024]{1,0:T(8,128)(2,1)S(1)}, bf16[128,1024]{1,0:T(8,128)(2,1)S(1)}, u32[]{:S(2)}, u32[]{:S(2)}) collective-permute-start(bf16[128,1024]{1,0:T(8,128)(2,1)S(1)} %get-tuple-element.205), channel_id=1, source_target_pairs={{0,0},{6,1},{3,2},{21,3},{18,4},{4,5},{1,6},{7,7},{16,8},{22,9},{1... | collective-permute-start | bytes 786440 | tf_op jit(solution)/shard_map/ppermute | solution.py:1813
  268.1 40.5 %collective-permute-start.62 = (bf16[128,1024]{1,0:T(8,128)(2,1)S(1)}, bf16[128,1024]{1,0:T(8,128)(2,1)S(1)}, u32[]{:S(2)}, u32[]{:S(2)}) collective-permute-start(bf16[128,1024]{1,0:T(8,128)(2,1)S(1)} %get-tuple-element.207), channel_id=1, source_target_pairs={{4,0},{2,1},{7,2},{17,3},{22,4},{0,5},{5,6},{3,7},{20,8},{18,9},{2... | collective-permute-start | bytes 786440 | tf_op jit(solution)/shard_map/ppermute | solution.py:1813
  277.7 14.5 %collective-permute-start.61 = (bf16[64,1024]{1,0:T(8,128)(2,1)S(1)}, bf16[64,1024]{1,0:T(8,128)(2,1)S(1)}, u32[]{:S(2)}, u32[]{:S(2)}) collective-permute-start(bf16[64,1024]{1,0:T(8,128)(2,1)S(1)} %get-tuple-element.206), channel_id=1, source_target_pairs={{1,0},{5,1},{16,2},{20,3},{19,4},{23,5},{2,6},{6,7},{17,8},{21,9},... | collective-permute-start | bytes 393224 | tf_op jit(solution)/shard_map/ppermute | solution.py:1813
  279.8 17.8 %collective-permute-start.63 = (bf16[64,1024]{1,0:T(8,128)(2,1)S(1)}, bf16[64,1024]{1,0:T(8,128)(2,1)S(1)}, u32[]{:S(2)}, u32[]{:S(2)}) collective-permute-start(bf16[64,1024]{1,0:T(8,128)(2,1)S(1)} %get-tuple-element.208), channel_id=1, source_target_pairs={{5,0},{1,1},{20,2},{16,3},{23,4},{19,5},{6,6},{2,7},{21,8},{17,9},... | collective-permute-start | bytes 393224 | tf_op jit(solution)/shard_map/ppermute | solution.py:1813
  288.4 10.6 %collective-permute-start.64 = (bf16[64,1280]{1,0:T(8,128)(2,1)S(1)}, bf16[64,1280]{1,0:T(8,128)(2,1)S(1)}, u32[]{:S(2)}, u32[]{:S(2)}) collective-permute-start(bf16[64,1280]{1,0:T(8,128)(2,1)S(1)} %get-tuple-element.210), channel_id=1, source_target_pairs={{0,1},{1,0},{2,3},{3,2},{4,5},{5,4},{6,7},{7,6},{8,9},{9,8},{10,11... | collective-permute-start | bytes 491528 | tf_op jit(solution)/shard_map/ppermute | solution.py:495
  292.2 12.9 %collective-permute-start.65 = (bf16[64,1280]{1,0:T(8,128)(2,1)S(1)}, bf16[64,1280]{1,0:T(8,128)(2,1)S(1)}, u32[]{:S(2)}, u32[]{:S(2)}) collective-permute-start(bf16[64,1280]{1,0:T(8,128)(2,1)S(1)} %get-tuple-element.211), channel_id=1, source_target_pairs={{0,2},{2,0},{1,3},{3,1},{4,6},{6,4},{5,7},{7,5},{8,10},{10,8},{9,1... | collective-permute-start | bytes 491528 | tf_op jit(solution)/shard_map/ppermute | solution.py:495
  297.6 8.6 %collective-permute-start.66 = (bf16[64,1280]{1,0:T(8,128)(2,1)S(1)}, bf16[64,1280]{1,0:T(8,128)(2,1)S(1)}, u32[]{:S(2)}, u32[]{:S(2)}) collective-permute-start(bf16[64,1280]{1,0:T(8,128)(2,1)S(1)} %get-tuple-element.212), channel_id=1, source_target_pairs={{0,3},{1,2},{2,1},{3,0},{4,7},{5,6},{6,5},{7,4},{8,11},{9,10},{10,... | collective-permute-start | bytes 491528 | tf_op jit(solution)/shard_map/ppermute | solution.py:585
  299.0 10.3 %collective-permute-start.69 = (bf16[64,1280]{1,0:T(8,128)(2,1)S(1)}, bf16[64,1280]{1,0:T(8,128)(2,1)S(1)}, u32[]{:S(2)}, u32[]{:S(2)}) collective-permute-start(bf16[64,1280]{1,0:T(8,128)(2,1)S(1)} %get-tuple-element.219.refs_0_), channel_id=1, source_target_pairs={{0,16},{16,0},{1,17},{17,1},{2,18},{18,2},{3,19},{19,3},{4,20},{20... | collective-permute-start | bytes 491528 | tf_op jit(solution)/shard_map/ppermute | solution.py:495
  299.0 10.4 %collective-permute-start.70 = (bf16[64,1280]{1,0:T(8,128)(2,1)S(1)}, bf16[64,1280]{1,0:T(8,128)(2,1)S(1)}, u32[]{:S(2)}, u32[]{:S(2)}) collective-permute-start(bf16[64,1280]{1,0:T(8,128)(2,1)S(1)} %collective-permute-done.64.refs_1_), channel_id=1, source_target_pairs={{0,16},{16,0},{1,17},{17,1},{2,18},{18,2},{3,19},{19,3},{4,20},{20... | collective-permute-start | bytes 491528 | tf_op jit(solution)/shard_map/ppermute | solution.py:495
  305.1 4.3 %collective-permute-start.71 = (bf16[64,1280]{1,0:T(8,128)(2,1)S(1)}, bf16[64,1280]{1,0:T(8,128)(2,1)S(1)}, u32[]{:S(2)}, u32[]{:S(2)}) collective-permute-start(bf16[64,1280]{1,0:T(8,128)(2,1)S(1)} %collective-permute-done.65.refs_2_), channel_id=1, source_target_pairs={{0,16},{16,0},{1,17},{17,1},{2,18},{18,2},{3,19},{19,3},{4,20},{20... | collective-permute-start | bytes 491528 | tf_op jit(solution)/shard_map/ppermute | solution.py:495
  308.6 3.4 %collective-permute-start.68 = (f32[128,1024]{1,0:T(8,128)S(1)}, f32[128,1024]{1,0:T(8,128)S(1)}, u32[]{:S(2)}, u32[]{:S(2)}) collective-permute-start(f32[128,1024]{1,0:T(8,128)S(1)} %get-tuple-element.218), channel_id=1, source_target_pairs={{0,16},{16,0},{1,17},{17,1},{2,18},{18,2},{3,19},{19,3},{4,20},{20... | collective-permute-start | bytes 1572872 | tf_op jit(solution)/shard_map/ppermute | solution.py:495
  309.3 4.3 %collective-permute-start.67 = (f32[192,1024]{1,0:T(8,128)S(1)}, f32[192,1024]{1,0:T(8,128)}, u32[]{:S(2)}, u32[]{:S(2)}) collective-permute-start(f32[192,1024]{1,0:T(8,128)S(1)} %shard_map.260), channel_id=1, source_target_pairs={{0,16},{16,0},{1,17},{17,1},{2,18},{18,2},{3,19},{19,3},{4,20},{20... | collective-permute-start | bytes 2359304 | tf_op jit(solution)/shard_map/ppermute | solution.py:495
  (67 other events, 497.1 us)
Sparse Core Ops, SparseCore 0:
  11.4 69.8 all-gather.2
  83.4 45.1 all-gather.4
  196.2 68.1 reduce-scatter.1

commit v3 on v2

--- a/solution.py
+++ b/solution.py
@@ -1378,7 +1378,9 @@
     sample = latent[:, :lat] + spread
     sample_low = to_low(sample)
     sample_ref[...] = sample_low
-    out_ref[...] = fed + halves_nt(sample_low, own_ref, other_ref, DEC_LANES) + vec_ref[8:9]
+    out_ref[...] = to_low(
+        fed + halves_nt(sample_low, own_ref, other_ref, DEC_LANES) + vec_ref[8:9]
+    )
     cot = cot_ref[...]
     dsample = core_order(
         product(cot, own_ref[:, DEC_LANES]), product(cot, other_ref[:, DEC_LANES])
@@ -1449,7 +1451,7 @@
         bottle_body,
         (attended, *parts, vec, *weights, noise, cot, means, logvars),
         [
-            wide_shape(rows, width),
+            low_shape(rows, width),
             low_shape(rows, width),
             low_shape(rows, lat),
             low_shape(rows, width),
@@ -1524,14 +1526,16 @@
 
 
 def last_grad_body(*refs):
-    out_ref, wholes = refs[8], refs[9:]
+    out_ref, lat_ref, dec_ref = refs[8:]
     half = out_ref.shape[1] // 8
     for i, ref in enumerate(refs[:8]):
         for block in range(4):
             place = chunk_place(block, NEAR[i % 4], i // 4)
             out_ref[:, pl.ds(place, 128)] = wide(ref[:, block * 128 : (block + 1) * 128])
-    for core in range(2):
-        wholes[core][...] = z_sum([ref.at[:, half:] for ref in refs[core * 4 : core * 4 + 4]])
+    for i in range(2):
+        total = z_sum([ref.at[:, half:] for ref in refs[i * 4 : i * 4 + 4]])
+        lat_ref[:, core_lanes(i, lat_ref.shape[1] // 2)] = total[:, LAT_LANES]
+        dec_ref[:, core_lanes(i, dec_ref.shape[1] // 2)] = total[:, DEC_LANES]
 
 
 def cells_back_body(
@@ -1557,7 +1561,7 @@
 ):
     grad = z_sum((keep_ref, came_x_ref, came_y_ref, came_far_ref))
     unit, scale = row_stats(wide(hidden_ref[...]))
-    grad_ref[...] = datt_ref[...] + norm_back(grad, unit, scale, vec_ref[0:1])
+    grad_ref[...] = to_low(datt_ref[...] + norm_back(grad, unit, scale, vec_ref[0:1]))
     width = grad.shape[1]
     count = packed_ref.shape[0]
     inner_ref[...] = jnp.zeros_like(inner_ref)
@@ -1613,12 +1617,31 @@
     out_ref[rows:, :PAIR] = small + rest
 
 
-def last_body(own_ref, other_ref, grad_ref, small_ref):
-    rows, half = grad_ref.shape[0], own_ref.shape[1]
-    for ref, place in ((own_ref, 0), (other_ref, 1)):
-        core = flip(lax.axis_index("grp"), place)
-        grad_ref[:, pl.ds(pl.multiple_of(core * half, half), half)] = ref[:rows]
-    small_ref[...] = own_ref[rows:, :PAIR] + other_ref[rows:, :PAIR]
+def core_lanes(core_step, width):
+    core = flip(lax.axis_index("grp"), core_step)
+    return pl.ds(pl.multiple_of(core * width, width), width)
+
+
+def last_body(own_ref, other_ref, grad_ref, vec_ref, inner_ref, means_ref, logvars_ref, kl_ref):
+    rows = grad_ref.shape[0]
+    for i, ref in enumerate((own_ref, other_ref)):
+        grad_ref[:, core_lanes(i, own_ref.shape[1])] = ref[:rows]
+    small = own_ref[rows:, :PAIR] + other_ref[rows:, :PAIR]
+    part = vec_ref.shape[1]
+    vec_ref[...] = small[:9, :part]
+    pieces = inner_ref.shape[1] // part
+    inner_ref[...] = jnp.concatenate(
+        [small[9 + i : 10 + i, :part] for i in range(pieces)], axis=1
+    )
+    lat = means_ref.shape[1]
+    means_ref[...] = small[:, part : part + lat]
+    logvars_ref[...] = small[:, part + lat :]
+    kl_ref[...] = small[14:15, :1]
+
+
+def in_grad_body(own_ref, other_ref, out_ref):
+    for i, ref in enumerate((own_ref, other_ref)):
+        out_ref[:, core_lanes(i, ref.shape[0])] = ref[...].T
 
 
 def cells_back(operands, inner):
@@ -1626,7 +1649,7 @@
     return whole_call(
         cells_back_body,
         operands,
-        [wide_shape(rows, width), low_shape(16, width // 16 + 2 * SMALL, PAIR)],
+        [low_shape(rows, width), low_shape(16, width // 16 + 2 * SMALL, PAIR)],
         [pltpu.VMEM((1, inner), jnp.float32), pltpu.VMEM((SMALL, width), jnp.float32)],
     )
 
@@ -1758,7 +1781,7 @@
     )
 
     rows_fed = plane_rows(dfed_low)
-    layer_out = from_slides(after(to_low(output), rows_fed).reshape(slots, span, width))
+    layer_out = from_slides(after(output, rows_fed).reshape(slots, span, width))
     whole_grad = whole_grads((dlat_low, fed_low, cot, sample_low))
     du_far, ff_far, norm_far = feed_back(rows_fed[4:], pair_w, slope_far)
     du, ff_sums, keep, *sends = feed_back(
@@ -1793,7 +1816,7 @@
         ),
         inner,
     )
-    grad_cells = wide(from_slides(to_low(grad_rows).reshape(slots, span, width)))
+    grad_cells = from_slides(grad_rows.reshape(slots, span, width))
     sum_in, *sums = whole_call(
         split_grad_body,
         (after(grads_sum, packed),),
@@ -1803,12 +1826,24 @@
     sums += [other_core(total) for total in sums]
 
     (last,) = whole_call(
-        last_sum_body, (exchange(packed, CHIPS),), [wide_shape(part + SMALL, 4 * PAIR)]
-    )
-    grad_out_w, small_sums = whole_call(
-        last_body, (last, other_core(last)), [wide_shape(part, width), wide_shape(SMALL, PAIR)]
-    )
-    grad_out_w = grad_out_w.T
+        last_sum_body,
+        (after(exchange(packed, CHIPS), (sums[1:4], grad_cells)),),
+        [wide_shape(part + SMALL, 4 * PAIR)],
+    )
+    grad_out_w, vec_out, inner_out, means_out, logvars_out, kl_sum = whole_call(
+        last_body,
+        (last, other_core(last)),
+        [
+            wide_shape(part, width),
+            wide_shape(9, part),
+            wide_shape(1, inner // 16),
+            wide_shape(comps, lat // 16),
+            wide_shape(comps, lat // 16),
+            wide_shape(1, 1),
+        ],
+    )
+    kl_mean = kl_sum[0, 0] / (32 * rows)
+
     homes = [
         lax.ppermute(grad, EVERY, [(there, here) for here, there in head_routes(single, k)])
         for grad, (single, k) in zip(homes, ARRIVALS)
@@ -1817,33 +1852,25 @@
         home_body, after(homes, (packed, sums[1:4])), [wide_shape(3 * HEAD_DIM, width)]
     )
     grad_qkv = (home + other_core(home)).T
-    vec_out = small_sums[:9, :part]
-    inner_out = small_sums[9 : 9 + inner // width, :part].reshape(1, -1)
-    means_out = small_sums[:, part : part + lat // 16]
-    logvars_out = small_sums[:, part + lat // 16 :]
-    kl_mean = small_sums[14, 0] / (32 * rows)
-
-    grad_in_w = ordered(sum_in.T, other_core(sum_in).T, "grp", 1)
-    grad_back_w, whole_own, whole_other = whole_call(
+
+    (grad_in_w,) = whole_call(
+        in_grad_body, (sum_in, other_core(sum_in)), [wide_shape(width, ff // 16)]
+    )
+    grad_back_w, grad_lat_w, grad_dec_w = whole_call(
         last_grad_body,
-        sums,
-        [wide_shape(part, ff)] + [wide_shape(part, shard_width)] * 2,
-    )
-    grad_back_w = grad_back_w.T
-    grad_lat_w, grad_dec_w = (
-        ordered(whole_own[:, lanes].T, whole_other[:, lanes].T, "grp", 0)
-        for lanes in (LAT_LANES, DEC_LANES)
+        after(sums, grad_in_w),
+        [wide_shape(part, ff), wide_shape(part, width), wide_shape(part, lat)],
     )
     return (
         wide(layer_out).reshape(1, slots, span, width),
-        grad_cells.reshape(1, slots, span, width),
+        wide(grad_cells).reshape(1, slots, span, width),
         kl_mean,
         grad_qkv[None],
-        grad_out_w[None],
+        grad_out_w.T[None],
         grad_in_w[None],
-        grad_back_w[None],
-        grad_lat_w[None],
-        grad_dec_w[None],
+        grad_back_w.T[None],
+        grad_lat_w.T[None],
+        grad_dec_w.T[None],
         vec_out[None],
         inner_out,
         means_out[None],

time: 327 us -> 322 us (0.985)
  starting transfers between devices: 102 us -> 94.6 us
    ppermute x4, waiting for transfers between devices: 0.01 us -> 7.49 us  [fast_device(): lax.ppermute(grad, EVERY, [(there, here) for here, there in head_routes(s...]
    ppermute x4, starting transfers between devices: 17.4 us -> 10.5 us  [fast_device(): lax.ppermute(grad, EVERY, [(there, here) for here, there in head_routes(s...]
    ppermute x49, waiting for transfers between devices: 108 us -> 102 us  [hop(): return lax.ppermute(values, axis, [(i, i ^ step) for i in range(size)])]
    pallas_call x25 -> x26, Pallas kernels: 53.8 us -> 55.2 us  [whole_call(): pl.pallas_call(run, out_shape=out_shapes, in_specs=[hbm if i in left_out...]
    unnamed x114 -> x121, local copies, waits for them, and re-layouts: 13.3 us -> 14.6 us
  transfers between devices with their start and end apart: 78 -> 78, of which waited for: 35 -> 34; matrix products, arithmetic and copies ran while one was open for 4% -> 3% of each run, Pallas kernels for 11% -> 11%
where the time goes in v3:
time: 322 us; the launch traced here: 318 us
  waiting for transfers between devices  123 us (38%)
  starting transfers between devices  94.6 us (29%)
  Pallas kernels  55.2 us (17%)
  local copies, waits for them, and re-layouts  18.9 us (6%)
  between operations  16.6 us (5%)
  other arithmetic  9.8 us (3%)
    ppermute x49, waiting for transfers between devices, hop(): return lax.ppermute(values, axis, [(i, i ^ step) for i in range(size)])  102 us
    pallas_call x26, Pallas kernels, whole_call(): pl.pallas_call(run, out_shape=out_shapes, in_specs=[hbm if i in left_out...  55.2 us
    ppermute x49, starting transfers between devices, hop(): return lax.ppermute(values, axis, [(i, i ^ step) for i in range(size)])  44.3 us
    unnamed x121, local copies, waits for them, and re-layouts  14.6 us
    all_to_all x2, starting transfers between devices, exchange(): return lax.all_to_all(blocks, axes, split_axis=0, concat_axis=0, tiled=True)  11.9 us
    ppermute x4, starting transfers between devices, fast_device(): lax.ppermute(grad, EVERY, [(there, here) for here, there in head_routes(s...  10.5 us
    ppermute x4, starting transfers between devices, fast_device(): lax.ppermute(head_parts[int(single)], EVERY, head_routes(single, k))  9.73 us
    ppermute x4, waiting for transfers between devices, fast_device(): lax.ppermute(grad, EVERY, [(there, here) for here, there in head_routes(s...  7.49 us
  transfers between devices with their start and end apart: 78, of which 34 were waited for; matrix products, arithmetic and copies ran while one was open for 3% of the time, Pallas kernels for 11%

profile of v3, /device:TPU:0, one launch (start us, length us, event | category | flops | bytes accessed | tf_op | source)
XLA Modules:
  0.0 318.0 jit_solution(5328289636875272943)
XLA Ops:
  12.4 8.3 %all-to-all-start = ((bf16[16,64,128]{2,1,0:T(8,128)(2,1)}), bf16[16,64,128]{2,1,0:T(8,128)(2,1)S(1)}, u32[]{:S(2)}, u32[]{:S(2)}) async-start(bf16[16,64,128]{2,1,0:T(8,128)(2,1)} %get-tuple-element.133), calls=%async_computation | async-start | bytes 524288 | tf_op jit(solution)/shard_map/all_to_all | solution.py:1658
  21.7 2.0 collective-permute-start.1
  24.5 3.6 %collective-permute-start.4 = (bf16[128,1024]{1,0:T(8,128)(2,1)}, bf16[128,1024]{1,0:T(8,128)(2,1)}, u32[]{:S(2)}, u32[]{:S(2)}) collective-permute-start(bf16[128,1024]{1,0:T(8,128)(2,1)} %dynamic-slice_bitcast_fusion), channel_id=1, source_target_pairs={{0,0},{1,6},{2,3},{3,21},{4,18},{5,4},{6,1},{7,7},{8,16},{9,22},{1... | collective-permute-start | bytes 786440 | tf_op jit(solution)/shard_map/ppermute | solution.py:1726
  31.1 3.0 collective-permute-start.3
  34.2 6.4 %collective-permute-done.3 = bf16[80,1024]{1,0:T(8,128)(2,1)S(1)} collective-permute-done((bf16[80,1024]{1,0:T(8,128)(2,1)S(1)}, bf16[80,1024]{1,0:T(8,128)(2,1)S(1)}, u32[]{:S(2)}, u32[]{:S(2)}) %collective-permute-start.3) | collective-permute-done | bytes 163872 | tf_op jit(solution)/shard_map/ppermute | solution.py:495
  42.2 6.0 %collective-permute-done.5.refs_3_ = bf16[64,1024]{1,0:T(8,128)(2,1)S(1)} collective-permute-done((bf16[64,1024]{1,0:T(8,128)(2,1)S(1)}, bf16[64,1024]{1,0:T(8,128)(2,1)S(1)}, u32[]{:S(2)}, u32[]{:S(2)}) %collective-permute-start.5) | collective-permute-done | bytes 131104 | tf_op jit(solution)/shard_map/ppermute | solution.py:1726
  48.9 2.4 collective-permute-start.7
  52.3 3.8 %collective-permute-start.9 = (bf16[64,1024]{1,0:T(8,128)(2,1)}, bf16[64,1024]{1,0:T(8,128)(2,1)S(1)}, u32[]{:S(2)}, u32[]{:S(2)}) collective-permute-start(bf16[64,1024]{1,0:T(8,128)(2,1)} %copy-done.48), channel_id=1, source_target_pairs={{0,5},{1,1},{2,20},{3,16},{4,23},{5,19},{6,6},{7,2},{8,21},{9,17},... | collective-permute-start | bytes 393224 | tf_op jit(solution)/shard_map/ppermute | solution.py:1726
  56.1 13.2 %collective-permute-done.6 = bf16[160,1024]{1,0:T(8,128)(2,1)S(1)} collective-permute-done((bf16[160,1024]{1,0:T(8,128)(2,1)}, bf16[160,1024]{1,0:T(8,128)(2,1)S(1)}, u32[]{:S(2)}, u32[]{:S(2)}) %collective-permute-start.6) | collective-permute-done | bytes 327712 | tf_op jit(solution)/shard_map/ppermute | solution.py:495
  73.9 11.0 %shard_map.240 = (f32[16,1024]{1,0:T(8,128)S(1)}, f32[16,512]{1,0:T(8,128)S(1)}, f32[16,512]{1,0:T(8,128)S(1)}, bf16[1024,1024]{1,0:T(8,128)(2,1)S(1)}, bf16[102...) custom-call(bf16[4,2,80,1024]{3,2,1,0:T(8,128)(2,1)S(1)} %bitcast.89, ...), custom_call_target="tpu_custom_call" | custom-call | flops 11000000512 | tf_op jit(solution)/shard_map/pallas_call | solution.py:676
  88.3 2.5 collective-permute-done.11.refs_2_
  91.3 6.0 %collective-permute-start.12 = (bf16[128,1024]{1,0:T(8,128)(2,1)S(1)}, bf16[128,1024]{1,0:T(8,128)(2,1)S(1)}, u32[]{:S(2)}, u32[]{:S(2)}) collective-permute-start(bf16[128,1024]{1,0:T(8,128)(2,1)S(1)} %get-tuple-element.154), channel_id=1, source_target_pairs={{0,1},{1,0},{2,3},{3,2},{4,5},{5,4},{6,7},{7,6},{8,9},{9,8},{10,11... | collective-permute-start | bytes 786440 | tf_op jit(solution)/shard_map/ppermute | solution.py:495
  97.3 1.9 collective-permute-start.13
  99.2 1.4 collective-permute-start.14
  100.6 3.8 %collective-permute-done.12.refs_1_ = bf16[128,1024]{1,0:T(8,128)(2,1)S(1)} collective-permute-done((bf16[128,1024]{1,0:T(8,128)(2,1)S(1)}, bf16[128,1024]{1,0:T(8,128)(2,1)S(1)}, u32[]{:S(2)}, u32[]{:S(2)}) %collective-permute-start.12) | collective-permute-done | bytes 262176 | tf_op jit(solution)/shard_map/ppermute | solution.py:495
  104.4 6.3 %collective-permute-done.13.refs_2_ = bf16[128,1024]{1,0:T(8,128)(2,1)S(1)} collective-permute-done((bf16[128,1024]{1,0:T(8,128)(2,1)S(1)}, bf16[128,1024]{1,0:T(8,128)(2,1)S(1)}, u32[]{:S(2)}, u32[]{:S(2)}) %collective-permute-start.13) | collective-permute-done | bytes 262176 | tf_op jit(solution)/shard_map/ppermute | solution.py:495
  110.7 1.8 collective-permute-done.14.refs_3_
  114.9 1.7 collective-permute-start.16
  117.8 5.8 %collective-permute-done.15.refs_1_.refs_9_ = bf16[128,1024]{1,0:T(8,128)(2,1)S(1)} collective-permute-done((bf16[128,1024]{1,0:T(8,128)(2,1)S(1)}, bf16[128,1024]{1,0:T(8,128)(2,1)S(1)}, u32[]{:S(2)}, u32[]{:S(2)}) %collective-permute-start.15) | collective-permute-done | bytes 262176 | tf_op jit(solution)/shard_map/ppermute | solution.py:495
  123.6 4.4 %collective-permute-done.16.refs_2_.refs_10_ = bf16[128,1024]{1,0:T(8,128)(2,1)S(1)} collective-permute-done((bf16[128,1024]{1,0:T(8,128)(2,1)S(1)}, bf16[128,1024]{1,0:T(8,128)(2,1)S(1)}, u32[]{:S(2)}, u32[]{:S(2)}) %collective-permute-start.16) | collective-permute-done | bytes 262176 | tf_op jit(solution)/shard_map/ppermute | solution.py:495
  130.0 4.8 %shard_map.244 = (bf16[512,512]{1,0:T(8,128)(2,1)S(1)}, f32[512,512]{1,0:T(8,128)S(1)}, bf16[512,1024]{1,0:T(8,128)(2,1)}) custom-call(bf16[128,1024]{1,0:T(8,128)(2,1)} %copy-done.52, bf16[128,1024]{1,0:T(8,128)(2,1)} %copy-done.53, bf16[128,1024]{1,0:T(8,128)(2,1)} %collective-permute-done.20.refs_2_.refs_14_, ...), custom_call_target="tpu_custom_call" | custom-call | flops 3849999872 | tf_op jit(solution)/shard_map/pallas_call | solution.py:676
  139.8 3.8 %shard_map.245 = (bf16[512,512]{1,0:T(8,128)(2,1)S(1)}, f32[512,512]{1,0:T(8,128)S(1)}, f32[128,1024]{1,0:T(8,128)S(1)}, bf16[128,1024]{1,0:T(8,128)(2,1)S(1)}, ...) custom-call(bf16[128,1024]{1,0:T(8,128)(2,1)} %copy-done.7, bf16[128,1024]{1,0:T(8,128)(2,1)} %copy-done.49, ...), custom_call_target="tpu_custom_call" | custom-call | flops 3849999872 | tf_op jit(solution)/shard_map/pallas_call | solution.py:676
  143.6 1.5 collective-permute-start.23
  145.1 2.0 collective-permute-start.24
  147.3 3.0 collective-permute-done.23.refs_2_
  150.3 8.1 %collective-permute-done.24.refs_3_ = bf16[128,1024]{1,0:T(8,128)(2,1)S(1)} collective-permute-done((bf16[128,1024]{1,0:T(8,128)(2,1)S(1)}, bf16[128,1024]{1,0:T(8,128)(2,1)S(1)}, u32[]{:S(2)}, u32[]{:S(2)}) %collective-permute-start.24) | collective-permute-done | bytes 262176 | tf_op jit(solution)/shard_map/ppermute | solution.py:495
  158.5 5.7 %shard_map.246 = (bf16[128,1024]{1,0:T(8,128)(2,1)S(1)}, bf16[128,1024]{1,0:T(8,128)(2,1)S(1)}, bf16[128,512]{1,0:T(8,128)(2,1)S(1)}, bf16[128,1024]{1,0:T(8,128...) custom-call(f32[128,1024]{1,0:T(8,128)S(1)} %copy-done.23, ...), custom_call_target="tpu_custom_call" | custom-call | flops 6270000128 | tf_op jit(solution)/shard_map/pallas_call | solution.py:676
  165.4 1.5 collective-permute-start.30
  166.9 1.4 collective-permute-start.31
  168.4 4.7 %collective-permute-done.29.refs_1_ = bf16[128,1024]{1,0:T(8,128)(2,1)S(1)} collective-permute-done((bf16[128,1024]{1,0:T(8,128)(2,1)S(1)}, bf16[128,1024]{1,0:T(8,128)(2,1)S(1)}, u32[]{:S(2)}, u32[]{:S(2)}) %collective-permute-start.29) | collective-permute-done | bytes 262176 | tf_op jit(solution)/shard_map/ppermute | solution.py:495
  173.8 5.2 %collective-permute-done.30.refs_2_ = bf16[128,1024]{1,0:T(8,128)(2,1)S(1)} collective-permute-done((bf16[128,1024]{1,0:T(8,128)(2,1)S(1)}, bf16[128,1024]{1,0:T(8,128)(2,1)S(1)}, u32[]{:S(2)}, u32[]{:S(2)}) %collective-permute-start.30) | collective-permute-done | bytes 262176 | tf_op jit(solution)/shard_map/ppermute | solution.py:495
  178.9 1.8 collective-permute-done.31.refs_3_
  180.8 1.5 collective-permute-done.35.refs_3_.refs_7_
  182.3 1.9 shard_map.247
  185.4 1.9 collective-permute-done.41.refs_5_
  188.9 1.9 shard_map.249
  190.8 5.2 %shard_map.250 = bf16[1792,1024]{1,0:T(8,128)(2,1)} custom-call(bf16[128,1024]{1,0:T(8,128)(2,1)S(1)} %get-tuple-element.169.refs_0_, bf16[128,1024]{1,0:T(8,128)(2,1)S(1)} %collective-permute-done.29.refs_1_, bf16[128,1024]{1,0:T(8,128)(2,1)S(1)} %collective-permute-done.30.refs_2_, bf16[128,1024]{1,0:T(8,128)(2,1)S(1)} %collective-permute-done.31.refs_3_, ...), custom_call_target="tpu_custom_call" | custom-call | flops 3740000000 | tf_op jit(solution)/shard_map/pallas_call | solution.py:676
  197.8 1.7 collective-permute-start.44
  201.9 2.8 collective-permute-done.43.refs_1_
  204.7 6.7 %collective-permute-done.44.refs_2_ = bf16[128,1024]{1,0:T(8,128)(2,1)S(1)} collective-permute-done((bf16[128,1024]{1,0:T(8,128)(2,1)S(1)}, bf16[128,1024]{1,0:T(8,128)(2,1)S(1)}, u32[]{:S(2)}, u32[]{:S(2)}) %collective-permute-start.44) | collective-permute-done | bytes 262176 | tf_op jit(solution)/shard_map/ppermute | solution.py:495
  212.0 1.9 collective-permute-start.46
  214.8 1.4 collective-permute-start.48
  216.5 4.1 %collective-permute-done.46.refs_1_ = bf16[128,1024]{1,0:T(8,128)(2,1)S(1)} collective-permute-done((bf16[128,1024]{1,0:T(8,128)(2,1)S(1)}, bf16[128,1024]{1,0:T(8,128)(2,1)S(1)}, u32[]{:S(2)}, u32[]{:S(2)}) %collective-permute-start.46) | collective-permute-done | bytes 262176 | tf_op jit(solution)/shard_map/ppermute | solution.py:495
  220.5 1.7 collective-permute-start.50
  222.3 4.4 %collective-permute-done.47.refs_2_ = bf16[128,1024]{1,0:T(8,128)(2,1)S(1)} collective-permute-done((bf16[128,1024]{1,0:T(8,128)(2,1)S(1)}, bf16[128,1024]{1,0:T(8,128)(2,1)S(1)}, u32[]{:S(2)}, u32[]{:S(2)}) %collective-permute-start.47) | collective-permute-done | bytes 262176 | tf_op jit(solution)/shard_map/ppermute | solution.py:495
  226.7 1.8 collective-permute-done.48.refs_3_
  228.6 1.5 collective-permute-done.52.refs_7_
  231.3 8.9 %shard_map.253 = (bf16[1024,384]{1,0:T(8,128)(2,1)S(1)}, bf16[512,1024]{1,0:T(8,128)(2,1)S(1)}) custom-call(bf16[1024,384]{1,0:T(8,128)(2,1)S(1)} %copy-done.35, f32[1,1024]{1,0:T(1,128)S(1)} %get-tuple-element.172.refs_1_, f32[1024,128]{1,0:T(8,128)S(1)} %copy-done.37, bf16[1024,128]{1,0:T(8,128)(2,1)S(1)} %bitcast.83, bf16[384,1024]{1,0:T(8,128)(2,1)S(1)} %copy-done.21, ...), custom_call_target="tpu_custom_call" | custom-call | flops 10119999488 | tf_op jit(solution)/shard_map/pallas_call | solution.py:676
  240.4 2.5 collective-permute-done.53.refs_2_
  244.9 1.4 collective-permute-start.55
  248.2 4.6 %collective-permute-done.54.refs_1_ = bf16[128,1024]{1,0:T(8,128)(2,1)S(1)} collective-permute-done((bf16[128,1024]{1,0:T(8,128)(2,1)S(1)}, bf16[128,1024]{1,0:T(8,128)(2,1)S(1)}, u32[]{:S(2)}, u32[]{:S(2)}) %collective-permute-start.54) | collective-permute-done | bytes 262176 | tf_op jit(solution)/shard_map/ppermute | solution.py:495
  252.8 5.8 %collective-permute-done.55.refs_2_ = bf16[128,1024]{1,0:T(8,128)(2,1)S(1)} collective-permute-done((bf16[128,1024]{1,0:T(8,128)(2,1)S(1)}, bf16[128,1024]{1,0:T(8,128)(2,1)S(1)}, u32[]{:S(2)}, u32[]{:S(2)}) %collective-permute-start.55) | collective-permute-done | bytes 262176 | tf_op jit(solution)/shard_map/ppermute | solution.py:495
  258.7 1.4 shard_map.256
  260.1 3.6 %all-to-all-start.1 = ((bf16[16,96,128]{2,1,0:T(8,128)(2,1)}), bf16[16,96,128]{2,1,0:T(8,128)(2,1)S(1)}, u32[]{:S(2)}, u32[]{:S(2)}) async-start(bf16[16,96,128]{2,1,0:T(8,128)(2,1)} %get-tuple-element.216), calls=%async_computation.1 | async-start | bytes 786432 | tf_op jit(solution)/shard_map/all_to_all | solution.py:1658
  263.6 3.7 %collective-permute-start.64 = (bf16[64,1024]{1,0:T(8,128)(2,1)S(1)}, bf16[64,1024]{1,0:T(8,128)(2,1)S(1)}, u32[]{:S(2)}, u32[]{:S(2)}) collective-permute-start(bf16[64,1024]{1,0:T(8,128)(2,1)S(1)} %get-tuple-element.224), channel_id=1, source_target_pairs={{1,0},{5,1},{16,2},{20,3},{19,4},{23,5},{2,6},{6,7},{17,8},{21,9},... | collective-permute-start | bytes 393224 | tf_op jit(solution)/shard_map/ppermute | solution.py:1848
  267.3 2.8 collective-permute-start.66
  270.8 3.3 %collective-permute-start.65 = (bf16[128,1024]{1,0:T(8,128)(2,1)S(1)}, bf16[128,1024]{1,0:T(8,128)(2,1)S(1)}, u32[]{:S(2)}, u32[]{:S(2)}) collective-permute-start(bf16[128,1024]{1,0:T(8,128)(2,1)S(1)} %get-tuple-element.225), channel_id=1, source_target_pairs={{4,0},{2,1},{7,2},{17,3},{22,4},{0,5},{5,6},{3,7},{20,8},{18,9},{2... | collective-permute-start | bytes 786440 | tf_op jit(solution)/shard_map/ppermute | solution.py:1848
  275.4 3.1 collective-permute-start.59
  278.5 7.5 %collective-permute-done.66.refs_3_ = bf16[64,1024]{1,0:T(8,128)(2,1)S(1)} collective-permute-done((bf16[64,1024]{1,0:T(8,128)(2,1)S(1)}, bf16[64,1024]{1,0:T(8,128)(2,1)S(1)}, u32[]{:S(2)}, u32[]{:S(2)}) %collective-permute-start.66) | collective-permute-done | bytes 131104 | tf_op jit(solution)/shard_map/ppermute | solution.py:1848
  286.8 3.0 collective-permute-start.57
  289.7 2.1 collective-permute-start.58
  291.9 3.8 %collective-permute-start.68 = (f32[128,1024]{1,0:T(8,128)S(1)}, f32[128,1024]{1,0:T(8,128)S(1)}, u32[]{:S(2)}, u32[]{:S(2)}) collective-permute-start(f32[128,1024]{1,0:T(8,128)S(1)} %get-tuple-element.232.refs_0_), channel_id=1, source_target_pairs={{0,16},{16,0},{1,17},{17,1},{2,18},{18,2},{3,19},{19,3},{4,20},{20... | collective-permute-start | bytes 1572872 | tf_op jit(solution)/shard_map/ppermute | solution.py:495
  301.4 1.4 collective-permute-start.69
  308.1 2.1 add_bitcast_fusion
  (271 shorter events, 61.4 us)
Async XLA Ops:
  7.2 81.1 %all-gather.3.cloned.1.call-start = ((), (), s32[]{:S(2)}) async-start(), calls=%async_computation.3 | async-start | bytes 1671168 | tf_op jit(solution)/shard_map/all_gather | solution.py:1693
  12.4 36.5 %all-to-all-start = ((bf16[16,64,128]{2,1,0:T(8,128)(2,1)}), bf16[16,64,128]{2,1,0:T(8,128)(2,1)S(1)}, u32[]{:S(2)}, u32[]{:S(2)}) async-start(bf16[16,64,128]{2,1,0:T(8,128)(2,1)} %get-tuple-element.133), calls=%async_computation | async-start | bytes 524288 | tf_op jit(solution)/shard_map/all_to_all | solution.py:1658
  20.7 108.0 %all-gather.5.cloned.1.call-start = ((), (), s32[]{:S(2)}) async-start(), calls=%async_computation.4 | async-start | bytes 2621440 | tf_op jit(solution)/shard_map/all_gather | solution.py:1757
  20.9 9.4 %collective-permute-start = (bf16[80,1024]{1,0:T(8,128)(2,1)S(1)}, bf16[80,1024]{1,0:T(8,128)(2,1)S(1)}, u32[]{:S(2)}, u32[]{:S(2)}) collective-permute-start(bf16[80,1024]{1,0:T(8,128)(2,1)S(1)} %get-tuple-element.135), channel_id=1, source_target_pairs={{0,0},{4,4},{8,16},{12,20},{16,8},{20,12},{24,24},{28,28},{1,1},{5... | collective-permute-start | bytes 491528 | tf_op jit(solution)/shard_map/ppermute | solution.py:1716
  21.7 9.4 %collective-permute-start.1 = (bf16[80,1024]{1,0:T(8,128)(2,1)S(1)}, bf16[80,1024]{1,0:T(8,128)(2,1)S(1)}, u32[]{:S(2)}, u32[]{:S(2)}) collective-permute-start(bf16[80,1024]{1,0:T(8,128)(2,1)S(1)} %get-tuple-element.136), channel_id=1, source_target_pairs={{0,4},{4,0},{8,20},{12,16},{16,12},{20,8},{24,28},{28,24},{1,5},{5... | collective-permute-start | bytes 491528 | tf_op jit(solution)/shard_map/ppermute | solution.py:1716
  24.5 24.4 %collective-permute-start.4 = (bf16[128,1024]{1,0:T(8,128)(2,1)}, bf16[128,1024]{1,0:T(8,128)(2,1)}, u32[]{:S(2)}, u32[]{:S(2)}) collective-permute-start(bf16[128,1024]{1,0:T(8,128)(2,1)} %dynamic-slice_bitcast_fusion), channel_id=1, source_target_pairs={{0,0},{1,6},{2,3},{3,21},{4,18},{5,4},{6,1},{7,7},{8,16},{9,22},{1... | collective-permute-start | bytes 786440 | tf_op jit(solution)/shard_map/ppermute | solution.py:1726
  28.1 20.1 %collective-permute-start.5 = (bf16[64,1024]{1,0:T(8,128)(2,1)S(1)}, bf16[64,1024]{1,0:T(8,128)(2,1)S(1)}, u32[]{:S(2)}, u32[]{:S(2)}) collective-permute-start(bf16[64,1024]{1,0:T(8,128)(2,1)S(1)} %dynamic-slice_bitcast_fusion.1), channel_id=1, source_target_pairs={{0,1},{1,5},{2,16},{3,20},{4,19},{5,23},{6,2},{7,6},{8,17},{9,21},... | collective-permute-start | bytes 393224 | tf_op jit(solution)/shard_map/ppermute | solution.py:1726
  30.3 11.0 %collective-permute-start.2 = (bf16[144,1024]{1,0:T(8,128)(2,1)S(1)}, bf16[144,1024]{1,0:T(8,128)(2,1)S(1)}, u32[]{:S(2)}, u32[]{:S(2)}) collective-permute-start(bf16[144,1024]{1,0:T(8,128)(2,1)S(1)} %pad_maximum_fusion.2), channel_id=1, source_target_pairs={{0,1},{1,0},{2,3},{3,2},{4,5},{5,4},{6,7},{7,6},{8,9},{9,8},{10,11... | collective-permute-start | bytes 884744 | tf_op jit(solution)/shard_map/ppermute | solution.py:495
  31.1 9.5 %collective-permute-start.3 = (bf16[80,1024]{1,0:T(8,128)(2,1)S(1)}, bf16[80,1024]{1,0:T(8,128)(2,1)S(1)}, u32[]{:S(2)}, u32[]{:S(2)}) collective-permute-start(bf16[80,1024]{1,0:T(8,128)(2,1)S(1)} %collective-permute-done.1), channel_id=1, source_target_pairs={{0,2},{2,0},{1,3},{3,1},{4,6},{6,4},{5,7},{7,5},{8,10},{10,8},{9,1... | collective-permute-start | bytes 491528 | tf_op jit(solution)/shard_map/ppermute | solution.py:495
  48.9 20.4 %collective-permute-start.6 = (bf16[160,1024]{1,0:T(8,128)(2,1)}, bf16[160,1024]{1,0:T(8,128)(2,1)S(1)}, u32[]{:S(2)}, u32[]{:S(2)}) collective-permute-start(bf16[160,1024]{1,0:T(8,128)(2,1)} %pad_maximum_fusion), channel_id=1, source_target_pairs={{0,1},{1,0},{2,3},{3,2},{4,5},{5,4},{6,7},{7,6},{8,9},{9,8},{10,11... | collective-permute-start | bytes 983048 | tf_op jit(solution)/shard_map/ppermute | solution.py:495
  48.9 20.4 %collective-permute-start.7 = (bf16[224,1024]{1,0:T(8,128)(2,1)}, bf16[224,1024]{1,0:T(8,128)(2,1)S(1)}, u32[]{:S(2)}, u32[]{:S(2)}) collective-permute-start(bf16[224,1024]{1,0:T(8,128)(2,1)} %maximum_maximum_fusion.1), channel_id=1, source_target_pairs={{0,2},{2,0},{1,3},{3,1},{4,6},{6,4},{5,7},{7,5},{8,10},{10,8},{9,1... | collective-permute-start | bytes 1376264 | tf_op jit(solution)/shard_map/ppermute | solution.py:495
  51.2 18.2 %collective-permute-start.8 = (bf16[128,1024]{1,0:T(8,128)(2,1)}, bf16[128,1024]{1,0:T(8,128)(2,1)S(1)}, u32[]{:S(2)}, u32[]{:S(2)}) collective-permute-start(bf16[128,1024]{1,0:T(8,128)(2,1)} %dynamic-slice_bitcast_fusion), channel_id=1, source_target_pairs={{0,4},{1,2},{2,7},{3,17},{4,22},{5,0},{6,5},{7,3},{8,20},{9,18},{1... | collective-permute-start | bytes 786440 | tf_op jit(solution)/shard_map/ppermute | solution.py:1726
  52.3 17.1 %collective-permute-start.9 = (bf16[64,1024]{1,0:T(8,128)(2,1)}, bf16[64,1024]{1,0:T(8,128)(2,1)S(1)}, u32[]{:S(2)}, u32[]{:S(2)}) collective-permute-start(bf16[64,1024]{1,0:T(8,128)(2,1)} %copy-done.48), channel_id=1, source_target_pairs={{0,5},{1,1},{2,20},{3,16},{4,23},{5,19},{6,6},{7,2},{8,21},{9,17},... | collective-permute-start | bytes 393224 | tf_op jit(solution)/shard_map/ppermute | solution.py:1726
  72.8 201.4 %reduce-scatter.2.cloned.1.call-start = ((), (), s32[]{:S(2)}) async-start(), calls=%async_computation.5 | async-start | bytes 4587520 | tf_op jit(solution)/shard_map/reduce_scatter | solution.py:1792
  91.3 13.1 %collective-permute-start.12 = (bf16[128,1024]{1,0:T(8,128)(2,1)S(1)}, bf16[128,1024]{1,0:T(8,128)(2,1)S(1)}, u32[]{:S(2)}, u32[]{:S(2)}) collective-permute-start(bf16[128,1024]{1,0:T(8,128)(2,1)S(1)} %get-tuple-element.154), channel_id=1, source_target_pairs={{0,1},{1,0},{2,3},{3,2},{4,5},{5,4},{6,7},{7,6},{8,9},{9,8},{10,11... | collective-permute-start | bytes 786440 | tf_op jit(solution)/shard_map/ppermute | solution.py:495
  97.3 13.4 %collective-permute-start.13 = (bf16[128,1024]{1,0:T(8,128)(2,1)S(1)}, bf16[128,1024]{1,0:T(8,128)(2,1)S(1)}, u32[]{:S(2)}, u32[]{:S(2)}) collective-permute-start(bf16[128,1024]{1,0:T(8,128)(2,1)S(1)} %get-tuple-element.155), channel_id=1, source_target_pairs={{0,2},{2,0},{1,3},{3,1},{4,6},{6,4},{5,7},{7,5},{8,10},{10,8},{9,1... | collective-permute-start | bytes 786440 | tf_op jit(solution)/shard_map/ppermute | solution.py:495
  99.2 13.3 %collective-permute-start.14 = (bf16[128,1024]{1,0:T(8,128)(2,1)S(1)}, bf16[128,1024]{1,0:T(8,128)(2,1)S(1)}, u32[]{:S(2)}, u32[]{:S(2)}) collective-permute-start(bf16[128,1024]{1,0:T(8,128)(2,1)S(1)} %get-tuple-element.156), channel_id=1, source_target_pairs={{0,3},{1,2},{2,1},{3,0},{4,7},{5,6},{6,5},{7,4},{8,11},{9,10},{10,... | collective-permute-start | bytes 786440 | tf_op jit(solution)/shard_map/ppermute | solution.py:585
  114.3 9.2 %collective-permute-start.15 = (bf16[128,1024]{1,0:T(8,128)(2,1)S(1)}, bf16[128,1024]{1,0:T(8,128)(2,1)S(1)}, u32[]{:S(2)}, u32[]{:S(2)}) collective-permute-start(bf16[128,1024]{1,0:T(8,128)(2,1)S(1)} %get-tuple-element.159.refs_0_.refs_8_), channel_id=1, source_target_pairs={{0,1},{1,0},{2,3},{3,2},{4,5},{5,4},{6,7},{7,6},{8,9},{9,8},{10,11... | collective-permute-start | bytes 786440 | tf_op jit(solution)/shard_map/ppermute | solution.py:495
  114.9 13.0 %collective-permute-start.16 = (bf16[128,1024]{1,0:T(8,128)(2,1)S(1)}, bf16[128,1024]{1,0:T(8,128)(2,1)S(1)}, u32[]{:S(2)}, u32[]{:S(2)}) collective-permute-start(bf16[128,1024]{1,0:T(8,128)(2,1)S(1)} %get-tuple-element.159.refs_0_.refs_8_), channel_id=1, source_target_pairs={{0,2},{2,0},{1,3},{3,1},{4,6},{6,4},{5,7},{7,5},{8,10},{10,8},{9,1... | collective-permute-start | bytes 786440 | tf_op jit(solution)/shard_map/ppermute | solution.py:495
  116.7 11.3 %collective-permute-start.17 = (bf16[128,1024]{1,0:T(8,128)(2,1)S(1)}, bf16[128,1024]{1,0:T(8,128)(2,1)S(1)}, u32[]{:S(2)}, u32[]{:S(2)}) collective-permute-start(bf16[128,1024]{1,0:T(8,128)(2,1)S(1)} %get-tuple-element.159.refs_0_.refs_8_), channel_id=1, source_target_pairs={{0,3},{1,2},{2,1},{3,0},{4,7},{5,6},{6,5},{7,4},{8,11},{9,10},{10,... | collective-permute-start | bytes 786440 | tf_op jit(solution)/shard_map/ppermute | solution.py:585
  117.8 10.6 %collective-permute-start.18 = (bf16[128,1024]{1,0:T(8,128)(2,1)S(1)}, bf16[128,1024]{1,0:T(8,128)(2,1)S(1)}, u32[]{:S(2)}, u32[]{:S(2)}) collective-permute-start(bf16[128,1024]{1,0:T(8,128)(2,1)S(1)} %get-tuple-element.159.refs_0_.refs_8_), channel_id=1, source_target_pairs={{0,16},{16,0},{1,17},{17,1},{2,18},{18,2},{3,19},{19,3},{4,20},{20... | collective-permute-start | bytes 786440 | tf_op jit(solution)/shard_map/ppermute | solution.py:495
  123.6 5.1 %collective-permute-start.19 = (bf16[128,1024]{1,0:T(8,128)(2,1)S(1)}, bf16[128,1024]{1,0:T(8,128)(2,1)S(1)}, u32[]{:S(2)}, u32[]{:S(2)}) collective-permute-start(bf16[128,1024]{1,0:T(8,128)(2,1)S(1)} %collective-permute-done.15.refs_1_.refs_9_), channel_id=1, source_target_pairs={{0,16},{16,0},{1,17},{17,1},{2,18},{18,2},{3,19},{19,3},{4,20},{20... | collective-permute-start | bytes 786440 | tf_op jit(solution)/shard_map/ppermute | solution.py:495
  136.7 10.6 %collective-permute-start.26 = (bf16[1024,768]{1,0:T(8,128)(2,1)S(1)}, bf16[1024,768]{1,0:T(8,128)(2,1)}, u32[]{:S(2)}, u32[]{:S(2)}) collective-permute-start(bf16[1024,768]{1,0:T(8,128)(2,1)S(1)} %copy-done.3), channel_id=1, source_target_pairs={{0,16},{16,0},{1,17},{17,1},{2,18},{18,2},{3,19},{19,3},{4,20},{20... | collective-permute-start | bytes 4718600 | tf_op jit(solution)/shard_map/ppermute | solution.py:495
  138.1 8.9 %collective-permute-start.27 = (bf16[128,1024]{1,0:T(8,128)(2,1)S(1)}, bf16[128,1024]{1,0:T(8,128)(2,1)S(1)}, u32[]{:S(2)}, u32[]{:S(2)}) collective-permute-start(bf16[128,1024]{1,0:T(8,128)(2,1)S(1)} %get-tuple-element.267), channel_id=1, source_target_pairs={{0,0},{4,4},{8,16},{12,20},{16,8},{20,12},{24,24},{28,28},{1,1},{5... | collective-permute-start | bytes 786440 | tf_op jit(solution)/shard_map/ppermute | solution.py:539
  139.2 8.0 %collective-permute-start.28 = (bf16[128,1024]{1,0:T(8,128)(2,1)S(1)}, bf16[128,1024]{1,0:T(8,128)(2,1)S(1)}, u32[]{:S(2)}, u32[]{:S(2)}) collective-permute-start(bf16[128,1024]{1,0:T(8,128)(2,1)S(1)} %get-tuple-element.266), channel_id=1, source_target_pairs={{0,4},{4,0},{8,20},{12,16},{16,12},{20,8},{24,28},{28,24},{1,5},{5... | collective-permute-start | bytes 786440 | tf_op jit(solution)/shard_map/ppermute | solution.py:539
  143.6 6.7 %collective-permute-start.23 = (bf16[128,1024]{1,0:T(8,128)(2,1)S(1)}, bf16[128,1024]{1,0:T(8,128)(2,1)S(1)}, u32[]{:S(2)}, u32[]{:S(2)}) collective-permute-start(bf16[128,1024]{1,0:T(8,128)(2,1)S(1)} %get-tuple-element.162), channel_id=1, source_target_pairs={{0,1},{1,0},{2,3},{3,2},{4,5},{5,4},{6,7},{7,6},{8,9},{9,8},{10,11... | collective-permute-start | bytes 786440 | tf_op jit(solution)/shard_map/ppermute | solution.py:495
  145.1 13.3 %collective-permute-start.24 = (bf16[128,1024]{1,0:T(8,128)(2,1)S(1)}, bf16[128,1024]{1,0:T(8,128)(2,1)S(1)}, u32[]{:S(2)}, u32[]{:S(2)}) collective-permute-start(bf16[128,1024]{1,0:T(8,128)(2,1)S(1)} %get-tuple-element.163), channel_id=1, source_target_pairs={{0,2},{2,0},{1,3},{3,1},{4,6},{6,4},{5,7},{7,5},{8,10},{10,8},{9,1... | collective-permute-start | bytes 786440 | tf_op jit(solution)/shard_map/ppermute | solution.py:495
  147.1 11.3 %collective-permute-start.25 = (bf16[128,1024]{1,0:T(8,128)(2,1)S(1)}, bf16[128,1024]{1,0:T(8,128)(2,1)S(1)}, u32[]{:S(2)}, u32[]{:S(2)}) collective-permute-start(bf16[128,1024]{1,0:T(8,128)(2,1)S(1)} %get-tuple-element.164), channel_id=1, source_target_pairs={{0,3},{1,2},{2,1},{3,0},{4,7},{5,6},{6,5},{7,4},{8,11},{9,10},{10,... | collective-permute-start | bytes 786440 | tf_op jit(solution)/shard_map/ppermute | solution.py:585
  164.2 9.0 %collective-permute-start.29 = (bf16[128,1024]{1,0:T(8,128)(2,1)S(1)}, bf16[128,1024]{1,0:T(8,128)(2,1)S(1)}, u32[]{:S(2)}, u32[]{:S(2)}) collective-permute-start(bf16[128,1024]{1,0:T(8,128)(2,1)S(1)} %get-tuple-element.169.refs_0_), channel_id=1, source_target_pairs={{0,1},{1,0},{2,3},{3,2},{4,5},{5,4},{6,7},{7,6},{8,9},{9,8},{10,11... | collective-permute-start | bytes 786440 | tf_op jit(solution)/shard_map/ppermute | solution.py:495
  165.4 13.6 %collective-permute-start.30 = (bf16[128,1024]{1,0:T(8,128)(2,1)S(1)}, bf16[128,1024]{1,0:T(8,128)(2,1)S(1)}, u32[]{:S(2)}, u32[]{:S(2)}) collective-permute-start(bf16[128,1024]{1,0:T(8,128)(2,1)S(1)} %get-tuple-element.169.refs_0_), channel_id=1, source_target_pairs={{0,2},{2,0},{1,3},{3,1},{4,6},{6,4},{5,7},{7,5},{8,10},{10,8},{9,1... | collective-permute-start | bytes 786440 | tf_op jit(solution)/shard_map/ppermute | solution.py:495
  166.9 13.9 %collective-permute-start.31 = (bf16[128,1024]{1,0:T(8,128)(2,1)S(1)}, bf16[128,1024]{1,0:T(8,128)(2,1)S(1)}, u32[]{:S(2)}, u32[]{:S(2)}) collective-permute-start(bf16[128,1024]{1,0:T(8,128)(2,1)S(1)} %get-tuple-element.169.refs_0_), channel_id=1, source_target_pairs={{0,3},{1,2},{2,1},{3,0},{4,7},{5,6},{6,5},{7,4},{8,11},{9,10},{10,... | collective-permute-start | bytes 786440 | tf_op jit(solution)/shard_map/ppermute | solution.py:585
  168.3 12.4 %collective-permute-start.32 = (bf16[128,1024]{1,0:T(8,128)(2,1)S(1)}, bf16[128,1024]{1,0:T(8,128)(2,1)S(1)}, u32[]{:S(2)}, u32[]{:S(2)}) collective-permute-start(bf16[128,1024]{1,0:T(8,128)(2,1)S(1)} %get-tuple-element.169.refs_0_), channel_id=1, source_target_pairs={{0,16},{16,0},{1,17},{17,1},{2,18},{18,2},{3,19},{19,3},{4,20},{20... | collective-permute-start | bytes 786440 | tf_op jit(solution)/shard_map/ppermute | solution.py:495
  173.1 7.6 %collective-permute-start.33 = (bf16[128,1024]{1,0:T(8,128)(2,1)S(1)}, bf16[128,1024]{1,0:T(8,128)(2,1)S(1)}, u32[]{:S(2)}, u32[]{:S(2)}) collective-permute-start(bf16[128,1024]{1,0:T(8,128)(2,1)S(1)} %collective-permute-done.29.refs_1_), channel_id=1, source_target_pairs={{0,16},{16,0},{1,17},{17,1},{2,18},{18,2},{3,19},{19,3},{4,20},{20... | collective-permute-start | bytes 786440 | tf_op jit(solution)/shard_map/ppermute | solution.py:495
  184.2 4.7 %collective-permute-start.38 = (bf16[512,1024]{1,0:T(8,128)(2,1)S(1)}, bf16[512,1024]{1,0:T(8,128)(2,1)S(1)}, u32[]{:S(2)}, u32[]{:S(2)}) collective-permute-start(bf16[512,1024]{1,0:T(8,128)(2,1)S(1)} %get-tuple-element.177), channel_id=1, source_target_pairs={{0,16},{16,0},{1,17},{17,1},{2,18},{18,2},{3,19},{19,3},{4,20},{20... | collective-permute-start | bytes 3145736 | tf_op jit(solution)/shard_map/ppermute | solution.py:495
  184.8 3.5 %collective-permute-start.39 = (bf16[128,1024]{1,0:T(8,128)(2,1)S(1)}, bf16[128,1024]{1,0:T(8,128)(2,1)S(1)}, u32[]{:S(2)}, u32[]{:S(2)}) collective-permute-start(bf16[128,1024]{1,0:T(8,128)(2,1)S(1)} %get-tuple-element.178.refs_0_), channel_id=1, source_target_pairs={{0,16},{16,0},{1,17},{17,1},{2,18},{18,2},{3,19},{19,3},{4,20},{20... | collective-permute-start | bytes 786440 | tf_op jit(solution)/shard_map/ppermute | solution.py:495
  196.1 5.0 %collective-permute-start.36 = (bf16[64,1024]{1,0:T(8,128)(2,1)S(1)}, bf16[64,1024]{1,0:T(8,128)(2,1)S(1)}, u32[]{:S(2)}, u32[]{:S(2)}) collective-permute-start(bf16[64,1024]{1,0:T(8,128)(2,1)S(1)} %get-tuple-element.279), channel_id=1, source_target_pairs={{4,0},{0,4},{20,8},{16,12},{12,16},{8,20},{28,24},{24,28},{5,1},{1... | collective-permute-start | bytes 393224 | tf_op jit(solution)/shard_map/ppermute | solution.py:545
  196.4 4.7 %collective-permute-start.37 = (bf16[64,1024]{1,0:T(8,128)(2,1)S(1)}, bf16[64,1024]{1,0:T(8,128)(2,1)S(1)}, u32[]{:S(2)}, u32[]{:S(2)}) collective-permute-start(bf16[64,1024]{1,0:T(8,128)(2,1)S(1)} %get-tuple-element.278), channel_id=1, source_target_pairs={{0,0},{4,4},{16,8},{20,12},{8,16},{12,20},{24,24},{28,28},{1,1},{5... | collective-permute-start | bytes 393224 | tf_op jit(solution)/shard_map/ppermute | solution.py:545
  197.1 7.6 %collective-permute-start.43 = (bf16[128,1024]{1,0:T(8,128)(2,1)S(1)}, bf16[128,1024]{1,0:T(8,128)(2,1)S(1)}, u32[]{:S(2)}, u32[]{:S(2)}) collective-permute-start(bf16[128,1024]{1,0:T(8,128)(2,1)S(1)} %get-tuple-element.183), channel_id=1, source_target_pairs={{0,1},{1,0},{2,3},{3,2},{4,5},{5,4},{6,7},{7,6},{8,9},{9,8},{10,11... | collective-permute-start | bytes 786440 | tf_op jit(solution)/shard_map/ppermute | solution.py:495
  197.8 13.5 %collective-permute-start.44 = (bf16[128,1024]{1,0:T(8,128)(2,1)S(1)}, bf16[128,1024]{1,0:T(8,128)(2,1)S(1)}, u32[]{:S(2)}, u32[]{:S(2)}) collective-permute-start(bf16[128,1024]{1,0:T(8,128)(2,1)S(1)} %get-tuple-element.184), channel_id=1, source_target_pairs={{0,2},{2,0},{1,3},{3,1},{4,6},{6,4},{5,7},{7,5},{8,10},{10,8},{9,1... | collective-permute-start | bytes 786440 | tf_op jit(solution)/shard_map/ppermute | solution.py:495
  199.6 11.8 %collective-permute-start.45 = (bf16[128,1024]{1,0:T(8,128)(2,1)S(1)}, bf16[128,1024]{1,0:T(8,128)(2,1)S(1)}, u32[]{:S(2)}, u32[]{:S(2)}) collective-permute-start(bf16[128,1024]{1,0:T(8,128)(2,1)S(1)} %get-tuple-element.185), channel_id=1, source_target_pairs={{0,3},{1,2},{2,1},{3,0},{4,7},{5,6},{6,5},{7,4},{8,11},{9,10},{10,... | collective-permute-start | bytes 786440 | tf_op jit(solution)/shard_map/ppermute | solution.py:585
  212.0 8.6 %collective-permute-start.46 = (bf16[128,1024]{1,0:T(8,128)(2,1)S(1)}, bf16[128,1024]{1,0:T(8,128)(2,1)S(1)}, u32[]{:S(2)}, u32[]{:S(2)}) collective-permute-start(bf16[128,1024]{1,0:T(8,128)(2,1)S(1)} %get-tuple-element.195.refs_0_), channel_id=1, source_target_pairs={{0,1},{1,0},{2,3},{3,2},{4,5},{5,4},{6,7},{7,6},{8,9},{9,8},{10,11... | collective-permute-start | bytes 786440 | tf_op jit(solution)/shard_map/ppermute | solution.py:495
  213.9 12.8 %collective-permute-start.47 = (bf16[128,1024]{1,0:T(8,128)(2,1)S(1)}, bf16[128,1024]{1,0:T(8,128)(2,1)S(1)}, u32[]{:S(2)}, u32[]{:S(2)}) collective-permute-start(bf16[128,1024]{1,0:T(8,128)(2,1)S(1)} %get-tuple-element.195.refs_0_), channel_id=1, source_target_pairs={{0,2},{2,0},{1,3},{3,1},{4,6},{6,4},{5,7},{7,5},{8,10},{10,8},{9,1... | collective-permute-start | bytes 786440 | tf_op jit(solution)/shard_map/ppermute | solution.py:495
  214.8 13.8 %collective-permute-start.48 = (bf16[128,1024]{1,0:T(8,128)(2,1)S(1)}, bf16[128,1024]{1,0:T(8,128)(2,1)S(1)}, u32[]{:S(2)}, u32[]{:S(2)}) collective-permute-start(bf16[128,1024]{1,0:T(8,128)(2,1)S(1)} %get-tuple-element.195.refs_0_), channel_id=1, source_target_pairs={{0,3},{1,2},{2,1},{3,0},{4,7},{5,6},{6,5},{7,4},{8,11},{9,10},{10,... | collective-permute-start | bytes 786440 | tf_op jit(solution)/shard_map/ppermute | solution.py:585
  216.1 12.4 %collective-permute-start.49 = (bf16[128,1024]{1,0:T(8,128)(2,1)S(1)}, bf16[128,1024]{1,0:T(8,128)(2,1)S(1)}, u32[]{:S(2)}, u32[]{:S(2)}) collective-permute-start(bf16[128,1024]{1,0:T(8,128)(2,1)S(1)} %get-tuple-element.195.refs_0_), channel_id=1, source_target_pairs={{0,16},{16,0},{1,17},{17,1},{2,18},{18,2},{3,19},{19,3},{4,20},{20... | collective-permute-start | bytes 786440 | tf_op jit(solution)/shard_map/ppermute | solution.py:495
  220.5 8.0 %collective-permute-start.50 = (bf16[128,1024]{1,0:T(8,128)(2,1)S(1)}, bf16[128,1024]{1,0:T(8,128)(2,1)S(1)}, u32[]{:S(2)}, u32[]{:S(2)}) collective-permute-start(bf16[128,1024]{1,0:T(8,128)(2,1)S(1)} %collective-permute-done.46.refs_1_), channel_id=1, source_target_pairs={{0,16},{16,0},{1,17},{17,1},{2,18},{18,2},{3,19},{19,3},{4,20},{20... | collective-permute-start | bytes 786440 | tf_op jit(solution)/shard_map/ppermute | solution.py:495
  243.6 9.2 %collective-permute-start.54 = (bf16[128,1024]{1,0:T(8,128)(2,1)S(1)}, bf16[128,1024]{1,0:T(8,128)(2,1)S(1)}, u32[]{:S(2)}, u32[]{:S(2)}) collective-permute-start(bf16[128,1024]{1,0:T(8,128)(2,1)S(1)} %get-tuple-element.200), channel_id=1, source_target_pairs={{0,1},{1,0},{2,3},{3,2},{4,5},{5,4},{6,7},{7,6},{8,9},{9,8},{10,11... | collective-permute-start | bytes 786440 | tf_op jit(solution)/shard_map/ppermute | solution.py:495
  244.9 13.7 %collective-permute-start.55 = (bf16[128,1024]{1,0:T(8,128)(2,1)S(1)}, bf16[128,1024]{1,0:T(8,128)(2,1)S(1)}, u32[]{:S(2)}, u32[]{:S(2)}) collective-permute-start(bf16[128,1024]{1,0:T(8,128)(2,1)S(1)} %get-tuple-element.201), channel_id=1, source_target_pairs={{0,2},{2,0},{1,3},{3,1},{4,6},{6,4},{5,7},{7,5},{8,10},{10,8},{9,1... | collective-permute-start | bytes 786440 | tf_op jit(solution)/shard_map/ppermute | solution.py:495
  246.4 12.3 %collective-permute-start.56 = (bf16[128,1024]{1,0:T(8,128)(2,1)S(1)}, bf16[128,1024]{1,0:T(8,128)(2,1)S(1)}, u32[]{:S(2)}, u32[]{:S(2)}) collective-permute-start(bf16[128,1024]{1,0:T(8,128)(2,1)S(1)} %get-tuple-element.202), channel_id=1, source_target_pairs={{0,3},{1,2},{2,1},{3,0},{4,7},{5,6},{6,5},{7,4},{8,11},{9,10},{10,... | collective-permute-start | bytes 786440 | tf_op jit(solution)/shard_map/ppermute | solution.py:585
  260.1 39.4 %all-to-all-start.1 = ((bf16[16,96,128]{2,1,0:T(8,128)(2,1)}), bf16[16,96,128]{2,1,0:T(8,128)(2,1)S(1)}, u32[]{:S(2)}, u32[]{:S(2)}) async-start(bf16[16,96,128]{2,1,0:T(8,128)(2,1)} %get-tuple-element.216), calls=%async_computation.1 | async-start | bytes 786432 | tf_op jit(solution)/shard_map/all_to_all | solution.py:1658
  263.6 14.9 %collective-permute-start.64 = (bf16[64,1024]{1,0:T(8,128)(2,1)S(1)}, bf16[64,1024]{1,0:T(8,128)(2,1)S(1)}, u32[]{:S(2)}, u32[]{:S(2)}) collective-permute-start(bf16[64,1024]{1,0:T(8,128)(2,1)S(1)} %get-tuple-element.224), channel_id=1, source_target_pairs={{1,0},{5,1},{16,2},{20,3},{19,4},{23,5},{2,6},{6,7},{17,8},{21,9},... | collective-permute-start | bytes 393224 | tf_op jit(solution)/shard_map/ppermute | solution.py:1848
  267.3 18.7 %collective-permute-start.66 = (bf16[64,1024]{1,0:T(8,128)(2,1)S(1)}, bf16[64,1024]{1,0:T(8,128)(2,1)S(1)}, u32[]{:S(2)}, u32[]{:S(2)}) collective-permute-start(bf16[64,1024]{1,0:T(8,128)(2,1)S(1)} %get-tuple-element.226), channel_id=1, source_target_pairs={{5,0},{1,1},{20,2},{16,3},{23,4},{19,5},{6,6},{2,7},{21,8},{17,9},... | collective-permute-start | bytes 393224 | tf_op jit(solution)/shard_map/ppermute | solution.py:1848
  270.1 16.6 %collective-permute-start.63 = (bf16[128,1024]{1,0:T(8,128)(2,1)S(1)}, bf16[128,1024]{1,0:T(8,128)(2,1)S(1)}, u32[]{:S(2)}, u32[]{:S(2)}) collective-permute-start(bf16[128,1024]{1,0:T(8,128)(2,1)S(1)} %get-tuple-element.223), channel_id=1, source_target_pairs={{0,0},{6,1},{3,2},{21,3},{18,4},{4,5},{1,6},{7,7},{16,8},{22,9},{1... | collective-permute-start | bytes 786440 | tf_op jit(solution)/shard_map/ppermute | solution.py:1848
  270.8 18.9 %collective-permute-start.65 = (bf16[128,1024]{1,0:T(8,128)(2,1)S(1)}, bf16[128,1024]{1,0:T(8,128)(2,1)S(1)}, u32[]{:S(2)}, u32[]{:S(2)}) collective-permute-start(bf16[128,1024]{1,0:T(8,128)(2,1)S(1)} %get-tuple-element.225), channel_id=1, source_target_pairs={{4,0},{2,1},{7,2},{17,3},{22,4},{0,5},{5,6},{3,7},{20,8},{18,9},{2... | collective-permute-start | bytes 786440 | tf_op jit(solution)/shard_map/ppermute | solution.py:1848
  275.4 16.4 %collective-permute-start.59 = (bf16[64,1280]{1,0:T(8,128)(2,1)S(1)}, bf16[64,1280]{1,0:T(8,128)(2,1)S(1)}, u32[]{:S(2)}, u32[]{:S(2)}) collective-permute-start(bf16[64,1280]{1,0:T(8,128)(2,1)S(1)} %get-tuple-element.218), channel_id=1, source_target_pairs={{0,1},{1,0},{2,3},{3,2},{4,5},{5,4},{6,7},{7,6},{8,9},{9,8},{10,11... | collective-permute-start | bytes 491528 | tf_op jit(solution)/shard_map/ppermute | solution.py:495
  278.5 17.2 %collective-permute-start.60 = (bf16[64,1280]{1,0:T(8,128)(2,1)S(1)}, bf16[64,1280]{1,0:T(8,128)(2,1)S(1)}, u32[]{:S(2)}, u32[]{:S(2)}) collective-permute-start(bf16[64,1280]{1,0:T(8,128)(2,1)S(1)} %get-tuple-element.219), channel_id=1, source_target_pairs={{0,2},{2,0},{1,3},{3,1},{4,6},{6,4},{5,7},{7,5},{8,10},{10,8},{9,1... | collective-permute-start | bytes 491528 | tf_op jit(solution)/shard_map/ppermute | solution.py:495
  286.0 9.8 %collective-permute-start.61 = (bf16[64,1280]{1,0:T(8,128)(2,1)S(1)}, bf16[64,1280]{1,0:T(8,128)(2,1)S(1)}, u32[]{:S(2)}, u32[]{:S(2)}) collective-permute-start(bf16[64,1280]{1,0:T(8,128)(2,1)S(1)} %get-tuple-element.220), channel_id=1, source_target_pairs={{0,3},{1,2},{2,1},{3,0},{4,7},{5,6},{6,5},{7,4},{8,11},{9,10},{10,... | collective-permute-start | bytes 491528 | tf_op jit(solution)/shard_map/ppermute | solution.py:585
  286.8 12.8 %collective-permute-start.57 = (bf16[64,1024]{1,0:T(8,128)(2,1)}, bf16[64,1024]{1,0:T(8,128)(2,1)}, u32[]{:S(2)}, u32[]{:S(2)}) collective-permute-start(bf16[64,1024]{1,0:T(8,128)(2,1)} %get-tuple-element.273), channel_id=1, source_target_pairs={{4,0},{0,4},{20,8},{16,12},{12,16},{8,20},{28,24},{24,28},{5,1},{1... | collective-permute-start | bytes 393224 | tf_op jit(solution)/shard_map/ppermute | solution.py:545
  289.7 9.9 %collective-permute-start.58 = (bf16[64,1024]{1,0:T(8,128)(2,1)}, bf16[64,1024]{1,0:T(8,128)(2,1)}, u32[]{:S(2)}, u32[]{:S(2)}) collective-permute-start(bf16[64,1024]{1,0:T(8,128)(2,1)} %get-tuple-element.272), channel_id=1, source_target_pairs={{0,0},{4,4},{16,8},{20,12},{8,16},{12,20},{24,24},{28,28},{1,1},{5... | collective-permute-start | bytes 393224 | tf_op jit(solution)/shard_map/ppermute | solution.py:545
  291.9 11.4 %collective-permute-start.68 = (f32[128,1024]{1,0:T(8,128)S(1)}, f32[128,1024]{1,0:T(8,128)S(1)}, u32[]{:S(2)}, u32[]{:S(2)}) collective-permute-start(f32[128,1024]{1,0:T(8,128)S(1)} %get-tuple-element.232.refs_0_), channel_id=1, source_target_pairs={{0,16},{16,0},{1,17},{17,1},{2,18},{18,2},{3,19},{19,3},{4,20},{20... | collective-permute-start | bytes 1572872 | tf_op jit(solution)/shard_map/ppermute | solution.py:495
  297.7 10.3 %collective-permute-start.67 = (f32[192,1024]{1,0:T(8,128)S(1)}, f32[192,1024]{1,0:T(8,128)}, u32[]{:S(2)}, u32[]{:S(2)}) collective-permute-start(f32[192,1024]{1,0:T(8,128)S(1)} %shard_map.260), channel_id=1, source_target_pairs={{0,16},{16,0},{1,17},{17,1},{2,18},{18,2},{3,19},{19,3},{4,20},{20... | collective-permute-start | bytes 2359304 | tf_op jit(solution)/shard_map/ppermute | solution.py:495
  301.4 5.3 %collective-permute-start.69 = (bf16[64,1280]{1,0:T(8,128)(2,1)S(1)}, bf16[64,1280]{1,0:T(8,128)(2,1)S(1)}, u32[]{:S(2)}, u32[]{:S(2)}) collective-permute-start(bf16[64,1280]{1,0:T(8,128)(2,1)S(1)} %get-tuple-element.234.refs_0_), channel_id=1, source_target_pairs={{0,16},{16,0},{1,17},{17,1},{2,18},{18,2},{3,19},{19,3},{4,20},{20... | collective-permute-start | bytes 491528 | tf_op jit(solution)/shard_map/ppermute | solution.py:495
  302.8 3.9 %collective-permute-start.70 = (bf16[64,1280]{1,0:T(8,128)(2,1)S(1)}, bf16[64,1280]{1,0:T(8,128)(2,1)S(1)}, u32[]{:S(2)}, u32[]{:S(2)}) collective-permute-start(bf16[64,1280]{1,0:T(8,128)(2,1)S(1)} %collective-permute-done.59.refs_1_), channel_id=1, source_target_pairs={{0,16},{16,0},{1,17},{17,1},{2,18},{18,2},{3,19},{19,3},{4,20},{20... | collective-permute-start | bytes 491528 | tf_op jit(solution)/shard_map/ppermute | solution.py:495
  302.8 3.9 %collective-permute-start.71 = (bf16[64,1280]{1,0:T(8,128)(2,1)S(1)}, bf16[64,1280]{1,0:T(8,128)(2,1)S(1)}, u32[]{:S(2)}, u32[]{:S(2)}) collective-permute-start(bf16[64,1280]{1,0:T(8,128)(2,1)S(1)} %collective-permute-done.60.refs_2_), channel_id=1, source_target_pairs={{0,16},{16,0},{1,17},{17,1},{2,18},{18,2},{3,19},{19,3},{4,20},{20... | collective-permute-start | bytes 491528 | tf_op jit(solution)/shard_map/ppermute | solution.py:495
  303.3 3.4 %collective-permute-start.72 = (bf16[64,1280]{1,0:T(8,128)(2,1)S(1)}, bf16[64,1280]{1,0:T(8,128)(2,1)S(1)}, u32[]{:S(2)}, u32[]{:S(2)}) collective-permute-start(bf16[64,1280]{1,0:T(8,128)(2,1)S(1)} %collective-permute-done.61.refs_3_), channel_id=1, source_target_pairs={{0,16},{16,0},{1,17},{17,1},{2,18},{18,2},{3,19},{19,3},{4,20},{20... | collective-permute-start | bytes 491528 | tf_op jit(solution)/shard_map/ppermute | solution.py:495
  (71 other events, 508.9 us)
Sparse Core Ops, SparseCore 0:
  11.4 69.8 all-gather.2
  83.4 45.1 all-gather.4
  196.2 68.1 reduce-scatter.1

commit v4 on v3

--- a/solution.py
+++ b/solution.py
@@ -605,7 +605,7 @@
     return jax.ShapeDtypeStruct(shape, jnp.float32)
 
 
-FLOPS_PER_US = 1.1e9
+FLOPS_PER_US = 1.5e9
 TIMES = {
     "attend_body": 10.0,
     "feed_body": 3.5,
@@ -1350,8 +1350,8 @@
     vec_ref,
     own_ref,
     other_ref,
-    noise_ref,
-    cot_ref,
+    extra_ref,
+    more_ref,
     means_ref,
     logvars_ref,
     out_ref,
@@ -1363,9 +1363,11 @@
     dmeans_ref,
     dlogvars_ref,
     sums_ref,
+    cot_ref,
 ):
     rows, width = attended_ref.shape
-    lat = noise_ref.shape[1]
+    lat = means_ref.shape[1]
+    span = rows // 2
     comps = means_ref.shape[0]
     parts = z_sum((keep_ref, came_x_ref, came_y_ref, came_far_ref))
     fed = attended_ref[...] + parts + vec_ref[7:8]
@@ -1373,7 +1375,8 @@
     fed_ref[...] = fed_low
     latent = halves_nt(fed_low, own_ref, other_ref, LAT_LANES) + vec_ref[LAT_ROW : LAT_ROW + 1]
     logvar = latent[:, lat:]
-    noise = noise_ref[...]
+    noise = jnp.concatenate([extra_ref[span:], more_ref[span:]])
+    noise = wide(noise[:, :lat]) + wide(noise[:, lat:])
     spread = jnp.exp(0.5 * logvar) * noise
     sample = latent[:, :lat] + spread
     sample_low = to_low(sample)
@@ -1381,12 +1384,12 @@
     out_ref[...] = to_low(
         fed + halves_nt(sample_low, own_ref, other_ref, DEC_LANES) + vec_ref[8:9]
     )
-    cot = cot_ref[...]
+    cot = jnp.concatenate([extra_ref[:span], more_ref[:span]])
+    cot_ref[...] = cot
     dsample = core_order(
         product(cot, own_ref[:, DEC_LANES]), product(cot, other_ref[:, DEC_LANES])
     )
 
-    span = rows // 2
     row = lax.broadcasted_iota(jnp.int32, (rows, 1), 0)
     block = lax.axis_index("y") * 2 + lax.axis_index("x")
     place = slide_place(lax.axis_index("grp"), block, row // span, row & (span - 1), span)
@@ -1395,17 +1398,13 @@
     own_term = jnp.sum(-0.5 * noise * noise - 0.5 * logvar, axis=-1, keepdims=True)
     logvars = logvars_ref[...]
     inverse = jnp.exp(-logvars)
+    falls = -0.5 * inverse
+    levels = -0.5 * jnp.sum(logvars, axis=-1, keepdims=True) - math.log(comps)
     terms = []
     for c in range(comps):
         offset = sample - means_ref[c : c + 1]
-        terms.append(
-            jnp.sum(
-                -0.5 * offset * offset * inverse[c : c + 1] - 0.5 * logvars[c : c + 1],
-                axis=-1,
-                keepdims=True,
-            )
-            - math.log(comps)
-        )
+        drop = jnp.sum(offset * offset * falls[c : c + 1], axis=-1, keepdims=True)
+        terms.append(drop + levels[c : c + 1])
     peak = terms[0]
     for term in terms[1:]:
         peak = jnp.maximum(peak, term)
@@ -1444,12 +1443,12 @@
     )
 
 
-def bottle_call(attended, parts, vec, weights, noise, cot, means, logvars):
+def bottle_call(attended, parts, vec, weights, extra, means, logvars):
     rows, width = attended.shape
-    lat = noise.shape[1]
+    lat = means.shape[1]
     return whole_call(
         bottle_body,
-        (attended, *parts, vec, *weights, noise, cot, means, logvars),
+        (attended, *parts, vec, *weights, *extra, means, logvars),
         [
             low_shape(rows, width),
             low_shape(rows, width),
@@ -1460,6 +1459,7 @@
             wide_shape(*means.shape),
             wide_shape(*means.shape),
             wide_shape(8, width),
+            low_shape(rows, width),
         ],
     )
 
@@ -1761,10 +1761,10 @@
     )
     mix_parts = mix_out(mixed, out_t, whole)
 
-    extra = to_slides(after(extra, mixed))
-    cot = extra[:, :span].reshape(rows, width)
-    noise = extra[:, span:].reshape(rows, width)
-    noise = wide(noise[:, :lat]) + wide(noise[:, lat:])
+    extra = after(extra, mixed)
+    extra = [
+        lax.ppermute(pick_slot(extra, k), ("grp", "z"), slide_routes(k)) for k in range(2)
+    ]
 
     attended, normed_two, hidden = project(mix_parts, first, vec)
     rows_two = plane_rows(normed_two)
@@ -1774,9 +1774,9 @@
     )
     fed_parts = (keep, *plane_hops(sends))
     wholes = (whole, other_core(whole))
-    output, fed_low, sample_low, dlat_low, dfed, dfed_low, dmeans, dlogvars, bottle_sums = (
+    output, fed_low, sample_low, dlat_low, dfed, dfed_low, dmeans, dlogvars, bottle_sums, cot = (
         bottle_call(
-            attended, fed_parts, vec, wholes, noise, cot, means, logvars
+            attended, fed_parts, vec, wholes, extra, means, logvars
         )
     )
 

time: 322 us -> 321 us (level)
    ppermute x49, waiting for transfers between devices: 102 us -> 97.8 us  [hop(): return lax.ppermute(values, axis, [(i, i ^ step) for i in range(size)])]
    ppermute x8, waiting for transfers between devices: 5.64 us -> 8.96 us  [plane_hops(): lax.ppermute(values[2], ('y', 'x'), [(i, i ^ 3) for i in range(4)])]
    unnamed x121 -> x119, local copies, waits for them, and re-layouts: 14.6 us -> 13.2 us
where the time goes in v4:
time: 321 us; the launch traced here: 317 us
  waiting for transfers between devices  121 us (38%)
  starting transfers between devices  97.1 us (30%)
  Pallas kernels  55.2 us (17%)
  local copies, waits for them, and re-layouts  17.5 us (5%)
  between operations  16.6 us (5%)
  other arithmetic  9.03 us (3%)
    ppermute x49, waiting for transfers between devices, hop(): return lax.ppermute(values, axis, [(i, i ^ step) for i in range(size)])  97.8 us
    pallas_call x26, Pallas kernels, whole_call(): pl.pallas_call(run, out_shape=out_shapes, in_specs=[hbm if i in left_out...  55.2 us
    ppermute x49, starting transfers between devices, hop(): return lax.ppermute(values, axis, [(i, i ^ step) for i in range(size)])  45.1 us
    unnamed x119, local copies, waits for them, and re-layouts  13.2 us
    all_to_all x2, starting transfers between devices, exchange(): return lax.all_to_all(blocks, axes, split_axis=0, concat_axis=0, tiled=True)  11.9 us
    ppermute x4, starting transfers between devices, fast_device(): lax.ppermute(grad, EVERY, [(there, here) for here, there in head_routes(s...  10.5 us
    ppermute x4, starting transfers between devices, fast_device(): lax.ppermute(head_parts[int(single)], EVERY, head_routes(single, k))  9.73 us
    ppermute x8, waiting for transfers between devices, plane_hops(): lax.ppermute(values[2], ('y', 'x'), [(i, i ^ 3) for i in range(4)])  8.96 us
  transfers between devices with their start and end apart: 78, of which 34 were waited for; matrix products, arithmetic and copies ran while one was open for 3% of the time, Pallas kernels for 11%

profile of v4, /device:TPU:0, one launch (start us, length us, event | category | flops | bytes accessed | tf_op | source)
XLA Modules:
  0.0 316.7 jit_solution(12579915119199307746)
XLA Ops:
  12.4 8.3 %all-to-all-start = ((bf16[16,64,128]{2,1,0:T(8,128)(2,1)}), bf16[16,64,128]{2,1,0:T(8,128)(2,1)S(1)}, u32[]{:S(2)}, u32[]{:S(2)}) async-start(bf16[16,64,128]{2,1,0:T(8,128)(2,1)} %get-tuple-element.134), calls=%async_computation | async-start | bytes 524288 | tf_op jit(solution)/shard_map/all_to_all | solution.py:1658
  21.7 2.0 collective-permute-start.1
  24.5 3.6 %collective-permute-start.4 = (bf16[128,1024]{1,0:T(8,128)(2,1)}, bf16[128,1024]{1,0:T(8,128)(2,1)}, u32[]{:S(2)}, u32[]{:S(2)}) collective-permute-start(bf16[128,1024]{1,0:T(8,128)(2,1)} %dynamic-slice_bitcast_fusion), channel_id=1, source_target_pairs={{0,0},{1,6},{2,3},{3,21},{4,18},{5,4},{6,1},{7,7},{8,16},{9,22},{1... | collective-permute-start | bytes 786440 | tf_op jit(solution)/shard_map/ppermute | solution.py:1726
  31.1 3.0 collective-permute-start.3
  34.2 6.4 %collective-permute-done.3 = bf16[80,1024]{1,0:T(8,128)(2,1)S(1)} collective-permute-done((bf16[80,1024]{1,0:T(8,128)(2,1)S(1)}, bf16[80,1024]{1,0:T(8,128)(2,1)S(1)}, u32[]{:S(2)}, u32[]{:S(2)}) %collective-permute-start.3) | collective-permute-done | bytes 163872 | tf_op jit(solution)/shard_map/ppermute | solution.py:495
  42.2 6.0 %collective-permute-done.5.refs_3_ = bf16[64,1024]{1,0:T(8,128)(2,1)S(1)} collective-permute-done((bf16[64,1024]{1,0:T(8,128)(2,1)S(1)}, bf16[64,1024]{1,0:T(8,128)(2,1)S(1)}, u32[]{:S(2)}, u32[]{:S(2)}) %collective-permute-start.5) | collective-permute-done | bytes 131104 | tf_op jit(solution)/shard_map/ppermute | solution.py:1726
  48.9 2.4 collective-permute-start.7
  52.3 3.8 %collective-permute-start.9 = (bf16[64,1024]{1,0:T(8,128)(2,1)}, bf16[64,1024]{1,0:T(8,128)(2,1)S(1)}, u32[]{:S(2)}, u32[]{:S(2)}) collective-permute-start(bf16[64,1024]{1,0:T(8,128)(2,1)} %copy-done.47), channel_id=1, source_target_pairs={{0,5},{1,1},{2,20},{3,16},{4,23},{5,19},{6,6},{7,2},{8,21},{9,17},... | collective-permute-start | bytes 393224 | tf_op jit(solution)/shard_map/ppermute | solution.py:1726
  56.1 13.2 %collective-permute-done.6 = bf16[160,1024]{1,0:T(8,128)(2,1)S(1)} collective-permute-done((bf16[160,1024]{1,0:T(8,128)(2,1)}, bf16[160,1024]{1,0:T(8,128)(2,1)S(1)}, u32[]{:S(2)}, u32[]{:S(2)}) %collective-permute-start.6) | collective-permute-done | bytes 327712 | tf_op jit(solution)/shard_map/ppermute | solution.py:495
  73.9 11.0 %shard_map.240 = (f32[16,1024]{1,0:T(8,128)S(1)}, f32[16,512]{1,0:T(8,128)S(1)}, f32[16,512]{1,0:T(8,128)S(1)}, bf16[1024,1024]{1,0:T(8,128)(2,1)S(1)}, bf16[102...) custom-call(bf16[4,2,80,1024]{3,2,1,0:T(8,128)(2,1)S(1)} %bitcast.82, ...), custom_call_target="tpu_custom_call" | custom-call | flops 15000000512 | tf_op jit(solution)/shard_map/pallas_call | solution.py:676
  87.7 2.5 collective-permute-done.11.refs_2_
  90.7 6.0 %collective-permute-start.12 = (bf16[128,1024]{1,0:T(8,128)(2,1)S(1)}, bf16[128,1024]{1,0:T(8,128)(2,1)S(1)}, u32[]{:S(2)}, u32[]{:S(2)}) collective-permute-start(bf16[128,1024]{1,0:T(8,128)(2,1)S(1)} %get-tuple-element.155), channel_id=1, source_target_pairs={{0,1},{1,0},{2,3},{3,2},{4,5},{5,4},{6,7},{7,6},{8,9},{9,8},{10,11... | collective-permute-start | bytes 786440 | tf_op jit(solution)/shard_map/ppermute | solution.py:495
  96.6 1.9 collective-permute-start.13
  98.5 1.4 collective-permute-start.14
  99.9 3.8 %collective-permute-done.12.refs_1_ = bf16[128,1024]{1,0:T(8,128)(2,1)S(1)} collective-permute-done((bf16[128,1024]{1,0:T(8,128)(2,1)S(1)}, bf16[128,1024]{1,0:T(8,128)(2,1)S(1)}, u32[]{:S(2)}, u32[]{:S(2)}) %collective-permute-start.12) | collective-permute-done | bytes 262176 | tf_op jit(solution)/shard_map/ppermute | solution.py:495
  103.7 6.3 %collective-permute-done.13.refs_2_ = bf16[128,1024]{1,0:T(8,128)(2,1)S(1)} collective-permute-done((bf16[128,1024]{1,0:T(8,128)(2,1)S(1)}, bf16[128,1024]{1,0:T(8,128)(2,1)S(1)}, u32[]{:S(2)}, u32[]{:S(2)}) %collective-permute-start.13) | collective-permute-done | bytes 262176 | tf_op jit(solution)/shard_map/ppermute | solution.py:495
  110.0 1.8 collective-permute-done.14.refs_3_
  114.3 1.7 collective-permute-start.16
  117.2 5.8 %collective-permute-done.15.refs_1_.refs_9_ = bf16[128,1024]{1,0:T(8,128)(2,1)S(1)} collective-permute-done((bf16[128,1024]{1,0:T(8,128)(2,1)S(1)}, bf16[128,1024]{1,0:T(8,128)(2,1)S(1)}, u32[]{:S(2)}, u32[]{:S(2)}) %collective-permute-start.15) | collective-permute-done | bytes 262176 | tf_op jit(solution)/shard_map/ppermute | solution.py:495
  123.0 4.4 %collective-permute-done.16.refs_2_.refs_10_ = bf16[128,1024]{1,0:T(8,128)(2,1)S(1)} collective-permute-done((bf16[128,1024]{1,0:T(8,128)(2,1)S(1)}, bf16[128,1024]{1,0:T(8,128)(2,1)S(1)}, u32[]{:S(2)}, u32[]{:S(2)}) %collective-permute-start.16) | collective-permute-done | bytes 262176 | tf_op jit(solution)/shard_map/ppermute | solution.py:495
  129.4 4.8 %shard_map.244 = (bf16[512,512]{1,0:T(8,128)(2,1)S(1)}, f32[512,512]{1,0:T(8,128)S(1)}, bf16[512,1024]{1,0:T(8,128)(2,1)}) custom-call(bf16[128,1024]{1,0:T(8,128)(2,1)} %copy-done.51, bf16[128,1024]{1,0:T(8,128)(2,1)} %copy-done.52, bf16[128,1024]{1,0:T(8,128)(2,1)} %collective-permute-done.20.refs_2_.refs_14_, ...), custom_call_target="tpu_custom_call" | custom-call | flops 5249999872 | tf_op jit(solution)/shard_map/pallas_call | solution.py:676
  139.3 3.8 %shard_map.245 = (bf16[512,512]{1,0:T(8,128)(2,1)S(1)}, f32[512,512]{1,0:T(8,128)S(1)}, f32[128,1024]{1,0:T(8,128)S(1)}, bf16[128,1024]{1,0:T(8,128)(2,1)S(1)}, ...) custom-call(bf16[128,1024]{1,0:T(8,128)(2,1)} %copy-done.7, bf16[128,1024]{1,0:T(8,128)(2,1)} %copy-done.48, ...), custom_call_target="tpu_custom_call" | custom-call | flops 5249999872 | tf_op jit(solution)/shard_map/pallas_call | solution.py:676
  143.1 2.1 collective-permute-start.23
  145.2 1.8 collective-permute-start.24
  147.1 3.1 collective-permute-done.23.refs_2_
  150.1 8.9 %collective-permute-done.24.refs_3_ = bf16[128,1024]{1,0:T(8,128)(2,1)S(1)} collective-permute-done((bf16[128,1024]{1,0:T(8,128)(2,1)S(1)}, bf16[128,1024]{1,0:T(8,128)(2,1)S(1)}, u32[]{:S(2)}, u32[]{:S(2)}) %collective-permute-start.24) | collective-permute-done | bytes 262176 | tf_op jit(solution)/shard_map/ppermute | solution.py:495
  159.0 5.5 %shard_map.246 = (bf16[128,1024]{1,0:T(8,128)(2,1)S(1)}, bf16[128,1024]{1,0:T(8,128)(2,1)S(1)}, bf16[128,512]{1,0:T(8,128)(2,1)S(1)}, bf16[128,1024]{1,0:T(8,128...) custom-call(f32[128,1024]{1,0:T(8,128)S(1)} %copy-done.23, ...), custom_call_target="tpu_custom_call" | custom-call | flops 8550000128 | tf_op jit(solution)/shard_map/pallas_call | solution.py:676
  165.8 1.4 collective-permute-start.30
  167.2 1.4 collective-permute-start.31
  168.6 5.2 %collective-permute-done.29.refs_1_ = bf16[128,1024]{1,0:T(8,128)(2,1)S(1)} collective-permute-done((bf16[128,1024]{1,0:T(8,128)(2,1)S(1)}, bf16[128,1024]{1,0:T(8,128)(2,1)S(1)}, u32[]{:S(2)}, u32[]{:S(2)}) %collective-permute-start.29) | collective-permute-done | bytes 262176 | tf_op jit(solution)/shard_map/ppermute | solution.py:495
  173.8 5.1 %collective-permute-done.30.refs_2_ = bf16[128,1024]{1,0:T(8,128)(2,1)S(1)} collective-permute-done((bf16[128,1024]{1,0:T(8,128)(2,1)S(1)}, bf16[128,1024]{1,0:T(8,128)(2,1)S(1)}, u32[]{:S(2)}, u32[]{:S(2)}) %collective-permute-start.30) | collective-permute-done | bytes 262176 | tf_op jit(solution)/shard_map/ppermute | solution.py:495
  178.9 1.6 collective-permute-done.31.refs_3_
  180.6 1.5 collective-permute-done.35.refs_3_.refs_7_
  182.1 1.9 shard_map.247
  185.2 2.8 collective-permute-done.42.refs_7_
  188.7 1.9 shard_map.249
  190.6 5.2 %shard_map.250 = bf16[1792,1024]{1,0:T(8,128)(2,1)} custom-call(bf16[128,1024]{1,0:T(8,128)(2,1)S(1)} %get-tuple-element.170.refs_0_, bf16[128,1024]{1,0:T(8,128)(2,1)S(1)} %collective-permute-done.29.refs_1_, bf16[128,1024]{1,0:T(8,128)(2,1)S(1)} %collective-permute-done.30.refs_2_, bf16[128,1024]{1,0:T(8,128)(2,1)S(1)} %collective-permute-done.31.refs_3_, ...), custom_call_target="tpu_custom_call" | custom-call | flops 5100000256 | tf_op jit(solution)/shard_map/pallas_call | solution.py:676
  197.7 2.1 collective-permute-start.44
  201.0 3.6 %collective-permute-done.43.refs_1_ = bf16[128,1024]{1,0:T(8,128)(2,1)S(1)} collective-permute-done((bf16[128,1024]{1,0:T(8,128)(2,1)S(1)}, bf16[128,1024]{1,0:T(8,128)(2,1)S(1)}, u32[]{:S(2)}, u32[]{:S(2)}) %collective-permute-start.43) | collective-permute-done | bytes 262176 | tf_op jit(solution)/shard_map/ppermute | solution.py:495
  204.6 1.7 collective-permute-done.44.refs_2_
  206.3 4.3 %collective-permute-done.45.refs_3_ = bf16[128,1024]{1,0:T(8,128)(2,1)S(1)} collective-permute-done((bf16[128,1024]{1,0:T(8,128)(2,1)S(1)}, bf16[128,1024]{1,0:T(8,128)(2,1)S(1)}, u32[]{:S(2)}, u32[]{:S(2)}) %collective-permute-start.45) | collective-permute-done | bytes 262176 | tf_op jit(solution)/shard_map/ppermute | solution.py:585
  211.2 1.9 collective-permute-start.46
  213.1 1.7 collective-permute-start.48
  214.8 1.7 collective-permute-start.49
  216.5 2.8 collective-permute-done.46.refs_1_
  219.3 2.7 collective-permute-start.50
  222.0 5.6 %collective-permute-done.47.refs_2_ = bf16[128,1024]{1,0:T(8,128)(2,1)S(1)} collective-permute-done((bf16[128,1024]{1,0:T(8,128)(2,1)S(1)}, bf16[128,1024]{1,0:T(8,128)(2,1)S(1)}, u32[]{:S(2)}, u32[]{:S(2)}) %collective-permute-start.47) | collective-permute-done | bytes 262176 | tf_op jit(solution)/shard_map/ppermute | solution.py:495
  230.9 8.9 %shard_map.253 = (bf16[1024,384]{1,0:T(8,128)(2,1)S(1)}, bf16[512,1024]{1,0:T(8,128)(2,1)S(1)}) custom-call(bf16[1024,384]{1,0:T(8,128)(2,1)S(1)} %copy-done.36, f32[1,1024]{1,0:T(1,128)S(1)} %get-tuple-element.173.refs_1_, f32[1024,128]{1,0:T(8,128)S(1)} %copy-done.38, bf16[1024,128]{1,0:T(8,128)(2,1)S(1)} %bitcast.79, bf16[384,1024]{1,0:T(8,128)(2,1)S(1)} %copy-done.21, ...), custom_call_target="tpu_custom_call" | custom-call | flops 13799999488 | tf_op jit(solution)/shard_map/pallas_call | solution.py:676
  240.2 2.3 collective-permute-done.53.refs_2_
  244.4 2.4 collective-permute-start.56
  247.9 4.6 %collective-permute-done.54.refs_1_ = bf16[128,1024]{1,0:T(8,128)(2,1)S(1)} collective-permute-done((bf16[128,1024]{1,0:T(8,128)(2,1)S(1)}, bf16[128,1024]{1,0:T(8,128)(2,1)S(1)}, u32[]{:S(2)}, u32[]{:S(2)}) %collective-permute-start.54) | collective-permute-done | bytes 262176 | tf_op jit(solution)/shard_map/ppermute | solution.py:495
  252.5 5.1 %collective-permute-done.55.refs_2_ = bf16[128,1024]{1,0:T(8,128)(2,1)S(1)} collective-permute-done((bf16[128,1024]{1,0:T(8,128)(2,1)S(1)}, bf16[128,1024]{1,0:T(8,128)(2,1)S(1)}, u32[]{:S(2)}, u32[]{:S(2)}) %collective-permute-start.55) | collective-permute-done | bytes 262176 | tf_op jit(solution)/shard_map/ppermute | solution.py:495
  257.6 1.4 shard_map.256
  259.0 3.6 %all-to-all-start.1 = ((bf16[16,96,128]{2,1,0:T(8,128)(2,1)}), bf16[16,96,128]{2,1,0:T(8,128)(2,1)S(1)}, u32[]{:S(2)}, u32[]{:S(2)}) async-start(bf16[16,96,128]{2,1,0:T(8,128)(2,1)} %get-tuple-element.218), calls=%async_computation.1 | async-start | bytes 786432 | tf_op jit(solution)/shard_map/all_to_all | solution.py:1658
  262.6 3.7 %collective-permute-start.64 = (bf16[64,1024]{1,0:T(8,128)(2,1)S(1)}, bf16[64,1024]{1,0:T(8,128)(2,1)S(1)}, u32[]{:S(2)}, u32[]{:S(2)}) collective-permute-start(bf16[64,1024]{1,0:T(8,128)(2,1)S(1)} %get-tuple-element.226), channel_id=1, source_target_pairs={{1,0},{5,1},{16,2},{20,3},{19,4},{23,5},{2,6},{6,7},{17,8},{21,9},... | collective-permute-start | bytes 393224 | tf_op jit(solution)/shard_map/ppermute | solution.py:1848
  266.3 2.8 collective-permute-start.66
  270.6 3.3 %collective-permute-start.65 = (bf16[128,1024]{1,0:T(8,128)(2,1)S(1)}, bf16[128,1024]{1,0:T(8,128)(2,1)S(1)}, u32[]{:S(2)}, u32[]{:S(2)}) collective-permute-start(bf16[128,1024]{1,0:T(8,128)(2,1)S(1)} %get-tuple-element.227), channel_id=1, source_target_pairs={{4,0},{2,1},{7,2},{17,3},{22,4},{0,5},{5,6},{3,7},{20,8},{18,9},{2... | collective-permute-start | bytes 786440 | tf_op jit(solution)/shard_map/ppermute | solution.py:1848
  275.2 3.1 collective-permute-start.59
  278.3 6.6 %collective-permute-done.66.refs_3_ = bf16[64,1024]{1,0:T(8,128)(2,1)S(1)} collective-permute-done((bf16[64,1024]{1,0:T(8,128)(2,1)S(1)}, bf16[64,1024]{1,0:T(8,128)(2,1)S(1)}, u32[]{:S(2)}, u32[]{:S(2)}) %collective-permute-start.66) | collective-permute-done | bytes 131104 | tf_op jit(solution)/shard_map/ppermute | solution.py:1848
  285.7 3.1 collective-permute-start.57
  288.8 2.2 collective-permute-start.58
  291.0 3.5 %collective-permute-start.68 = (f32[128,1024]{1,0:T(8,128)S(1)}, f32[128,1024]{1,0:T(8,128)S(1)}, u32[]{:S(2)}, u32[]{:S(2)}) collective-permute-start(f32[128,1024]{1,0:T(8,128)S(1)} %get-tuple-element.234.refs_0_), channel_id=1, source_target_pairs={{0,16},{16,0},{1,17},{17,1},{2,18},{18,2},{3,19},{19,3},{4,20},{20... | collective-permute-start | bytes 1572872 | tf_op jit(solution)/shard_map/ppermute | solution.py:495
  300.0 1.4 collective-permute-start.69
  306.7 2.1 add_bitcast_fusion
  (267 shorter events, 58.7 us)
Async XLA Ops:
  7.2 80.5 %all-gather.3.cloned.1.call-start = ((), (), s32[]{:S(2)}) async-start(), calls=%async_computation.3 | async-start | bytes 1671168 | tf_op jit(solution)/shard_map/all_gather | solution.py:1693
  12.4 36.5 %all-to-all-start = ((bf16[16,64,128]{2,1,0:T(8,128)(2,1)}), bf16[16,64,128]{2,1,0:T(8,128)(2,1)S(1)}, u32[]{:S(2)}, u32[]{:S(2)}) async-start(bf16[16,64,128]{2,1,0:T(8,128)(2,1)} %get-tuple-element.134), calls=%async_computation | async-start | bytes 524288 | tf_op jit(solution)/shard_map/all_to_all | solution.py:1658
  20.7 108.0 %all-gather.5.cloned.1.call-start = ((), (), s32[]{:S(2)}) async-start(), calls=%async_computation.4 | async-start | bytes 2621440 | tf_op jit(solution)/shard_map/all_gather | solution.py:1757
  20.9 9.4 %collective-permute-start = (bf16[80,1024]{1,0:T(8,128)(2,1)S(1)}, bf16[80,1024]{1,0:T(8,128)(2,1)S(1)}, u32[]{:S(2)}, u32[]{:S(2)}) collective-permute-start(bf16[80,1024]{1,0:T(8,128)(2,1)S(1)} %get-tuple-element.136), channel_id=1, source_target_pairs={{0,0},{4,4},{8,16},{12,20},{16,8},{20,12},{24,24},{28,28},{1,1},{5... | collective-permute-start | bytes 491528 | tf_op jit(solution)/shard_map/ppermute | solution.py:1716
  21.7 9.4 %collective-permute-start.1 = (bf16[80,1024]{1,0:T(8,128)(2,1)S(1)}, bf16[80,1024]{1,0:T(8,128)(2,1)S(1)}, u32[]{:S(2)}, u32[]{:S(2)}) collective-permute-start(bf16[80,1024]{1,0:T(8,128)(2,1)S(1)} %get-tuple-element.137), channel_id=1, source_target_pairs={{0,4},{4,0},{8,20},{12,16},{16,12},{20,8},{24,28},{28,24},{1,5},{5... | collective-permute-start | bytes 491528 | tf_op jit(solution)/shard_map/ppermute | solution.py:1716
  24.5 24.4 %collective-permute-start.4 = (bf16[128,1024]{1,0:T(8,128)(2,1)}, bf16[128,1024]{1,0:T(8,128)(2,1)}, u32[]{:S(2)}, u32[]{:S(2)}) collective-permute-start(bf16[128,1024]{1,0:T(8,128)(2,1)} %dynamic-slice_bitcast_fusion), channel_id=1, source_target_pairs={{0,0},{1,6},{2,3},{3,21},{4,18},{5,4},{6,1},{7,7},{8,16},{9,22},{1... | collective-permute-start | bytes 786440 | tf_op jit(solution)/shard_map/ppermute | solution.py:1726
  28.1 20.1 %collective-permute-start.5 = (bf16[64,1024]{1,0:T(8,128)(2,1)S(1)}, bf16[64,1024]{1,0:T(8,128)(2,1)S(1)}, u32[]{:S(2)}, u32[]{:S(2)}) collective-permute-start(bf16[64,1024]{1,0:T(8,128)(2,1)S(1)} %dynamic-slice_bitcast_fusion.1), channel_id=1, source_target_pairs={{0,1},{1,5},{2,16},{3,20},{4,19},{5,23},{6,2},{7,6},{8,17},{9,21},... | collective-permute-start | bytes 393224 | tf_op jit(solution)/shard_map/ppermute | solution.py:1726
  30.3 11.0 %collective-permute-start.2 = (bf16[144,1024]{1,0:T(8,128)(2,1)S(1)}, bf16[144,1024]{1,0:T(8,128)(2,1)S(1)}, u32[]{:S(2)}, u32[]{:S(2)}) collective-permute-start(bf16[144,1024]{1,0:T(8,128)(2,1)S(1)} %pad_maximum_fusion.2), channel_id=1, source_target_pairs={{0,1},{1,0},{2,3},{3,2},{4,5},{5,4},{6,7},{7,6},{8,9},{9,8},{10,11... | collective-permute-start | bytes 884744 | tf_op jit(solution)/shard_map/ppermute | solution.py:495
  31.1 9.5 %collective-permute-start.3 = (bf16[80,1024]{1,0:T(8,128)(2,1)S(1)}, bf16[80,1024]{1,0:T(8,128)(2,1)S(1)}, u32[]{:S(2)}, u32[]{:S(2)}) collective-permute-start(bf16[80,1024]{1,0:T(8,128)(2,1)S(1)} %collective-permute-done.1), channel_id=1, source_target_pairs={{0,2},{2,0},{1,3},{3,1},{4,6},{6,4},{5,7},{7,5},{8,10},{10,8},{9,1... | collective-permute-start | bytes 491528 | tf_op jit(solution)/shard_map/ppermute | solution.py:495
  48.9 20.4 %collective-permute-start.6 = (bf16[160,1024]{1,0:T(8,128)(2,1)}, bf16[160,1024]{1,0:T(8,128)(2,1)S(1)}, u32[]{:S(2)}, u32[]{:S(2)}) collective-permute-start(bf16[160,1024]{1,0:T(8,128)(2,1)} %pad_maximum_fusion), channel_id=1, source_target_pairs={{0,1},{1,0},{2,3},{3,2},{4,5},{5,4},{6,7},{7,6},{8,9},{9,8},{10,11... | collective-permute-start | bytes 983048 | tf_op jit(solution)/shard_map/ppermute | solution.py:495
  48.9 20.4 %collective-permute-start.7 = (bf16[224,1024]{1,0:T(8,128)(2,1)}, bf16[224,1024]{1,0:T(8,128)(2,1)S(1)}, u32[]{:S(2)}, u32[]{:S(2)}) collective-permute-start(bf16[224,1024]{1,0:T(8,128)(2,1)} %maximum_maximum_fusion.1), channel_id=1, source_target_pairs={{0,2},{2,0},{1,3},{3,1},{4,6},{6,4},{5,7},{7,5},{8,10},{10,8},{9,1... | collective-permute-start | bytes 1376264 | tf_op jit(solution)/shard_map/ppermute | solution.py:495
  51.2 18.2 %collective-permute-start.8 = (bf16[128,1024]{1,0:T(8,128)(2,1)}, bf16[128,1024]{1,0:T(8,128)(2,1)S(1)}, u32[]{:S(2)}, u32[]{:S(2)}) collective-permute-start(bf16[128,1024]{1,0:T(8,128)(2,1)} %dynamic-slice_bitcast_fusion), channel_id=1, source_target_pairs={{0,4},{1,2},{2,7},{3,17},{4,22},{5,0},{6,5},{7,3},{8,20},{9,18},{1... | collective-permute-start | bytes 786440 | tf_op jit(solution)/shard_map/ppermute | solution.py:1726
  52.3 17.1 %collective-permute-start.9 = (bf16[64,1024]{1,0:T(8,128)(2,1)}, bf16[64,1024]{1,0:T(8,128)(2,1)S(1)}, u32[]{:S(2)}, u32[]{:S(2)}) collective-permute-start(bf16[64,1024]{1,0:T(8,128)(2,1)} %copy-done.47), channel_id=1, source_target_pairs={{0,5},{1,1},{2,20},{3,16},{4,23},{5,19},{6,6},{7,2},{8,21},{9,17},... | collective-permute-start | bytes 393224 | tf_op jit(solution)/shard_map/ppermute | solution.py:1726
  72.8 201.1 %reduce-scatter.2.cloned.1.call-start = ((), (), s32[]{:S(2)}) async-start(), calls=%async_computation.5 | async-start | bytes 4587520 | tf_op jit(solution)/shard_map/reduce_scatter | solution.py:1792
  90.7 13.1 %collective-permute-start.12 = (bf16[128,1024]{1,0:T(8,128)(2,1)S(1)}, bf16[128,1024]{1,0:T(8,128)(2,1)S(1)}, u32[]{:S(2)}, u32[]{:S(2)}) collective-permute-start(bf16[128,1024]{1,0:T(8,128)(2,1)S(1)} %get-tuple-element.155), channel_id=1, source_target_pairs={{0,1},{1,0},{2,3},{3,2},{4,5},{5,4},{6,7},{7,6},{8,9},{9,8},{10,11... | collective-permute-start | bytes 786440 | tf_op jit(solution)/shard_map/ppermute | solution.py:495
  96.6 13.4 %collective-permute-start.13 = (bf16[128,1024]{1,0:T(8,128)(2,1)S(1)}, bf16[128,1024]{1,0:T(8,128)(2,1)S(1)}, u32[]{:S(2)}, u32[]{:S(2)}) collective-permute-start(bf16[128,1024]{1,0:T(8,128)(2,1)S(1)} %get-tuple-element.156), channel_id=1, source_target_pairs={{0,2},{2,0},{1,3},{3,1},{4,6},{6,4},{5,7},{7,5},{8,10},{10,8},{9,1... | collective-permute-start | bytes 786440 | tf_op jit(solution)/shard_map/ppermute | solution.py:495
  98.5 13.3 %collective-permute-start.14 = (bf16[128,1024]{1,0:T(8,128)(2,1)S(1)}, bf16[128,1024]{1,0:T(8,128)(2,1)S(1)}, u32[]{:S(2)}, u32[]{:S(2)}) collective-permute-start(bf16[128,1024]{1,0:T(8,128)(2,1)S(1)} %get-tuple-element.157), channel_id=1, source_target_pairs={{0,3},{1,2},{2,1},{3,0},{4,7},{5,6},{6,5},{7,4},{8,11},{9,10},{10,... | collective-permute-start | bytes 786440 | tf_op jit(solution)/shard_map/ppermute | solution.py:585
  113.7 9.2 %collective-permute-start.15 = (bf16[128,1024]{1,0:T(8,128)(2,1)S(1)}, bf16[128,1024]{1,0:T(8,128)(2,1)S(1)}, u32[]{:S(2)}, u32[]{:S(2)}) collective-permute-start(bf16[128,1024]{1,0:T(8,128)(2,1)S(1)} %get-tuple-element.160.refs_0_.refs_8_), channel_id=1, source_target_pairs={{0,1},{1,0},{2,3},{3,2},{4,5},{5,4},{6,7},{7,6},{8,9},{9,8},{10,11... | collective-permute-start | bytes 786440 | tf_op jit(solution)/shard_map/ppermute | solution.py:495
  114.3 13.0 %collective-permute-start.16 = (bf16[128,1024]{1,0:T(8,128)(2,1)S(1)}, bf16[128,1024]{1,0:T(8,128)(2,1)S(1)}, u32[]{:S(2)}, u32[]{:S(2)}) collective-permute-start(bf16[128,1024]{1,0:T(8,128)(2,1)S(1)} %get-tuple-element.160.refs_0_.refs_8_), channel_id=1, source_target_pairs={{0,2},{2,0},{1,3},{3,1},{4,6},{6,4},{5,7},{7,5},{8,10},{10,8},{9,1... | collective-permute-start | bytes 786440 | tf_op jit(solution)/shard_map/ppermute | solution.py:495
  116.0 11.3 %collective-permute-start.17 = (bf16[128,1024]{1,0:T(8,128)(2,1)S(1)}, bf16[128,1024]{1,0:T(8,128)(2,1)S(1)}, u32[]{:S(2)}, u32[]{:S(2)}) collective-permute-start(bf16[128,1024]{1,0:T(8,128)(2,1)S(1)} %get-tuple-element.160.refs_0_.refs_8_), channel_id=1, source_target_pairs={{0,3},{1,2},{2,1},{3,0},{4,7},{5,6},{6,5},{7,4},{8,11},{9,10},{10,... | collective-permute-start | bytes 786440 | tf_op jit(solution)/shard_map/ppermute | solution.py:585
  117.2 10.6 %collective-permute-start.18 = (bf16[128,1024]{1,0:T(8,128)(2,1)S(1)}, bf16[128,1024]{1,0:T(8,128)(2,1)S(1)}, u32[]{:S(2)}, u32[]{:S(2)}) collective-permute-start(bf16[128,1024]{1,0:T(8,128)(2,1)S(1)} %get-tuple-element.160.refs_0_.refs_8_), channel_id=1, source_target_pairs={{0,16},{16,0},{1,17},{17,1},{2,18},{18,2},{3,19},{19,3},{4,20},{20... | collective-permute-start | bytes 786440 | tf_op jit(solution)/shard_map/ppermute | solution.py:495
  122.9 5.7 %collective-permute-start.19 = (bf16[128,1024]{1,0:T(8,128)(2,1)S(1)}, bf16[128,1024]{1,0:T(8,128)(2,1)S(1)}, u32[]{:S(2)}, u32[]{:S(2)}) collective-permute-start(bf16[128,1024]{1,0:T(8,128)(2,1)S(1)} %collective-permute-done.15.refs_1_.refs_9_), channel_id=1, source_target_pairs={{0,16},{16,0},{1,17},{17,1},{2,18},{18,2},{3,19},{19,3},{4,20},{20... | collective-permute-start | bytes 786440 | tf_op jit(solution)/shard_map/ppermute | solution.py:495
  136.1 11.0 %collective-permute-start.26 = (bf16[1024,768]{1,0:T(8,128)(2,1)S(1)}, bf16[1024,768]{1,0:T(8,128)(2,1)}, u32[]{:S(2)}, u32[]{:S(2)}) collective-permute-start(bf16[1024,768]{1,0:T(8,128)(2,1)S(1)} %copy-done.3), channel_id=1, source_target_pairs={{0,16},{16,0},{1,17},{17,1},{2,18},{18,2},{3,19},{19,3},{4,20},{20... | collective-permute-start | bytes 4718600 | tf_op jit(solution)/shard_map/ppermute | solution.py:495
  137.5 9.5 %collective-permute-start.27 = (bf16[128,1024]{1,0:T(8,128)(2,1)S(1)}, bf16[128,1024]{1,0:T(8,128)(2,1)S(1)}, u32[]{:S(2)}, u32[]{:S(2)}) collective-permute-start(bf16[128,1024]{1,0:T(8,128)(2,1)S(1)} %get-tuple-element.267), channel_id=1, source_target_pairs={{0,0},{4,4},{8,16},{12,20},{16,8},{20,12},{24,24},{28,28},{1,1},{5... | collective-permute-start | bytes 786440 | tf_op jit(solution)/shard_map/ppermute | solution.py:1766
  138.7 8.4 %collective-permute-start.28 = (bf16[128,1024]{1,0:T(8,128)(2,1)S(1)}, bf16[128,1024]{1,0:T(8,128)(2,1)S(1)}, u32[]{:S(2)}, u32[]{:S(2)}) collective-permute-start(bf16[128,1024]{1,0:T(8,128)(2,1)S(1)} %get-tuple-element.266), channel_id=1, source_target_pairs={{0,4},{4,0},{8,20},{12,16},{16,12},{20,8},{24,28},{28,24},{1,5},{5... | collective-permute-start | bytes 786440 | tf_op jit(solution)/shard_map/ppermute | solution.py:1766
  143.1 7.0 %collective-permute-start.23 = (bf16[128,1024]{1,0:T(8,128)(2,1)S(1)}, bf16[128,1024]{1,0:T(8,128)(2,1)S(1)}, u32[]{:S(2)}, u32[]{:S(2)}) collective-permute-start(bf16[128,1024]{1,0:T(8,128)(2,1)S(1)} %get-tuple-element.163), channel_id=1, source_target_pairs={{0,1},{1,0},{2,3},{3,2},{4,5},{5,4},{6,7},{7,6},{8,9},{9,8},{10,11... | collective-permute-start | bytes 786440 | tf_op jit(solution)/shard_map/ppermute | solution.py:495
  145.2 13.8 %collective-permute-start.24 = (bf16[128,1024]{1,0:T(8,128)(2,1)S(1)}, bf16[128,1024]{1,0:T(8,128)(2,1)S(1)}, u32[]{:S(2)}, u32[]{:S(2)}) collective-permute-start(bf16[128,1024]{1,0:T(8,128)(2,1)S(1)} %get-tuple-element.164), channel_id=1, source_target_pairs={{0,2},{2,0},{1,3},{3,1},{4,6},{6,4},{5,7},{7,5},{8,10},{10,8},{9,1... | collective-permute-start | bytes 786440 | tf_op jit(solution)/shard_map/ppermute | solution.py:495
  147.1 11.9 %collective-permute-start.25 = (bf16[128,1024]{1,0:T(8,128)(2,1)S(1)}, bf16[128,1024]{1,0:T(8,128)(2,1)S(1)}, u32[]{:S(2)}, u32[]{:S(2)}) collective-permute-start(bf16[128,1024]{1,0:T(8,128)(2,1)S(1)} %get-tuple-element.165), channel_id=1, source_target_pairs={{0,3},{1,2},{2,1},{3,0},{4,7},{5,6},{6,5},{7,4},{8,11},{9,10},{10,... | collective-permute-start | bytes 786440 | tf_op jit(solution)/shard_map/ppermute | solution.py:585
  164.6 9.2 %collective-permute-start.29 = (bf16[128,1024]{1,0:T(8,128)(2,1)S(1)}, bf16[128,1024]{1,0:T(8,128)(2,1)S(1)}, u32[]{:S(2)}, u32[]{:S(2)}) collective-permute-start(bf16[128,1024]{1,0:T(8,128)(2,1)S(1)} %get-tuple-element.170.refs_0_), channel_id=1, source_target_pairs={{0,1},{1,0},{2,3},{3,2},{4,5},{5,4},{6,7},{7,6},{8,9},{9,8},{10,11... | collective-permute-start | bytes 786440 | tf_op jit(solution)/shard_map/ppermute | solution.py:495
  165.8 13.1 %collective-permute-start.30 = (bf16[128,1024]{1,0:T(8,128)(2,1)S(1)}, bf16[128,1024]{1,0:T(8,128)(2,1)S(1)}, u32[]{:S(2)}, u32[]{:S(2)}) collective-permute-start(bf16[128,1024]{1,0:T(8,128)(2,1)S(1)} %get-tuple-element.170.refs_0_), channel_id=1, source_target_pairs={{0,2},{2,0},{1,3},{3,1},{4,6},{6,4},{5,7},{7,5},{8,10},{10,8},{9,1... | collective-permute-start | bytes 786440 | tf_op jit(solution)/shard_map/ppermute | solution.py:495
  167.2 13.4 %collective-permute-start.31 = (bf16[128,1024]{1,0:T(8,128)(2,1)S(1)}, bf16[128,1024]{1,0:T(8,128)(2,1)S(1)}, u32[]{:S(2)}, u32[]{:S(2)}) collective-permute-start(bf16[128,1024]{1,0:T(8,128)(2,1)S(1)} %get-tuple-element.170.refs_0_), channel_id=1, source_target_pairs={{0,3},{1,2},{2,1},{3,0},{4,7},{5,6},{6,5},{7,4},{8,11},{9,10},{10,... | collective-permute-start | bytes 786440 | tf_op jit(solution)/shard_map/ppermute | solution.py:585
  168.6 12.0 %collective-permute-start.32 = (bf16[128,1024]{1,0:T(8,128)(2,1)S(1)}, bf16[128,1024]{1,0:T(8,128)(2,1)S(1)}, u32[]{:S(2)}, u32[]{:S(2)}) collective-permute-start(bf16[128,1024]{1,0:T(8,128)(2,1)S(1)} %get-tuple-element.170.refs_0_), channel_id=1, source_target_pairs={{0,16},{16,0},{1,17},{17,1},{2,18},{18,2},{3,19},{19,3},{4,20},{20... | collective-permute-start | bytes 786440 | tf_op jit(solution)/shard_map/ppermute | solution.py:495
  173.8 6.8 %collective-permute-start.33 = (bf16[128,1024]{1,0:T(8,128)(2,1)S(1)}, bf16[128,1024]{1,0:T(8,128)(2,1)S(1)}, u32[]{:S(2)}, u32[]{:S(2)}) collective-permute-start(bf16[128,1024]{1,0:T(8,128)(2,1)S(1)} %collective-permute-done.29.refs_1_), channel_id=1, source_target_pairs={{0,16},{16,0},{1,17},{17,1},{2,18},{18,2},{3,19},{19,3},{4,20},{20... | collective-permute-start | bytes 786440 | tf_op jit(solution)/shard_map/ppermute | solution.py:495
  184.0 4.7 %collective-permute-start.38 = (bf16[512,1024]{1,0:T(8,128)(2,1)S(1)}, bf16[512,1024]{1,0:T(8,128)(2,1)S(1)}, u32[]{:S(2)}, u32[]{:S(2)}) collective-permute-start(bf16[512,1024]{1,0:T(8,128)(2,1)S(1)} %get-tuple-element.178), channel_id=1, source_target_pairs={{0,16},{16,0},{1,17},{17,1},{2,18},{18,2},{3,19},{19,3},{4,20},{20... | collective-permute-start | bytes 3145736 | tf_op jit(solution)/shard_map/ppermute | solution.py:495
  184.2 3.8 %collective-permute-start.39 = (bf16[128,1024]{1,0:T(8,128)(2,1)S(1)}, bf16[128,1024]{1,0:T(8,128)(2,1)S(1)}, u32[]{:S(2)}, u32[]{:S(2)}) collective-permute-start(bf16[128,1024]{1,0:T(8,128)(2,1)S(1)} %get-tuple-element.179.refs_0_), channel_id=1, source_target_pairs={{0,16},{16,0},{1,17},{17,1},{2,18},{18,2},{3,19},{19,3},{4,20},{20... | collective-permute-start | bytes 786440 | tf_op jit(solution)/shard_map/ppermute | solution.py:495
  195.9 5.0 %collective-permute-start.36 = (bf16[64,1024]{1,0:T(8,128)(2,1)S(1)}, bf16[64,1024]{1,0:T(8,128)(2,1)S(1)}, u32[]{:S(2)}, u32[]{:S(2)}) collective-permute-start(bf16[64,1024]{1,0:T(8,128)(2,1)S(1)} %get-tuple-element.279), channel_id=1, source_target_pairs={{4,0},{0,4},{20,8},{16,12},{12,16},{8,20},{28,24},{24,28},{5,1},{1... | collective-permute-start | bytes 393224 | tf_op jit(solution)/shard_map/ppermute | solution.py:545
  196.4 4.5 %collective-permute-start.37 = (bf16[64,1024]{1,0:T(8,128)(2,1)S(1)}, bf16[64,1024]{1,0:T(8,128)(2,1)S(1)}, u32[]{:S(2)}, u32[]{:S(2)}) collective-permute-start(bf16[64,1024]{1,0:T(8,128)(2,1)S(1)} %get-tuple-element.278), channel_id=1, source_target_pairs={{0,0},{4,4},{16,8},{20,12},{8,16},{12,20},{24,24},{28,28},{1,1},{5... | collective-permute-start | bytes 393224 | tf_op jit(solution)/shard_map/ppermute | solution.py:545
  197.0 7.6 %collective-permute-start.43 = (bf16[128,1024]{1,0:T(8,128)(2,1)S(1)}, bf16[128,1024]{1,0:T(8,128)(2,1)S(1)}, u32[]{:S(2)}, u32[]{:S(2)}) collective-permute-start(bf16[128,1024]{1,0:T(8,128)(2,1)S(1)} %get-tuple-element.185), channel_id=1, source_target_pairs={{0,1},{1,0},{2,3},{3,2},{4,5},{5,4},{6,7},{7,6},{8,9},{9,8},{10,11... | collective-permute-start | bytes 786440 | tf_op jit(solution)/shard_map/ppermute | solution.py:495
  197.7 8.5 %collective-permute-start.44 = (bf16[128,1024]{1,0:T(8,128)(2,1)S(1)}, bf16[128,1024]{1,0:T(8,128)(2,1)S(1)}, u32[]{:S(2)}, u32[]{:S(2)}) collective-permute-start(bf16[128,1024]{1,0:T(8,128)(2,1)S(1)} %get-tuple-element.186), channel_id=1, source_target_pairs={{0,2},{2,0},{1,3},{3,1},{4,6},{6,4},{5,7},{7,5},{8,10},{10,8},{9,1... | collective-permute-start | bytes 786440 | tf_op jit(solution)/shard_map/ppermute | solution.py:495
  199.9 10.7 %collective-permute-start.45 = (bf16[128,1024]{1,0:T(8,128)(2,1)S(1)}, bf16[128,1024]{1,0:T(8,128)(2,1)S(1)}, u32[]{:S(2)}, u32[]{:S(2)}) collective-permute-start(bf16[128,1024]{1,0:T(8,128)(2,1)S(1)} %get-tuple-element.187), channel_id=1, source_target_pairs={{0,3},{1,2},{2,1},{3,0},{4,7},{5,6},{6,5},{7,4},{8,11},{9,10},{10,... | collective-permute-start | bytes 786440 | tf_op jit(solution)/shard_map/ppermute | solution.py:585
  211.2 8.1 %collective-permute-start.46 = (bf16[128,1024]{1,0:T(8,128)(2,1)S(1)}, bf16[128,1024]{1,0:T(8,128)(2,1)S(1)}, u32[]{:S(2)}, u32[]{:S(2)}) collective-permute-start(bf16[128,1024]{1,0:T(8,128)(2,1)S(1)} %get-tuple-element.197.refs_0_), channel_id=1, source_target_pairs={{0,1},{1,0},{2,3},{3,2},{4,5},{5,4},{6,7},{7,6},{8,9},{9,8},{10,11... | collective-permute-start | bytes 786440 | tf_op jit(solution)/shard_map/ppermute | solution.py:495
  213.1 14.5 %collective-permute-start.47 = (bf16[128,1024]{1,0:T(8,128)(2,1)S(1)}, bf16[128,1024]{1,0:T(8,128)(2,1)S(1)}, u32[]{:S(2)}, u32[]{:S(2)}) collective-permute-start(bf16[128,1024]{1,0:T(8,128)(2,1)S(1)} %get-tuple-element.197.refs_0_), channel_id=1, source_target_pairs={{0,2},{2,0},{1,3},{3,1},{4,6},{6,4},{5,7},{7,5},{8,10},{10,8},{9,1... | collective-permute-start | bytes 786440 | tf_op jit(solution)/shard_map/ppermute | solution.py:495
  213.1 15.0 %collective-permute-start.48 = (bf16[128,1024]{1,0:T(8,128)(2,1)S(1)}, bf16[128,1024]{1,0:T(8,128)(2,1)S(1)}, u32[]{:S(2)}, u32[]{:S(2)}) collective-permute-start(bf16[128,1024]{1,0:T(8,128)(2,1)S(1)} %get-tuple-element.197.refs_0_), channel_id=1, source_target_pairs={{0,3},{1,2},{2,1},{3,0},{4,7},{5,6},{6,5},{7,4},{8,11},{9,10},{10,... | collective-permute-start | bytes 786440 | tf_op jit(solution)/shard_map/ppermute | solution.py:585
  214.8 13.4 %collective-permute-start.49 = (bf16[128,1024]{1,0:T(8,128)(2,1)S(1)}, bf16[128,1024]{1,0:T(8,128)(2,1)S(1)}, u32[]{:S(2)}, u32[]{:S(2)}) collective-permute-start(bf16[128,1024]{1,0:T(8,128)(2,1)S(1)} %get-tuple-element.197.refs_0_), channel_id=1, source_target_pairs={{0,16},{16,0},{1,17},{17,1},{2,18},{18,2},{3,19},{19,3},{4,20},{20... | collective-permute-start | bytes 786440 | tf_op jit(solution)/shard_map/ppermute | solution.py:495
  219.3 8.8 %collective-permute-start.50 = (bf16[128,1024]{1,0:T(8,128)(2,1)S(1)}, bf16[128,1024]{1,0:T(8,128)(2,1)S(1)}, u32[]{:S(2)}, u32[]{:S(2)}) collective-permute-start(bf16[128,1024]{1,0:T(8,128)(2,1)S(1)} %collective-permute-done.46.refs_1_), channel_id=1, source_target_pairs={{0,16},{16,0},{1,17},{17,1},{2,18},{18,2},{3,19},{19,3},{4,20},{20... | collective-permute-start | bytes 786440 | tf_op jit(solution)/shard_map/ppermute | solution.py:495
  243.3 9.2 %collective-permute-start.54 = (bf16[128,1024]{1,0:T(8,128)(2,1)S(1)}, bf16[128,1024]{1,0:T(8,128)(2,1)S(1)}, u32[]{:S(2)}, u32[]{:S(2)}) collective-permute-start(bf16[128,1024]{1,0:T(8,128)(2,1)S(1)} %get-tuple-element.202), channel_id=1, source_target_pairs={{0,1},{1,0},{2,3},{3,2},{4,5},{5,4},{6,7},{7,6},{8,9},{9,8},{10,11... | collective-permute-start | bytes 786440 | tf_op jit(solution)/shard_map/ppermute | solution.py:495
  243.5 14.0 %collective-permute-start.55 = (bf16[128,1024]{1,0:T(8,128)(2,1)S(1)}, bf16[128,1024]{1,0:T(8,128)(2,1)S(1)}, u32[]{:S(2)}, u32[]{:S(2)}) collective-permute-start(bf16[128,1024]{1,0:T(8,128)(2,1)S(1)} %get-tuple-element.203), channel_id=1, source_target_pairs={{0,2},{2,0},{1,3},{3,1},{4,6},{6,4},{5,7},{7,5},{8,10},{10,8},{9,1... | collective-permute-start | bytes 786440 | tf_op jit(solution)/shard_map/ppermute | solution.py:495
  244.4 13.2 %collective-permute-start.56 = (bf16[128,1024]{1,0:T(8,128)(2,1)S(1)}, bf16[128,1024]{1,0:T(8,128)(2,1)S(1)}, u32[]{:S(2)}, u32[]{:S(2)}) collective-permute-start(bf16[128,1024]{1,0:T(8,128)(2,1)S(1)} %get-tuple-element.204), channel_id=1, source_target_pairs={{0,3},{1,2},{2,1},{3,0},{4,7},{5,6},{6,5},{7,4},{8,11},{9,10},{10,... | collective-permute-start | bytes 786440 | tf_op jit(solution)/shard_map/ppermute | solution.py:585
  259.0 38.5 %all-to-all-start.1 = ((bf16[16,96,128]{2,1,0:T(8,128)(2,1)}), bf16[16,96,128]{2,1,0:T(8,128)(2,1)S(1)}, u32[]{:S(2)}, u32[]{:S(2)}) async-start(bf16[16,96,128]{2,1,0:T(8,128)(2,1)} %get-tuple-element.218), calls=%async_computation.1 | async-start | bytes 786432 | tf_op jit(solution)/shard_map/all_to_all | solution.py:1658
  262.6 15.7 %collective-permute-start.64 = (bf16[64,1024]{1,0:T(8,128)(2,1)S(1)}, bf16[64,1024]{1,0:T(8,128)(2,1)S(1)}, u32[]{:S(2)}, u32[]{:S(2)}) collective-permute-start(bf16[64,1024]{1,0:T(8,128)(2,1)S(1)} %get-tuple-element.226), channel_id=1, source_target_pairs={{1,0},{5,1},{16,2},{20,3},{19,4},{23,5},{2,6},{6,7},{17,8},{21,9},... | collective-permute-start | bytes 393224 | tf_op jit(solution)/shard_map/ppermute | solution.py:1848
  266.3 18.7 %collective-permute-start.66 = (bf16[64,1024]{1,0:T(8,128)(2,1)S(1)}, bf16[64,1024]{1,0:T(8,128)(2,1)S(1)}, u32[]{:S(2)}, u32[]{:S(2)}) collective-permute-start(bf16[64,1024]{1,0:T(8,128)(2,1)S(1)} %get-tuple-element.228), channel_id=1, source_target_pairs={{5,0},{1,1},{20,2},{16,3},{23,4},{19,5},{6,6},{2,7},{21,8},{17,9},... | collective-permute-start | bytes 393224 | tf_op jit(solution)/shard_map/ppermute | solution.py:1848
  269.9 15.8 %collective-permute-start.63 = (bf16[128,1024]{1,0:T(8,128)(2,1)S(1)}, bf16[128,1024]{1,0:T(8,128)(2,1)S(1)}, u32[]{:S(2)}, u32[]{:S(2)}) collective-permute-start(bf16[128,1024]{1,0:T(8,128)(2,1)S(1)} %get-tuple-element.225), channel_id=1, source_target_pairs={{0,0},{6,1},{3,2},{21,3},{18,4},{4,5},{1,6},{7,7},{16,8},{22,9},{1... | collective-permute-start | bytes 786440 | tf_op jit(solution)/shard_map/ppermute | solution.py:1848
  270.6 18.2 %collective-permute-start.65 = (bf16[128,1024]{1,0:T(8,128)(2,1)S(1)}, bf16[128,1024]{1,0:T(8,128)(2,1)S(1)}, u32[]{:S(2)}, u32[]{:S(2)}) collective-permute-start(bf16[128,1024]{1,0:T(8,128)(2,1)S(1)} %get-tuple-element.227), channel_id=1, source_target_pairs={{4,0},{2,1},{7,2},{17,3},{22,4},{0,5},{5,6},{3,7},{20,8},{18,9},{2... | collective-permute-start | bytes 786440 | tf_op jit(solution)/shard_map/ppermute | solution.py:1848
  275.2 15.8 %collective-permute-start.59 = (bf16[64,1280]{1,0:T(8,128)(2,1)S(1)}, bf16[64,1280]{1,0:T(8,128)(2,1)S(1)}, u32[]{:S(2)}, u32[]{:S(2)}) collective-permute-start(bf16[64,1280]{1,0:T(8,128)(2,1)S(1)} %get-tuple-element.220), channel_id=1, source_target_pairs={{0,1},{1,0},{2,3},{3,2},{4,5},{5,4},{6,7},{7,6},{8,9},{9,8},{10,11... | collective-permute-start | bytes 491528 | tf_op jit(solution)/shard_map/ppermute | solution.py:495
  278.3 16.1 %collective-permute-start.60 = (bf16[64,1280]{1,0:T(8,128)(2,1)S(1)}, bf16[64,1280]{1,0:T(8,128)(2,1)S(1)}, u32[]{:S(2)}, u32[]{:S(2)}) collective-permute-start(bf16[64,1280]{1,0:T(8,128)(2,1)S(1)} %get-tuple-element.221), channel_id=1, source_target_pairs={{0,2},{2,0},{1,3},{3,1},{4,6},{6,4},{5,7},{7,5},{8,10},{10,8},{9,1... | collective-permute-start | bytes 491528 | tf_op jit(solution)/shard_map/ppermute | solution.py:495
  284.9 10.7 %collective-permute-start.61 = (bf16[64,1280]{1,0:T(8,128)(2,1)S(1)}, bf16[64,1280]{1,0:T(8,128)(2,1)S(1)}, u32[]{:S(2)}, u32[]{:S(2)}) collective-permute-start(bf16[64,1280]{1,0:T(8,128)(2,1)S(1)} %get-tuple-element.222), channel_id=1, source_target_pairs={{0,3},{1,2},{2,1},{3,0},{4,7},{5,6},{6,5},{7,4},{8,11},{9,10},{10,... | collective-permute-start | bytes 491528 | tf_op jit(solution)/shard_map/ppermute | solution.py:585
  285.7 12.5 %collective-permute-start.57 = (bf16[64,1024]{1,0:T(8,128)(2,1)}, bf16[64,1024]{1,0:T(8,128)(2,1)}, u32[]{:S(2)}, u32[]{:S(2)}) collective-permute-start(bf16[64,1024]{1,0:T(8,128)(2,1)} %get-tuple-element.273), channel_id=1, source_target_pairs={{4,0},{0,4},{20,8},{16,12},{12,16},{8,20},{28,24},{24,28},{5,1},{1... | collective-permute-start | bytes 393224 | tf_op jit(solution)/shard_map/ppermute | solution.py:545
  288.8 9.4 %collective-permute-start.58 = (bf16[64,1024]{1,0:T(8,128)(2,1)}, bf16[64,1024]{1,0:T(8,128)(2,1)}, u32[]{:S(2)}, u32[]{:S(2)}) collective-permute-start(bf16[64,1024]{1,0:T(8,128)(2,1)} %get-tuple-element.272), channel_id=1, source_target_pairs={{0,0},{4,4},{16,8},{20,12},{8,16},{12,20},{24,24},{28,28},{1,1},{5... | collective-permute-start | bytes 393224 | tf_op jit(solution)/shard_map/ppermute | solution.py:545
  291.0 11.0 %collective-permute-start.68 = (f32[128,1024]{1,0:T(8,128)S(1)}, f32[128,1024]{1,0:T(8,128)S(1)}, u32[]{:S(2)}, u32[]{:S(2)}) collective-permute-start(f32[128,1024]{1,0:T(8,128)S(1)} %get-tuple-element.234.refs_0_), channel_id=1, source_target_pairs={{0,16},{16,0},{1,17},{17,1},{2,18},{18,2},{3,19},{19,3},{4,20},{20... | collective-permute-start | bytes 1572872 | tf_op jit(solution)/shard_map/ppermute | solution.py:495
  297.5 9.2 %collective-permute-start.67 = (f32[192,1024]{1,0:T(8,128)S(1)}, f32[192,1024]{1,0:T(8,128)}, u32[]{:S(2)}, u32[]{:S(2)}) collective-permute-start(f32[192,1024]{1,0:T(8,128)S(1)} %shard_map.260), channel_id=1, source_target_pairs={{0,16},{16,0},{1,17},{17,1},{2,18},{18,2},{3,19},{19,3},{4,20},{20... | collective-permute-start | bytes 2359304 | tf_op jit(solution)/shard_map/ppermute | solution.py:495
  297.7 3.8 %collective-permute-start.62 = (f32[80,512]{1,0:T(8,128)S(1)}, f32[80,512]{1,0:T(8,128)S(1)}, u32[]{:S(2)}, u32[]{:S(2)}) collective-permute-start(f32[80,512]{1,0:T(8,128)S(1)} %shard_map.258.refs_0_), channel_id=1, source_target_pairs={{0,16},{16,0},{1,17},{17,1},{2,18},{18,2},{3,19},{19,3},{4,20},{20... | collective-permute-start | bytes 491528 | tf_op jit(solution)/shard_map/ppermute | solution.py:495
  300.0 5.3 %collective-permute-start.69 = (bf16[64,1280]{1,0:T(8,128)(2,1)S(1)}, bf16[64,1280]{1,0:T(8,128)(2,1)S(1)}, u32[]{:S(2)}, u32[]{:S(2)}) collective-permute-start(bf16[64,1280]{1,0:T(8,128)(2,1)S(1)} %get-tuple-element.236.refs_0_), channel_id=1, source_target_pairs={{0,16},{16,0},{1,17},{17,1},{2,18},{18,2},{3,19},{19,3},{4,20},{20... | collective-permute-start | bytes 491528 | tf_op jit(solution)/shard_map/ppermute | solution.py:495
  301.5 3.9 %collective-permute-start.70 = (bf16[64,1280]{1,0:T(8,128)(2,1)S(1)}, bf16[64,1280]{1,0:T(8,128)(2,1)S(1)}, u32[]{:S(2)}, u32[]{:S(2)}) collective-permute-start(bf16[64,1280]{1,0:T(8,128)(2,1)S(1)} %collective-permute-done.59.refs_1_), channel_id=1, source_target_pairs={{0,16},{16,0},{1,17},{17,1},{2,18},{18,2},{3,19},{19,3},{4,20},{20... | collective-permute-start | bytes 491528 | tf_op jit(solution)/shard_map/ppermute | solution.py:495
  301.5 3.9 %collective-permute-start.71 = (bf16[64,1280]{1,0:T(8,128)(2,1)S(1)}, bf16[64,1280]{1,0:T(8,128)(2,1)S(1)}, u32[]{:S(2)}, u32[]{:S(2)}) collective-permute-start(bf16[64,1280]{1,0:T(8,128)(2,1)S(1)} %collective-permute-done.60.refs_2_), channel_id=1, source_target_pairs={{0,16},{16,0},{1,17},{17,1},{2,18},{18,2},{3,19},{19,3},{4,20},{20... | collective-permute-start | bytes 491528 | tf_op jit(solution)/shard_map/ppermute | solution.py:495
  (70 other events, 548.4 us)
Sparse Core Ops, SparseCore 0:
  11.4 69.8 all-gather.2
  83.5 45.1 all-gather.4
  196.0 68.1 reduce-scatter.1
